TPU v7x, 32 devices: a whole 2x2x4 slice. The times are simulated.
32 devices in a mesh: dp: 8 (over z, y), tensor: 4 (over x, core).
Axes of the slice: x: 2, y: 2, z: 4, core: 2. Of those that a mesh axis runs over, the one named last changes fastest.
Arguments:
- tokens: bfloat16 [4096, 1536], P('dp'), may hold values from -6 to 6
- document_numbers: int32 [8, 512], P('dp'), may hold values from 0 to 31, never falling along the last dimension, each value on 1 to 256 neighbouring positions
- picks: int32 [4096, 8], P('dp'), may hold values from 0 to 63, all different within a row
- drop_order: int32 [8, 4096], P('dp'), may hold values from 0 to 4095, each once within a row
- w_query: bfloat16 [1536, 1536], P('dp', 'tensor'), may hold values from -0.15625 to 0.15625
- key_matrix: bfloat16 [1536, 512], P('dp', 'tensor'), may hold values from -0.15625 to 0.15625
- value_matrix: bfloat16 [1536, 512], P('dp', 'tensor'), may hold values from -0.15625 to 0.15625
- w_out: bfloat16 [1536, 1536], P('tensor', 'dp'), may hold values from -0.625 to 0.625
- w_router: bfloat16 [1536, 64], P('dp'), may hold values from -0.078125 to 0.078125
- gain_attn: bfloat16 [1536], P('dp'), may hold values from 0.5 to 1.5
- gain_moe: bfloat16 [1536], P('dp'), may hold values from 0.5 to 1.5
- expert_gate: bfloat16 [64, 1536, 512], P('dp', None, 'tensor'), may hold values from -0.15625 to 0.15625
- expert_up: bfloat16 [64, 1536, 512], P('dp', None, 'tensor'), may hold values from -0.15625 to 0.15625
- expert_down: bfloat16 [64, 512, 1536], P('dp', 'tensor'), may hold values from -0.5 to 0.5
- cotangent: bfloat16 [4096, 1536], P('dp'), may hold values from -6 to 6
Outputs:
- mixed: bfloat16 [4096, 1536], P('dp', 'tensor')
- grad_tokens: float32 [4096, 1536], P('dp', 'tensor')
- grad_query: float32 [1536, 1536], P('dp', 'tensor')
- grad_key: float32 [1536, 512], P('dp', 'tensor')
- grad_value: float32 [1536, 512], P('dp', 'tensor')
- grad_out: float32 [1536, 1536], P('tensor', 'dp')
- grad_router: float32 [1536, 64], P('dp')
- grad_gain_attn: float32 [1536], P('dp')
- grad_gain_moe: float32 [1536], P('dp')
- grad_expert_gate: float32 [64, 1536, 512], P('dp', None, 'tensor')
- grad_expert_up: float32 [64, 1536, 512], P('dp', None, 'tensor')
- grad_expert_down: float32 [64, 512, 1536], P('dp', 'tensor')
Inputs may be any that keep to these rules, and one draw needn't show every extreme that they name: `picks`: each token names 8 different experts. `document_numbers`: segment numbers never fall along a sequence; each document has at most half of 512 tokens. `drop_order`: each row holds every number once.
All inputs are finite; a program needn't handle non-finite values.
Results may differ from a plain program's by a relative error of at most 0.018.
Values may be sent and summed in bfloat16 or wider, within the bound.
No kernel may reach another device: no remote copies, remote signals or barrier semaphores. Data moves between devices by JAX's collectives and lax.ppermute only.
A program may use at most 320 MiB of HBM per device.

v0:
```python
import jax
import jax.numpy as jnp
from jax import lax
from jax.sharding import PartitionSpec as P

HEAD_SIZE = 64


epsilon = 1e-05
negative_big = -1e30
rope_base = 10000.0


def rotary_tables(positions, head_width):
    half_width = head_width // 2
    inverse = rope_base ** (-(2.0 * jnp.arange(half_width, dtype=jnp.float32)) / head_width)
    angles = positions.astype(jnp.float32)[:, None] * inverse[None, :]
    return (jnp.cos(angles)[:, None, :], jnp.sin(angles)[:, None, :])


def apply_pair_rotation(values, cosine_values, sine_values):
    half_width = values.shape[-1] // 2
    first_half = values[..., :half_width]
    second_half = values[..., half_width:]
    return jnp.concatenate(
        [
            first_half * cosine_values - second_half * sine_values,
            second_half * cosine_values + first_half * sine_values,
        ],
        axis=-1,
    )


def unrotate_pairs(values, cosine_values, sine_values):
    half_width = values.shape[-1] // 2
    first_half = values[..., :half_width]
    second_half = values[..., half_width:]
    return jnp.concatenate(
        [
            first_half * cosine_values + second_half * sine_values,
            second_half * cosine_values - first_half * sine_values,
        ],
        axis=-1,
    )


def slot_table(chosen_rows, order_row, expert_count, capacity):
    flat_experts = chosen_rows.reshape(-1)
    pair_count = flat_experts.shape[0]
    sort_keys = flat_experts * pair_count + order_row
    ordering = jnp.argsort(sort_keys)
    sorted_experts = flat_experts[ordering]
    expert_ids = jnp.arange(expert_count, dtype=jnp.int32)
    counts = jnp.sum(
        (flat_experts[:, None] == expert_ids[None, :]).astype(jnp.int32), axis=0, dtype=jnp.int32
    )
    starts = jnp.cumsum(counts, dtype=jnp.int32) - counts
    ranks_sorted = jnp.arange(pair_count, dtype=jnp.int32) - starts[sorted_experts]
    ranks = jnp.zeros((pair_count,), jnp.int32).at[ordering].set(ranks_sorted)
    destination = jnp.where(
        ranks < capacity, flat_experts * capacity + ranks, expert_count * capacity
    )
    table = jnp.full((expert_count * capacity + 1,), pair_count, jnp.int32)
    table = table.at[destination].set(jnp.arange(pair_count, dtype=jnp.int32))
    return (table[: expert_count * capacity], destination)


def on_device(
    tokens,
    document_numbers,
    picks,
    drop_order,
    w_query,
    key_matrix,
    value_matrix,
    w_out,
    w_router,
    gain_attn,
    gain_moe,
    expert_gate,
    expert_up,
    expert_down,
    cotangent,
):
    ranks_dp = lax.axis_size("dp")
    tensor_index = lax.axis_index("tensor")
    wq, wk, wv, wo, wr, g_attn, g_moe = (
        lax.all_gather(w_query, "dp", axis=0, tiled=True),
        lax.all_gather(key_matrix, "dp", axis=0, tiled=True),
        lax.all_gather(value_matrix, "dp", axis=0, tiled=True),
        lax.all_gather(w_out, "dp", axis=1, tiled=True),
        lax.all_gather(w_router, "dp", axis=0, tiled=True),
        lax.all_gather(gain_attn, "dp", axis=0, tiled=True),
        lax.all_gather(gain_moe, "dp", axis=0, tiled=True),
    )
    tok_count, width = tokens.shape
    col_width = width // lax.axis_size("tensor")
    col_start = tensor_index * col_width
    q_heads = wq.shape[1] // HEAD_SIZE
    kv_heads = wk.shape[1] // HEAD_SIZE
    group_repeats = q_heads // kv_heads
    score_scale = HEAD_SIZE ** (-0.5)
    seg_row = document_numbers.reshape(-1)
    positions = jnp.arange(tok_count, dtype=jnp.int32)
    cosine_values, sine_values = rotary_tables(positions, HEAD_SIZE)
    x_full = tokens.astype(jnp.float32)
    r_attn = lax.rsqrt(jnp.mean(x_full * x_full, axis=-1, keepdims=True) + epsilon)
    x_hat = x_full * r_attn
    gain_one = g_attn.astype(jnp.float32)
    x_low = (x_hat * gain_one).astype(jnp.bfloat16)
    q_proj = jnp.dot(x_low, wq, preferred_element_type=jnp.float32)
    key_projected = jnp.dot(x_low, wk, preferred_element_type=jnp.float32)
    value_projected = jnp.dot(x_low, wv, preferred_element_type=jnp.float32)
    query_rotated = apply_pair_rotation(
        q_proj.reshape(tok_count, q_heads, HEAD_SIZE), cosine_values, sine_values
    ).astype(jnp.bfloat16)
    query_rotated = query_rotated.reshape(tok_count, kv_heads, group_repeats, HEAD_SIZE)
    key_rotated = apply_pair_rotation(
        key_projected.reshape(tok_count, kv_heads, HEAD_SIZE), cosine_values, sine_values
    ).astype(jnp.bfloat16)
    value_reduced = value_projected.astype(jnp.bfloat16).reshape(tok_count, kv_heads, HEAD_SIZE)
    block_rows = min(512, tok_count)
    block_count = tok_count // block_rows
    q_blocks = query_rotated.reshape(block_count, block_rows, kv_heads, group_repeats, HEAD_SIZE)
    seg_blocks = seg_row.reshape(block_count, block_rows)
    pos_blocks = positions.reshape(block_count, block_rows)

    def masked_scores(q_block, seg_block, pos_block):
        raw_scores = (
            jnp.einsum("qgrd,kgd->grqk", q_block, key_rotated, preferred_element_type=jnp.float32)
            * score_scale
        )
        allowed = (seg_block[:, None] == seg_row[None, :]) & (
            positions[None, :] <= pos_block[:, None]
        )
        return jnp.where(allowed, raw_scores, negative_big)

    def forward_block(inputs):
        q_block, seg_block, pos_block = inputs
        scores = masked_scores(q_block, seg_block, pos_block)
        highest_score = jnp.max(scores, axis=-1, keepdims=True)
        weights = jnp.exp(scores - highest_score)
        totals = jnp.sum(weights, axis=-1, keepdims=True)
        probs = (weights / totals).astype(jnp.bfloat16)
        heads_block = jnp.einsum(
            "grqk,kgd->qgrd", probs, value_reduced, preferred_element_type=jnp.float32
        )
        return (heads_block.astype(jnp.bfloat16), highest_score + jnp.log(totals))

    head_outputs, log_totals = lax.map(forward_block, (q_blocks, seg_blocks, pos_blocks))
    o_low = head_outputs.reshape(tok_count, q_heads * HEAD_SIZE)
    attn_terms = jnp.dot(o_low, wo, preferred_element_type=jnp.float32)
    attn = lax.psum(attn_terms, "tensor")
    h_full = x_full + attn
    r_moe = lax.rsqrt(jnp.mean(h_full * h_full, axis=-1, keepdims=True) + epsilon)
    h_hat = h_full * r_moe
    gain_two = g_moe.astype(jnp.float32)
    a_low = (h_hat * gain_two).astype(jnp.bfloat16)
    logits = jnp.dot(a_low, wr, preferred_element_type=jnp.float32)
    chosen = jnp.take_along_axis(logits, picks, axis=1)
    gates = jax.nn.softmax(chosen, axis=-1)
    top_count = picks.shape[1]
    experts_all = wr.shape[1]
    capacity = 9 * tok_count * top_count // (8 * experts_all)
    table, destination = slot_table(picks, drop_order.reshape(-1), experts_all, capacity)
    slot_tokens = table // top_count
    local_count = expert_gate.shape[0]
    h_cols = lax.dynamic_slice_in_dim(h_full, col_start, col_width, 1)
    d_out = cotangent.astype(jnp.float32)
    d_out_cols = lax.dynamic_slice_in_dim(d_out, col_start, col_width, 1)
    send_rows = jnp.concatenate([a_low, jnp.zeros((1, width), jnp.bfloat16)], axis=0)[slot_tokens]
    expert_in = lax.all_to_all(
        send_rows.reshape(ranks_dp, -1, width), "dp", split_axis=0, concat_axis=0, tiled=True
    )
    expert_in = expert_in.reshape(ranks_dp, local_count, capacity, width)
    gate_val = jnp.einsum(
        "sjcd,jdf->sjcf", expert_in, expert_gate, preferred_element_type=jnp.float32
    )
    up_val = jnp.einsum("sjcd,jdf->sjcf", expert_in, expert_up, preferred_element_type=jnp.float32)
    sigmoid_gate = jax.nn.sigmoid(gate_val)
    silu_gate = gate_val * sigmoid_gate
    hidden_low = (silu_gate * up_val).astype(jnp.bfloat16)
    slab_count = 4
    slab_rows = ranks_dp // slab_count
    out_pieces = []
    for slab_index in range(slab_count):
        lower = slab_index * slab_rows
        partial_out = jnp.einsum(
            "sjcf,jfd->sjcd",
            hidden_low[lower : lower + slab_rows],
            expert_down,
            preferred_element_type=jnp.float32,
        )
        out_pieces.append(
            lax.psum_scatter(
                partial_out.astype(jnp.bfloat16), "tensor", scatter_dimension=3, tiled=True
            )
        )
    expert_out = jnp.concatenate(out_pieces, axis=0).reshape(
        ranks_dp, local_count * capacity, col_width
    )
    returned = lax.all_to_all(expert_out, "dp", split_axis=0, concat_axis=0, tiled=True).reshape(
        experts_all * capacity, col_width
    )
    returned = jnp.concatenate([returned, jnp.zeros((1, col_width), jnp.bfloat16)], axis=0)
    pair_outs = returned[destination].reshape(tok_count, top_count, col_width).astype(jnp.float32)
    mixed = (h_cols + jnp.sum(gates[:, :, None] * pair_outs, axis=1)).astype(jnp.bfloat16)
    d_gate_terms = jnp.sum(pair_outs * d_out_cols[:, None, :], axis=2)
    d_pairs = (
        (gates[:, :, None] * d_out_cols[:, None, :]).astype(jnp.bfloat16).reshape(-1, col_width)
    )
    d_pairs = jnp.concatenate([d_pairs, jnp.zeros((1, col_width), jnp.bfloat16)], axis=0)
    d_send = d_pairs[table].reshape(ranks_dp, local_count * capacity, col_width)
    d_arrived = lax.all_to_all(d_send, "dp", split_axis=0, concat_axis=0, tiled=True)
    d_arrived = d_arrived.reshape(ranks_dp, local_count, capacity, col_width)
    grad_expert_gate = jnp.zeros(expert_gate.shape, jnp.float32)
    grad_expert_up = jnp.zeros(expert_up.shape, jnp.float32)
    grad_expert_down = jnp.zeros(expert_down.shape, jnp.float32)
    back_pieces = []
    for slab_index in range(slab_count):
        lower = slab_index * slab_rows
        upper = lower + slab_rows
        d_expert_out = lax.all_gather(d_arrived[lower:upper], "tensor", axis=3, tiled=True)
        d_hidden = jnp.einsum(
            "sjcd,jfd->sjcf", d_expert_out, expert_down, preferred_element_type=jnp.float32
        )
        grad_expert_down = grad_expert_down + jnp.einsum(
            "sjcf,sjcd->jfd",
            hidden_low[lower:upper],
            d_expert_out,
            preferred_element_type=jnp.float32,
        )
        slab_gate = gate_val[lower:upper]
        slab_sigmoid = sigmoid_gate[lower:upper]
        d_gate_low = (
            d_hidden * up_val[lower:upper] * slab_sigmoid * (1.0 + slab_gate * (1.0 - slab_sigmoid))
        ).astype(jnp.bfloat16)
        d_up_low = (d_hidden * silu_gate[lower:upper]).astype(jnp.bfloat16)
        slab_inputs = expert_in[lower:upper]
        grad_expert_gate = grad_expert_gate + jnp.einsum(
            "sjcd,sjcf->jdf", slab_inputs, d_gate_low, preferred_element_type=jnp.float32
        )
        grad_expert_up = grad_expert_up + jnp.einsum(
            "sjcd,sjcf->jdf", slab_inputs, d_up_low, preferred_element_type=jnp.float32
        )
        d_in_terms = jnp.einsum(
            "sjcf,jdf->sjcd", d_gate_low, expert_gate, preferred_element_type=jnp.float32
        ) + jnp.einsum("sjcf,jdf->sjcd", d_up_low, expert_up, preferred_element_type=jnp.float32)
        back_pieces.append(
            lax.psum_scatter(
                d_in_terms.astype(jnp.bfloat16), "tensor", scatter_dimension=3, tiled=True
            )
        )
    d_expert_in = jnp.concatenate(back_pieces, axis=0).reshape(
        ranks_dp, local_count * capacity, col_width
    )
    d_returned = lax.all_to_all(d_expert_in, "dp", split_axis=0, concat_axis=0, tiled=True).reshape(
        experts_all * capacity, col_width
    )
    d_returned = jnp.concatenate([d_returned, jnp.zeros((1, col_width), jnp.bfloat16)], axis=0)
    d_token_cols = jnp.sum(
        d_returned[destination].reshape(tok_count, top_count, col_width).astype(jnp.float32), axis=1
    )
    d_experts_full, d_gate_parts = (
        lax.all_gather(d_token_cols.astype(jnp.bfloat16), "tensor", axis=1, tiled=True).astype(
            d_token_cols.dtype
        ),
        lax.all_gather(d_gate_terms.astype(jnp.bfloat16), "tensor", axis=1, tiled=True).astype(
            d_gate_terms.dtype
        ),
    )
    d_gates = jnp.sum(d_gate_parts.reshape(tok_count, -1, top_count), axis=1)
    d_chosen = gates * (d_gates - jnp.sum(gates * d_gates, axis=-1, keepdims=True))
    one_hot = (picks[:, :, None] == jnp.arange(experts_all, dtype=jnp.int32)[None, None, :]).astype(
        jnp.float32
    )
    d_logits = jnp.sum(d_chosen[:, :, None] * one_hot, axis=1).astype(jnp.bfloat16)
    grad_router = jnp.dot(a_low.T, d_logits, preferred_element_type=jnp.float32)
    d_norm_moe = d_experts_full + jnp.dot(d_logits, wr.T, preferred_element_type=jnp.float32)
    grad_gain_moe = jnp.sum(d_norm_moe * h_hat, axis=0)
    d_scaled = d_norm_moe * gain_two
    d_h = d_out + r_moe * (d_scaled - h_hat * jnp.mean(d_scaled * h_hat, axis=-1, keepdims=True))
    d_h_low = d_h.astype(jnp.bfloat16)
    grad_out = jnp.dot(o_low.T, d_h_low, preferred_element_type=jnp.float32)
    d_heads = jnp.dot(d_h_low, wo.T, preferred_element_type=jnp.float32).astype(jnp.bfloat16)
    d_blocks = d_heads.reshape(block_count, block_rows, kv_heads, group_repeats, HEAD_SIZE)

    def backward_block(inputs):
        q_block, d_block, log_block, seg_block, pos_block = inputs
        scores = masked_scores(q_block, seg_block, pos_block)
        probs = jnp.exp(scores - log_block)
        d_probs = jnp.einsum(
            "qgrd,kgd->grqk", d_block, value_reduced, preferred_element_type=jnp.float32
        )
        centre = jnp.sum(probs * d_probs, axis=-1, keepdims=True)
        d_scores = (probs * (d_probs - centre)).astype(jnp.bfloat16)
        d_query = (
            jnp.einsum("grqk,kgd->qgrd", d_scores, key_rotated, preferred_element_type=jnp.float32)
            * score_scale
        )
        d_key = (
            jnp.einsum("grqk,qgrd->kgd", d_scores, q_block, preferred_element_type=jnp.float32)
            * score_scale
        )
        d_value = jnp.einsum(
            "grqk,qgrd->kgd",
            probs.astype(jnp.bfloat16),
            d_block,
            preferred_element_type=jnp.float32,
        )
        return (d_query, d_key, d_value)

    d_query_all, d_key_parts, d_value_parts = lax.map(
        backward_block, (q_blocks, d_blocks, log_totals, seg_blocks, pos_blocks)
    )
    d_query_low = unrotate_pairs(
        d_query_all.reshape(tok_count, q_heads, HEAD_SIZE), cosine_values, sine_values
    )
    d_query_low = d_query_low.astype(jnp.bfloat16).reshape(tok_count, q_heads * HEAD_SIZE)
    d_key_low = unrotate_pairs(jnp.sum(d_key_parts, axis=0), cosine_values, sine_values)
    d_key_low = d_key_low.astype(jnp.bfloat16).reshape(tok_count, kv_heads * HEAD_SIZE)
    d_value_low = (
        jnp.sum(d_value_parts, axis=0).astype(jnp.bfloat16).reshape(tok_count, kv_heads * HEAD_SIZE)
    )
    grad_query = jnp.dot(x_low.T, d_query_low, preferred_element_type=jnp.float32)
    grad_key = jnp.dot(x_low.T, d_key_low, preferred_element_type=jnp.float32)
    grad_value = jnp.dot(x_low.T, d_value_low, preferred_element_type=jnp.float32)
    d_norm_terms = (
        jnp.dot(d_query_low, wq.T, preferred_element_type=jnp.float32)
        + jnp.dot(d_key_low, wk.T, preferred_element_type=jnp.float32)
        + jnp.dot(d_value_low, wv.T, preferred_element_type=jnp.float32)
    )
    d_norm_attn = lax.psum(d_norm_terms.astype(jnp.bfloat16), "tensor").astype(jnp.float32)
    grad_gain_attn = jnp.sum(d_norm_attn * x_hat, axis=0)
    d_scaled_in = d_norm_attn * gain_one
    d_input = d_h + r_attn * (
        d_scaled_in - x_hat * jnp.mean(d_scaled_in * x_hat, axis=-1, keepdims=True)
    )
    grad_tokens = lax.dynamic_slice_in_dim(d_input, col_start, col_width, 1)
    grad_query, grad_key, grad_value, grad_out, grad_router, grad_gain_attn, grad_gain_moe = (
        lax.psum_scatter(grad_query, "dp", scatter_dimension=0, tiled=True),
        lax.psum_scatter(grad_key, "dp", scatter_dimension=0, tiled=True),
        lax.psum_scatter(grad_value, "dp", scatter_dimension=0, tiled=True),
        lax.psum_scatter(grad_out, "dp", scatter_dimension=1, tiled=True),
        lax.psum_scatter(grad_router, "dp", scatter_dimension=0, tiled=True),
        lax.psum_scatter(grad_gain_attn, "dp", scatter_dimension=0, tiled=True),
        lax.psum_scatter(grad_gain_moe, "dp", scatter_dimension=0, tiled=True),
    )
    return (
        mixed,
        grad_tokens,
        grad_query,
        grad_key,
        grad_value,
        grad_out,
        grad_router,
        grad_gain_attn,
        grad_gain_moe,
        grad_expert_gate,
        grad_expert_up,
        grad_expert_down,
    )


def solution(mesh):
    return jax.shard_map(
        on_device,
        mesh=mesh,
        in_specs=(
            P("dp", None),
            P("dp", None),
            P("dp", None),
            P("dp", None),
            P("dp", "tensor"),
            P("dp", "tensor"),
            P("dp", "tensor"),
            P("tensor", "dp"),
            P("dp", None),
            P("dp"),
            P("dp"),
            P("dp", None, "tensor"),
            P("dp", None, "tensor"),
            P("dp", "tensor", None),
            P("dp", None),
        ),
        out_specs=(
            P("dp", "tensor"),
            P("dp", "tensor"),
            P("dp", "tensor"),
            P("dp", "tensor"),
            P("dp", "tensor"),
            P("tensor", "dp"),
            P("dp", None),
            P("dp"),
            P("dp"),
            P("dp", None, "tensor"),
            P("dp", None, "tensor"),
            P("dp", "tensor", None),
        ),
        check_vma=False,
    )
```

profile of v0, /device:TPU:0, one launch (start us, length us, event | category | flops | bytes accessed | tf_op | source)
XLA Modules:
  0.0 1695.3 jit_solution(7954968163074974394)
XLA Ops:
  17.2 23.8 %all-reduce.9 = (bf16[1536]{0:T(1024)(128)(2,1)S(1)}, bf16[1536]{0:T(1024)(128)(2,1)S(1)}) all-reduce(bf16[1536]{0:T(1024)(128)(2,1)S(1)} %dynamic-update-slice, bf16[1536]{0:T(1024)(128)(2,1)S(1)} %dynamic-update-slice.1), channel_id=1, replica_groups=mesh['dp'=8,'tensor'=4] {'dp'}, use_global_device_ids=true, to_apply=%add.4 | all-reduce | flops 3072 | bytes 12288
  43.4 5.8 sort.17
  49.8 40.5 %gather_fusion = s32[4096]{0:T(1024)} fusion(s32[4096]{0:T(1024)S(1)} %reshape.322, s32[4096]{0:T(1024)S(1)} %get-tuple-element.181), kind=kCustom, calls=%fused_computation | custom fusion | bytes 49152 | tf_op jit(solution)/shard_map/gather | solution.py:52
  90.3 31.1 %all_gather.41 = bf16[1536,128]{1,0:T(8,128)(2,1)S(1)} all-gather(bf16[192,128]{1,0:T(8,128)(2,1)S(1)} %copy-done.83), channel_id=1, replica_groups=mesh['dp'=8,'tensor'=4] {'dp'}, dimensions={0}, use_global_device_ids=true | all-gather | bytes 442368 | tf_op jit(solution)/shard_map/all_gather | solution.py:89
  121.5 31.2 %all_gather.40 = bf16[1536,128]{1,0:T(8,128)(2,1)S(1)} all-gather(bf16[192,128]{1,0:T(8,128)(2,1)S(1)} %copy-done.84), channel_id=1, replica_groups=mesh['dp'=8,'tensor'=4] {'dp'}, dimensions={0}, use_global_device_ids=true | all-gather | bytes 442368 | tf_op jit(solution)/shard_map/all_gather | solution.py:90
  157.5 5.1 compare_select_fusion.1
  175.8 30.9 %all-gather = bf16[8,192,64]{1,2,0:T(8,128)(2,1)S(1)} all-gather(bf16[1,192,64]{1,2,0:T(8,128)(2,1)S(1)} %bitcast.439), channel_id=1, replica_groups=mesh['dp'=8,'tensor'=4] {'dp'}, dimensions={0}, use_global_device_ids=true | all-gather | bytes 221184 | tf_op jit(solution)/shard_map/all_gather | solution.py:92
  216.7 36.0 %select_subtract_fusion = s32[4096]{0:T(1024)} fusion(pred[4096]{0:T(1024)(128)(4,1)S(1)} %get-tuple-element.139, pred[4096]{0:T(1024)(128)(4,1)S(1)} %get-tuple-element.138, pred[4096]{0:T(1024)(128)(4,1)S(1)} %get-tuple-element.137, pred[4096]{0:T(1024)(128)(4,1)S(1)} %get-tuple-element.136, pred[4096]{0:T(1024)(128)(4,1)S(1)} %get-tuple-element.135, ...), kind=kLoop, calls=%fused_computation.278 | loop fusion | flops 237568 | bytes 266468 | tf_op jit(solution)/shard_map/sub | solution.py:58
  252.7 15.7 scatter_custom_fusion
  269.0 15.5 scatter_custom_fusion.1
  293.8 33.0 %gather_fusion.5 = f32[4096]{0:T(1024)S(1)} fusion(f32[512,64]{0,1:T(8,128)S(1)} %fusion.150, s32[4096]{0:T(1024)S(1)} %reshape.451), kind=kCustom, calls=%fused_computation.5 | custom fusion | bytes 65536 | tf_op jit(solution)/shard_map/jit(take_along_axis)/gather | solution.py:160
  331.2 15.0 gather_fusion.3
  353.3 30.0 %gather_fusion.1 = bf16[4608,1536]{1,0:T(8,128)(2,1)} fusion(bf16[513,1536]{1,0:T(8,128)(2,1)} %concatenate.43, s32[5120]{0:T(1024)S(1)} %get-tuple-element.259), kind=kCustom, calls=%fused_computation.1 | custom fusion | bytes 28329984 | tf_op jit(solution)/shard_map/gather | solution.py:171
  383.3 26.6 %all-to-all-done.2 = bf16[8,576,384]{2,1,0:T(8,128)(2,1)} async-done(((bf16[8,576,384]{2,1,0:T(8,128)(2,1)}), bf16[8,576,384]{2,1,0:T(8,128)(2,1)}, u32[]{:S(2)}, u32[]{:S(2)}) %all-to-all-start.2) | async-done | bytes 3538976 | tf_op jit(solution)/shard_map/all_to_all | solution.py:214
  409.9 41.3 %all-to-all-start = ((bf16[8,576,1536]{2,1,0:T(8,128)(2,1)}), bf16[8,576,1536]{2,1,0:T(8,128)(2,1)}, u32[]{:S(2)}, u32[]{:S(2)}) async-start(bf16[8,576,1536]{2,1,0:T(8,128)(2,1)} %bitcast.384), calls=%async_computation | async-start | bytes 28311552 | tf_op jit(solution)/shard_map/all_to_all | solution.py:172
  462.8 24.8 %all-gather.19.cloned.1.call-done = bf16[2,8,72,1536]{3,2,0,1:T(8,128)(2,1)} async-done(((bf16[2,8,72,384]{3,2,0,1:T(8,128)(2,1)}), bf16[2,8,72,1536]{3,2,0,1:T(8,128)(2,1)}) %all-gather.19.cloned.1.call-update) | async-done | bytes 3538960 | tf_op jit(solution)/shard_map/all_gather | solution.py:223
  492.6 27.3 %all-gather.17.cloned.1.call-done = bf16[2,8,72,1536]{3,2,0,1:T(8,128)(2,1)} async-done(((bf16[2,8,72,384]{3,2,0,1:T(8,128)(2,1)}), bf16[2,8,72,1536]{3,2,0,1:T(8,128)(2,1)}) %all-gather.17.cloned.1.call-update) | async-done | bytes 3538960 | tf_op jit(solution)/shard_map/all_gather | solution.py:223
  519.8 4.9 fusion.70
  524.8 27.8 %all-gather.15.cloned.1.call-done = bf16[2,8,72,1536]{3,2,0,1:T(8,128)(2,1)} async-done(((bf16[2,8,72,384]{3,2,0,1:T(8,128)(2,1)}), bf16[2,8,72,1536]{3,2,0,1:T(8,128)(2,1)}) %all-gather.15.cloned.1.call-update) | async-done | bytes 3538960 | tf_op jit(solution)/shard_map/all_gather | solution.py:223
  557.5 154.8 %all-to-all-done = bf16[8,576,1536]{2,1,0:T(8,128)(2,1)} async-done(((bf16[8,576,1536]{2,1,0:T(8,128)(2,1)}), bf16[8,576,1536]{2,1,0:T(8,128)(2,1)}, u32[]{:S(2)}, u32[]{:S(2)}) %all-to-all-start) | async-done | bytes 14155808 | tf_op jit(solution)/shard_map/all_to_all | solution.py:172
  712.3 11.2 fusion.58
  723.6 13.0 fusion.138
  736.6 7.7 fusion.107
  753.7 15.6 copy.229
  769.3 18.7 %reshape.665 = bf16[1536,1152]{1,0:T(8,128)(2,1)} reshape(bf16[1536,8,2,72]{3,2,1,0:T(2,128)(2,1)} %bitcast.395) | data formatting | bytes 7077888
  795.4 15.7 copy.235
  811.1 18.7 %reshape.671 = bf16[1536,1152]{1,0:T(8,128)(2,1)} reshape(bf16[1536,8,2,72]{3,2,1,0:T(2,128)(2,1)} %bitcast.396) | data formatting | bytes 7077888
  837.4 15.8 copy.233
  853.2 18.7 %reshape.669 = bf16[1536,1152]{1,0:T(8,128)(2,1)} reshape(bf16[1536,8,2,72]{3,2,1,0:T(2,128)(2,1)} %bitcast.397) | data formatting | bytes 7077888
  879.2 15.8 copy.231
  895.0 18.7 %reshape.667 = bf16[1536,1152]{1,0:T(8,128)(2,1)} reshape(bf16[1536,8,2,72]{3,2,1,0:T(2,128)(2,1)} %bitcast.398) | data formatting | bytes 7077888
  919.4 15.8 copy.227
  935.3 18.7 %reshape.663 = bf16[1536,1152]{1,0:T(8,128)(2,1)} reshape(bf16[1536,8,2,72]{3,2,1,0:T(2,128)(2,1)} %bitcast.399) | data formatting | bytes 7077888
  957.9 15.9 copy.225
  973.8 18.7 %reshape.661 = bf16[1536,1152]{1,0:T(8,128)(2,1)} reshape(bf16[1536,8,2,72]{3,2,1,0:T(2,128)(2,1)} %bitcast.400) | data formatting | bytes 7077888
  996.3 15.8 copy.221
  1012.2 18.7 %reshape.657 = bf16[1536,1152]{1,0:T(8,128)(2,1)} reshape(bf16[1536,8,2,72]{3,2,1,0:T(2,128)(2,1)} %bitcast.401) | data formatting | bytes 7077888
  1034.9 16.0 copy.223
  1050.9 18.7 %reshape.659 = bf16[1536,1152]{1,0:T(8,128)(2,1)} reshape(bf16[1536,8,2,72]{3,2,1,0:T(2,128)(2,1)} %bitcast.402) | data formatting | bytes 7077888
  1069.6 7.2 reshape.666
  1078.3 7.2 reshape.672
  1088.4 7.2 reshape.670
  1098.6 7.2 reshape.668
  1117.7 7.2 reshape.664
  1126.3 7.2 reshape.662
  1136.4 7.2 reshape.658
  1146.6 7.2 reshape.660
  1161.0 25.1 %all-to-all-done.3 = bf16[8,576,384]{2,1,0:T(8,128)(2,1)} async-done(((bf16[8,576,384]{2,1,0:T(8,128)(2,1)}), bf16[8,576,384]{2,1,0:T(8,128)(2,1)}, u32[]{:S(2)}, u32[]{:S(2)}) %all-to-all-start.3) | async-done | bytes 3538976 | tf_op jit(solution)/shard_map/all_to_all | solution.py:257
  1195.0 16.5 gather_fusion.4
  1215.1 51.1 %all-to-all-done.1 = bf16[8,576,384]{2,1,0:T(8,128)(2,1)} async-done(((bf16[8,576,384]{2,1,0:T(8,128)(2,1)}), bf16[8,576,384]{2,1,0:T(8,128)(2,1)}, u32[]{:S(2)}, u32[]{:S(2)}) %all-to-all-start.1) | async-done | bytes 3538976 | tf_op jit(solution)/shard_map/all_to_all | solution.py:202
  1270.3 19.2 %gather_fusion.2 = bf16[4096,384]{1,0:T(8,128)(2,1)} fusion(bf16[4609,384]{1,0:T(8,128)(2,1)} %concatenate.45, s32[4096]{0:T(1024)S(1)} %copy-done.71), kind=kCustom, calls=%fused_computation.2 | custom fusion | bytes 6307840 | tf_op jit(solution)/shard_map/gather | solution.py:206
  1289.6 6.2 fusion.5
  1295.9 5.3 all_gather.51
  1332.0 7.7 fusion.139
  1373.9 7.0 fusion.121
  1384.7 11.8 bitcast_add_fusion.3
  1396.5 11.8 bitcast_add_fusion.6
  1408.3 10.4 bitcast_add_fusion
  1422.2 5.6 fusion.20
  1427.9 35.3 %all-reduce.8 = (f32[1536]{0:T(1024)S(1)}, f32[1536]{0:T(1024)S(1)}) all-reduce(f32[1536]{0:T(1024)S(1)} %get-tuple-element.67, f32[1536]{0:T(1024)S(1)} %get-tuple-element.65), channel_id=15, replica_groups=mesh['dp'=8,'tensor'=4] {'dp'}, use_global_device_ids=true, to_apply=%region_36.37.clone | all-reduce | flops 3072 | bytes 24576
  1467.3 10.6 reduce-scatter.36.cloned.1.call-done
  1477.9 65.2 %reduce-scatter.34.cloned.1.call-done = f32[192,128]{1,0:T(8,128)} async-done(((f32[1536,128]{1,0:T(8,128)}), f32[192,128]{1,0:T(8,128)}) %reduce-scatter.34.cloned.1.call-update) | async-done | bytes 98320 | tf_op jit(solution)/shard_map/reduce_scatter | solution.py:342
  1543.1 72.5 %reduce-scatter.38.cloned.1.call-done = f32[384,192]{0,1:T(8,128)} async-done(((f32[384,1536]{0,1:T(8,128)}), f32[384,192]{0,1:T(8,128)}) %reduce-scatter.38.cloned.1.call-update) | async-done | bytes 294928 | tf_op jit(solution)/shard_map/reduce_scatter | solution.py:344
  1615.6 72.6 %reduce-scatter.32.cloned.1.call-done = f32[192,384]{1,0:T(8,128)} async-done(((f32[1536,384]{1,0:T(8,128)}), f32[192,384]{1,0:T(8,128)}) %reduce-scatter.32.cloned.1.call-update) | async-done | bytes 294928 | tf_op jit(solution)/shard_map/reduce_scatter | solution.py:341
  (391 shorter events, 257.2 us)
Async XLA Ops:
  7.2 716.4 %copy-start = (bf16[8,1536,128]{2,1,0:T(8,128)(2,1)S(1)}, bf16[8,1536,128]{2,1,0:T(8,128)(2,1)}, u32[]{:S(2)}) copy-start(bf16[8,1536,128]{2,1,0:T(8,128)(2,1)} %param.26) | copy-start | bytes 9437188
  7.2 155.4 %all-gather.9.cloned.1.call-start = ((), (), s32[]{:S(2)}) async-start(), calls=%async_computation.17 | async-start | bytes 1327104 | tf_op jit(solution)/shard_map/all_gather | solution.py:88
  7.9 163.3 %all-gather.11.cloned.1.call-start = ((), (), s32[]{:S(2)}) async-start(), calls=%async_computation.18 | async-start | bytes 1327104 | tf_op jit(solution)/shard_map/all_gather | solution.py:91
  8.7 278.6 %all-reduce.13.cloned.1.call-start = ((), (), s32[]{:S(2)}) async-start(), calls=%async_computation.19 | async-start | bytes 6291456 | tf_op jit(solution)/shard_map/psum | solution.py:153
  13.5 139.1 %copy-start.88 = (f32[512]{0:T(512)}, f32[512]{0:T(512)S(1)}, u32[]{:S(2)}) copy-start(f32[512]{0:T(512)S(1)} %add_rsqrt_fusion.1) | copy-start | bytes 6148
  41.0 111.7 %copy-start.75 = (f32[1536]{0:T(1024)}, f32[1536]{0:T(1024)S(1)}, u32[]{:S(2)}) copy-start(f32[1536]{0:T(1024)S(1)} %convert_element_type.221) | copy-start | bytes 18436
  41.0 249.1 %copy-start.72 = (f32[1536]{0:T(1024)}, f32[1536]{0:T(1024)S(1)}, u32[]{:S(2)}) copy-start(f32[1536]{0:T(1024)S(1)} %convert_element_type.228) | copy-start | bytes 18436
  49.8 40.6 %copy-start.83 = (bf16[192,128]{1,0:T(8,128)(2,1)S(1)}, bf16[192,128]{1,0:T(8,128)(2,1)}, u32[]{:S(2)}) copy-start(bf16[192,128]{1,0:T(8,128)(2,1)} %param.20) | copy-start | bytes 147460
  49.8 71.7 %copy-start.84 = (bf16[192,128]{1,0:T(8,128)(2,1)S(1)}, bf16[192,128]{1,0:T(8,128)(2,1)}, u32[]{:S(2)}) copy-start(bf16[192,128]{1,0:T(8,128)(2,1)} %param.21) | copy-start | bytes 147460
  121.5 35.0 %copy-start.24 = (bf16[1536,128]{1,0:T(8,128)(2,1)}, bf16[1536,128]{1,0:T(8,128)(2,1)S(1)}, u32[]{:S(2)}) copy-start(bf16[1536,128]{1,0:T(8,128)(2,1)S(1)} %all_gather.41) | copy-start | bytes 1179652
  155.8 11.8 copy-start.62
  156.8 9.8 copy-start.48
  156.8 9.8 copy-start.50
  157.5 9.1 copy-start.64
  171.3 4.5 copy-start.87
  175.7 38.0 %copy-start.81 = (s32[4096,1]{0,1:T(1,128)S(1)}, s32[4096,1]{0,1:T(1,128)}, u32[]{:S(2)}) copy-start(s32[4096,1]{0,1:T(1,128)} %get-tuple-element.147) | copy-start | bytes 49156
  208.7 83.3 %copy-start.46 = (bf16[1536,64]{0,1:T(8,128)(2,1)}, bf16[1536,64]{0,1:T(8,128)(2,1)S(1)}, u32[]{:S(2)}) copy-start(bf16[1536,64]{0,1:T(8,128)(2,1)S(1)} %reshape.625) | copy-start | bytes 589828
  346.2 63.7 %all-to-all-start.2 = ((bf16[8,576,384]{2,1,0:T(8,128)(2,1)}), bf16[8,576,384]{2,1,0:T(8,128)(2,1)}, u32[]{:S(2)}, u32[]{:S(2)}) async-start(bf16[8,576,384]{2,1,0:T(8,128)(2,1)} %bitcast.405), calls=%async_computation.2 | async-start | bytes 7077888 | tf_op jit(solution)/shard_map/all_to_all | solution.py:214
  409.9 302.4 %all-to-all-start = ((bf16[8,576,1536]{2,1,0:T(8,128)(2,1)}), bf16[8,576,1536]{2,1,0:T(8,128)(2,1)}, u32[]{:S(2)}, u32[]{:S(2)}) async-start(bf16[8,576,1536]{2,1,0:T(8,128)(2,1)} %bitcast.384), calls=%async_computation | async-start | bytes 28311552 | tf_op jit(solution)/shard_map/all_to_all | solution.py:172
  451.2 36.5 %all-gather.19.cloned.1.call-start = ((), (), s32[]{:S(2)}) async-start(), calls=%async_computation.23 | async-start | bytes 4423680 | tf_op jit(solution)/shard_map/all_gather | solution.py:223
  455.8 64.0 %all-gather.17.cloned.1.call-start = ((), (), s32[]{:S(2)}) async-start(), calls=%async_computation.22 | async-start | bytes 4423680 | tf_op jit(solution)/shard_map/all_gather | solution.py:223
  458.1 94.5 %all-gather.15.cloned.1.call-start = ((), (), s32[]{:S(2)}) async-start(), calls=%async_computation.21 | async-start | bytes 4423680 | tf_op jit(solution)/shard_map/all_gather | solution.py:223
  460.3 276.3 %all-gather.13.cloned.1.call-start = ((), (), s32[]{:S(2)}) async-start(), calls=%async_computation.20 | async-start | bytes 4423680 | tf_op jit(solution)/shard_map/all_gather | solution.py:223
  462.6 607.0 %reduce-scatter.48.cloned.1.call-start = ((), (), s32[]{:S(2)}) async-start(), calls=%async_computation.34 | async-start | bytes 4423680
  748.3 126.9 %copy-start.29 = (bf16[2,8,72,128]{3,2,0,1:T(8,128)(2,1)}, bf16[2,8,72,128]{3,2,0,1:T(8,128)(2,1)S(1)}, u32[]{:S(2)}) copy-start(bf16[2,8,72,128]{3,2,0,1:T(8,128)(2,1)S(1)} %get-tuple-element.164) | copy-start | bytes 884740
  788.0 290.3 %reduce-scatter.54.cloned.1.call-start = ((), (), s32[]{:S(2)}) async-start(), calls=%async_computation.37 | async-start | bytes 4423680
  829.8 258.6 %reduce-scatter.52.cloned.1.call-start = ((), (), s32[]{:S(2)}) async-start(), calls=%async_computation.36 | async-start | bytes 4423680
  871.9 226.8 %reduce-scatter.50.cloned.1.call-start = ((), (), s32[]{:S(2)}) async-start(), calls=%async_computation.35 | async-start | bytes 4423680
  913.7 203.9 %reduce-scatter.46.cloned.1.call-start = ((), (), s32[]{:S(2)}) async-start(), calls=%async_computation.33 | async-start | bytes 4423680
  954.0 172.4 %reduce-scatter.44.cloned.1.call-start = ((), (), s32[]{:S(2)}) async-start(), calls=%async_computation.32 | async-start | bytes 4423680
  992.5 144.0 %reduce-scatter.40.cloned.1.call-start = ((), (), s32[]{:S(2)}) async-start(), calls=%async_computation.30 | async-start | bytes 4423680
  1030.9 115.7 %reduce-scatter.42.cloned.1.call-start = ((), (), s32[]{:S(2)}) async-start(), calls=%async_computation.31 | async-start | bytes 4423680
  1113.1 72.9 %all-to-all-start.3 = ((bf16[8,576,384]{2,1,0:T(8,128)(2,1)}), bf16[8,576,384]{2,1,0:T(8,128)(2,1)}, u32[]{:S(2)}, u32[]{:S(2)}) async-start(bf16[8,576,384]{2,1,0:T(8,128)(2,1)} %bitcast.403), calls=%async_computation.3 | async-start | bytes 7077888 | tf_op jit(solution)/shard_map/all_to_all | solution.py:257
  1186.0 80.2 %all-to-all-start.1 = ((bf16[8,576,384]{2,1,0:T(8,128)(2,1)}), bf16[8,576,384]{2,1,0:T(8,128)(2,1)}, u32[]{:S(2)}, u32[]{:S(2)}) async-start(bf16[8,576,384]{2,1,0:T(8,128)(2,1)} %bitcast.404), calls=%async_computation.1 | async-start | bytes 7077888 | tf_op jit(solution)/shard_map/all_to_all | solution.py:202
  1190.5 115.8 %all-gather.21.cloned.1.call-start = ((), (), s32[]{:S(2)}) async-start(), calls=%async_computation.24 | async-start | bytes 1966080 | tf_op jit(solution)/shard_map/all_gather | solution.py:265
  1190.8 4.2 copy-start.71
  1214.4 206.2 %reduce-scatter.56.cloned.1.call-start = ((), (), s32[]{:S(2)}) async-start(), calls=%async_computation.38 | async-start | bytes 884736
  1270.3 19.2 %copy-start.39 = (f32[512,8]{1,0:T(8,128)S(1)}, f32[512,8]{1,0:T(8,128)}, u32[]{:S(2)}) copy-start(f32[512,8]{1,0:T(8,128)} %copy-done.38) | copy-start | bytes 49156
  1289.6 13.1 copy-start.61
  1289.6 16.8 copy-start.7
  1295.8 10.5 copy-start.47
  1305.8 116.4 %all-reduce.15.cloned.1.call-start = ((), (), s32[]{:S(2)}) async-start(), calls=%async_computation.25 | async-start | bytes 3145728 | tf_op jit(solution)/shard_map/psum | solution.py:333
  1309.1 4.3 slice-start.1
  1310.5 4.3 copy-start.12
  1323.6 154.3 %reduce-scatter.36.cloned.1.call-start = ((), (), s32[]{:S(2)}) async-start(), calls=%async_computation.28 | async-start | bytes 884736 | tf_op jit(solution)/shard_map/reduce_scatter | solution.py:343
  1325.2 218.0 %reduce-scatter.34.cloned.1.call-start = ((), (), s32[]{:S(2)}) async-start(), calls=%async_computation.27 | async-start | bytes 884736 | tf_op jit(solution)/shard_map/reduce_scatter | solution.py:342
  1326.8 288.8 %reduce-scatter.38.cloned.1.call-start = ((), (), s32[]{:S(2)}) async-start(), calls=%async_computation.29 | async-start | bytes 2654208 | tf_op jit(solution)/shard_map/reduce_scatter | solution.py:344
  1331.9 7.8 copy-start.32
  1331.9 356.3 %reduce-scatter.32.cloned.1.call-start = ((), (), s32[]{:S(2)}) async-start(), calls=%async_computation.26 | async-start | bytes 2654208 | tf_op jit(solution)/shard_map/reduce_scatter | solution.py:341
  1339.7 19.5 %copy-start.13 = (bf16[2,576,1536]{2,1,0:T(8,128)(2,1)}, bf16[2,576,1536]{2,1,0:T(8,128)(2,1)S(1)}, u32[]{:S(2)}) copy-start(bf16[2,576,1536]{2,1,0:T(8,128)(2,1)S(1)} %get-tuple-element.153) | copy-start | bytes 10616836
  1339.7 4.9 copy-start.44
  1344.6 4.9 copy-start.30
  1349.5 4.8 copy-start.43
  1354.3 4.9 copy-start.28
  1359.2 4.8 copy-start.15
  1359.2 4.8 copy-start.23
  1373.9 7.0 copy-start.17
  1384.7 11.8 copy-start.45
  1384.7 23.6 %slice-start.2 = ((s8[6291456]{0:T(1024)(128)(4,1)}), s8[4194304]{0:T(1024)(128)(4,1)S(1)}, s32[]{:S(2)}) async-start(s8[6291456]{0:T(1024)(128)(4,1)} %bitcast.393), calls=%async_computation.41 | async-start | bytes 8388608
  1396.4 11.8 slice-start.3
  1408.3 10.4 copy-start.26
  1408.3 14.0 copy-start.76
  1408.3 14.0 copy-start.89
  1422.2 266.0 %copy-start.1 = (bf16[8,1536,128]{2,1,0:T(8,128)(2,1)S(1)}, bf16[8,1536,128]{2,1,0:T(8,128)(2,1)}, u32[]{:S(2)}) copy-start(bf16[8,1536,128]{2,1,0:T(8,128)(2,1)} %param.26) | copy-start | bytes 9437188
  (56 other events, 135.8 us)
Sparse Core Ops, SparseCore 0:
  10.2 44.2 all-gather.8
  56.7 40.1 all-gather.10
  175.5 65.5 all-reduce.12
  455.9 31.7 all-gather.18
  489.1 30.7 all-gather.16
  521.8 30.7 all-gather.14
  554.2 30.7 all-gather.12
  788.1 38.3 reduce-scatter.47
  829.9 39.7 reduce-scatter.53
  872.1 40.3 reduce-scatter.51
  915.3 40.4 reduce-scatter.49
  958.7 40.3 reduce-scatter.45
  1001.9 40.4 reduce-scatter.43
  1044.8 40.3 reduce-scatter.39
  1087.8 40.3 reduce-scatter.41
  1214.5 20.6 all-gather.20
  1305.9 60.8 reduce-scatter.55
  1369.2 41.8 all-reduce.14
  1415.3 62.5 reduce-scatter.35
  1481.6 61.4 reduce-scatter.33
  1547.6 67.9 reduce-scatter.37
  1620.1 68.0 reduce-scatter.31
where the time goes:
time: 1710 us; the launch traced here: 1700 us
  local copies, waits for them, and re-layouts  602 us (35%)
  waiting for transfers between devices  560 us (33%)
  matrix products  203 us (12%)
  blocking collectives  158 us (9%)
  other arithmetic  98.3 us (6%)
  starting transfers between devices  56.9 us (3%)
  between operations  17.4 us (1%)
    unnamed x230, local copies, waits for them, and re-layouts  374 us
    all_to_all x1, waiting for transfers between devices, on_device(): lax.all_to_all(send_rows.reshape(ranks_dp, -1, width), 'dp', split_axis=0...  155 us
    all_gather x4, waiting for transfers between devices, on_device(): lax.all_gather(d_arrived[lower:upper], 'tensor', axis=3, tiled=True)  79.9 us
    reduce_scatter x1, waiting for transfers between devices, on_device(): lax.psum_scatter(grad_query, 'dp', scatter_dimension=0, tiled=True)  72.6 us
    reduce_scatter x1, waiting for transfers between devices, on_device(): lax.psum_scatter(grad_out, 'dp', scatter_dimension=1, tiled=True)  72.5 us
    reduce_scatter x1, waiting for transfers between devices, on_device(): lax.psum_scatter(grad_key, 'dp', scatter_dimension=0, tiled=True)  65.2 us
    unnamed x2, blocking collectives  59.1 us
    all_to_all x1, waiting for transfers between devices, on_device(): lax.all_to_all(expert_out, 'dp', split_axis=0, concat_axis=0, tiled=True)  51.1 us
  transfers between devices with their start and end apart: 26, of which 11 were waited for; matrix products, arithmetic and copies ran while one was open for 46% of the time, Pallas kernels for 0%

commit v1 on v0

--- a/solution.py
+++ b/solution.py
@@ -1,6 +1,11 @@
+import functools
+
 import jax
 import jax.numpy as jnp
+import numpy as np
 from jax import lax
+from jax.experimental import pallas as pl
+from jax.experimental.pallas import tpu as pltpu
 from jax.sharding import PartitionSpec as P
 
 HEAD_SIZE = 64
@@ -9,6 +14,11 @@
 epsilon = 1e-05
 negative_big = -1e30
 rope_base = 10000.0
+F32 = jnp.float32
+BF16 = jnp.bfloat16
+BLK = 256
+PAD = 80
+VMEM_LIMIT = 62 * 1024 * 1024
 
 
 def rotary_tables(positions, head_width):
@@ -362,9 +372,639 @@
     )
 
 
+def mm(a, b):
+    return jnp.dot(a, b, preferred_element_type=F32)
+
+
+def mm_nt(a, b):
+    return lax.dot_general(a, b, (((1,), (1,)), ((), ())), preferred_element_type=F32)
+
+
+def mm_tn(a, b):
+    return lax.dot_general(a, b, (((0,), (0,)), ((), ())), preferred_element_type=F32)
+
+
+def kernel_call(body, outs, ins, scratch=(), flops=0, name=None):
+    smem = pl.BlockSpec(memory_space=pltpu.SMEM)
+    vmem = pl.BlockSpec(memory_space=pltpu.VMEM)
+    nbytes = sum(int(np.prod(a.shape)) * a.dtype.itemsize for a in list(ins[1:]) + list(outs))
+    return pl.pallas_call(
+        body,
+        out_shape=[jax.ShapeDtypeStruct(o.shape, o.dtype) for o in outs],
+        in_specs=[smem] + [vmem] * (len(ins) - 1),
+        out_specs=[vmem] * len(outs),
+        scratch_shapes=list(scratch),
+        compiler_params=pltpu.CompilerParams(vmem_limit_bytes=VMEM_LIMIT),
+        cost_estimate=pl.CostEstimate(flops=int(flops), bytes_accessed=int(nbytes), transcendentals=0),
+        name=name,
+    )(*ins)
+
+
+def sds(shape, dtype):
+    return jax.ShapeDtypeStruct(shape, dtype)
+
+
+def slots_body(capacity, idx, picks_ref, order_ref, pos_ref):
+    experts, tok = pos_ref.shape
+    ids = lax.broadcasted_iota(jnp.int32, (experts, tok), 0)
+    never = 1 << 28
+    order = jnp.full((experts, tok), never, jnp.int32)
+    for k in range(picks_ref.shape[0]):
+        order = jnp.where(picks_ref[k : k + 1, :] == ids, order_ref[k : k + 1, :], order)
+    limit = jnp.zeros((experts, 1), jnp.int32)
+    step = 1
+    while step < picks_ref.shape[0] * tok:
+        step *= 2
+    while step:
+        tried = limit + step
+        count = jnp.sum((order < tried).astype(F32), axis=1, keepdims=True)
+        limit = jnp.where(count <= capacity, tried, limit)
+        step //= 2
+    kept = order < limit
+    rows = lax.broadcasted_iota(jnp.int32, (tok, tok), 0)
+    cols = lax.broadcasted_iota(jnp.int32, (tok, tok), 1)
+    before = (rows < cols).astype(F32).astype(BF16)
+    place = mm(kept.astype(F32).astype(BF16), before)
+    pos_ref[...] = jnp.where(kept, place, jnp.where(order < never, -1.0, -2.0)).astype(BF16)
+
+
+def place_body(nz, idx, *refs):
+    out = refs[-1]
+    rows = refs[0].shape[0]
+    for k in range(nz):
+        base = lax.rem(idx[1] - k + nz, nz) * 2
+        for q in range(2):
+            block = base + (idx[2] if q == 0 else 1 - idx[2])
+            out[pl.ds(pl.multiple_of(block * rows, rows), rows), :] = refs[q * nz + k][...]
+
+
+def rotate(v, cos, sin, lane_low):
+    swapped = jnp.where(lane_low, pltpu.roll(v, 96, 1), pltpu.roll(v, 32, 1))
+    return v * cos + swapped * sin
+
+
+def low_lanes(tok):
+    return lax.rem(lax.broadcasted_iota(jnp.int32, (tok, 128), 1), 64) < 32
+
+
+def attend_body(nz, idx, *refs):
+    blocks = refs[: 2 * nz]
+    x_ref, seg_row, seg_col, cos_ref, sin_ref = refs[2 * nz : 2 * nz + 5]
+    o_ref, q_ref, k_ref, v_ref, p_ref, w_ref, aux_ref, bias_ref, qkv_ref = refs[2 * nz + 5 :]
+    place_body(nz, idx, *blocks, w_ref)
+    tok, width = x_ref.shape
+    qd, kd = q_ref.shape[1], k_ref.shape[1]
+    used = qd + 2 * kd
+    aux = w_ref[:, used:].astype(F32).T
+    aux_ref[...] = aux.astype(BF16)
+    x = x_ref[...].astype(F32)
+    r1 = lax.rsqrt(jnp.mean(x * x, axis=1, keepdims=True) + epsilon)
+    x_low = (x * r1 * aux[64:65, :]).astype(BF16)
+    qkv_ref[...] = mm(x_low, w_ref[:, :used])
+    lanes = low_lanes(tok)
+    cos, sin = cos_ref[...], sin_ref[...]
+    for b in range(qd // 128):
+        rot = rotate(qkv_ref[:, b * 128 : b * 128 + 128], cos, sin, lanes).astype(BF16)
+        q_ref[:, b * 128 : b * 128 + 128] = (rot.astype(F32) * HEAD_SIZE**-0.5).astype(BF16)
+    for b in range(kd // 128):
+        rot = rotate(qkv_ref[:, qd + b * 128 : qd + b * 128 + 128], cos, sin, lanes)
+        k_ref[:, b * 128 : b * 128 + 128] = rot.astype(BF16)
+    v_ref[...] = qkv_ref[:, qd + kd :].astype(BF16)
+    rows = lax.broadcasted_iota(jnp.int32, (tok, tok), 0)
+    cols = lax.broadcasted_iota(jnp.int32, (tok, tok), 1)
+    allowed = (seg_col[...] == seg_row[...]) & (cols <= rows)
+    bias_ref[...] = jnp.where(allowed, 0.0, negative_big)
+    heads, groups = qd // HEAD_SIZE, kd // HEAD_SIZE
+    for h in range(heads):
+        g = h // (heads // groups)
+        a, b = h * HEAD_SIZE, g * HEAD_SIZE
+        s = mm_nt(q_ref[:, a : a + HEAD_SIZE], k_ref[:, b : b + HEAD_SIZE]) + bias_ref[...]
+        e = jnp.exp(s - jnp.max(s, axis=1, keepdims=True))
+        p = (e / jnp.sum(e, axis=1, keepdims=True)).astype(BF16)
+        p_ref[h] = p
+        o_ref[:, a : a + HEAD_SIZE] = mm(p, v_ref[:, b : b + HEAD_SIZE]).astype(BF16)
+
+
+def column_blocks(idx):
+    x, c = idx[3], idx[4]
+    own = [c, 2 + 2 * x + c, 2 + 2 * (1 - x) + c]
+    return own, [1 - c, 2 + 2 * x + 1 - c, 2 + 2 * (1 - x) + 1 - c]
+
+
+def out_body(idx, x_ref, o0, o1, o23, w0, w1, w23, aux_ref, h_ref, low_ref, own_ref, ring_ref):
+    attn = mm_nt(o0[...], w0[...]) + mm_nt(o1[...], w1[...])
+    attn = attn + (mm_nt(o23[0], w23[0]) + mm_nt(o23[1], w23[1]))
+    h = x_ref[...].astype(F32) + attn
+    h_ref[...] = h
+    r2 = lax.rsqrt(jnp.mean(h * h, axis=1, keepdims=True) + epsilon)
+    low_ref[...] = (h * r2 * aux_ref[64:66, :].astype(F32)[1:2, :]).astype(BF16)
+    own, _ = column_blocks(idx)
+    for m in range(3):
+        block = low_ref[:, pl.ds(pl.multiple_of(own[m] * BLK, BLK), BLK)]
+        own_ref[:, m * BLK : m * BLK + BLK] = block
+        if m < 2:
+            ring_ref[:, m * BLK : m * BLK + BLK] = block
+
+
+def masked_gates(logits, pos):
+    picked = pos > -1.5
+    shown = jnp.where(picked, logits, negative_big)
+    e = jnp.where(picked, jnp.exp(shown - jnp.max(shown, axis=0, keepdims=True)), 0.0)
+    return e / jnp.sum(e, axis=0, keepdims=True)
+
+
+def split16(v):
+    high = v.astype(BF16)
+    return high, (v - high.astype(F32)).astype(BF16)
+
+
+def experts_body(
+    local, idx, am_ref, an_ref, dm_ref, dn_ref, gu_ref, down_ref, aux_ref, sel_ref, selt_ref, slot_ref, slott_ref,
+    dxm_ref, dxn_ref, ym_ref, yn_ref, xe_ref, dy_ref, dgu_ref, hd_ref,
+    pos_s, gate_s, d0_s, acc_s, acc2_s, dgr_s, oh_s, oht_s,
+):
+    tok = am_ref.shape[1]
+    half = pos_s.shape[0] // 2
+    c = idx[4]
+    mine, theirs = column_blocks(idx)
+    parts = list(zip(mine + theirs, [0, 1, 2] * 2, [0] * 3 + [1] * 3))
+    hidden = down_ref.shape[1]
+    sel, selt = sel_ref[...], selt_ref[...]
+    for q in range(2):
+        pos_s[pl.ds(pl.multiple_of(c * half, half), half), :] = dm_ref[q, tok:, :tok]
+        pos_s[pl.ds(pl.multiple_of((1 - c) * half, half), half), :] = dn_ref[q, tok:, :tok]
+        pos = pos_s[...]
+        logits = jnp.zeros(pos.shape, F32)
+        for b, m, side in parts:
+            rows = (an_ref if side else am_ref)[q, :, m * BLK : m * BLK + BLK]
+            router = aux_ref[: pos.shape[0], pl.ds(pl.multiple_of(b * BLK, BLK), BLK)]
+            logits = logits + mm_nt(router, rows)
+        gates = masked_gates(logits, pos.astype(F32))
+        hot = (mm(sel, pos) == slot_ref[...]).astype(F32).astype(BF16)
+        oh_s[q] = hot
+        oht_s[q] = (mm_tn(pos, selt) == slott_ref[...]).astype(F32).astype(BF16)
+        high, low = split16(gates)
+        spread = (mm_nt(hot, high) + mm_nt(hot, low)) * sel.astype(F32)
+        gate = jnp.sum(spread, axis=1, keepdims=True)
+        gate_s[:, q] = gate.reshape(local, PAD, 1)
+        for b, m, side in parts:
+            rows = (an_ref if side else am_ref)[q, :, m * BLK : m * BLK + BLK]
+            xe_ref[b, :, q] = mm(hot, rows).astype(BF16).reshape(local, PAD, BLK)
+            rows = (dn_ref if side else dm_ref)[q, :tok, m * BLK : m * BLK + BLK]
+            got = mm(hot, rows)
+            d0_s[b, :, q] = got.astype(BF16).reshape(local, PAD, BLK)
+            dy_ref[b, :, q] = (got * gate).astype(BF16).reshape(local, PAD, BLK)
+    blocks = xe_ref.shape[0]
+    both = 2 * PAD
+    for j in range(local):
+        gu = jnp.zeros((both, 2 * hidden), F32)
+        t = jnp.zeros((both, hidden), F32)
+        for b in range(blocks):
+            gu = gu + mm(xe_ref[b, j].reshape(both, BLK), gu_ref[j, b * BLK : b * BLK + BLK, :])
+            t = t + mm_nt(d0_s[b, j].reshape(both, BLK), down_ref[j, :, b * BLK : b * BLK + BLK])
+        gate = gate_s[:, :][j].reshape(both, 1)
+        g, u = gu[:, :hidden], gu[:, hidden:]
+        sg = jax.nn.sigmoid(g)
+        silu = g * sg
+        hd = (silu * u).astype(BF16)
+        dhd = gate * t
+        dg = (dhd * u * sg * (1.0 + g * (1.0 - sg))).astype(BF16)
+        du = (dhd * silu).astype(BF16)
+        dgate = jnp.sum(hd.astype(F32) * t, axis=1, keepdims=True)
+        dgr_s[j] = jnp.broadcast_to(dgate, (both, dgr_s.shape[3])).reshape(2, PAD, dgr_s.shape[3])
+        hd_ref[j] = hd.reshape(2, PAD, hidden)
+        dgu_ref[j, :, :, :hidden] = dg.reshape(2, PAD, hidden)
+        dgu_ref[j, :, :, hidden:] = du.reshape(2, PAD, hidden)
+        dgu = jnp.concatenate([dg, du], axis=1)
+        for b in range(blocks):
+            y = mm(hd, down_ref[j, :, b * BLK : b * BLK + BLK])
+            acc_s[b, j] = (y.astype(BF16).astype(F32) * gate).astype(BF16).reshape(2, PAD, BLK)
+            dx = mm_nt(dgu, gu_ref[j, b * BLK : b * BLK + BLK, :])
+            acc2_s[b, j] = dx.astype(BF16).reshape(2, PAD, BLK)
+    slots = local * PAD
+    x = idx[3]
+    for q in range(2):
+        hot, hott = oh_s[q], oht_s[q]
+        for b, m, side in parts:
+            dx = mm(hott, acc2_s[b, :, q].reshape(slots, BLK)).astype(BF16)
+            (dxn_ref if side else dxm_ref)[q, :tok, m * BLK : m * BLK + BLK] = dx
+            y = mm(hott, acc_s[b, :, q].reshape(slots, BLK)).astype(BF16)
+            (yn_ref if side else ym_ref)[q, :, m * BLK : m * BLK + BLK] = y
+        weights = (dgr_s[:, :, :, :][:, q].reshape(slots, -1) * sel.astype(F32)).astype(BF16)
+        pos_s[...] = mm_tn(weights, hot).astype(BF16)
+        for ref, at in ((dxm_ref, c), (dxn_ref, 1 - c)):
+            got = pos_s[pl.ds(pl.multiple_of(at * half, half), half), :]
+            ref[q, tok:, :BLK] = got[:, :BLK]
+            ref[q, tok:, BLK : 2 * BLK] = (got[:, BLK:].astype(F32) * (1 - x).astype(F32)).astype(BF16)
+            ref[q, tok:, 2 * BLK :] = (got[:, BLK:].astype(F32) * x.astype(F32)).astype(BF16)
+
+
+def hidden_back_body(idx, fm_ref, fn_ref, h_ref, low_ref, aux_ref, pos_ref, dout_ref, o_ref, w_ref,
+                     dh_ref, do_ref, rs_ref, full_s, dg_s):
+    tok, width = h_ref.shape
+    c, experts = idx[4], pos_ref.shape[0]
+    half = experts // 2
+    mine, theirs = column_blocks(idx)
+    for ref, order in ((fm_ref, mine), (fn_ref, theirs)):
+        for m in range(3):
+            at = pl.ds(pl.multiple_of(order[m] * BLK, BLK), BLK)
+            full_s[:, at] = ref[:tok, m * BLK : m * BLK + BLK].astype(F32)
+    for ref, at in ((fm_ref, c), (fn_ref, 1 - c)):
+        at = pl.ds(pl.multiple_of(at * half, half), half)
+        dg_s[at, :BLK] = ref[tok:, :BLK].astype(F32)
+        dg_s[at, BLK:] = ref[tok:, BLK : 2 * BLK].astype(F32) + ref[tok:, 2 * BLK :].astype(F32)
+    low = low_ref[...]
+    router = aux_ref[:experts, :]
+    gates = masked_gates(mm_nt(router, low), pos_ref[...].astype(F32))
+    dgates = dg_s[...]
+    dlogits = (gates * (dgates - jnp.sum(gates * dgates, axis=0, keepdims=True))).astype(BF16)
+    h = h_ref[...]
+    r2 = lax.rsqrt(jnp.mean(h * h, axis=1, keepdims=True) + epsilon)
+    ah = h * r2
+    da = full_s[...] + mm_tn(dlogits, router)
+    gain_grad = jnp.sum(da * ah, axis=0, keepdims=True)
+    scaled = da * aux_ref[64:66, :].astype(F32)[1:2, :]
+    dh = dout_ref[...].astype(F32) + r2 * (scaled - ah * jnp.mean(scaled * ah, axis=1, keepdims=True))
+    full_s[...] = dh
+    cols = dh_ref.shape[1]
+    t = idx[3] * 2 + c
+    dh_ref[...] = full_s[:, pl.ds(pl.multiple_of(t * cols, 128), cols)]
+    dhb = dh.astype(BF16)
+    do_ref[...] = mm(dhb, w_ref[...]).astype(BF16)
+    rs_ref[:, :cols] = mm_tn(dhb, o_ref[...]).astype(BF16)
+    side = jnp.concatenate([mm(dlogits, low), gain_grad, jnp.zeros((63, width), F32)], axis=0)
+    rs_ref[:, cols:] = side.T.astype(BF16)
+
+
+def attend_back_body(idx, do_ref, p_ref, q_ref, k_ref, v_ref, w_ref, x_ref, aux_ref, cos_ref, sin_ref,
+                     rs_ref, dm_ref, dn_ref, dq_s, dqkv_s, dxn_s):
+    tok, width = x_ref.shape
+    qd, kd = q_ref.shape[1], k_ref.shape[1]
+    heads, groups = qd // HEAD_SIZE, kd // HEAD_SIZE
+    scale = HEAD_SIZE**-0.5
+    each = heads // groups
+    for g in range(groups):
+        b = g * HEAD_SIZE
+        kg, vg = k_ref[:, b : b + HEAD_SIZE], v_ref[:, b : b + HEAD_SIZE]
+        dk = jnp.zeros((tok, HEAD_SIZE), F32)
+        dv = jnp.zeros((tok, HEAD_SIZE), F32)
+        for h in range(g * each, (g + 1) * each):
+            a = h * HEAD_SIZE
+            doh = do_ref[:, a : a + HEAD_SIZE]
+            p = p_ref[h].astype(F32)
+            dp = mm_nt(doh, vg)
+            ds = (p * (dp - jnp.sum(p * dp, axis=1, keepdims=True))).astype(BF16)
+            dq_s[:, a : a + HEAD_SIZE] = mm(ds, kg) * scale
+            dk = dk + mm_tn(ds, q_ref[:, a : a + HEAD_SIZE])
+            dv = dv + mm_tn(p_ref[h], doh)
+        dq_s[:, qd + b : qd + b + HEAD_SIZE] = dk
+        dqkv_s[:, qd + kd + b : qd + kd + b + HEAD_SIZE] = dv.astype(BF16)
+    lanes = low_lanes(tok)
+    cos, sin = cos_ref[...], -sin_ref[...]
+    for b in range((qd + kd) // 128):
+        at = slice(b * 128, b * 128 + 128)
+        dqkv_s[:, at] = rotate(dq_s[:, at], cos, sin, lanes).astype(BF16)
+    used = qd + 2 * kd
+    x = x_ref[...].astype(F32)
+    r1 = lax.rsqrt(jnp.mean(x * x, axis=1, keepdims=True) + epsilon)
+    xh = x * r1
+    gain = aux_ref[64:65, :].astype(F32)
+    x_low = (xh * gain).astype(BF16)
+    dqkv = dqkv_s[...]
+    rows = width // rs_ref.shape[0]
+    grads = mm_tn(x_low, dqkv).astype(BF16)
+    dxn = mm_nt(dqkv, w_ref[:, :used])
+    gain_high, gain_low = split16(jnp.sum(dxn * xh, axis=0, keepdims=True))
+    pads = jnp.zeros((14, rows), BF16)
+    for i in range(rs_ref.shape[0]):
+        rs_ref[i, :rows, :] = grads[i * rows : i * rows + rows, :]
+        at = slice(i * rows, i * rows + rows)
+        tail = jnp.concatenate([gain_high[:, at].astype(F32), gain_low[:, at].astype(F32), pads.astype(F32)], axis=0)
+        rs_ref[i, rows:, :] = jnp.zeros((16, used), BF16)
+        rs_ref[i, rows:, :rows] = tail.astype(BF16)
+    total = jnp.sum(dxn * xh * gain, axis=1, keepdims=True)
+    high, low = split16(total)
+    lane = lax.broadcasted_iota(jnp.int32, (tok, 128), 1)
+    side = jnp.where(lane == 0, high.astype(F32), jnp.where(lane == 1, low.astype(F32), 0.0)).astype(BF16)
+    cols = width // 4
+    for i in range(4):
+        dxn_s[i] = dxn[:, i * cols : i * cols + cols].astype(BF16)
+    ix, c = idx[3], idx[4]
+    for ref, core in ((dm_ref, c), (dn_ref, 1 - c)):
+        ref[:, :cols] = dxn_s[2 * ix + core]
+        ref[:, cols : 2 * cols] = dxn_s[2 * (1 - ix) + core]
+        ref[:, 2 * cols :] = side
+
+
+def mixed_body(idx, fm_ref, fn_ref, h_ref, out_ref, full_s):
+    mine, theirs = column_blocks(idx)
+    for ref, order in ((fm_ref, mine), (fn_ref, theirs)):
+        for m in range(3):
+            at = pl.ds(pl.multiple_of(order[m] * BLK, BLK), BLK)
+            full_s[:, at] = ref[:, m * BLK : m * BLK + BLK].astype(F32)
+    cols = out_ref.shape[1]
+    at = pl.ds(pl.multiple_of((idx[3] * 2 + idx[4]) * cols, 128), cols)
+    out_ref[...] = (full_s[:, at] + h_ref[:, at]).astype(BF16)
+
+
+def expert_grads_body(count, *refs):
+    xe, dy, dgu, hd = (refs[i * count : i * count + count] for i in range(4))
+    gate_ref, up_ref, down_ref = refs[4 * count :]
+    hidden = gate_ref.shape[2]
+    rows = 2 * PAD
+
+    def join(group, b=None):
+        got = [(r[0] if b is None else r[b, 0]) for r in group]
+        return jnp.concatenate([v.reshape(rows, v.shape[-1]) for v in got], axis=0)
+
+    d_gu, hd_all = join(dgu), join(hd)
+    for b in range(xe[0].shape[0]):
+        at = slice(b * BLK, b * BLK + BLK)
+        both = mm_tn(join(xe, b), d_gu)
+        gate_ref[0, at, :] = both[:, :hidden]
+        up_ref[0, at, :] = both[:, hidden:]
+        down_ref[0, :, at] = mm_tn(hd_all, join(dy, b))
+
+
+def expert_grads(xe, dy, dgu, hd, local, width, hidden):
+    count = len(xe)
+    blocks = width // BLK
+    wide = pl.BlockSpec((blocks, 1, 2, PAD, BLK), lambda e: (0, e, 0, 0, 0))
+    specs = [wide] * (2 * count)
+    specs += [pl.BlockSpec((1, 2, PAD, 2 * hidden), lambda e: (e, 0, 0, 0))] * count
+    specs += [pl.BlockSpec((1, 2, PAD, hidden), lambda e: (e, 0, 0, 0))] * count
+    slots = count * 2 * PAD * local
+    return pl.pallas_call(
+        functools.partial(expert_grads_body, count),
+        grid=(local,),
+        out_shape=[sds((local, width, hidden), F32), sds((local, width, hidden), F32), sds((local, hidden, width), F32)],
+        in_specs=specs,
+        out_specs=[pl.BlockSpec((1, width, hidden), lambda e: (e, 0, 0))] * 2
+        + [pl.BlockSpec((1, hidden, width), lambda e: (e, 0, 0))],
+        compiler_params=pltpu.CompilerParams(vmem_limit_bytes=VMEM_LIMIT),
+        cost_estimate=pl.CostEstimate(
+            flops=6 * slots * width * hidden, bytes_accessed=slots * width * 4 + 12 * local * width * hidden, transcendentals=0
+        ),
+        name="expert_grads",
+    )(*xe, *dy, *dgu, *hd)
+
+
+def add16(a, b):
+    return (a.astype(F32) + b.astype(F32)).astype(BF16)
+
+
+def on_device_gathered(
+    tokens,
+    document_numbers,
+    picks,
+    drop_order,
+    w_query,
+    key_matrix,
+    value_matrix,
+    w_out,
+    w_router,
+    gain_attn,
+    gain_moe,
+    expert_gate,
+    expert_up,
+    expert_down,
+    cotangent,
+):
+    n_dp = lax.axis_size("dp")
+    nz = n_dp // 2
+    r, t = lax.axis_index("dp"), lax.axis_index("tensor")
+    z, y, x, c = r // 2, r % 2, t // 2, t % 2
+    idx = jnp.stack([r, z, y, x, c]).astype(jnp.int32)
+
+    def shift_z(v):
+        return lax.ppermute(v, "dp", [(i, ((i // 2 + 1) % nz) * 2 + i % 2) for i in range(n_dp)])
+
+    def swap_y(v):
+        return lax.ppermute(v, "dp", [(i, i ^ 1) for i in range(n_dp)])
+
+    def swap_x(v):
+        return lax.ppermute(v, "tensor", [(i, i ^ 2) for i in range(4)])
+
+    def swap_c(v):
+        return lax.ppermute(v, "tensor", [(i, i ^ 1) for i in range(4)])
+
+    def ring(v):
+        zs = [v]
+        for _ in range(nz - 1):
+            zs.append(shift_z(zs[-1]))
+        return zs, [swap_y(b) for b in zs]
+
+    tok, width = tokens.shape
+    rows = w_query.shape[0]
+    qd, kd = w_query.shape[1], key_matrix.shape[1]
+    used = qd + 2 * kd
+    experts = w_router.shape[1]
+    local, _, hidden = expert_gate.shape
+    capacity = 9 * tok * picks.shape[1] // (8 * experts)
+    cols = width // 4
+
+    aux = jnp.concatenate(
+        [w_router, gain_attn[:, None], gain_moe[:, None], jnp.zeros((rows, 128 - experts - 2), BF16)], axis=1
+    )
+    w_zs, w_ys = ring(jnp.concatenate([w_query, key_matrix, value_matrix, aux], axis=1))
+    wo_zs, wo_ys = ring(w_out.T)
+
+    pos = kernel_call(
+        functools.partial(slots_body, capacity),
+        [sds((experts, tok), BF16)],
+        [idx, picks.T, drop_order.reshape(tok, -1).T],
+        name="slots",
+    )[0]
+
+    half = experts // 2
+
+    def columns(v, m):
+        return lax.dynamic_slice_in_dim(v, m * BLK, BLK, 1)
+
+    mine, _ = column_blocks(idx)
+    d_own = jnp.concatenate([columns(cotangent, m) for m in mine], axis=1)
+    pos_own = jnp.concatenate(
+        [lax.dynamic_slice_in_dim(pos, c * half, half, 0), jnp.zeros((half, 3 * BLK - tok), BF16)], axis=1
+    )
+    d_own = jnp.concatenate([d_own, pos_own], axis=0)
+
+    def gather(own, ring_own):
+        zs, ys = ring(ring_own)
+        got = []
+        for k in range(nz):
+            if k == 0:
+                far = swap_x(ys[0][:, BLK:])
+                m = jnp.stack([own, jnp.concatenate([ys[0], far], axis=1)])
+            else:
+                pair = jnp.stack([zs[k], ys[k]])
+                far = swap_x(pair[:, :, BLK:])
+                m = jnp.concatenate([pair, far], axis=2)
+            got.append((m, swap_c(m)))
+        return got
+
+    d_all = gather(d_own, d_own[:, : 2 * BLK])
+
+    positions = np.arange(tok, dtype=np.float32)
+    inverse = rope_base ** (-(2.0 * np.arange(HEAD_SIZE // 2, dtype=np.float32)) / HEAD_SIZE)
+    angles = positions[:, None] * inverse.astype(np.float32)[None, :]
+    cos = jnp.asarray(np.tile(np.cos(angles), (1, 4)).astype(np.float32))
+    sin = np.sin(angles)
+    sin = jnp.asarray(np.tile(np.concatenate([-sin, sin], axis=1), (1, 2)).astype(np.float32))
+    heads = qd // HEAD_SIZE
+    seg_row = document_numbers.reshape(1, tok)
+    o, q, k, v, p, w_all, aux_t = kernel_call(
+        functools.partial(attend_body, nz),
+        [sds((tok, qd), BF16), sds((tok, qd), BF16), sds((tok, kd), BF16), sds((tok, kd), BF16),
+         sds((heads, tok, tok), BF16), sds((width, used + 128), BF16), sds((128, width), BF16)],
+        [idx, *w_zs, *w_ys, tokens, seg_row, seg_row.T, cos, sin],
+        scratch=[pltpu.VMEM((tok, tok), F32), pltpu.VMEM((tok, used), F32)],
+        flops=4e9,
+        name="attend",
+    )
+    wo = kernel_call(
+        functools.partial(place_body, nz), [sds((width, qd), BF16)], [idx, *wo_zs, *wo_ys], name="place"
+    )[0]
+    wo_x = swap_x(wo)
+    wo_c = swap_c(jnp.stack([wo, wo_x]))
+    o_x = swap_x(o)
+    o_c = swap_c(jnp.stack([o, o_x]))
+    h, low, a_own, a_ring = kernel_call(
+        out_body,
+        [sds((tok, width), F32), sds((tok, width), BF16), sds((tok, 3 * BLK), BF16), sds((tok, 2 * BLK), BF16)],
+        [idx, tokens, o, o_x, o_c, wo, wo_x, wo_c, aux_t],
+        flops=5e9,
+        name="out",
+    )
+    a_all = gather(a_own, a_ring)
+
+    gu = jnp.concatenate([expert_gate, expert_up], axis=2)
+    slot_ids = np.arange(local * PAD)
+    sel = (r * local + slot_ids[:, None] // PAD == jnp.arange(experts)[None, :]).astype(BF16)
+    slot_col = jnp.asarray((slot_ids % PAD).astype(np.float32)[:, None])
+    slot_row = jnp.asarray((slot_ids % PAD).astype(np.float32)[None, :])
+    slots = local * PAD
+    blocks = width // BLK
+    big = (blocks, local, 2, PAD, BLK)
+    done = []
+    for kk in range(nz):
+        am, an = a_all[kk]
+        dm, dn = d_all[kk]
+        done.append(
+            kernel_call(
+                functools.partial(experts_body, local),
+                [sds(dm.shape, BF16), sds(dm.shape, BF16), sds(am.shape, BF16), sds(am.shape, BF16),
+                 sds(big, BF16), sds(big, BF16), sds((local, 2, PAD, 2 * hidden), BF16), sds((local, 2, PAD, hidden), BF16)],
+                [idx, am, an, dm, dn, gu, expert_down, aux_t, sel, sel.T, slot_col, slot_row],
+                scratch=[
+                    pltpu.VMEM((experts, tok), BF16), pltpu.VMEM((local, 2, PAD, 1), F32), pltpu.VMEM(big, BF16),
+                    pltpu.VMEM(big, BF16), pltpu.VMEM(big, BF16), pltpu.VMEM((local, 2, PAD, experts), F32),
+                    pltpu.VMEM((2, slots, tok), BF16), pltpu.VMEM((2, tok, slots), BF16),
+                ],
+                flops=12e9,
+                name="experts",
+            )
+        )
+
+    def collect(parts):
+        total = None
+        for kk in list(range(1, nz)) + [0]:
+            m, n = parts[kk]
+            s = add16(m, swap_c(n))
+            own = add16(s[:, :, BLK : 2 * BLK], swap_x(s[:, :, 2 * BLK :]))
+            s = jnp.concatenate([s[:, :, :BLK], own], axis=2)
+            s = add16(s[0], swap_y(s[1])) if total is None else (
+                s[0].astype(F32) + swap_y(s[1]).astype(F32) + shift_z(total).astype(F32)
+            ).astype(BF16)
+            total = s
+        far = swap_x(total)
+        whole = jnp.concatenate([add16(total[:, :BLK], far[:, :BLK]), total[:, BLK:], far[:, BLK:]], axis=1)
+        return whole, swap_c(whole)
+
+    fm, fn = collect([d[0:2] for d in done])
+    ym, yn = collect([d[2:4] for d in done])
+    mixed = kernel_call(
+        mixed_body, [sds((tok, cols), BF16)], [idx, ym, yn, h], scratch=[pltpu.VMEM((tok, width), F32)], name="mixed"
+    )[0]
+
+    def scatter_dp(v):
+        def block(kk, yy):
+            return lax.dynamic_index_in_dim(v, ((z - kk) % nz) * 2 + yy, 0, keepdims=False)
+
+        total = None
+        for kk in list(range(1, nz)) + [0]:
+            s = block(kk, y).astype(F32) + swap_y(block(kk, 1 - y)).astype(F32)
+            if total is not None:
+                s = s + shift_z(total).astype(F32)
+            total = s.astype(BF16)
+        return s
+
+    d_h, d_o, early = kernel_call(
+        hidden_back_body,
+        [sds((tok, cols), F32), sds((tok, qd), BF16), sds((width, qd + 128), BF16)],
+        [idx, fm, fn, h, low, aux_t, pos, cotangent, o, wo],
+        scratch=[pltpu.VMEM((tok, width), F32), pltpu.VMEM((experts, tok), F32)],
+        flops=3e9,
+        name="hidden_back",
+    )
+    early = scatter_dp(early.reshape(n_dp, rows, qd + 128))
+    grad_out = early[:, :qd].T
+    grad_router = early[:, qd : qd + experts]
+    grad_gain_moe = early[:, qd + experts]
+    late, dxm, dxn = kernel_call(
+        attend_back_body,
+        [sds((n_dp, rows + 16, used), BF16), sds((tok, 2 * cols + 128), BF16), sds((tok, 2 * cols + 128), BF16)],
+        [idx, d_o, p, q, k, v, w_all, tokens, aux_t, cos, sin],
+        scratch=[pltpu.VMEM((tok, used), F32), pltpu.VMEM((tok, used), BF16), pltpu.VMEM((4, tok, cols), BF16)],
+        flops=5e9,
+        name="attend_back",
+    )
+    late = scatter_dp(late)
+    grad_query = late[:rows, :qd]
+    grad_key = late[:rows, qd : qd + kd]
+    grad_value = late[:rows, qd + kd :]
+    gain_part = late[rows, :rows] + late[rows + 1, :rows]
+    gain_part = gain_part + swap_c(gain_part)
+    grad_gain_attn = gain_part + swap_x(gain_part)
+
+    got = swap_c(dxn)
+    ours = dxm.astype(F32) + got.astype(F32)
+    mean_part = ours[:, 2 * cols] + ours[:, 2 * cols + 1]
+    high, lowp = split16(mean_part)
+    send = jnp.concatenate(
+        [ours[:, cols : 2 * cols].astype(BF16), high[:, None], lowp[:, None], jnp.zeros((tok, 126), BF16)], axis=1
+    )
+    got = swap_x(send)
+    d_norm = ours[:, :cols] + got[:, :cols].astype(F32)
+    mean = (mean_part + got[:, cols].astype(F32) + got[:, cols + 1].astype(F32))[:, None] / width
+    x_full = tokens.astype(F32)
+    r1 = lax.rsqrt(jnp.mean(x_full * x_full, axis=-1, keepdims=True) + epsilon)
+    x_cols = lax.dynamic_slice_in_dim(tokens, t * cols, cols, 1).astype(F32) * r1
+    gain_row = lax.dynamic_slice_in_dim(aux_t[64:65], t * cols, cols, 1).astype(F32)
+    grad_tokens = d_h + r1 * (d_norm * gain_row - x_cols * mean)
+
+    grad_gate, grad_up, grad_down = expert_grads(
+        [d[4] for d in done], [d[5] for d in done], [d[6] for d in done], [d[7] for d in done], local, width, hidden
+    )
+    return (
+        mixed,
+        grad_tokens,
+        grad_query,
+        grad_key,
+        grad_value,
+        grad_out,
+        grad_router,
+        grad_gain_attn,
+        grad_gain_moe,
+        grad_gate,
+        grad_up,
+        grad_down,
+    )
+
+
 def solution(mesh):
+    few = mesh.shape["tensor"] == 4 and mesh.shape["dp"] in (4, 8)
     return jax.shard_map(
-        on_device,
+        on_device_gathered if few else on_device,
         mesh=mesh,
         in_specs=(
             P("dp", None),

time: 1710 us -> 647 us (0.38)
  local copies, waits for them, and re-layouts: 602 us -> 33 us
  waiting for transfers between devices: 560 us -> 278 us
  matrix products: 203 us -> 0 us
  Pallas kernels: 0 us -> 188 us
  blocking collectives: 158 us -> 0 us
  other arithmetic: 98.3 us -> 57 us
  starting transfers between devices: 56.9 us -> 78.9 us
    unnamed x230 -> x120, local copies, waits for them, and re-layouts: 374 us -> 10.4 us
    ppermute x0 -> x100, waiting for transfers between devices: none -> 278 us  [the longest x22 111 us: swap_x(): return lax.ppermute(v, 'tensor', [(i, i ^ 2) for i in range(4)])]
    all_to_all x4 -> x0, waiting for transfers between devices: 258 us -> none  [the longest x1 155 us: on_device(): lax.all_to_all(send_rows.reshape(ranks_dp, -1, width), 'dp', split_axis=0...]
    reduce_scatter x4 -> x0, waiting for transfers between devices: 221 us -> none  [the longest x1 72.6 us: on_device(): lax.psum_scatter(grad_query, 'dp', scatter_dimension=0, tiled=True)]
    dot_general x50 -> x0, matrix products: 200 us -> none  [the longest x4 28.5 us: on_device(): jnp.einsum('sjcd,sjcf->jdf', slab_inputs, d_gate_low, preferred_element_t...]
    pallas_call x0 -> x12, Pallas kernels: none -> 188 us  [the longest x11 167 us: kernel_call(): pl.pallas_call(body, out_shape=[jax.ShapeDtypeStruct(o.shape, o.dtype) fo...]
    gather x14 -> x0, local copies, waits for them, and re-layouts: 158 us -> none  [the longest x1 40.5 us: slot_table(): sorted_experts = flat_experts[ordering]]
    all_gather x4 -> x0, blocking collectives: 98.5 us -> none  [the longest x1 31.2 us: on_device(): lax.all_gather(value_matrix, 'dp', axis=0, tiled=True)]
  transfers between devices with their start and end apart: 26 -> 100, of which waited for: 11 -> 43; matrix products, arithmetic and copies ran while one was open for 46% -> 12% of each run, Pallas kernels for 0% -> 28%
where the time goes in v1:
time: 647 us; the launch traced here: 638 us
  waiting for transfers between devices  278 us (43%)
  Pallas kernels  188 us (29%)
  starting transfers between devices  78.9 us (12%)
  other arithmetic  57 us (9%)
  local copies, waits for them, and re-layouts  33 us (5%)
    pallas_call x11, Pallas kernels, kernel_call(): pl.pallas_call(body, out_shape=[jax.ShapeDtypeStruct(o.shape, o.dtype) fo...  167 us
    ppermute x22, waiting for transfers between devices, swap_x(): return lax.ppermute(v, 'tensor', [(i, i ^ 2) for i in range(4)])  111 us
    ppermute x32, waiting for transfers between devices, swap_y(): return lax.ppermute(v, 'dp', [(i, i ^ 1) for i in range(n_dp)])  102 us
    ppermute x24, waiting for transfers between devices, shift_z(): lax.ppermute(v, 'dp', [(i, (i // 2 + 1) % nz * 2 + i % 2) for i in range(...  65.6 us
    ppermute x32, starting transfers between devices, swap_y(): return lax.ppermute(v, 'dp', [(i, i ^ 1) for i in range(n_dp)])  34 us
    ppermute x22, starting transfers between devices, swap_x(): return lax.ppermute(v, 'tensor', [(i, i ^ 2) for i in range(4)])  27.4 us
    pallas_call x1, Pallas kernels, expert_grads(): pl.pallas_call(functools.partial(expert_grads_body, count), grid=(local,)...  21.2 us
    convert_element_type x20, other arithmetic, add16(): return (a.astype(F32) + b.astype(F32)).astype(BF16)  16.2 us
  transfers between devices with their start and end apart: 100, of which 43 were waited for; matrix products, arithmetic and copies ran while one was open for 12% of the time, Pallas kernels for 28%

profile of v1, /device:TPU:0, one launch (start us, length us, event | category | flops | bytes accessed | tf_op | source)
XLA Modules:
  0.0 637.9 jit_solution(17928607341038511549)
XLA Ops:
  0.7 3.1 collective-permute-start.9
  3.8 6.1 collective-permute-done.9.refs_1_
  9.9 6.9 %collective-permute-done.10.refs_2_ = bf16[192,384]{1,0:T(8,128)(2,1)S(1)} collective-permute-done((bf16[192,384]{1,0:T(8,128)(2,1)S(1)}, bf16[192,384]{1,0:T(8,128)(2,1)S(1)}, u32[]{:S(2)}, u32[]{:S(2)}) %collective-permute-start.10) | collective-permute-done | bytes 147488 | tf_op jit(solution)/shard_map/ppermute | solution.py:780
  20.4 3.4 collective-permute-done.11.refs_3_
  31.1 2.5 place.1.w0.w_ref
  35.4 8.5 %collective-permute-done.refs_1_ = bf16[192,768]{1,0:T(8,128)(2,1)S(1)} collective-permute-done((bf16[192,768]{1,0:T(8,128)(2,1)S(1)}, bf16[192,768]{1,0:T(8,128)(2,1)S(1)}, u32[]{:S(2)}, u32[]{:S(2)}) %collective-permute-start) | collective-permute-done | bytes 294944 | tf_op jit(solution)/shard_map/ppermute | solution.py:780
  43.9 14.9 %collective-permute-done.16.w1 = bf16[1536,384]{1,0:T(8,128)(2,1)S(1)} collective-permute-done((bf16[1536,384]{1,0:T(8,128)(2,1)}, bf16[1536,384]{1,0:T(8,128)(2,1)S(1)}, u32[]{:S(2)}, u32[]{:S(2)}) %collective-permute-start.16) | collective-permute-done | bytes 1179680 | tf_op jit(solution)/shard_map/ppermute | solution.py:786
  58.9 3.4 pad_maximum_fusion
  65.5 8.1 %collective-permute-done.2.refs_3_ = bf16[192,768]{1,0:T(8,128)(2,1)} collective-permute-done((bf16[192,768]{1,0:T(8,128)(2,1)S(1)}, bf16[192,768]{1,0:T(8,128)(2,1)}, u32[]{:S(2)}, u32[]{:S(2)}) %collective-permute-start.2) | collective-permute-done | bytes 294944 | tf_op jit(solution)/shard_map/ppermute | solution.py:780
  77.6 2.7 slots.1.pos_ref
  81.5 3.5 collective-permute-done.5.refs_6_
  85.0 5.9 collective-permute-done.6.refs_7_
  90.9 10.7 %attend.1 = (bf16[512,384]{1,0:T(8,128)(2,1)}, bf16[512,384]{1,0:T(8,128)(2,1)}, bf16[512,128]{1,0:T(8,128)(2,1)}, bf16[512,128]{1,0:T(8,128)(2,1)}, bf16[6,512,...) custom-call(s32[5]{0:T(128)} %stack.113.idx, bf16[192,768]{1,0:T(8,128)(2,1)} %copy-done.28, ...), custom_call_target="tpu_custom_call" | custom-call | flops 4000000000 | bytes 11407360 | tf_op jit(solution)/shard_map/attend/pallas_call | solution.py:391
  103.6 9.0 %collective-permute-done.7.o1 = bf16[512,384]{1,0:T(8,128)(2,1)S(1)} collective-permute-done((bf16[512,384]{1,0:T(8,128)(2,1)}, bf16[512,384]{1,0:T(8,128)(2,1)S(1)}, u32[]{:S(2)}, u32[]{:S(2)}) %collective-permute-start.7) | collective-permute-done | bytes 393248 | tf_op jit(solution)/shard_map/ppermute | solution.py:786
  112.8 6.8 %collective-permute-done.33 = bf16[544,512]{1,0:T(8,128)(2,1)S(1)} collective-permute-done((bf16[544,512]{1,0:T(8,128)(2,1)}, bf16[544,512]{1,0:T(8,128)(2,1)S(1)}, u32[]{:S(2)}, u32[]{:S(2)}) %collective-permute-start.33) | collective-permute-done | bytes 557088 | tf_op jit(solution)/shard_map/ppermute | solution.py:780
  121.1 1.9 constant_dynamic-update-slice_fusion.1
  123.4 10.9 %collective-permute-done.34 = bf16[544,512]{1,0:T(8,128)(2,1)S(1)} collective-permute-done((bf16[544,512]{1,0:T(8,128)(2,1)S(1)}, bf16[544,512]{1,0:T(8,128)(2,1)S(1)}, u32[]{:S(2)}, u32[]{:S(2)}) %collective-permute-start.34) | collective-permute-done | bytes 557088 | tf_op jit(solution)/shard_map/ppermute | solution.py:780
  137.2 9.7 %out.1 = (f32[512,1536]{1,0:T(8,128)}, bf16[512,1536]{1,0:T(8,128)(2,1)}, bf16[512,768]{1,0:T(8,128)(2,1)}, bf16[512,512]{1,0:T(8,128)(2,1)}) custom-call(s32[5]{0:T(128)} %stack.113.idx, bf16[512,1536]{1,0:T(8,128)(2,1)} %x_ref.3, bf16[512,384]{1,0:T(8,128)(2,1)} %get-tuple-element.64.o0.o_ref, bf16[512,384]{1,0:T(8,128)(2,1)} %copy-done.27, ...), custom_call_target="tpu_custom_call" | custom-call | flops 5000000000 | bytes 14286848 | tf_op jit(solution)/shard_map/out/pallas_call | solution.py:391
  147.5 3.8 constant_dynamic-update-slice_fusion.gu_ref
  154.4 4.9 collective-permute-done.45
  161.3 6.5 %collective-permute-done.18 = bf16[512,512]{1,0:T(8,128)(2,1)S(1)} collective-permute-done((bf16[512,512]{1,0:T(8,128)(2,1)}, bf16[512,512]{1,0:T(8,128)(2,1)S(1)}, u32[]{:S(2)}, u32[]{:S(2)}) %collective-permute-start.18) | collective-permute-done | bytes 524320 | tf_op jit(solution)/shard_map/ppermute | solution.py:783
  174.1 14.4 %collective-permute-done.19 = bf16[512,256]{1,0:T(8,128)(2,1)S(1)} collective-permute-done((bf16[512,256]{1,0:T(8,128)(2,1)S(1)}, bf16[512,256]{1,0:T(8,128)(2,1)S(1)}, u32[]{:S(2)}, u32[]{:S(2)}) %collective-permute-start.19) | collective-permute-done | bytes 262176 | tf_op jit(solution)/shard_map/ppermute | solution.py:786
  192.7 11.5 %collective-permute-done.36 = bf16[544,512]{1,0:T(8,128)(2,1)S(1)} collective-permute-done((bf16[544,512]{1,0:T(8,128)(2,1)}, bf16[544,512]{1,0:T(8,128)(2,1)S(1)}, u32[]{:S(2)}, u32[]{:S(2)}) %collective-permute-start.36) | collective-permute-done | bytes 557088 | tf_op jit(solution)/shard_map/ppermute | solution.py:783
  206.9 5.0 collective-permute-done.42
  213.9 2.3 pad_maximum_fusion.4.dm_ref
  216.3 2.1 collective-permute-start.43
  218.4 2.3 pad_maximum_fusion.3.dm_ref
  222.0 6.0 collective-permute-done.37
  228.5 2.3 pad_maximum_fusion.2.dm_ref
  230.9 5.7 collective-permute-done.43
  240.7 28.3 %experts.4 = (bf16[2,544,768]{2,1,0:T(8,128)(2,1)}, bf16[2,544,768]{2,1,0:T(8,128)(2,1)}, bf16[2,512,768]{2,1,0:T(8,128)(2,1)}, bf16[2,512,768]{2,1,0:T(8,128)(2...) custom-call(s32[5]{0:T(128)} %stack.113.idx, ...), custom_call_target="tpu_custom_call" | custom-call | flops 12000000000 | bytes 31822848 | tf_op jit(solution)/shard_map/experts/pallas_call | solution.py:391
  269.1 2.3 pad_maximum_fusion.6.am_ref
  272.0 28.6 %experts.7 = (bf16[2,544,768]{2,1,0:T(8,128)(2,1)}, bf16[2,544,768]{2,1,0:T(8,128)(2,1)}, bf16[2,512,768]{2,1,0:T(8,128)(2,1)}, bf16[2,512,768]{2,1,0:T(8,128)(2...) custom-call(s32[5]{0:T(128)} %stack.113.idx, ...), custom_call_target="tpu_custom_call" | custom-call | flops 12000000000 | bytes 31822848 | tf_op jit(solution)/shard_map/experts/pallas_call | solution.py:391
  301.2 28.5 %experts.6 = (bf16[2,544,768]{2,1,0:T(8,128)(2,1)}, bf16[2,544,768]{2,1,0:T(8,128)(2,1)}, bf16[2,512,768]{2,1,0:T(8,128)(2,1)}, bf16[2,512,768]{2,1,0:T(8,128)(2...) custom-call(s32[5]{0:T(128)} %stack.113.idx, ...), custom_call_target="tpu_custom_call" | custom-call | flops 12000000000 | bytes 31822848 | tf_op jit(solution)/shard_map/experts/pallas_call | solution.py:391
  330.2 2.3 add_convert_fusion.7
  335.2 1.9 add_convert_fusion.3
  339.3 28.8 %experts.5 = (bf16[2,544,768]{2,1,0:T(8,128)(2,1)}, bf16[2,544,768]{2,1,0:T(8,128)(2,1)}, bf16[2,512,768]{2,1,0:T(8,128)(2,1)}, bf16[2,512,768]{2,1,0:T(8,128)(2...) custom-call(s32[5]{0:T(128)} %stack.113.idx, ...), custom_call_target="tpu_custom_call" | custom-call | flops 12000000000 | bytes 31822848 | tf_op jit(solution)/shard_map/experts/pallas_call | solution.py:391
  370.5 2.0 add_convert_fusion.4
  373.9 1.9 add_convert_fusion
  379.1 14.4 %collective-permute-done.58 = bf16[2,512,256]{2,1,0:T(8,128)(2,1)S(1)} collective-permute-done((bf16[2,512,256]{2,1,0:T(8,128)(2,1)S(1)}, bf16[2,512,256]{2,1,0:T(8,128)(2,1)S(1)}, u32[]{:S(2)}, u32[]{:S(2)}) %collective-permute-start.58) | collective-permute-done | bytes 524320 | tf_op jit(solution)/shard_map/ppermute | solution.py:786
  395.9 1.9 add_convert_fusion.1
  397.8 11.3 %collective-permute-done.75 = bf16[2,544,256]{2,1,0:T(8,128)(2,1)S(1)} collective-permute-done((bf16[2,544,256]{2,1,0:T(8,128)(2,1)S(1)}, bf16[2,544,256]{2,1,0:T(8,128)(2,1)S(1)}, u32[]{:S(2)}, u32[]{:S(2)}) %collective-permute-start.75) | collective-permute-done | bytes 557088 | tf_op jit(solution)/shard_map/ppermute | solution.py:786
  414.5 17.8 %collective-permute-done.72 = bf16[2,544,256]{2,1,0:T(8,128)(2,1)S(1)} collective-permute-done((bf16[2,544,256]{2,1,0:T(8,128)(2,1)S(1)}, bf16[2,544,256]{2,1,0:T(8,128)(2,1)S(1)}, u32[]{:S(2)}, u32[]{:S(2)}) %collective-permute-start.72) | collective-permute-done | bytes 557088 | tf_op jit(solution)/shard_map/ppermute | solution.py:786
  434.4 8.1 %collective-permute-done.69 = bf16[2,544,256]{2,1,0:T(8,128)(2,1)S(1)} collective-permute-done((bf16[2,544,256]{2,1,0:T(8,128)(2,1)S(1)}, bf16[2,544,256]{2,1,0:T(8,128)(2,1)S(1)}, u32[]{:S(2)}, u32[]{:S(2)}) %collective-permute-start.69) | collective-permute-done | bytes 557088 | tf_op jit(solution)/shard_map/ppermute | solution.py:786
  448.3 9.1 %collective-permute-done.59 = bf16[512,512]{1,0:T(8,128)(2,1)S(1)} collective-permute-done((bf16[512,512]{1,0:T(8,128)(2,1)S(1)}, bf16[512,512]{1,0:T(8,128)(2,1)S(1)}, u32[]{:S(2)}, u32[]{:S(2)}) %collective-permute-start.59) | collective-permute-done | bytes 524320 | tf_op jit(solution)/shard_map/ppermute | solution.py:783
  458.4 10.9 %collective-permute-done.70 = bf16[544,512]{1,0:T(8,128)(2,1)S(1)} collective-permute-done((bf16[544,512]{1,0:T(8,128)(2,1)S(1)}, bf16[544,512]{1,0:T(8,128)(2,1)S(1)}, u32[]{:S(2)}, u32[]{:S(2)}) %collective-permute-start.70) | collective-permute-done | bytes 557088 | tf_op jit(solution)/shard_map/ppermute | solution.py:783
  471.0 2.1 collective-permute-start.79
  473.2 16.9 %collective-permute-done.50 = bf16[512,512]{1,0:T(8,128)(2,1)S(1)} collective-permute-done((bf16[512,512]{1,0:T(8,128)(2,1)S(1)}, bf16[512,512]{1,0:T(8,128)(2,1)S(1)}, u32[]{:S(2)}, u32[]{:S(2)}) %collective-permute-start.50) | collective-permute-done | bytes 524320 | tf_op jit(solution)/shard_map/ppermute | solution.py:783
  493.0 2.1 collective-permute-start.80
  496.8 8.1 %collective-permute-done.41 = bf16[512,512]{1,0:T(8,128)(2,1)S(1)} collective-permute-done((bf16[512,512]{1,0:T(8,128)(2,1)S(1)}, bf16[512,512]{1,0:T(8,128)(2,1)S(1)}, u32[]{:S(2)}, u32[]{:S(2)}) %collective-permute-start.41) | collective-permute-done | bytes 524320 | tf_op jit(solution)/shard_map/ppermute | solution.py:783
  506.5 6.4 %collective-permute-done.26 = bf16[512,512]{1,0:T(8,128)(2,1)S(1)} collective-permute-done((bf16[512,512]{1,0:T(8,128)(2,1)S(1)}, bf16[512,512]{1,0:T(8,128)(2,1)S(1)}, u32[]{:S(2)}, u32[]{:S(2)}) %collective-permute-start.26) | collective-permute-done | bytes 524320 | tf_op jit(solution)/shard_map/ppermute | solution.py:783
  512.9 4.2 collective-permute-done.62
  517.3 2.3 collective-permute-start.63
  520.0 7.5 %collective-permute-done.63 = bf16[512,512]{1,0:T(8,128)(2,1)S(1)} collective-permute-done((bf16[512,512]{1,0:T(8,128)(2,1)S(1)}, bf16[512,512]{1,0:T(8,128)(2,1)S(1)}, u32[]{:S(2)}, u32[]{:S(2)}) %collective-permute-start.63) | collective-permute-done | bytes 524320 | tf_op jit(solution)/shard_map/ppermute | solution.py:786
  527.6 9.7 %hidden_back.1 = (f32[512,384]{1,0:T(8,128)}, bf16[512,384]{1,0:T(8,128)(2,1)}, bf16[1536,512]{1,0:T(8,128)(2,1)}) custom-call(s32[5]{0:T(128)} %stack.113.idx, bf16[544,768]{1,0:T(8,128)(2,1)} %copy-done.23, bf16[544,768]{1,0:T(8,128)(2,1)} %collective-permute-done.81.fn_ref, f32[512,1536]{1,0:T(8,128)} %get-tuple-element.76.h_ref, ...), custom_call_target="tpu_custom_call" | custom-call | flops 3000000000 | bytes 12746752 | tf_op jit(solution)/shard_map/hidden_back/pallas_call | solution.py:391
  541.0 14.3 %attend_back.1 = (bf16[8,208,640]{2,1,0:T(8,128)(2,1)}, bf16[512,896]{1,0:T(8,128)(2,1)}, bf16[512,896]{1,0:T(8,128)(2,1)}) custom-call(s32[5]{0:T(128)} %stack.113.idx, bf16[512,384]{1,0:T(8,128)(2,1)} %get-tuple-element.87.do_ref, bf16[6,512,512]{2,1,0:T(8,128)(2,1)} %get-tuple-element.88.p_ref, bf16[512,384]{1,0:T(8,128)(2,1)} %get-tuple-element.89.q_ref, ...), custom_call_target="tpu_custom_call" | custom-call | flops 5000000000 | bytes 13008896 | tf_op jit(solution)/shard_map/attend_back/pallas_call | solution.py:391
  555.4 2.1 dynamic-slice_bitcast_fusion.3
  570.7 3.8 collective-permute-done.95
  581.0 5.7 collective-permute-done.92
  589.9 21.2 %expert_grads.1 = (f32[8,1536,128]{2,1,0:T(8,128)}, f32[8,1536,128]{2,1,0:T(8,128)}, f32[8,128,1536]{2,1,0:T(8,128)}) custom-call(bf16[6,8,2,80,256]{4,3,2,1,0:T(8,128)(2,1)} %get-tuple-element.97.refs_0_, bf16[6,8,2,80,256]{4,3,2,1,0:T(8,128)(2,1)} %get-tuple-element.98.refs_1_, bf16[6,8,2,80,256]{4,3,2,1,0:T(8,128)(2,1)} %get-tuple-element.99.refs_2_, ...), custom_call_target="tpu_custom_call" | custom-call | flops 6039797760 | bytes 50331648 | tf_op jit(solution)/shard_map/expert_grads/pallas_call | solution.py:737
  611.1 3.5 mixed.1
  617.9 1.9 collective-permute-start.90
  623.6 2.9 collective-permute-done.90
  635.6 2.2 fusion.19
  (389 shorter events, 135.9 us)
Async XLA Ops:
  33.6 25.3 %collective-permute-start.16 = (bf16[1536,384]{1,0:T(8,128)(2,1)}, bf16[1536,384]{1,0:T(8,128)(2,1)S(1)}, u32[]{:S(2)}, u32[]{:S(2)}) collective-permute-start(bf16[1536,384]{1,0:T(8,128)(2,1)} %place.1.w0.w_ref), channel_id=1, source_target_pairs={{0,2},{1,3},{2,0},{3,1},{4,6},{5,7},{6,4},{7,5},{8,10},{9,11},{10,... | collective-permute-start | bytes 3538952 | tf_op jit(solution)/shard_map/ppermute | solution.py:786
  43.9 18.4 %collective-permute-start.1 = (bf16[192,768]{1,0:T(8,128)(2,1)S(1)}, bf16[192,768]{1,0:T(8,128)(2,1)S(1)}, u32[]{:S(2)}, u32[]{:S(2)}) collective-permute-start(bf16[192,768]{1,0:T(8,128)(2,1)S(1)} %collective-permute-done.refs_1_), channel_id=1, source_target_pairs={{0,8},{4,12},{8,16},{12,20},{16,24},{20,28},{24,0},{28,4},{1,9},{5... | collective-permute-start | bytes 884744 | tf_op jit(solution)/shard_map/ppermute | solution.py:780
  62.3 74.9 %collective-permute-start.17 = (bf16[2,1536,384]{2,1,0:T(8,128)(2,1)}, bf16[2,1536,384]{2,1,0:T(8,128)(2,1)}, u32[]{:S(2)}, u32[]{:S(2)}) collective-permute-start(bf16[2,1536,384]{2,1,0:T(8,128)(2,1)} %pad_maximum_fusion), channel_id=1, source_target_pairs={{0,1},{1,0},{2,3},{3,2},{4,5},{5,4},{6,7},{7,6},{8,9},{9,8},{10,11... | collective-permute-start | bytes 7077896 | tf_op jit(solution)/shard_map/ppermute | solution.py:789
  62.4 19.1 %collective-permute-start.3 = (bf16[192,768]{1,0:T(8,128)(2,1)S(1)}, bf16[192,768]{1,0:T(8,128)(2,1)}, u32[]{:S(2)}, u32[]{:S(2)}) collective-permute-start(bf16[192,768]{1,0:T(8,128)(2,1)S(1)} %concatenate.72.refs_0_), channel_id=1, source_target_pairs={{0,4},{4,0},{8,12},{12,8},{16,20},{20,16},{24,28},{28,24},{1,5},{5... | collective-permute-start | bytes 884744 | tf_op jit(solution)/shard_map/ppermute | solution.py:783
  63.5 18.0 %collective-permute-start.4 = (bf16[192,768]{1,0:T(8,128)(2,1)S(1)}, bf16[192,768]{1,0:T(8,128)(2,1)}, u32[]{:S(2)}, u32[]{:S(2)}) collective-permute-start(bf16[192,768]{1,0:T(8,128)(2,1)S(1)} %collective-permute-done.refs_1_), channel_id=1, source_target_pairs={{0,4},{4,0},{8,12},{12,8},{16,20},{20,16},{24,28},{28,24},{1,5},{5... | collective-permute-start | bytes 884744 | tf_op jit(solution)/shard_map/ppermute | solution.py:783
  64.5 20.5 %collective-permute-start.5 = (bf16[192,768]{1,0:T(8,128)(2,1)S(1)}, bf16[192,768]{1,0:T(8,128)(2,1)}, u32[]{:S(2)}, u32[]{:S(2)}) collective-permute-start(bf16[192,768]{1,0:T(8,128)(2,1)S(1)} %collective-permute-done.1.refs_2_), channel_id=1, source_target_pairs={{0,4},{4,0},{8,12},{12,8},{16,20},{20,16},{24,28},{28,24},{1,5},{5... | collective-permute-start | bytes 884744 | tf_op jit(solution)/shard_map/ppermute | solution.py:783
  73.6 17.3 %collective-permute-start.6 = (bf16[192,768]{1,0:T(8,128)(2,1)}, bf16[192,768]{1,0:T(8,128)(2,1)}, u32[]{:S(2)}, u32[]{:S(2)}) collective-permute-start(bf16[192,768]{1,0:T(8,128)(2,1)} %collective-permute-done.2.refs_3_), channel_id=1, source_target_pairs={{0,4},{4,0},{8,12},{12,8},{16,20},{20,16},{24,28},{28,24},{1,5},{5... | collective-permute-start | bytes 884744 | tf_op jit(solution)/shard_map/ppermute | solution.py:783
  112.7 23.2 %collective-permute-start.8 = (bf16[2,512,384]{2,1,0:T(8,128)(2,1)S(1)}, bf16[2,512,384]{2,1,0:T(8,128)(2,1)S(1)}, u32[]{:S(2)}, u32[]{:S(2)}) collective-permute-start(bf16[2,512,384]{2,1,0:T(8,128)(2,1)S(1)} %pad_maximum_fusion.10), channel_id=1, source_target_pairs={{0,1},{1,0},{2,3},{3,2},{4,5},{5,4},{6,7},{7,6},{8,9},{9,8},{10,11... | collective-permute-start | bytes 2359304 | tf_op jit(solution)/shard_map/ppermute | solution.py:789
  119.5 27.4 %collective-permute-start.21 = (bf16[544,512]{1,0:T(8,128)(2,1)}, bf16[544,512]{1,0:T(8,128)(2,1)}, u32[]{:S(2)}, u32[]{:S(2)}) collective-permute-start(bf16[544,512]{1,0:T(8,128)(2,1)} %slice.294), channel_id=1, source_target_pairs={{0,4},{4,0},{8,12},{12,8},{16,20},{20,16},{24,28},{28,24},{1,5},{5... | collective-permute-start | bytes 1671176 | tf_op jit(solution)/shard_map/ppermute | solution.py:783
  122.9 29.4 %collective-permute-start.54 = (bf16[544,512]{1,0:T(8,128)(2,1)S(1)}, bf16[544,512]{1,0:T(8,128)(2,1)}, u32[]{:S(2)}, u32[]{:S(2)}) collective-permute-start(bf16[544,512]{1,0:T(8,128)(2,1)S(1)} %collective-permute-done.33), channel_id=1, source_target_pairs={{0,4},{4,0},{8,12},{12,8},{16,20},{20,16},{24,28},{28,24},{1,5},{5... | collective-permute-start | bytes 1671176 | tf_op jit(solution)/shard_map/ppermute | solution.py:783
  134.3 25.0 %collective-permute-start.45 = (bf16[544,512]{1,0:T(8,128)(2,1)S(1)}, bf16[544,512]{1,0:T(8,128)(2,1)}, u32[]{:S(2)}, u32[]{:S(2)}) collective-permute-start(bf16[544,512]{1,0:T(8,128)(2,1)S(1)} %collective-permute-done.34), channel_id=1, source_target_pairs={{0,4},{4,0},{8,12},{12,8},{16,20},{20,16},{24,28},{28,24},{1,5},{5... | collective-permute-start | bytes 1671176 | tf_op jit(solution)/shard_map/ppermute | solution.py:783
  136.7 34.8 %collective-permute-start.35 = (bf16[544,512]{1,0:T(8,128)(2,1)S(1)}, bf16[544,512]{1,0:T(8,128)(2,1)}, u32[]{:S(2)}, u32[]{:S(2)}) collective-permute-start(bf16[544,512]{1,0:T(8,128)(2,1)S(1)} %collective-permute-done.34), channel_id=1, source_target_pairs={{0,8},{4,12},{8,16},{12,20},{16,24},{20,28},{24,0},{28,4},{1,9},{5... | collective-permute-start | bytes 1671176 | tf_op jit(solution)/shard_map/ppermute | solution.py:780
  146.9 23.1 %collective-permute-start.27 = (bf16[512,512]{1,0:T(8,128)(2,1)}, bf16[512,512]{1,0:T(8,128)(2,1)S(1)}, u32[]{:S(2)}, u32[]{:S(2)}) collective-permute-start(bf16[512,512]{1,0:T(8,128)(2,1)} %get-tuple-element.67), channel_id=1, source_target_pairs={{0,8},{4,12},{8,16},{12,20},{16,24},{20,28},{24,0},{28,4},{1,9},{5... | collective-permute-start | bytes 1572872 | tf_op jit(solution)/shard_map/ppermute | solution.py:780
  146.9 20.9 %collective-permute-start.18 = (bf16[512,512]{1,0:T(8,128)(2,1)}, bf16[512,512]{1,0:T(8,128)(2,1)S(1)}, u32[]{:S(2)}, u32[]{:S(2)}) collective-permute-start(bf16[512,512]{1,0:T(8,128)(2,1)} %get-tuple-element.67), channel_id=1, source_target_pairs={{0,4},{4,0},{8,12},{12,8},{16,20},{20,16},{24,28},{28,24},{1,5},{5... | collective-permute-start | bytes 1572872 | tf_op jit(solution)/shard_map/ppermute | solution.py:783
  152.3 16.6 %collective-permute-start.22 = (bf16[544,256]{1,0:T(8,128)(2,1)S(1)}, bf16[544,256]{1,0:T(8,128)(2,1)S(1)}, u32[]{:S(2)}, u32[]{:S(2)}) collective-permute-start(bf16[544,256]{1,0:T(8,128)(2,1)S(1)} %slice.295), channel_id=1, source_target_pairs={{0,2},{1,3},{2,0},{3,1},{4,6},{5,7},{6,4},{7,5},{8,10},{9,11},{10,... | collective-permute-start | bytes 835592 | tf_op jit(solution)/shard_map/ppermute | solution.py:786
  159.3 30.9 %collective-permute-start.55 = (bf16[2,544,256]{2,1,0:T(8,128)(2,1)S(1)}, bf16[2,544,256]{2,1,0:T(8,128)(2,1)S(1)}, u32[]{:S(2)}, u32[]{:S(2)}) collective-permute-start(bf16[2,544,256]{2,1,0:T(8,128)(2,1)S(1)} %pad_maximum_fusion.16), channel_id=1, source_target_pairs={{0,2},{1,3},{2,0},{3,1},{4,6},{5,7},{6,4},{7,5},{8,10},{9,11},{10,... | collective-permute-start | bytes 1671176 | tf_op jit(solution)/shard_map/ppermute | solution.py:786
  167.9 22.4 %collective-permute-start.46 = (bf16[2,544,256]{2,1,0:T(8,128)(2,1)S(1)}, bf16[2,544,256]{2,1,0:T(8,128)(2,1)S(1)}, u32[]{:S(2)}, u32[]{:S(2)}) collective-permute-start(bf16[2,544,256]{2,1,0:T(8,128)(2,1)S(1)} %pad_maximum_fusion.17), channel_id=1, source_target_pairs={{0,2},{1,3},{2,0},{3,1},{4,6},{5,7},{6,4},{7,5},{8,10},{9,11},{10,... | collective-permute-start | bytes 1671176 | tf_op jit(solution)/shard_map/ppermute | solution.py:786
  168.9 19.5 %collective-permute-start.19 = (bf16[512,256]{1,0:T(8,128)(2,1)S(1)}, bf16[512,256]{1,0:T(8,128)(2,1)S(1)}, u32[]{:S(2)}, u32[]{:S(2)}) collective-permute-start(bf16[512,256]{1,0:T(8,128)(2,1)S(1)} %slice.293), channel_id=1, source_target_pairs={{0,2},{1,3},{2,0},{3,1},{4,6},{5,7},{6,4},{7,5},{8,10},{9,11},{10,... | collective-permute-start | bytes 786440 | tf_op jit(solution)/shard_map/ppermute | solution.py:786
  170.0 21.3 %collective-permute-start.51 = (bf16[512,512]{1,0:T(8,128)(2,1)S(1)}, bf16[512,512]{1,0:T(8,128)(2,1)S(1)}, u32[]{:S(2)}, u32[]{:S(2)}) collective-permute-start(bf16[512,512]{1,0:T(8,128)(2,1)S(1)} %collective-permute-done.27), channel_id=1, source_target_pairs={{0,4},{4,0},{8,12},{12,8},{16,20},{20,16},{24,28},{28,24},{1,5},{5... | collective-permute-start | bytes 1572872 | tf_op jit(solution)/shard_map/ppermute | solution.py:783
  171.5 19.3 %collective-permute-start.28 = (bf16[512,512]{1,0:T(8,128)(2,1)S(1)}, bf16[512,512]{1,0:T(8,128)(2,1)S(1)}, u32[]{:S(2)}, u32[]{:S(2)}) collective-permute-start(bf16[512,512]{1,0:T(8,128)(2,1)S(1)} %collective-permute-done.27), channel_id=1, source_target_pairs={{0,8},{4,12},{8,16},{12,20},{16,24},{20,28},{24,0},{28,4},{1,9},{5... | collective-permute-start | bytes 1572872 | tf_op jit(solution)/shard_map/ppermute | solution.py:780
  190.2 47.6 %collective-permute-start.23 = (bf16[2,544,768]{2,1,0:T(8,128)(2,1)S(1)}, bf16[2,544,768]{2,1,0:T(8,128)(2,1)S(1)}, u32[]{:S(2)}, u32[]{:S(2)}) collective-permute-start(bf16[2,544,768]{2,1,0:T(8,128)(2,1)S(1)} %pad_maximum_fusion.1.dm_ref), channel_id=1, source_target_pairs={{0,1},{1,0},{2,3},{3,2},{4,5},{5,4},{6,7},{7,6},{8,9},{9,8},{10,11... | collective-permute-start | bytes 5013512 | tf_op jit(solution)/shard_map/ppermute | solution.py:789
  190.3 48.6 %collective-permute-start.20 = (bf16[2,512,768]{2,1,0:T(8,128)(2,1)S(1)}, bf16[2,512,768]{2,1,0:T(8,128)(2,1)S(1)}, u32[]{:S(2)}, u32[]{:S(2)}) collective-permute-start(bf16[2,512,768]{2,1,0:T(8,128)(2,1)S(1)} %pad_maximum_fusion.5.am_ref), channel_id=1, source_target_pairs={{0,1},{1,0},{2,3},{3,2},{4,5},{5,4},{6,7},{7,6},{8,9},{9,8},{10,11... | collective-permute-start | bytes 4718600 | tf_op jit(solution)/shard_map/ppermute | solution.py:789
  190.8 21.1 %collective-permute-start.42 = (bf16[512,512]{1,0:T(8,128)(2,1)S(1)}, bf16[512,512]{1,0:T(8,128)(2,1)S(1)}, u32[]{:S(2)}, u32[]{:S(2)}) collective-permute-start(bf16[512,512]{1,0:T(8,128)(2,1)S(1)} %collective-permute-done.28), channel_id=1, source_target_pairs={{0,4},{4,0},{8,12},{12,8},{16,20},{20,16},{24,28},{28,24},{1,5},{5... | collective-permute-start | bytes 1572872 | tf_op jit(solution)/shard_map/ppermute | solution.py:783
  191.3 21.7 %collective-permute-start.29 = (bf16[512,512]{1,0:T(8,128)(2,1)S(1)}, bf16[512,512]{1,0:T(8,128)(2,1)S(1)}, u32[]{:S(2)}, u32[]{:S(2)}) collective-permute-start(bf16[512,512]{1,0:T(8,128)(2,1)S(1)} %collective-permute-done.28), channel_id=1, source_target_pairs={{0,8},{4,12},{8,16},{12,20},{16,24},{20,28},{24,0},{28,4},{1,9},{5... | collective-permute-start | bytes 1572872 | tf_op jit(solution)/shard_map/ppermute | solution.py:780
  216.3 20.2 %collective-permute-start.43 = (bf16[2,512,256]{2,1,0:T(8,128)(2,1)S(1)}, bf16[2,512,256]{2,1,0:T(8,128)(2,1)S(1)}, u32[]{:S(2)}, u32[]{:S(2)}) collective-permute-start(bf16[2,512,256]{2,1,0:T(8,128)(2,1)S(1)} %pad_maximum_fusion.22), channel_id=1, source_target_pairs={{0,2},{1,3},{2,0},{3,1},{4,6},{5,7},{6,4},{7,5},{8,10},{9,11},{10,... | collective-permute-start | bytes 1572872 | tf_op jit(solution)/shard_map/ppermute | solution.py:786
  228.0 43.5 %collective-permute-start.56 = (bf16[2,544,768]{2,1,0:T(8,128)(2,1)}, bf16[2,544,768]{2,1,0:T(8,128)(2,1)}, u32[]{:S(2)}, u32[]{:S(2)}) collective-permute-start(bf16[2,544,768]{2,1,0:T(8,128)(2,1)} %pad_maximum_fusion.4.dm_ref), channel_id=1, source_target_pairs={{0,1},{1,0},{2,3},{3,2},{4,5},{5,4},{6,7},{7,6},{8,9},{9,8},{10,11... | collective-permute-start | bytes 5013512 | tf_op jit(solution)/shard_map/ppermute | solution.py:789
  228.0 43.9 %collective-permute-start.53 = (bf16[2,512,768]{2,1,0:T(8,128)(2,1)}, bf16[2,512,768]{2,1,0:T(8,128)(2,1)}, u32[]{:S(2)}, u32[]{:S(2)}) collective-permute-start(bf16[2,512,768]{2,1,0:T(8,128)(2,1)} %pad_maximum_fusion.8.am_ref), channel_id=1, source_target_pairs={{0,1},{1,0},{2,3},{3,2},{4,5},{5,4},{6,7},{7,6},{8,9},{9,8},{10,11... | collective-permute-start | bytes 4718600 | tf_op jit(solution)/shard_map/ppermute | solution.py:789
  236.6 64.0 %collective-permute-start.47 = (bf16[2,544,768]{2,1,0:T(8,128)(2,1)}, bf16[2,544,768]{2,1,0:T(8,128)(2,1)}, u32[]{:S(2)}, u32[]{:S(2)}) collective-permute-start(bf16[2,544,768]{2,1,0:T(8,128)(2,1)} %pad_maximum_fusion.3.dm_ref), channel_id=1, source_target_pairs={{0,1},{1,0},{2,3},{3,2},{4,5},{5,4},{6,7},{7,6},{8,9},{9,8},{10,11... | collective-permute-start | bytes 5013512 | tf_op jit(solution)/shard_map/ppermute | solution.py:789
  237.8 31.2 %collective-permute-start.31 = (bf16[2,512,256]{2,1,0:T(8,128)(2,1)S(1)}, bf16[2,512,256]{2,1,0:T(8,128)(2,1)}, u32[]{:S(2)}, u32[]{:S(2)}) collective-permute-start(bf16[2,512,256]{2,1,0:T(8,128)(2,1)S(1)} %pad_maximum_fusion.24), channel_id=1, source_target_pairs={{0,2},{1,3},{2,0},{3,1},{4,6},{5,7},{6,4},{7,5},{8,10},{9,11},{10,... | collective-permute-start | bytes 1572872 | tf_op jit(solution)/shard_map/ppermute | solution.py:786
  240.2 60.9 %collective-permute-start.44 = (bf16[2,512,768]{2,1,0:T(8,128)(2,1)}, bf16[2,512,768]{2,1,0:T(8,128)(2,1)}, u32[]{:S(2)}, u32[]{:S(2)}) collective-permute-start(bf16[2,512,768]{2,1,0:T(8,128)(2,1)} %pad_maximum_fusion.7.am_ref), channel_id=1, source_target_pairs={{0,1},{1,0},{2,3},{3,2},{4,5},{5,4},{6,7},{7,6},{8,9},{9,8},{10,11... | collective-permute-start | bytes 4718600 | tf_op jit(solution)/shard_map/ppermute | solution.py:789
  269.0 69.1 %collective-permute-start.38 = (bf16[2,544,768]{2,1,0:T(8,128)(2,1)}, bf16[2,544,768]{2,1,0:T(8,128)(2,1)}, u32[]{:S(2)}, u32[]{:S(2)}) collective-permute-start(bf16[2,544,768]{2,1,0:T(8,128)(2,1)} %pad_maximum_fusion.2.dm_ref), channel_id=1, source_target_pairs={{0,1},{1,0},{2,3},{3,2},{4,5},{5,4},{6,7},{7,6},{8,9},{9,8},{10,11... | collective-permute-start | bytes 5013512 | tf_op jit(solution)/shard_map/ppermute | solution.py:789
  271.4 58.3 %collective-permute-start.24 = (bf16[2,512,768]{2,1,0:T(8,128)(2,1)}, bf16[2,512,768]{2,1,0:T(8,128)(2,1)}, u32[]{:S(2)}, u32[]{:S(2)}) collective-permute-start(bf16[2,512,768]{2,1,0:T(8,128)(2,1)} %get-tuple-element.69), channel_id=1, source_target_pairs={{0,1},{1,0},{2,3},{3,2},{4,5},{5,4},{6,7},{7,6},{8,9},{9,8},{10,11... | collective-permute-start | bytes 4718600 | tf_op jit(solution)/shard_map/ppermute | solution.py:789
  271.9 61.6 %collective-permute-start.65 = (bf16[2,544,768]{2,1,0:T(8,128)(2,1)}, bf16[2,544,768]{2,1,0:T(8,128)(2,1)S(1)}, u32[]{:S(2)}, u32[]{:S(2)}) collective-permute-start(bf16[2,544,768]{2,1,0:T(8,128)(2,1)} %get-tuple-element.78), channel_id=1, source_target_pairs={{0,1},{1,0},{2,3},{3,2},{4,5},{5,4},{6,7},{7,6},{8,9},{9,8},{10,11... | collective-permute-start | bytes 5013512 | tf_op jit(solution)/shard_map/ppermute | solution.py:789
  300.6 37.6 %collective-permute-start.32 = (bf16[2,512,768]{2,1,0:T(8,128)(2,1)}, bf16[2,512,768]{2,1,0:T(8,128)(2,1)}, u32[]{:S(2)}, u32[]{:S(2)}) collective-permute-start(bf16[2,512,768]{2,1,0:T(8,128)(2,1)} %pad_maximum_fusion.6.am_ref), channel_id=1, source_target_pairs={{0,1},{1,0},{2,3},{3,2},{4,5},{5,4},{6,7},{7,6},{8,9},{9,8},{10,11... | collective-permute-start | bytes 4718600 | tf_op jit(solution)/shard_map/ppermute | solution.py:789
  301.1 69.3 %collective-permute-start.57 = (bf16[2,512,768]{2,1,0:T(8,128)(2,1)}, bf16[2,512,768]{2,1,0:T(8,128)(2,1)}, u32[]{:S(2)}, u32[]{:S(2)}) collective-permute-start(bf16[2,512,768]{2,1,0:T(8,128)(2,1)} %get-tuple-element.75), channel_id=1, source_target_pairs={{0,1},{1,0},{2,3},{3,2},{4,5},{5,4},{6,7},{7,6},{8,9},{9,8},{10,11... | collective-permute-start | bytes 4718600 | tf_op jit(solution)/shard_map/ppermute | solution.py:789
  329.7 42.8 %collective-permute-start.74 = (bf16[2,544,768]{2,1,0:T(8,128)(2,1)}, bf16[2,544,768]{2,1,0:T(8,128)(2,1)}, u32[]{:S(2)}, u32[]{:S(2)}) collective-permute-start(bf16[2,544,768]{2,1,0:T(8,128)(2,1)} %get-tuple-element.84), channel_id=1, source_target_pairs={{0,1},{1,0},{2,3},{3,2},{4,5},{5,4},{6,7},{7,6},{8,9},{9,8},{10,11... | collective-permute-start | bytes 5013512 | tf_op jit(solution)/shard_map/ppermute | solution.py:789
  333.6 42.3 %collective-permute-start.48 = (bf16[2,512,768]{2,1,0:T(8,128)(2,1)}, bf16[2,512,768]{2,1,0:T(8,128)(2,1)}, u32[]{:S(2)}, u32[]{:S(2)}) collective-permute-start(bf16[2,512,768]{2,1,0:T(8,128)(2,1)} %get-tuple-element.73), channel_id=1, source_target_pairs={{0,1},{1,0},{2,3},{3,2},{4,5},{5,4},{6,7},{7,6},{8,9},{9,8},{10,11... | collective-permute-start | bytes 4718600 | tf_op jit(solution)/shard_map/ppermute | solution.py:789
  338.1 56.6 %collective-permute-start.71 = (bf16[2,544,768]{2,1,0:T(8,128)(2,1)}, bf16[2,544,768]{2,1,0:T(8,128)(2,1)}, u32[]{:S(2)}, u32[]{:S(2)}) collective-permute-start(bf16[2,544,768]{2,1,0:T(8,128)(2,1)} %get-tuple-element.82), channel_id=1, source_target_pairs={{0,1},{1,0},{2,3},{3,2},{4,5},{5,4},{6,7},{7,6},{8,9},{9,8},{10,11... | collective-permute-start | bytes 5013512 | tf_op jit(solution)/shard_map/ppermute | solution.py:789
  338.2 29.8 %collective-permute-start.66 = (bf16[2,544,256]{2,1,0:T(8,128)(2,1)}, bf16[2,544,256]{2,1,0:T(8,128)(2,1)}, u32[]{:S(2)}, u32[]{:S(2)}) collective-permute-start(bf16[2,544,256]{2,1,0:T(8,128)(2,1)} %get-tuple-element.159), channel_id=1, source_target_pairs={{0,2},{1,3},{2,0},{3,1},{4,6},{5,7},{6,4},{7,5},{8,10},{9,11},{10,... | collective-permute-start | bytes 1671176 | tf_op jit(solution)/shard_map/ppermute | solution.py:786
  368.1 127.0 %collective-permute-start.25 = (bf16[2,512,256]{2,1,0:T(8,128)(2,1)}, bf16[2,512,256]{2,1,0:T(8,128)(2,1)S(1)}, u32[]{:S(2)}, u32[]{:S(2)}) collective-permute-start(bf16[2,512,256]{2,1,0:T(8,128)(2,1)} %get-tuple-element.175), channel_id=1, source_target_pairs={{0,2},{1,3},{2,0},{3,1},{4,6},{5,7},{6,4},{7,5},{8,10},{9,11},{10,... | collective-permute-start | bytes 1572872 | tf_op jit(solution)/shard_map/ppermute | solution.py:786
  370.4 39.9 %collective-permute-start.39 = (bf16[2,512,768]{2,1,0:T(8,128)(2,1)}, bf16[2,512,768]{2,1,0:T(8,128)(2,1)S(1)}, u32[]{:S(2)}, u32[]{:S(2)}) collective-permute-start(bf16[2,512,768]{2,1,0:T(8,128)(2,1)} %get-tuple-element.71), channel_id=1, source_target_pairs={{0,1},{1,0},{2,3},{3,2},{4,5},{5,4},{6,7},{7,6},{8,9},{9,8},{10,11... | collective-permute-start | bytes 4718600 | tf_op jit(solution)/shard_map/ppermute | solution.py:789
  372.6 39.8 %collective-permute-start.68 = (bf16[2,544,768]{2,1,0:T(8,128)(2,1)S(1)}, bf16[2,544,768]{2,1,0:T(8,128)(2,1)S(1)}, u32[]{:S(2)}, u32[]{:S(2)}) collective-permute-start(bf16[2,544,768]{2,1,0:T(8,128)(2,1)S(1)} %copy-done.51), channel_id=1, source_target_pairs={{0,1},{1,0},{2,3},{3,2},{4,5},{5,4},{6,7},{7,6},{8,9},{9,8},{10,11... | collective-permute-start | bytes 5013512 | tf_op jit(solution)/shard_map/ppermute | solution.py:789
  375.9 17.7 %collective-permute-start.58 = (bf16[2,512,256]{2,1,0:T(8,128)(2,1)S(1)}, bf16[2,512,256]{2,1,0:T(8,128)(2,1)S(1)}, u32[]{:S(2)}, u32[]{:S(2)}) collective-permute-start(bf16[2,512,256]{2,1,0:T(8,128)(2,1)S(1)} %get-tuple-element.181), channel_id=1, source_target_pairs={{0,2},{1,3},{2,0},{3,1},{4,6},{5,7},{6,4},{7,5},{8,10},{9,11},{10,... | collective-permute-start | bytes 1572872 | tf_op jit(solution)/shard_map/ppermute | solution.py:786
  394.7 53.2 %collective-permute-start.49 = (bf16[2,512,256]{2,1,0:T(8,128)(2,1)S(1)}, bf16[2,512,256]{2,1,0:T(8,128)(2,1)S(1)}, u32[]{:S(2)}, u32[]{:S(2)}) collective-permute-start(bf16[2,512,256]{2,1,0:T(8,128)(2,1)S(1)} %get-tuple-element.179), channel_id=1, source_target_pairs={{0,2},{1,3},{2,0},{3,1},{4,6},{5,7},{6,4},{7,5},{8,10},{9,11},{10,... | collective-permute-start | bytes 1572872 | tf_op jit(solution)/shard_map/ppermute | solution.py:786
  409.1 23.2 %collective-permute-start.72 = (bf16[2,544,256]{2,1,0:T(8,128)(2,1)S(1)}, bf16[2,544,256]{2,1,0:T(8,128)(2,1)S(1)}, u32[]{:S(2)}, u32[]{:S(2)}) collective-permute-start(bf16[2,544,256]{2,1,0:T(8,128)(2,1)S(1)} %get-tuple-element.163), channel_id=1, source_target_pairs={{0,2},{1,3},{2,0},{3,1},{4,6},{5,7},{6,4},{7,5},{8,10},{9,11},{10,... | collective-permute-start | bytes 1671176 | tf_op jit(solution)/shard_map/ppermute | solution.py:786
  410.3 23.3 %collective-permute-start.76 = (bf16[544,512]{1,0:T(8,128)(2,1)S(1)}, bf16[544,512]{1,0:T(8,128)(2,1)S(1)}, u32[]{:S(2)}, u32[]{:S(2)}) collective-permute-start(bf16[544,512]{1,0:T(8,128)(2,1)S(1)} %fusion.28), channel_id=1, source_target_pairs={{0,4},{4,0},{8,12},{12,8},{16,20},{20,16},{24,28},{28,24},{1,5},{5... | collective-permute-start | bytes 1671176 | tf_op jit(solution)/shard_map/ppermute | solution.py:783
  413.9 28.7 %collective-permute-start.69 = (bf16[2,544,256]{2,1,0:T(8,128)(2,1)S(1)}, bf16[2,544,256]{2,1,0:T(8,128)(2,1)S(1)}, u32[]{:S(2)}, u32[]{:S(2)}) collective-permute-start(bf16[2,544,256]{2,1,0:T(8,128)(2,1)S(1)} %get-tuple-element.161), channel_id=1, source_target_pairs={{0,2},{1,3},{2,0},{3,1},{4,6},{5,7},{6,4},{7,5},{8,10},{9,11},{10,... | collective-permute-start | bytes 1671176 | tf_op jit(solution)/shard_map/ppermute | solution.py:786
  444.0 27.0 %collective-permute-start.40 = (bf16[2,512,256]{2,1,0:T(8,128)(2,1)S(1)}, bf16[2,512,256]{2,1,0:T(8,128)(2,1)S(1)}, u32[]{:S(2)}, u32[]{:S(2)}) collective-permute-start(bf16[2,512,256]{2,1,0:T(8,128)(2,1)S(1)} %get-tuple-element.177), channel_id=1, source_target_pairs={{0,2},{1,3},{2,0},{3,1},{4,6},{5,7},{6,4},{7,5},{8,10},{9,11},{10,... | collective-permute-start | bytes 1572872 | tf_op jit(solution)/shard_map/ppermute | solution.py:786
  446.4 22.9 %collective-permute-start.70 = (bf16[544,512]{1,0:T(8,128)(2,1)S(1)}, bf16[544,512]{1,0:T(8,128)(2,1)S(1)}, u32[]{:S(2)}, u32[]{:S(2)}) collective-permute-start(bf16[544,512]{1,0:T(8,128)(2,1)S(1)} %fusion.30), channel_id=1, source_target_pairs={{0,4},{4,0},{8,12},{12,8},{16,20},{20,16},{24,28},{28,24},{1,5},{5... | collective-permute-start | bytes 1671176 | tf_op jit(solution)/shard_map/ppermute | solution.py:783
  448.0 22.2 %collective-permute-start.78 = (bf16[544,512]{1,0:T(8,128)(2,1)S(1)}, bf16[544,512]{1,0:T(8,128)(2,1)S(1)}, u32[]{:S(2)}, u32[]{:S(2)}) collective-permute-start(bf16[544,512]{1,0:T(8,128)(2,1)S(1)} %fusion.3), channel_id=1, source_target_pairs={{0,8},{4,12},{8,16},{12,20},{16,24},{20,28},{24,0},{28,4},{1,9},{5... | collective-permute-start | bytes 1671176 | tf_op jit(solution)/shard_map/ppermute | solution.py:780
  457.4 34.2 %collective-permute-start.67 = (bf16[544,512]{1,0:T(8,128)(2,1)S(1)}, bf16[544,512]{1,0:T(8,128)(2,1)S(1)}, u32[]{:S(2)}, u32[]{:S(2)}) collective-permute-start(bf16[544,512]{1,0:T(8,128)(2,1)S(1)} %fusion.31), channel_id=1, source_target_pairs={{0,4},{4,0},{8,12},{12,8},{16,20},{20,16},{24,28},{28,24},{1,5},{5... | collective-permute-start | bytes 1671176 | tf_op jit(solution)/shard_map/ppermute | solution.py:783
  469.3 20.8 %collective-permute-start.50 = (bf16[512,512]{1,0:T(8,128)(2,1)S(1)}, bf16[512,512]{1,0:T(8,128)(2,1)S(1)}, u32[]{:S(2)}, u32[]{:S(2)}) collective-permute-start(bf16[512,512]{1,0:T(8,128)(2,1)S(1)} %fusion.47), channel_id=1, source_target_pairs={{0,4},{4,0},{8,12},{12,8},{16,20},{20,16},{24,28},{28,24},{1,5},{5... | collective-permute-start | bytes 1572872 | tf_op jit(solution)/shard_map/ppermute | solution.py:783
  470.2 20.6 %collective-permute-start.60 = (bf16[512,512]{1,0:T(8,128)(2,1)S(1)}, bf16[512,512]{1,0:T(8,128)(2,1)S(1)}, u32[]{:S(2)}, u32[]{:S(2)}) collective-permute-start(bf16[512,512]{1,0:T(8,128)(2,1)S(1)} %fusion.8), channel_id=1, source_target_pairs={{0,8},{4,12},{8,16},{12,20},{16,24},{20,28},{24,0},{28,4},{1,9},{5... | collective-permute-start | bytes 1572872 | tf_op jit(solution)/shard_map/ppermute | solution.py:780
  471.0 21.8 %collective-permute-start.79 = (bf16[544,512]{1,0:T(8,128)(2,1)S(1)}, bf16[544,512]{1,0:T(8,128)(2,1)S(1)}, u32[]{:S(2)}, u32[]{:S(2)}) collective-permute-start(bf16[544,512]{1,0:T(8,128)(2,1)S(1)} %fusion.5), channel_id=1, source_target_pairs={{0,8},{4,12},{8,16},{12,20},{16,24},{20,28},{24,0},{28,4},{1,9},{5... | collective-permute-start | bytes 1671176 | tf_op jit(solution)/shard_map/ppermute | solution.py:780
  496.3 16.6 %collective-permute-start.26 = (bf16[512,512]{1,0:T(8,128)(2,1)S(1)}, bf16[512,512]{1,0:T(8,128)(2,1)S(1)}, u32[]{:S(2)}, u32[]{:S(2)}) collective-permute-start(bf16[512,512]{1,0:T(8,128)(2,1)S(1)} %fusion.49), channel_id=1, source_target_pairs={{0,4},{4,0},{8,12},{12,8},{16,20},{20,16},{24,28},{28,24},{1,5},{5... | collective-permute-start | bytes 1572872 | tf_op jit(solution)/shard_map/ppermute | solution.py:783
  506.5 21.2 %collective-permute-start.81 = (bf16[544,768]{1,0:T(8,128)(2,1)S(1)}, bf16[544,768]{1,0:T(8,128)(2,1)}, u32[]{:S(2)}, u32[]{:S(2)}) collective-permute-start(bf16[544,768]{1,0:T(8,128)(2,1)S(1)} %pad_maximum_fusion.9.fm_ref), channel_id=1, source_target_pairs={{0,1},{1,0},{2,3},{3,2},{4,5},{5,4},{6,7},{7,6},{8,9},{9,8},{10,11... | collective-permute-start | bytes 2506760 | tf_op jit(solution)/shard_map/ppermute | solution.py:789
  539.8 21.7 %collective-permute-start.94 = (bf16[192,512]{0,1:T(8,128)(2,1)}, bf16[192,512]{0,1:T(8,128)(2,1)}, u32[]{:S(2)}, u32[]{:S(2)}) collective-permute-start(bf16[192,512]{0,1:T(8,128)(2,1)} %bitcast.61), channel_id=1, source_target_pairs={{0,4},{4,0},{8,12},{12,8},{16,20},{20,16},{24,28},{28,24},{1,5},{5... | collective-permute-start | bytes 589832 | tf_op jit(solution)/shard_map/ppermute | solution.py:783
  558.3 30.7 %collective-permute-start.64 = (bf16[512,768]{1,0:T(8,128)(2,1)S(1)}, bf16[512,768]{1,0:T(8,128)(2,1)}, u32[]{:S(2)}, u32[]{:S(2)}) collective-permute-start(bf16[512,768]{1,0:T(8,128)(2,1)S(1)} %pad_maximum_fusion.11.fm_ref), channel_id=1, source_target_pairs={{0,1},{1,0},{2,3},{3,2},{4,5},{5,4},{6,7},{7,6},{8,9},{9,8},{10,11... | collective-permute-start | bytes 2359304 | tf_op jit(solution)/shard_map/ppermute | solution.py:789
  560.8 16.2 %collective-permute-start.86 = (bf16[208,640]{1,0:T(8,128)(2,1)}, bf16[208,640]{1,0:T(8,128)(2,1)S(1)}, u32[]{:S(2)}, u32[]{:S(2)}) collective-permute-start(bf16[208,640]{1,0:T(8,128)(2,1)} %get-tuple-element.156), channel_id=1, source_target_pairs={{0,4},{4,0},{8,12},{12,8},{16,20},{20,16},{24,28},{28,24},{1,5},{5... | collective-permute-start | bytes 798728 | tf_op jit(solution)/shard_map/ppermute | solution.py:783
  570.7 49.1 %collective-permute-start.82 = (bf16[512,896]{1,0:T(8,128)(2,1)}, bf16[512,896]{1,0:T(8,128)(2,1)}, u32[]{:S(2)}, u32[]{:S(2)}) collective-permute-start(bf16[512,896]{1,0:T(8,128)(2,1)} %get-tuple-element.94), channel_id=1, source_target_pairs={{0,1},{1,0},{2,3},{3,2},{4,5},{5,4},{6,7},{7,6},{8,9},{9,8},{10,11... | collective-permute-start | bytes 2752520 | tf_op jit(solution)/shard_map/ppermute | solution.py:789
  574.5 40.2 %collective-permute-start.91 = (bf16[192,512]{0,1:T(8,128)(2,1)}, bf16[192,512]{0,1:T(8,128)(2,1)}, u32[]{:S(2)}, u32[]{:S(2)}) collective-permute-start(bf16[192,512]{0,1:T(8,128)(2,1)} %bitcast.55), channel_id=1, source_target_pairs={{0,4},{4,0},{8,12},{12,8},{16,20},{20,16},{24,28},{28,24},{1,5},{5... | collective-permute-start | bytes 589832 | tf_op jit(solution)/shard_map/ppermute | solution.py:783
  586.7 30.0 %collective-permute-start.85 = (bf16[208,640]{1,0:T(8,128)(2,1)S(1)}, bf16[208,640]{1,0:T(8,128)(2,1)S(1)}, u32[]{:S(2)}, u32[]{:S(2)}) collective-permute-start(bf16[208,640]{1,0:T(8,128)(2,1)S(1)} %copy-done.30), channel_id=1, source_target_pairs={{0,4},{4,0},{8,12},{12,8},{16,20},{20,16},{24,28},{28,24},{1,5},{5... | collective-permute-start | bytes 798728 | tf_op jit(solution)/shard_map/ppermute | solution.py:783
  588.2 28.5 %collective-permute-start.89 = (bf16[208,640]{1,0:T(8,128)(2,1)}, bf16[208,640]{1,0:T(8,128)(2,1)}, u32[]{:S(2)}, u32[]{:S(2)}) collective-permute-start(bf16[208,640]{1,0:T(8,128)(2,1)} %fusion.34), channel_id=1, source_target_pairs={{0,8},{4,12},{8,16},{12,20},{16,24},{20,28},{24,0},{28,4},{1,9},{5... | collective-permute-start | bytes 798728 | tf_op jit(solution)/shard_map/ppermute | solution.py:780
  589.1 26.5 %collective-permute-start.97 = (bf16[192,512]{0,1:T(8,128)(2,1)}, bf16[192,512]{0,1:T(8,128)(2,1)}, u32[]{:S(2)}, u32[]{:S(2)}) collective-permute-start(bf16[192,512]{0,1:T(8,128)(2,1)} %fusion.54), channel_id=1, source_target_pairs={{0,8},{4,12},{8,16},{12,20},{16,24},{20,28},{24,0},{28,4},{1,9},{5... | collective-permute-start | bytes 589832 | tf_op jit(solution)/shard_map/ppermute | solution.py:780
  (93 other events, 1064.7 us)

commit v2 on v1

--- a/solution.py
+++ b/solution.py
@@ -384,18 +384,31 @@
     return lax.dot_general(a, b, (((0,), (0,)), ((), ())), preferred_element_type=F32)
 
 
+def bytes_of(arrays):
+    return sum(int(np.prod(a.shape)) * jnp.dtype(a.dtype).itemsize for a in arrays)
+
+
+def after(v, *done):
+    return lax.optimization_barrier((v, *done))[0]
+
+
+def sync(*values):
+    return lax.optimization_barrier(values)
+
+
 def kernel_call(body, outs, ins, scratch=(), flops=0, name=None):
     smem = pl.BlockSpec(memory_space=pltpu.SMEM)
     vmem = pl.BlockSpec(memory_space=pltpu.VMEM)
-    nbytes = sum(int(np.prod(a.shape)) * a.dtype.itemsize for a in list(ins[1:]) + list(outs))
+    nbytes = bytes_of(list(ins[1:]) + list(outs))
+    need = nbytes + bytes_of(scratch) + (16 << 20)
     return pl.pallas_call(
         body,
-        out_shape=[jax.ShapeDtypeStruct(o.shape, o.dtype) for o in outs],
+        out_shape=[sds(o.shape, o.dtype) for o in outs],
         in_specs=[smem] + [vmem] * (len(ins) - 1),
         out_specs=[vmem] * len(outs),
         scratch_shapes=list(scratch),
-        compiler_params=pltpu.CompilerParams(vmem_limit_bytes=VMEM_LIMIT),
-        cost_estimate=pl.CostEstimate(flops=int(flops), bytes_accessed=int(nbytes), transcendentals=0),
+        compiler_params=pltpu.CompilerParams(vmem_limit_bytes=min(need, VMEM_LIMIT)),
+        cost_estimate=pl.CostEstimate(flops=int(flops), bytes_accessed=nbytes, transcendentals=0),
         name=name,
     )(*ins)
 
@@ -430,12 +443,24 @@
 
 def place_body(nz, idx, *refs):
     out = refs[-1]
+    rows, cols = refs[0].shape[0], out.shape[1]
+    for k in range(nz):
+        base = lax.rem(idx[1] - k + nz, nz) * 2
+        for q in range(2):
+            block = base + (idx[2] if q == 0 else 1 - idx[2])
+            out[pl.ds(pl.multiple_of(block * rows, rows), rows), :] = refs[q * nz + k][:, :cols]
+
+
+def place_both_body(nz, idx, *refs):
+    out = refs[-1]
     rows = refs[0].shape[0]
     for k in range(nz):
         base = lax.rem(idx[1] - k + nz, nz) * 2
         for q in range(2):
             block = base + (idx[2] if q == 0 else 1 - idx[2])
-            out[pl.ds(pl.multiple_of(block * rows, rows), rows), :] = refs[q * nz + k][...]
+            at = pl.ds(pl.multiple_of(block * rows, rows), rows)
+            out[0, at, :] = refs[q * nz + k][:, refs[0].shape[1] - out.shape[2] :]
+            out[1, at, :] = refs[2 * nz + k][q]
 
 
 def rotate(v, cos, sin, lane_low):
@@ -450,7 +475,8 @@
 def attend_body(nz, idx, *refs):
     blocks = refs[: 2 * nz]
     x_ref, seg_row, seg_col, cos_ref, sin_ref = refs[2 * nz : 2 * nz + 5]
-    o_ref, q_ref, k_ref, v_ref, p_ref, w_ref, aux_ref, bias_ref, qkv_ref = refs[2 * nz + 5 :]
+    refs = refs[2 * nz + 5 :]
+    (o_ref, q_ref, k_ref, v_ref, w_ref, aux_ref), heads_p, (bias_ref, qkv_ref) = refs[:6], refs[6:-2], refs[-2:]
     place_body(nz, idx, *blocks, w_ref)
     tok, width = x_ref.shape
     qd, kd = q_ref.shape[1], k_ref.shape[1]
@@ -481,29 +507,31 @@
         s = mm_nt(q_ref[:, a : a + HEAD_SIZE], k_ref[:, b : b + HEAD_SIZE]) + bias_ref[...]
         e = jnp.exp(s - jnp.max(s, axis=1, keepdims=True))
         p = (e / jnp.sum(e, axis=1, keepdims=True)).astype(BF16)
-        p_ref[h] = p
+        heads_p[h][...] = p
         o_ref[:, a : a + HEAD_SIZE] = mm(p, v_ref[:, b : b + HEAD_SIZE]).astype(BF16)
 
 
-def column_blocks(idx):
+def column_places(idx, width):
     x, c = idx[3], idx[4]
-    own = [c, 2 + 2 * x + c, 2 + 2 * (1 - x) + c]
-    return own, [1 - c, 2 + 2 * x + 1 - c, 2 + 2 * (1 - x) + 1 - c]
-
-
-def out_body(idx, x_ref, o0, o1, o23, w0, w1, w23, aux_ref, h_ref, low_ref, own_ref, ring_ref):
-    attn = mm_nt(o0[...], w0[...]) + mm_nt(o1[...], w1[...])
+    part = width // 4
+
+    def at(b):
+        return pl.ds(pl.multiple_of(b * part, 128), part)
+
+    return [at(2 * x + c), at(2 * (1 - x) + c)], [at(2 * x + 1 - c), at(2 * (1 - x) + 1 - c)]
+
+
+def out_body(idx, x_ref, o0, o1, o23, w01, w23, aux_ref, h_ref, low_ref, ring_ref):
+    tok, width = x_ref.shape
+    attn = mm_nt(o0[...], w01[0]) + mm_nt(o1[...], w01[1])
     attn = attn + (mm_nt(o23[0], w23[0]) + mm_nt(o23[1], w23[1]))
     h = x_ref[...].astype(F32) + attn
     h_ref[...] = h
     r2 = lax.rsqrt(jnp.mean(h * h, axis=1, keepdims=True) + epsilon)
     low_ref[...] = (h * r2 * aux_ref[64:66, :].astype(F32)[1:2, :]).astype(BF16)
-    own, _ = column_blocks(idx)
-    for m in range(3):
-        block = low_ref[:, pl.ds(pl.multiple_of(own[m] * BLK, BLK), BLK)]
-        own_ref[:, m * BLK : m * BLK + BLK] = block
-        if m < 2:
-            ring_ref[:, m * BLK : m * BLK + BLK] = block
+    part = width // 4
+    for m, at in enumerate(column_places(idx, width)[0]):
+        ring_ref[:, m * part : m * part + part] = low_ref[:, at]
 
 
 def masked_gates(logits, pos):
@@ -519,50 +547,75 @@
 
 
 def experts_body(
-    local, idx, am_ref, an_ref, dm_ref, dn_ref, gu_ref, down_ref, aux_ref, sel_ref, selt_ref, slot_ref, slott_ref,
-    dxm_ref, dxn_ref, ym_ref, yn_ref, xe_ref, dy_ref, dgu_ref, hd_ref,
-    pos_s, gate_s, d0_s, acc_s, acc2_s, dgr_s, oh_s, oht_s,
+    local, idx, aux_ref, sel_ref, selt_ref, slot_ref, slott_ref, *refs
 ):
-    tok = am_ref.shape[1]
+    rows_hbm, d_hbm, (gu_hbm, down_hbm), refs = refs[:4], refs[4:8], refs[8:10], refs[10:]
+    dx_hbm, y_hbm, (xe_hbm, d0_hbm, dgu_hbm, hd_hbm) = refs[:2], refs[2:4], refs[4:8]
+    am_s, an_s, dm_s, dn_s, gu_s, down_s = refs[8:14]
+    dx_out, y_out, (xe_s, d0_s, dgu_s, hd_s) = refs[14:16], refs[16:18], refs[18:22]
+    pos_s, gate_s, y_s, dx_s, dgr_s, oh_s, oht_s, in_sem, w_sem, out_sem = refs[22:]
+    tok, width = am_s.shape[1], xe_s.shape[3]
     half = pos_s.shape[0] // 2
-    c = idx[4]
-    mine, theirs = column_blocks(idx)
-    parts = list(zip(mine + theirs, [0, 1, 2] * 2, [0] * 3 + [1] * 3))
-    hidden = down_ref.shape[1]
+    x, c = idx[3], idx[4]
+    part = width // 4
+    sides = column_places(idx, width)
+    hidden = down_s.shape[1]
+    both, slots = 2 * PAD, local * PAD
+
+    def arriving(q):
+        pairs = [(rows_hbm[q], am_s.at[q]), (rows_hbm[2 + q], an_s.at[q])]
+        for i, d_s in enumerate((dm_s, dn_s)):
+            for m in range(2):
+                pairs.append((d_hbm[2 * i + m].at[q], d_s.at[q, :, m * part : m * part + part]))
+        return [pltpu.make_async_copy(h, v, in_sem.at[q, i]) for i, (h, v) in enumerate(pairs)]
+
+    weights = [pltpu.make_async_copy(gu_hbm, gu_s, w_sem.at[0]), pltpu.make_async_copy(down_hbm, down_s, w_sem.at[1])]
+    for cp in arriving(0):
+        cp.start()
+    for cp in arriving(1):
+        cp.start()
+    for cp in weights:
+        cp.start()
+    leaving = []
+
+    def leave(src, dst):
+        cp = pltpu.make_async_copy(src, dst, out_sem.at[len(leaving)])
+        cp.start()
+        leaving.append(cp)
+
     sel, selt = sel_ref[...], selt_ref[...]
     for q in range(2):
-        pos_s[pl.ds(pl.multiple_of(c * half, half), half), :] = dm_ref[q, tok:, :tok]
-        pos_s[pl.ds(pl.multiple_of((1 - c) * half, half), half), :] = dn_ref[q, tok:, :tok]
+        for cp in arriving(q):
+            cp.wait()
+        for d_s, core in ((dm_s, c), (dn_s, 1 - c)):
+            for m, chip in enumerate((x, 1 - x)):
+                at = pl.ds(pl.multiple_of((2 * chip + core) * 128, 128), 128)
+                pos_s[:, at] = d_s[q, tok:, m * part : m * part + 128]
         pos = pos_s[...]
         logits = jnp.zeros(pos.shape, F32)
-        for b, m, side in parts:
-            rows = (an_ref if side else am_ref)[q, :, m * BLK : m * BLK + BLK]
-            router = aux_ref[: pos.shape[0], pl.ds(pl.multiple_of(b * BLK, BLK), BLK)]
-            logits = logits + mm_nt(router, rows)
+        for rows, places in zip((am_s, an_s), sides):
+            for m, at in enumerate(places):
+                logits = logits + mm_nt(aux_ref[: pos.shape[0], at], rows[q, :, m * part : m * part + part])
         gates = masked_gates(logits, pos.astype(F32))
         hot = (mm(sel, pos) == slot_ref[...]).astype(F32).astype(BF16)
         oh_s[q] = hot
         oht_s[q] = (mm_tn(pos, selt) == slott_ref[...]).astype(F32).astype(BF16)
         high, low = split16(gates)
         spread = (mm_nt(hot, high) + mm_nt(hot, low)) * sel.astype(F32)
-        gate = jnp.sum(spread, axis=1, keepdims=True)
-        gate_s[:, q] = gate.reshape(local, PAD, 1)
-        for b, m, side in parts:
-            rows = (an_ref if side else am_ref)[q, :, m * BLK : m * BLK + BLK]
-            xe_ref[b, :, q] = mm(hot, rows).astype(BF16).reshape(local, PAD, BLK)
-            rows = (dn_ref if side else dm_ref)[q, :tok, m * BLK : m * BLK + BLK]
-            got = mm(hot, rows)
-            d0_s[b, :, q] = got.astype(BF16).reshape(local, PAD, BLK)
-            dy_ref[b, :, q] = (got * gate).astype(BF16).reshape(local, PAD, BLK)
-    blocks = xe_ref.shape[0]
-    both = 2 * PAD
+        gate_s[:, q] = jnp.sum(spread, axis=1, keepdims=True).reshape(local, PAD, 1)
+        for rows, outs in (((am_s, an_s), xe_s), ((dm_s, dn_s), d0_s)):
+            for side, places in enumerate(sides):
+                got = mm(hot, rows[side][q, :tok, :]).astype(BF16)
+                for m, at in enumerate(places):
+                    outs[:, q, :, at] = got[:, m * part : m * part + part].reshape(local, PAD, part)
+    leave(xe_s, xe_hbm)
+    leave(d0_s, d0_hbm)
+    for cp in weights:
+        cp.wait()
     for j in range(local):
-        gu = jnp.zeros((both, 2 * hidden), F32)
-        t = jnp.zeros((both, hidden), F32)
-        for b in range(blocks):
-            gu = gu + mm(xe_ref[b, j].reshape(both, BLK), gu_ref[j, b * BLK : b * BLK + BLK, :])
-            t = t + mm_nt(d0_s[b, j].reshape(both, BLK), down_ref[j, :, b * BLK : b * BLK + BLK])
-        gate = gate_s[:, :][j].reshape(both, 1)
+        gu = mm(xe_s[j].reshape(both, width), gu_s[j])
+        t = mm_nt(d0_s[j].reshape(both, width), down_s[j])
+        gate = gate_s[j].reshape(both, 1)
         g, u = gu[:, :hidden], gu[:, hidden:]
         sg = jax.nn.sigmoid(g)
         silu = g * sg
@@ -572,47 +625,94 @@
         du = (dhd * silu).astype(BF16)
         dgate = jnp.sum(hd.astype(F32) * t, axis=1, keepdims=True)
         dgr_s[j] = jnp.broadcast_to(dgate, (both, dgr_s.shape[3])).reshape(2, PAD, dgr_s.shape[3])
-        hd_ref[j] = hd.reshape(2, PAD, hidden)
-        dgu_ref[j, :, :, :hidden] = dg.reshape(2, PAD, hidden)
-        dgu_ref[j, :, :, hidden:] = du.reshape(2, PAD, hidden)
+        hd_s[j] = (hd.astype(F32) * gate).astype(BF16).reshape(2, PAD, hidden)
         dgu = jnp.concatenate([dg, du], axis=1)
-        for b in range(blocks):
-            y = mm(hd, down_ref[j, :, b * BLK : b * BLK + BLK])
-            acc_s[b, j] = (y.astype(BF16).astype(F32) * gate).astype(BF16).reshape(2, PAD, BLK)
-            dx = mm_nt(dgu, gu_ref[j, b * BLK : b * BLK + BLK, :])
-            acc2_s[b, j] = dx.astype(BF16).reshape(2, PAD, BLK)
-    slots = local * PAD
-    x = idx[3]
+        dgu_s[j] = dgu.reshape(2, PAD, 2 * hidden)
+        dx_s[j] = mm_nt(dgu, gu_s[j]).astype(BF16).reshape(2, PAD, width)
+        y = mm(hd, down_s[j])
+        y_s[j] = (y.astype(BF16).astype(F32) * gate).astype(BF16).reshape(2, PAD, width)
+    leave(hd_s, hd_hbm)
+    leave(dgu_s, dgu_hbm)
     for q in range(2):
         hot, hott = oh_s[q], oht_s[q]
-        for b, m, side in parts:
-            dx = mm(hott, acc2_s[b, :, q].reshape(slots, BLK)).astype(BF16)
-            (dxn_ref if side else dxm_ref)[q, :tok, m * BLK : m * BLK + BLK] = dx
-            y = mm(hott, acc_s[b, :, q].reshape(slots, BLK)).astype(BF16)
-            (yn_ref if side else ym_ref)[q, :, m * BLK : m * BLK + BLK] = y
-        weights = (dgr_s[:, :, :, :][:, q].reshape(slots, -1) * sel.astype(F32)).astype(BF16)
-        pos_s[...] = mm_tn(weights, hot).astype(BF16)
-        for ref, at in ((dxm_ref, c), (dxn_ref, 1 - c)):
-            got = pos_s[pl.ds(pl.multiple_of(at * half, half), half), :]
-            ref[q, tok:, :BLK] = got[:, :BLK]
-            ref[q, tok:, BLK : 2 * BLK] = (got[:, BLK:].astype(F32) * (1 - x).astype(F32)).astype(BF16)
-            ref[q, tok:, 2 * BLK :] = (got[:, BLK:].astype(F32) * x.astype(F32)).astype(BF16)
-
-
-def hidden_back_body(idx, fm_ref, fn_ref, h_ref, low_ref, aux_ref, pos_ref, dout_ref, o_ref, w_ref,
-                     dh_ref, do_ref, rs_ref, full_s, dg_s):
+
+        def scatter(rows_s, outs):
+            for out, places in zip(outs, sides):
+                rows = [rows_s[:, q, :, at].reshape(slots, part) for at in places]
+                out[q, :tok, :] = mm(hott, jnp.concatenate(rows, axis=1)).astype(BF16)
+
+        scatter(dx_s, dx_out)
+        spread = (dgr_s[:, q].reshape(slots, -1) * sel.astype(F32)).astype(BF16)
+        pos_s[...] = mm_tn(spread, hot).astype(BF16)
+        for out, at in zip(dx_out, (c, 1 - c)):
+            out[q, tok:, :tok] = pos_s[pl.ds(pl.multiple_of(at * half, half), half), :]
+            out[q, tok:, tok:] = jnp.zeros((half, out.shape[2] - tok), BF16)
+        for v, h in zip(dx_out, dx_hbm):
+            leave(v.at[q], h.at[q])
+        scatter(y_s, y_out)
+        for v, h in zip(y_out, y_hbm):
+            leave(v.at[q], h.at[q])
+    for cp in leaving:
+        cp.wait()
+
+
+def experts_call(idx, a, d, gu, down, aux_t, sel, slot_col, slot_row):
+    local, width, hidden2 = gu.shape
+    hidden = hidden2 // 2
+    experts = sel.shape[1]
+    tok = a[0].shape[0]
+    rows = tok + experts // 2
+    slots = local * PAD
+    big = (local, 2, PAD, width)
+    outs = [sds((2, n, width // 2), BF16) for n in (rows, rows, tok, tok)]
+    outs += [sds(big, BF16), sds(big, BF16), sds((local, 2, PAD, hidden2), BF16), sds((local, 2, PAD, hidden), BF16)]
+    kept = [idx, aux_t, sel, sel.T, slot_col, slot_row]
+    scratch = [pltpu.VMEM((2, n, width // 2), BF16) for n in (tok, tok, tok + experts, tok + experts)]
+    scratch += [pltpu.VMEM(v.shape, v.dtype) for v in [gu, down] + outs]
+    scratch += [
+        pltpu.VMEM((experts, tok), BF16), pltpu.VMEM((local, 2, PAD, 1), F32), pltpu.VMEM(big, BF16), pltpu.VMEM(big, BF16),
+        pltpu.VMEM((local, 2, PAD, experts), F32), pltpu.VMEM((2, slots, tok), BF16), pltpu.VMEM((2, tok, slots), BF16),
+    ]
+    scratch += [pltpu.SemaphoreType.DMA((2, 6)), pltpu.SemaphoreType.DMA((2,)), pltpu.SemaphoreType.DMA((20,))]
+    moved = [*a, *d, gu, down]
+    smem = pl.BlockSpec(memory_space=pltpu.SMEM)
+    vmem = pl.BlockSpec(memory_space=pltpu.VMEM)
+    hbm = pl.BlockSpec(memory_space=pl.ANY)
+    return pl.pallas_call(
+        functools.partial(experts_body, local),
+        out_shape=outs,
+        in_specs=[smem] + [vmem] * 5 + [hbm] * len(moved),
+        out_specs=[hbm] * len(outs),
+        scratch_shapes=scratch,
+        compiler_params=pltpu.CompilerParams(vmem_limit_bytes=VMEM_LIMIT),
+        cost_estimate=pl.CostEstimate(
+            flops=16 * slots * tok * width + 36 * slots * width * hidden,
+            bytes_accessed=bytes_of(moved + outs),
+            transcendentals=0,
+        ),
+        name="experts",
+    )(*kept, *moved)
+
+
+def in_ring_order(nz, idx, blocks_s, outs):
+    for k in range(nz):
+        base = lax.rem(idx[1] - k + nz, nz) * 2
+        outs[k][...] = blocks_s[base + idx[2]]
+        outs[nz + k][...] = blocks_s[base + 1 - idx[2]]
+
+
+def hidden_back_body(nz, idx, fm_ref, fn_ref, h_ref, low_ref, aux_ref, pos_ref, dout_ref, o_ref, w_ref,
+                     dh_ref, do_ref, *refs):
+    outs, (full_s, dg_s, rs_s) = refs[:-3], refs[-3:]
     tok, width = h_ref.shape
     c, experts = idx[4], pos_ref.shape[0]
     half = experts // 2
-    mine, theirs = column_blocks(idx)
-    for ref, order in ((fm_ref, mine), (fn_ref, theirs)):
-        for m in range(3):
-            at = pl.ds(pl.multiple_of(order[m] * BLK, BLK), BLK)
-            full_s[:, at] = ref[:tok, m * BLK : m * BLK + BLK].astype(F32)
+    part = width // 4
+    for ref, places in zip((fm_ref, fn_ref), column_places(idx, width)):
+        for m, at in enumerate(places):
+            full_s[:, at] = ref[:tok, m * part : m * part + part].astype(F32)
     for ref, at in ((fm_ref, c), (fn_ref, 1 - c)):
-        at = pl.ds(pl.multiple_of(at * half, half), half)
-        dg_s[at, :BLK] = ref[tok:, :BLK].astype(F32)
-        dg_s[at, BLK:] = ref[tok:, BLK : 2 * BLK].astype(F32) + ref[tok:, 2 * BLK :].astype(F32)
+        dg_s[pl.ds(pl.multiple_of(at * half, half), half), :] = ref[tok:, :tok].astype(F32)
     low = low_ref[...]
     router = aux_ref[:experts, :]
     gates = masked_gates(mm_nt(router, low), pos_ref[...].astype(F32))
@@ -630,14 +730,20 @@
     t = idx[3] * 2 + c
     dh_ref[...] = full_s[:, pl.ds(pl.multiple_of(t * cols, 128), cols)]
     dhb = dh.astype(BF16)
-    do_ref[...] = mm(dhb, w_ref[...]).astype(BF16)
-    rs_ref[:, :cols] = mm_tn(dhb, o_ref[...]).astype(BF16)
+    do_ref[...] = mm(dhb, w_ref[0]).astype(BF16)
+    turned = mm_tn(dhb, o_ref[...]).astype(BF16)
     side = jnp.concatenate([mm(dlogits, low), gain_grad, jnp.zeros((63, width), F32)], axis=0)
-    rs_ref[:, cols:] = side.T.astype(BF16)
-
-
-def attend_back_body(idx, do_ref, p_ref, q_ref, k_ref, v_ref, w_ref, x_ref, aux_ref, cos_ref, sin_ref,
-                     rs_ref, dm_ref, dn_ref, dq_s, dqkv_s, dxn_s):
+    side = side.T.astype(BF16)
+    rows = rs_s.shape[1]
+    for i in range(2 * nz):
+        rs_s[i, :, :cols] = turned[i * rows : i * rows + rows]
+        rs_s[i, :, cols:] = side[i * rows : i * rows + rows]
+    in_ring_order(nz, idx, rs_s, outs)
+
+
+def attend_back_body(nz, idx, do_ref, v_ref, k_ref, q_ref, cos_ref, sin_ref, x_ref, aux_ref, w_ref, *refs):
+    heads_p, refs = refs[: q_ref.shape[1] // HEAD_SIZE], refs[q_ref.shape[1] // HEAD_SIZE :]
+    dm_ref, dn_ref, outs, (dq_s, dqkv_s, dxn_s, rs_ref) = refs[0], refs[1], refs[2:-4], refs[-4:]
     tok, width = x_ref.shape
     qd, kd = q_ref.shape[1], k_ref.shape[1]
     heads, groups = qd // HEAD_SIZE, kd // HEAD_SIZE
@@ -651,12 +757,12 @@
         for h in range(g * each, (g + 1) * each):
             a = h * HEAD_SIZE
             doh = do_ref[:, a : a + HEAD_SIZE]
-            p = p_ref[h].astype(F32)
+            p = heads_p[h][...].astype(F32)
             dp = mm_nt(doh, vg)
             ds = (p * (dp - jnp.sum(p * dp, axis=1, keepdims=True))).astype(BF16)
             dq_s[:, a : a + HEAD_SIZE] = mm(ds, kg) * scale
             dk = dk + mm_tn(ds, q_ref[:, a : a + HEAD_SIZE])
-            dv = dv + mm_tn(p_ref[h], doh)
+            dv = dv + mm_tn(heads_p[h][...], doh)
         dq_s[:, qd + b : qd + b + HEAD_SIZE] = dk
         dqkv_s[:, qd + kd + b : qd + kd + b + HEAD_SIZE] = dv.astype(BF16)
     lanes = low_lanes(tok)
@@ -682,6 +788,7 @@
         tail = jnp.concatenate([gain_high[:, at].astype(F32), gain_low[:, at].astype(F32), pads.astype(F32)], axis=0)
         rs_ref[i, rows:, :] = jnp.zeros((16, used), BF16)
         rs_ref[i, rows:, :rows] = tail.astype(BF16)
+    in_ring_order(nz, idx, rs_ref, outs)
     total = jnp.sum(dxn * xh * gain, axis=1, keepdims=True)
     high, low = split16(total)
     lane = lax.broadcasted_iota(jnp.int32, (tok, 128), 1)
@@ -696,57 +803,79 @@
         ref[:, 2 * cols :] = side
 
 
-def mixed_body(idx, fm_ref, fn_ref, h_ref, out_ref, full_s):
-    mine, theirs = column_blocks(idx)
-    for ref, order in ((fm_ref, mine), (fn_ref, theirs)):
-        for m in range(3):
-            at = pl.ds(pl.multiple_of(order[m] * BLK, BLK), BLK)
-            full_s[:, at] = ref[:, m * BLK : m * BLK + BLK].astype(F32)
-    cols = out_ref.shape[1]
-    at = pl.ds(pl.multiple_of((idx[3] * 2 + idx[4]) * cols, 128), cols)
-    out_ref[...] = (full_s[:, at] + h_ref[:, at]).astype(BF16)
+def early_end_body(idx, kept, side, ring, out_ref, router_ref, gain_ref):
+    total = kept[...].astype(F32) + side[...].astype(F32) + ring[...].astype(F32)
+    cols, experts = out_ref.shape[0], router_ref.shape[1]
+    out_ref[...] = total[:, :cols].T
+    router_ref[...] = total[:, cols : cols + experts]
+    gain_ref[...] = total[:, cols:].T[experts : experts + 8]
+
+
+def late_end_body(idx, kept, side, ring, query_ref, key_ref, value_ref, gain_ref):
+    total = kept[...].astype(F32) + side[...].astype(F32) + ring[...].astype(F32)
+    rows, qd = query_ref.shape
+    kd = key_ref.shape[1]
+    gain_ref[...] = total[rows : rows + 8, : gain_ref.shape[1]]
+    query_ref[...] = total[:rows, :qd]
+    key_ref[...] = total[:rows, qd : qd + kd]
+    value_ref[...] = total[:rows, qd + kd :]
 
 
 def expert_grads_body(count, *refs):
-    xe, dy, dgu, hd = (refs[i * count : i * count + count] for i in range(4))
+    xe, d0, dgu, hd = (refs[i * count : i * count + count] for i in range(4))
     gate_ref, up_ref, down_ref = refs[4 * count :]
     hidden = gate_ref.shape[2]
-    rows = 2 * PAD
-
-    def join(group, b=None):
-        got = [(r[0] if b is None else r[b, 0]) for r in group]
-        return jnp.concatenate([v.reshape(rows, v.shape[-1]) for v in got], axis=0)
+
+    def join(group, at=slice(None)):
+        return jnp.concatenate([r[0, :, :, at].reshape(2 * PAD, -1) for r in group], axis=0)
 
     d_gu, hd_all = join(dgu), join(hd)
-    for b in range(xe[0].shape[0]):
+    for b in range(gate_ref.shape[1] // BLK):
         at = slice(b * BLK, b * BLK + BLK)
-        both = mm_tn(join(xe, b), d_gu)
+        both = mm_tn(join(xe, at), d_gu)
         gate_ref[0, at, :] = both[:, :hidden]
         up_ref[0, at, :] = both[:, hidden:]
-        down_ref[0, :, at] = mm_tn(hd_all, join(dy, b))
-
-
-def expert_grads(xe, dy, dgu, hd, local, width, hidden):
-    count = len(xe)
-    blocks = width // BLK
-    wide = pl.BlockSpec((blocks, 1, 2, PAD, BLK), lambda e: (0, e, 0, 0, 0))
-    specs = [wide] * (2 * count)
-    specs += [pl.BlockSpec((1, 2, PAD, 2 * hidden), lambda e: (e, 0, 0, 0))] * count
-    specs += [pl.BlockSpec((1, 2, PAD, hidden), lambda e: (e, 0, 0, 0))] * count
-    slots = count * 2 * PAD * local
-    return pl.pallas_call(
-        functools.partial(expert_grads_body, count),
-        grid=(local,),
-        out_shape=[sds((local, width, hidden), F32), sds((local, width, hidden), F32), sds((local, hidden, width), F32)],
-        in_specs=specs,
-        out_specs=[pl.BlockSpec((1, width, hidden), lambda e: (e, 0, 0))] * 2
-        + [pl.BlockSpec((1, hidden, width), lambda e: (e, 0, 0))],
-        compiler_params=pltpu.CompilerParams(vmem_limit_bytes=VMEM_LIMIT),
-        cost_estimate=pl.CostEstimate(
-            flops=6 * slots * width * hidden, bytes_accessed=slots * width * 4 + 12 * local * width * hidden, transcendentals=0
-        ),
-        name="expert_grads",
-    )(*xe, *dy, *dgu, *hd)
+        down_ref[0, :, at] = mm_tn(hd_all, join(d0, at))
+
+
+class ExpertGrads:
+    def __init__(self, xe, d0, dgu, hd, pieces=4):
+        self.ins, self.outs = (*xe, *d0, *dgu, *hd), {}
+        self.count, self.pieces = len(xe), pieces
+        self.local, _, _, self.width = xe[0].shape
+        self.hidden = hd[0].shape[3]
+
+    def run(self, piece):
+        local, width, hidden, count = self.local, self.width, self.hidden, self.count
+        each = local // self.pieces
+        first = each * piece
+
+        def whole(n):
+            return pl.BlockSpec((1, 2, PAD, n), lambda e: (e + first, 0, 0, 0))
+
+        slots = count * 2 * PAD * each
+        earlier = list(self.outs[0]) if self.outs else []
+        body = functools.partial(expert_grads_body, count)
+        n = len(self.ins)
+
+        def with_earlier(*refs):
+            body(*refs[:n], *refs[n + len(earlier) :])
+
+        self.outs[0] = pl.pallas_call(
+            with_earlier,
+            grid=(each,),
+            out_shape=[sds((local, width, hidden), F32), sds((local, width, hidden), F32), sds((local, hidden, width), F32)],
+            in_specs=[whole(width)] * (2 * count) + [whole(2 * hidden)] * count + [whole(hidden)] * count
+            + [pl.BlockSpec(memory_space=pl.ANY)] * len(earlier),
+            out_specs=[pl.BlockSpec((1, width, hidden), lambda e: (e + first, 0, 0))] * 2
+            + [pl.BlockSpec((1, hidden, width), lambda e: (e + first, 0, 0))],
+            input_output_aliases={n + i: i for i in range(len(earlier))},
+            compiler_params=pltpu.CompilerParams(vmem_limit_bytes=32 << 20),
+            cost_estimate=pl.CostEstimate(
+                flops=6 * slots * width * hidden, bytes_accessed=slots * width * 4 + 12 * each * width * hidden, transcendentals=0
+            ),
+            name="expert_grads",
+        )(*self.ins, *earlier)
 
 
 def add16(a, b):
@@ -788,12 +917,6 @@
     def swap_c(v):
         return lax.ppermute(v, "tensor", [(i, i ^ 1) for i in range(4)])
 
-    def ring(v):
-        zs = [v]
-        for _ in range(nz - 1):
-            zs.append(shift_z(zs[-1]))
-        return zs, [swap_y(b) for b in zs]
-
     tok, width = tokens.shape
     rows = w_query.shape[0]
     qd, kd = w_query.shape[1], key_matrix.shape[1]
@@ -806,8 +929,11 @@
     aux = jnp.concatenate(
         [w_router, gain_attn[:, None], gain_moe[:, None], jnp.zeros((rows, 128 - experts - 2), BF16)], axis=1
     )
-    w_zs, w_ys = ring(jnp.concatenate([w_query, key_matrix, value_matrix, aux], axis=1))
-    wo_zs, wo_ys = ring(w_out.T)
+    wz = [jnp.concatenate([w_query, key_matrix, value_matrix, aux, w_out.T], axis=1)]
+    wy, wx = [], []
+
+    def out_pair(k):
+        return swap_x(jnp.stack([wz[k][:, used + 128 :], wy[k][:, used + 128 :]]))
 
     pos = kernel_call(
         functools.partial(slots_body, capacity),
@@ -815,34 +941,76 @@
         [idx, picks.T, drop_order.reshape(tok, -1).T],
         name="slots",
     )[0]
-
-    half = experts // 2
-
-    def columns(v, m):
-        return lax.dynamic_slice_in_dim(v, m * BLK, BLK, 1)
-
-    mine, _ = column_blocks(idx)
-    d_own = jnp.concatenate([columns(cotangent, m) for m in mine], axis=1)
-    pos_own = jnp.concatenate(
-        [lax.dynamic_slice_in_dim(pos, c * half, half, 0), jnp.zeros((half, 3 * BLK - tok), BF16)], axis=1
-    )
-    d_own = jnp.concatenate([d_own, pos_own], axis=0)
-
-    def gather(own, ring_own):
-        zs, ys = ring(ring_own)
-        got = []
-        for k in range(nz):
-            if k == 0:
-                far = swap_x(ys[0][:, BLK:])
-                m = jnp.stack([own, jnp.concatenate([ys[0], far], axis=1)])
-            else:
-                pair = jnp.stack([zs[k], ys[k]])
-                far = swap_x(pair[:, :, BLK:])
-                m = jnp.concatenate([pair, far], axis=2)
-            got.append((m, swap_c(m)))
-        return got
-
-    d_all = gather(d_own, d_own[:, : 2 * BLK])
+    part = tok // 4
+    pos_own = lax.dynamic_slice_in_dim(pos, t * part, part, 1)
+    d_own = jnp.concatenate(
+        [
+            lax.dynamic_slice_in_dim(cotangent, t * cols, cols, 1),
+            jnp.concatenate([pos_own, jnp.zeros((experts, cols - part), BF16)], axis=1),
+        ],
+        axis=0,
+    )
+
+    class Rows:
+        def __init__(self, own):
+            self.z, self.y, self.cz, self.cy = {0: own}, {}, {}, {}
+
+        def ring(self, k):
+            self.z[k] = shift_z(self.z[k - 1])
+
+        def side(self, k):
+            self.y[k] = swap_y(self.z[k])
+
+        def core_ring(self, k):
+            self.cz[k] = swap_c(self.z[k])
+
+        def core_side(self, k):
+            self.cy[k] = swap_c(self.y[k])
+
+        def all(self, k):
+            return [v[k] for v in (self.z, self.y, self.cz, self.cy)]
+
+    class Split(Rows):
+        def __init__(self, own):
+            super().__init__(own)
+            self.s, self.x, self.cs, self.cx = {}, {}, {}, {}
+
+        def chip(self, k):
+            self.s[k] = jnp.stack([self.z[k], self.y[k]])
+            self.x[k] = swap_x(self.s[k])
+
+        def core_own(self, k):
+            self.cs[k] = swap_c(self.s[k])
+
+        def core(self, k):
+            self.cx[k] = swap_c(self.x[k])
+
+        def all(self, k):
+            return [v[k] for v in (self.s, self.x, self.cs, self.cx)]
+
+    def meet(*items):
+        places = [(getattr(o, n), k) for o, names, k in items for n in names.split()]
+        values = sync(*[d[k] for d, k in places])
+        for (d, k), v in zip(places, values):
+            d[k] = v
+
+    last = nz - 1
+    for k in range(last):
+        wz.append(shift_z(wz[k]))
+        wy.append(swap_y(wz[k]))
+        if k:
+            wx.append(out_pair(k - 1))
+        if k == 0:
+            wz[1], wy[0], d_own = sync(wz[1], wy[0], d_own)
+        else:
+            wz[k + 1], wy[k] = sync(wz[k + 1], wy[k])
+    wx.append(out_pair(last - 1))
+    wy.append(swap_y(wz[last]))
+    d = Split(after(d_own, wz[last]))
+    d.ring(1)
+    gu = jnp.concatenate([expert_gate, expert_up], axis=2)
+    wy[last], wx[0], gu = sync(wy[last], wx[0], gu)
+    wx.append(out_pair(last))
 
     positions = np.arange(tok, dtype=np.float32)
     inverse = rope_base ** (-(2.0 * np.arange(HEAD_SIZE // 2, dtype=np.float32)) / HEAD_SIZE)
@@ -852,121 +1020,222 @@
     sin = jnp.asarray(np.tile(np.concatenate([-sin, sin], axis=1), (1, 2)).astype(np.float32))
     heads = qd // HEAD_SIZE
     seg_row = document_numbers.reshape(1, tok)
-    o, q, k, v, p, w_all, aux_t = kernel_call(
+    o, q, k_rot, v, w_all, aux_t, *heads_p = kernel_call(
         functools.partial(attend_body, nz),
         [sds((tok, qd), BF16), sds((tok, qd), BF16), sds((tok, kd), BF16), sds((tok, kd), BF16),
-         sds((heads, tok, tok), BF16), sds((width, used + 128), BF16), sds((128, width), BF16)],
-        [idx, *w_zs, *w_ys, tokens, seg_row, seg_row.T, cos, sin],
+         sds((width, used + 128), BF16), sds((128, width), BF16)] + [sds((tok, tok), BF16)] * heads,
+        [idx, *wz, *wy, tokens, seg_row, seg_row.T, cos, sin],
         scratch=[pltpu.VMEM((tok, tok), F32), pltpu.VMEM((tok, used), F32)],
         flops=4e9,
         name="attend",
     )
+    o, d.z[1], d.z[0], *wx[1:] = sync(o, d.z[1], d.z[0], *wx[1:])
+    o_x = swap_x(o)
+    d.ring(2)
+    d.side(0)
     wo = kernel_call(
-        functools.partial(place_body, nz), [sds((width, qd), BF16)], [idx, *wo_zs, *wo_ys], name="place"
+        functools.partial(place_both_body, nz), [sds((2, width, qd), BF16)], [idx, *wz, *wy, *wx], name="place"
     )[0]
-    wo_x = swap_x(wo)
-    wo_c = swap_c(jnp.stack([wo, wo_x]))
-    o_x = swap_x(o)
-    o_c = swap_c(jnp.stack([o, o_x]))
-    h, low, a_own, a_ring = kernel_call(
-        out_body,
-        [sds((tok, width), F32), sds((tok, width), BF16), sds((tok, 3 * BLK), BF16), sds((tok, 2 * BLK), BF16)],
-        [idx, tokens, o, o_x, o_c, wo, wo_x, wo_c, aux_t],
-        flops=5e9,
-        name="out",
-    )
-    a_all = gather(a_own, a_ring)
-
-    gu = jnp.concatenate([expert_gate, expert_up], axis=2)
+    wo_c = swap_c(wo)
     slot_ids = np.arange(local * PAD)
     sel = (r * local + slot_ids[:, None] // PAD == jnp.arange(experts)[None, :]).astype(BF16)
     slot_col = jnp.asarray((slot_ids % PAD).astype(np.float32)[:, None])
     slot_row = jnp.asarray((slot_ids % PAD).astype(np.float32)[None, :])
-    slots = local * PAD
-    blocks = width // BLK
-    big = (blocks, local, 2, PAD, BLK)
-    done = []
-    for kk in range(nz):
-        am, an = a_all[kk]
-        dm, dn = d_all[kk]
-        done.append(
-            kernel_call(
-                functools.partial(experts_body, local),
-                [sds(dm.shape, BF16), sds(dm.shape, BF16), sds(am.shape, BF16), sds(am.shape, BF16),
-                 sds(big, BF16), sds(big, BF16), sds((local, 2, PAD, 2 * hidden), BF16), sds((local, 2, PAD, hidden), BF16)],
-                [idx, am, an, dm, dn, gu, expert_down, aux_t, sel, sel.T, slot_col, slot_row],
-                scratch=[
-                    pltpu.VMEM((experts, tok), BF16), pltpu.VMEM((local, 2, PAD, 1), F32), pltpu.VMEM(big, BF16),
-                    pltpu.VMEM(big, BF16), pltpu.VMEM(big, BF16), pltpu.VMEM((local, 2, PAD, experts), F32),
-                    pltpu.VMEM((2, slots, tok), BF16), pltpu.VMEM((2, tok, slots), BF16),
-                ],
-                flops=12e9,
-                name="experts",
-            )
-        )
-
-    def collect(parts):
-        total = None
-        for kk in list(range(1, nz)) + [0]:
-            m, n = parts[kk]
-            s = add16(m, swap_c(n))
-            own = add16(s[:, :, BLK : 2 * BLK], swap_x(s[:, :, 2 * BLK :]))
-            s = jnp.concatenate([s[:, :, :BLK], own], axis=2)
-            s = add16(s[0], swap_y(s[1])) if total is None else (
-                s[0].astype(F32) + swap_y(s[1]).astype(F32) + shift_z(total).astype(F32)
-            ).astype(BF16)
-            total = s
-        far = swap_x(total)
-        whole = jnp.concatenate([add16(total[:, :BLK], far[:, :BLK]), total[:, BLK:], far[:, BLK:]], axis=1)
-        return whole, swap_c(whole)
-
-    fm, fn = collect([d[0:2] for d in done])
-    ym, yn = collect([d[2:4] for d in done])
-    mixed = kernel_call(
-        mixed_body, [sds((tok, cols), BF16)], [idx, ym, yn, h], scratch=[pltpu.VMEM((tok, width), F32)], name="mixed"
-    )[0]
-
-    def scatter_dp(v):
-        def block(kk, yy):
-            return lax.dynamic_index_in_dim(v, ((z - kk) % nz) * 2 + yy, 0, keepdims=False)
-
-        total = None
-        for kk in list(range(1, nz)) + [0]:
-            s = block(kk, y).astype(F32) + swap_y(block(kk, 1 - y)).astype(F32)
-            if total is not None:
-                s = s + shift_z(total).astype(F32)
-            total = s.astype(BF16)
-        return s
-
-    d_h, d_o, early = kernel_call(
-        hidden_back_body,
-        [sds((tok, cols), F32), sds((tok, qd), BF16), sds((width, qd + 128), BF16)],
+    o_x, wo_c, sel, d.z[2], d.y[0] = sync(o_x, wo_c, sel, d.z[2], d.y[0])
+    d.ring(3)
+    d.side(1)
+    d.chip(0)
+    d.core_own(0)
+    o_c = swap_c(jnp.stack([o, o_x]))
+    h, low, ring0 = kernel_call(
+        out_body,
+        [sds((tok, width), F32), sds((tok, width), BF16), sds((tok, 2 * cols), BF16)],
+        [idx, tokens, o, o_x, o_c, wo, wo_c, aux_t],
+        flops=5e9,
+        name="out",
+    )
+    ring0, d.z[3], d.y[1], d.x[0], d.cs[0] = sync(ring0, d.z[3], d.y[1], d.x[0], d.cs[0])
+    a = Rows(ring0)
+    done = {}
+
+    def run_experts(k):
+        done[k] = experts_call(idx, a.all(k), d.all(k), gu, expert_down, aux_t, sel, slot_col, slot_row)
+
+    class Sums:
+        def __init__(self, at):
+            self.at, self.c, self.s, self.y, self.total = at, {}, {}, {}, {}
+
+        def core(self, k):
+            self.c[k] = swap_c(done[k][self.at + 1])
+
+        def side(self, k):
+            m, n = done[k][self.at], self.c[k]
+            self.s[k] = add16(m[0], n[0])
+            self.y[k] = swap_y(add16(m[1], n[1]))
+
+        def ring(self, k):
+            total = self.s[k].astype(F32) + self.y[k].astype(F32)
+            if self.total:
+                total = total + self.total[0].astype(F32)
+            total = total.astype(BF16)
+            self.total[0] = total if k == 0 else shift_z(total)
+
+    class SplitSums(Sums):
+        def __init__(self, at):
+            super().__init__(at)
+            self.x = {}
+
+        def chip(self, k):
+            self.x[k] = swap_x(add16(done[k][self.at][:, :, cols:], self.c[k][:, :, cols:]))
+
+        def side(self, k):
+            m, n, far = done[k][self.at], self.c[k], self.x[k]
+            own = [(m[q, :, :cols].astype(F32) + n[q, :, :cols].astype(F32) + far[q].astype(F32)).astype(BF16) for q in (0, 1)]
+            self.s[k] = own[0]
+            self.y[k] = swap_y(own[1])
+
+    sx, sy = Sums(0), SplitSums(2)
+
+    class Ran:
+        out = done
+
+    ran = Ran()
+    a.ring(1)
+    a.side(0)
+    a.core_ring(0)
+    d.chip(1)
+    d.core_own(1)
+    d.core(0)
+    meet((a, "z", 1), (a, "y cz", 0), (d, "x cs", 1), (d, "cx", 0))
+    a.ring(2)
+    a.side(1)
+    a.core_side(0)
+    a.core_ring(1)
+    d.side(2)
+    d.core(1)
+    run_experts(0)
+    meet((a, "z", 2), (a, "y cz", 1), (ran, "out", 0), (d, "y", 2), (d, "cx", 1))
+    a.ring(3)
+    a.side(2)
+    a.core_side(1)
+    a.core_ring(2)
+    d.side(3)
+    d.chip(2)
+    d.core_own(2)
+    run_experts(1)
+    meet((a, "z", 3), (a, "y cz", 2), (ran, "out", 1), (d, "y", 3), (d, "x cs", 2))
+    a.side(3)
+    a.core_side(2)
+    d.core(2)
+    sx.core(1)
+    meet((a, "cy", 2), (sx, "c", 1), (d, "cx", 2), (ran, "out", 1))
+    a.core_ring(3)
+    d.chip(3)
+    d.core_own(3)
+    sx.side(1)
+    sy.core(1)
+    run_experts(2)
+    meet((a, "y cz", 3), (sx, "s y", 1), (sy, "c", 1), (ran, "out", 2), (d, "x cs", 3))
+    sx.ring(1)
+    a.core_side(3)
+    d.core(3)
+    sx.core(2)
+    meet((a, "cy", 3), (sx, "c", 2), (d, "cx", 3), (ran, "out", 1), (ran, "out", 2), (sy, "c", 1))
+    sx.side(2)
+    sy.chip(1)
+    sy.core(2)
+    run_experts(3)
+    meet((sx, "s y", 2), (sx, "total", 0), (sy, "x", 1), (sy, "c", 2), (ran, "out", 3))
+    grads = ExpertGrads(*[[done[k][i] for k in range(nz)] for i in range(4, 8)])
+    sx.ring(2)
+    sx.core(3)
+    meet((sx, "c", 3), (ran, "out", 3), (sy, "c", 2))
+    sx.side(3)
+    sx.core(0)
+    sy.chip(2)
+    sy.core(3)
+    grads.run(0)
+    grads.run(1)
+    meet((sx, "s y", 3), (sx, "total", 0), (sx, "c", 0), (sy, "x", 2), (sy, "c", 3), (grads, "outs", 0))
+    sx.ring(3)
+    sx.side(0)
+    sy.chip(3)
+    sy.core(0)
+    grads.run(2)
+    meet((sx, "s y", 0), (sx, "total", 0), (sy, "x", 3), (sy, "c", 0), (grads, "outs", 0))
+    sx.ring(0)
+    far = swap_x(sx.total[0])
+    sy.side(1)
+    sy.side(2)
+    grads.run(3)
+    sx.total[0], far, *rest = sync(sx.total[0], far, sy.s[1], sy.y[1], sy.s[2], sy.y[2], sy.x[3], sy.c[0], grads.outs[0])
+    sy.s[1], sy.y[1], sy.s[2], sy.y[2], sy.x[3], sy.c[0], grads.outs[0] = rest
+    mine = sx.total[0].astype(F32) + jnp.concatenate([far[:, cols:], far[:, :cols]], axis=1).astype(F32)
+    head, tail = mine[:tok], sx.total[0][tok:].astype(F32) + far[tok:].astype(F32)
+    fm = jnp.concatenate([head.astype(BF16), tail.astype(BF16)], axis=0)
+    fn = swap_c(fm)
+    fm, fn, sy.y[1], sy.x[3], sy.c[0] = sync(fm, fn, sy.y[1], sy.x[3], sy.c[0])
+    sy.side(3)
+    sy.ring(1)
+    sy.chip(0)
+    d_h, d_o, *early = kernel_call(
+        functools.partial(hidden_back_body, nz),
+        [sds((tok, cols), F32), sds((tok, qd), BF16)] + [sds((rows, qd + 128), BF16)] * n_dp,
         [idx, fm, fn, h, low, aux_t, pos, cotangent, o, wo],
-        scratch=[pltpu.VMEM((tok, width), F32), pltpu.VMEM((experts, tok), F32)],
+        scratch=[pltpu.VMEM((tok, width), F32), pltpu.VMEM((experts, tok), F32), pltpu.VMEM((n_dp, rows, qd + 128), BF16)],
         flops=3e9,
         name="hidden_back",
     )
-    early = scatter_dp(early.reshape(n_dp, rows, qd + 128))
-    grad_out = early[:, :qd].T
-    grad_router = early[:, qd : qd + experts]
-    grad_gain_moe = early[:, qd + experts]
-    late, dxm, dxn = kernel_call(
-        attend_back_body,
-        [sds((n_dp, rows + 16, used), BF16), sds((tok, 2 * cols + 128), BF16), sds((tok, 2 * cols + 128), BF16)],
-        [idx, d_o, p, q, k, v, w_all, tokens, aux_t, cos, sin],
-        scratch=[pltpu.VMEM((tok, used), F32), pltpu.VMEM((tok, used), BF16), pltpu.VMEM((4, tok, cols), BF16)],
+    d_o, early, sy.total[0], sy.s[3], sy.y[3], sy.x[0] = sync(d_o, early, sy.total[0], sy.s[3], sy.y[3], sy.x[0])
+
+    class Weights:
+        def __init__(self, v):
+            self.kept, self.sent, self.y, self.total = v[:nz], v[nz:], {}, {}
+
+        def side(self, k):
+            self.y[k] = swap_y(self.sent[k])
+
+        def ring(self, k):
+            total = self.kept[k].astype(F32) + self.y[k].astype(F32)
+            if self.total:
+                total = total + self.total[0].astype(F32)
+            self.total[0] = shift_z(total.astype(BF16))
+
+        def last(self):
+            return self.kept[0], self.y[0], self.total[0]
+
+    early = Weights(early)
+    early.side(1)
+    sy.side(0)
+    sy.ring(2)
+    late, dxm, dxn = [], None, None
+    dxm, dxn, *late = kernel_call(
+        functools.partial(attend_back_body, nz),
+        [sds((tok, 2 * cols + 128), BF16), sds((tok, 2 * cols + 128), BF16)] + [sds((rows + 16, used), BF16)] * n_dp,
+        [idx, d_o, v, k_rot, q, cos, sin, tokens, aux_t, w_all, *heads_p],
+        scratch=[
+            pltpu.VMEM((tok, used), F32), pltpu.VMEM((tok, used), BF16), pltpu.VMEM((4, tok, cols), BF16),
+            pltpu.VMEM((n_dp, rows + 16, used), BF16),
+        ],
         flops=5e9,
         name="attend_back",
     )
-    late = scatter_dp(late)
-    grad_query = late[:rows, :qd]
-    grad_key = late[:rows, qd : qd + kd]
-    grad_value = late[:rows, qd + kd :]
-    gain_part = late[rows, :rows] + late[rows + 1, :rows]
-    gain_part = gain_part + swap_c(gain_part)
-    grad_gain_attn = gain_part + swap_x(gain_part)
-
+    late, dxm, dxn, early.y[1], sy.y[0], sy.s[0], sy.total[0] = sync(
+        late, dxm, dxn, early.y[1], sy.y[0], sy.s[0], sy.total[0]
+    )
+    late = Weights(late)
+    late.side(1)
+    early.side(2)
+    early.ring(1)
+    sy.ring(3)
     got = swap_c(dxn)
+    late.y[1], early.y[2], early.total[0], sy.total[0], got = sync(
+        late.y[1], early.y[2], early.total[0], sy.total[0], got
+    )
+    late.side(2)
+    late.ring(1)
+    early.side(3)
+    early.ring(2)
     ours = dxm.astype(F32) + got.astype(F32)
     mean_part = ours[:, 2 * cols] + ours[:, 2 * cols + 1]
     high, lowp = split16(mean_part)
@@ -974,17 +1243,45 @@
         [ours[:, cols : 2 * cols].astype(BF16), high[:, None], lowp[:, None], jnp.zeros((tok, 126), BF16)], axis=1
     )
     got = swap_x(send)
+    y_sum = sy.s[0].astype(F32) + sy.y[0].astype(F32) + sy.total[0].astype(F32)
+    mixed = (y_sum + lax.dynamic_slice_in_dim(h, t * cols, cols, 1)).astype(BF16)
+    late.y[2], late.total[0], early.y[3], early.total[0], got, mixed = sync(
+        late.y[2], late.total[0], early.y[3], early.total[0], got, mixed
+    )
+    late.side(3)
+    late.ring(2)
+    early.side(0)
+    early.ring(3)
+    x_full = tokens.astype(F32)
+    r1 = lax.rsqrt(jnp.mean(x_full * x_full, axis=-1, keepdims=True) + epsilon)
     d_norm = ours[:, :cols] + got[:, :cols].astype(F32)
     mean = (mean_part + got[:, cols].astype(F32) + got[:, cols + 1].astype(F32))[:, None] / width
-    x_full = tokens.astype(F32)
-    r1 = lax.rsqrt(jnp.mean(x_full * x_full, axis=-1, keepdims=True) + epsilon)
     x_cols = lax.dynamic_slice_in_dim(tokens, t * cols, cols, 1).astype(F32) * r1
     gain_row = lax.dynamic_slice_in_dim(aux_t[64:65], t * cols, cols, 1).astype(F32)
     grad_tokens = d_h + r1 * (d_norm * gain_row - x_cols * mean)
-
-    grad_gate, grad_up, grad_down = expert_grads(
-        [d[4] for d in done], [d[5] for d in done], [d[6] for d in done], [d[7] for d in done], local, width, hidden
-    )
+    late.y[3], late.total[0], early.y[0], early.total[0], grad_tokens = sync(
+        late.y[3], late.total[0], early.y[0], early.total[0], grad_tokens
+    )
+    late.side(0)
+    late.ring(3)
+    grad_out, grad_router, gain_rows = kernel_call(
+        early_end_body,
+        [sds((qd, rows), F32), sds((rows, experts), F32), sds((8, rows), F32)],
+        [idx, *early.last()],
+        name="early_end",
+    )
+    grad_gain_moe = gain_rows[0]
+    late.y[0], late.total[0], grad_out = sync(late.y[0], late.total[0], grad_out)
+    grad_query, grad_key, grad_value, gain_rows = kernel_call(
+        late_end_body,
+        [sds((rows, qd), F32), sds((rows, kd), F32), sds((rows, kd), F32), sds((8, rows), F32)],
+        [idx, *late.last()],
+        name="late_end",
+    )
+    gain_part = gain_rows[0] + gain_rows[1]
+    gain_part = gain_part + swap_c(gain_part)
+    grad_gain_attn = gain_part + swap_x(gain_part)
+    grad_gate, grad_up, grad_down = grads.outs[0]
     return (
         mixed,
         grad_tokens,

time: 647 us -> 472 us (0.73)
  waiting for transfers between devices: 278 us -> 176 us
  Pallas kernels: 188 us -> 156 us
  other arithmetic: 57 us -> 41.2 us
  starting transfers between devices: 78.9 us -> 63.9 us
  local copies, waits for them, and re-layouts: 33 us -> 25.3 us
    ppermute x22 -> x16, waiting for transfers between devices: 111 us -> 35 us  [swap_x(): return lax.ppermute(v, 'tensor', [(i, i ^ 2) for i in range(4)])]
    pallas_call x12 -> x16, Pallas kernels: 188 us -> 156 us  [the longest x4 102 us: experts_call(): pl.pallas_call(functools.partial(experts_body, local), out_shape=outs, in...]
    ppermute x32 -> x28, waiting for transfers between devices: 102 us -> 71.5 us  [swap_y(): return lax.ppermute(v, 'dp', [(i, i ^ 1) for i in range(n_dp)])]
    ppermute x22 -> x29, waiting for transfers between devices: 0.06 us -> 15.9 us  [swap_c(): return lax.ppermute(v, 'tensor', [(i, i ^ 1) for i in range(4)])]
    ppermute x24 -> x21, waiting for transfers between devices: 65.6 us -> 53.2 us  [shift_z(): lax.ppermute(v, 'dp', [(i, (i // 2 + 1) % nz * 2 + i % 2) for i in range(...]
    unnamed x120 -> x178, local copies, waits for them, and re-layouts: 10.4 us -> 19.4 us
    ppermute x22 -> x16, starting transfers between devices: 27.4 us -> 18.6 us  [swap_x(): return lax.ppermute(v, 'tensor', [(i, i ^ 2) for i in range(4)])]
    convert_element_type x20 -> x8, other arithmetic: 16.2 us -> 9.95 us  [add16(): return (a.astype(F32) + b.astype(F32)).astype(BF16)]
  transfers between devices with their start and end apart: 100 -> 94, of which waited for: 43 -> 37; matrix products, arithmetic and copies ran while one was open for 12% -> 9% of each run, Pallas kernels for 28% -> 33%
where the time goes in v2:
time: 472 us; the launch traced here: 464 us
  waiting for transfers between devices  176 us (37%)
  Pallas kernels  156 us (33%)
  starting transfers between devices  63.9 us (14%)
  other arithmetic  41.2 us (9%)
  local copies, waits for them, and re-layouts  25.3 us (5%)
    pallas_call x4, Pallas kernels, experts_call(): pl.pallas_call(functools.partial(experts_body, local), out_shape=outs, in...  102 us
    ppermute x28, waiting for transfers between devices, swap_y(): return lax.ppermute(v, 'dp', [(i, i ^ 1) for i in range(n_dp)])  71.5 us
    ppermute x21, waiting for transfers between devices, shift_z(): lax.ppermute(v, 'dp', [(i, (i // 2 + 1) % nz * 2 + i % 2) for i in range(...  53.2 us
    ppermute x16, waiting for transfers between devices, swap_x(): return lax.ppermute(v, 'tensor', [(i, i ^ 2) for i in range(4)])  35 us
    pallas_call x8, Pallas kernels, kernel_call(): pl.pallas_call(body, out_shape=[sds(o.shape, o.dtype) for o in outs], in_...  33.4 us
    ppermute x28, starting transfers between devices, swap_y(): return lax.ppermute(v, 'dp', [(i, i ^ 1) for i in range(n_dp)])  29.6 us
    pallas_call x4, Pallas kernels, run(): pl.pallas_call(with_earlier, grid=(each,), out_shape=[sds((local, width,...  20.8 us
    unnamed x178, local copies, waits for them, and re-layouts  19.4 us
  transfers between devices with their start and end apart: 94, of which 37 were waited for; matrix products, arithmetic and copies ran while one was open for 9% of the time, Pallas kernels for 33%

profile of v2, /device:TPU:0, one launch (start us, length us, event | category | flops | bytes accessed | tf_op | source)
XLA Modules:
  0.0 464.2 jit_solution(385896880864716617)
XLA Ops:
  4.2 3.0 collective-permute-start.1
  7.3 1.6 collective-permute-start
  11.1 1.9 slots.1.pos_ref
  15.0 6.3 %pad_maximum_fusion.refs_8_ = bf16[8,1536,256]{2,1,0:T(8,128)(2,1)} fusion(bf16[8,1536,128]{2,1,0:T(8,128)(2,1)} %param.32, bf16[8,1536,128]{2,1,0:T(8,128)(2,1)} %param.31), kind=kLoop, calls=%fused_computation | loop fusion | flops 12582912 | bytes 12582912 | tf_op jit(solution)/shard_map/concatenate | solution.py:1011
  21.9 1.6 collective-permute-start.2
  25.1 7.6 %collective-permute-done.3.refs_5_ = bf16[192,1152]{1,0:T(8,128)(2,1)S(1)} collective-permute-done((bf16[192,1152]{1,0:T(8,128)(2,1)S(1)}, bf16[192,1152]{1,0:T(8,128)(2,1)S(1)}, u32[]{:S(2)}, u32[]{:S(2)}) %collective-permute-start.3) | collective-permute-done | bytes 442400 | tf_op jit(solution)/shard_map/ppermute | solution.py:912
  32.7 2.0 collective-permute-done.2.refs_2_
  36.3 1.6 collective-permute-start.9
  37.9 7.0 %collective-permute-done.5.refs_6_ = bf16[192,1152]{1,0:T(8,128)(2,1)S(1)} collective-permute-done((bf16[192,1152]{1,0:T(8,128)(2,1)S(1)}, bf16[192,1152]{1,0:T(8,128)(2,1)S(1)}, u32[]{:S(2)}, u32[]{:S(2)}) %collective-permute-start.5) | collective-permute-done | bytes 442400 | tf_op jit(solution)/shard_map/ppermute | solution.py:912
  44.9 3.0 collective-permute-done.4.refs_3_
  50.1 6.8 %collective-permute-done.6.refs_7_ = bf16[192,1152]{1,0:T(8,128)(2,1)S(1)} collective-permute-done((bf16[192,1152]{1,0:T(8,128)(2,1)S(1)}, bf16[192,1152]{1,0:T(8,128)(2,1)S(1)}, u32[]{:S(2)}, u32[]{:S(2)}) %collective-permute-start.6) | collective-permute-done | bytes 442400 | tf_op jit(solution)/shard_map/ppermute | solution.py:912
  56.9 1.6 collective-permute-start.11
  58.5 7.5 %attend.1 = (bf16[512,384]{1,0:T(8,128)(2,1)S(1)}, bf16[512,384]{1,0:T(8,128)(2,1)S(1)}, bf16[512,128]{1,0:T(8,128)(2,1)S(1)}, bf16[512,128]{1,0:T(8,128)(2,1)S(...) custom-call(s32[5]{0:T(128)S(1)} %stack.104.idx, ...), custom_call_target="tpu_custom_call" | custom-call | flops 4000000000 | bytes 12587008 | tf_op jit(solution)/shard_map/attend/pallas_call | solution.py:404
  71.6 10.1 %collective-permute-done.12.o1 = bf16[512,384]{1,0:T(8,128)(2,1)} collective-permute-done((bf16[512,384]{1,0:T(8,128)(2,1)S(1)}, bf16[512,384]{1,0:T(8,128)(2,1)}, u32[]{:S(2)}, u32[]{:S(2)}) %collective-permute-start.12) | collective-permute-done | bytes 393248 | tf_op jit(solution)/shard_map/ppermute | solution.py:915
  82.6 2.1 collective-permute-done.14
  90.2 5.8 %out.1 = (f32[512,1536]{1,0:T(8,128)S(1)}, bf16[512,1536]{1,0:T(8,128)(2,1)S(1)}, bf16[512,768]{1,0:T(8,128)(2,1)S(1)}) custom-call(s32[5]{0:T(128)S(1)} %stack.104.idx, bf16[512,1536]{1,0:T(8,128)(2,1)S(1)} %copy-done.17, bf16[512,384]{1,0:T(8,128)(2,1)S(1)} %get-tuple-element.306.o0.o_ref, bf16[512,384]{1,0:T(8,128)(2,1)} %collective-permute-done.12.o1, ...), custom_call_target="tpu_custom_call" | custom-call | flops 5000000000 | bytes 13762560 | tf_op jit(solution)/shard_map/out/pallas_call | solution.py:404
  96.1 1.7 copy-done.14
  100.5 3.3 collective-permute-done.17
  103.8 5.7 %collective-permute-done.19.refs_5_ = bf16[2,576,384]{2,1,0:T(8,128)(2,1)S(1)} collective-permute-done((bf16[2,576,384]{2,1,0:T(8,128)(2,1)S(1)}, bf16[2,576,384]{2,1,0:T(8,128)(2,1)S(1)}, u32[]{:S(2)}, u32[]{:S(2)}) %collective-permute-start.19) | collective-permute-done | bytes 884768 | tf_op jit(solution)/shard_map/ppermute | solution.py:915
  113.4 18.3 %collective-permute-done.22.refs_1_ = bf16[512,768]{1,0:T(8,128)(2,1)S(1)} collective-permute-done((bf16[512,768]{1,0:T(8,128)(2,1)S(1)}, bf16[512,768]{1,0:T(8,128)(2,1)S(1)}, u32[]{:S(2)}, u32[]{:S(2)}) %collective-permute-start.22) | collective-permute-done | bytes 786464 | tf_op jit(solution)/shard_map/ppermute | solution.py:912
  131.7 3.2 collective-permute-done.21.refs_0_
  139.9 32.7 %experts.4 = (bf16[2,544,768]{2,1,0:T(8,128)(2,1)}, bf16[2,544,768]{2,1,0:T(8,128)(2,1)}, bf16[2,512,768]{2,1,0:T(8,128)(2,1)}, bf16[2,512,768]{2,1,0:T(8,128)(2...) custom-call(s32[5]{0:T(128)} %copy-done.29, ...), custom_call_target="tpu_custom_call" | custom-call | flops 12582912000 | bytes 31457280 | tf_op jit(solution)/shard_map/experts/pallas_call | solution.py:681
  176.2 9.9 %collective-permute-done.37 = bf16[576,384]{1,0:T(8,128)(2,1)S(1)} collective-permute-done((bf16[576,384]{1,0:T(8,128)(2,1)}, bf16[576,384]{1,0:T(8,128)(2,1)S(1)}, u32[]{:S(2)}, u32[]{:S(2)}) %collective-permute-start.37) | collective-permute-done | bytes 442400 | tf_op jit(solution)/shard_map/ppermute | solution.py:912
  189.3 23.1 %experts.5 = (bf16[2,544,768]{2,1,0:T(8,128)(2,1)}, bf16[2,544,768]{2,1,0:T(8,128)(2,1)}, bf16[2,512,768]{2,1,0:T(8,128)(2,1)}, bf16[2,512,768]{2,1,0:T(8,128)(2...) custom-call(s32[5]{0:T(128)} %copy-done.29, ...), custom_call_target="tpu_custom_call" | custom-call | flops 12582912000 | bytes 31457280 | tf_op jit(solution)/shard_map/experts/pallas_call | solution.py:681
  214.0 5.7 %collective-permute-done.42.refs_3_ = bf16[512,768]{1,0:T(8,128)(2,1)S(1)} collective-permute-done((bf16[512,768]{1,0:T(8,128)(2,1)}, bf16[512,768]{1,0:T(8,128)(2,1)S(1)}, u32[]{:S(2)}, u32[]{:S(2)}) %collective-permute-start.42) | collective-permute-done | bytes 786464 | tf_op jit(solution)/shard_map/ppermute | solution.py:918
  221.0 2.2 pad_maximum_fusion.4.refs_4_
  225.8 22.8 %experts.6 = (bf16[2,544,768]{2,1,0:T(8,128)(2,1)}, bf16[2,544,768]{2,1,0:T(8,128)(2,1)}, bf16[2,512,768]{2,1,0:T(8,128)(2,1)}, bf16[2,512,768]{2,1,0:T(8,128)(2...) custom-call(s32[5]{0:T(128)} %copy-done.29, ...), custom_call_target="tpu_custom_call" | custom-call | flops 12582912000 | bytes 31457280 | tf_op jit(solution)/shard_map/experts/pallas_call | solution.py:681
  248.7 2.6 collective-permute-done.45
  251.8 2.2 add_convert_fusion.7
  254.0 3.4 collective-permute-done.49.refs_3_
  257.7 2.6 add_convert_fusion.16
  260.8 1.7 fusion.4
  263.0 23.2 %experts.7 = (bf16[2,544,768]{2,1,0:T(8,128)(2,1)}, bf16[2,544,768]{2,1,0:T(8,128)(2,1)}, bf16[2,512,768]{2,1,0:T(8,128)(2,1)}, bf16[2,512,768]{2,1,0:T(8,128)(2...) custom-call(s32[5]{0:T(128)} %copy-done.29, ...), custom_call_target="tpu_custom_call" | custom-call | flops 12582912000 | bytes 31457280 | tf_op jit(solution)/shard_map/experts/pallas_call | solution.py:681
  286.8 3.3 collective-permute-done.56
  290.2 2.1 add_convert_fusion.4
  292.4 2.0 fusion.6
  294.4 1.6 collective-permute-start.57
  295.9 1.6 add_convert_fusion.15
  297.5 1.6 collective-permute-start.60
  299.2 2.1 copy-done.2
  301.3 2.1 copy-done.3
  304.4 5.2 %expert_grads.4 = (f32[8,1536,128]{2,1,0:T(8,128)}, f32[8,1536,128]{2,1,0:T(8,128)}, f32[8,128,1536]{2,1,0:T(8,128)}) custom-call(bf16[8,2,80,1536]{3,2,1,0:T(8,128)(2,1)S(1)} %copy-done, bf16[8,2,80,1536]{3,2,1,0:T(8,128)(2,1)S(1)} %copy-done.1, bf16[8,2,80,1536]{3,2,1,0:T(8,128)(2,1)S(1)} %copy-done.2, bf16[8,2,80,1536]{3,2,1,0:T(8,128)(2,1)S(1)} %copy-done.3, ...), custom_call_target="tpu_custom_call" | custom-call | flops 1509949440 | bytes 12582912 | tf_op jit(solution)/shard_map/expert_grads/pallas_call | solution.py:864
  309.5 5.2 %expert_grads.5 = (f32[8,1536,128]{2,1,0:T(8,128)}, f32[8,1536,128]{2,1,0:T(8,128)}, f32[8,128,1536]{2,1,0:T(8,128)}) custom-call(bf16[8,2,80,1536]{3,2,1,0:T(8,128)(2,1)S(1)} %copy-done, bf16[8,2,80,1536]{3,2,1,0:T(8,128)(2,1)S(1)} %copy-done.1, ...), custom_call_target="tpu_custom_call", output_to_operand_aliasing={{0}: (16, {}), {1}: (17, {}), {2}: (18, {})} | custom-call | flops 1509949440 | bytes 12582912 | tf_op jit(solution)/shard_map/expert_grads/pallas_call | solution.py:864
  315.3 1.8 collective-permute-done.60
  321.8 1.6 collective-permute-start.64
  323.3 5.2 %expert_grads.6 = (f32[8,1536,128]{2,1,0:T(8,128)}, f32[8,1536,128]{2,1,0:T(8,128)}, f32[8,128,1536]{2,1,0:T(8,128)}) custom-call(bf16[8,2,80,1536]{3,2,1,0:T(8,128)(2,1)S(1)} %copy-done, bf16[8,2,80,1536]{3,2,1,0:T(8,128)(2,1)S(1)} %copy-done.1, ...), custom_call_target="tpu_custom_call", output_to_operand_aliasing={{0}: (16, {}), {1}: (17, {}), {2}: (18, {})} | custom-call | flops 1509949440 | bytes 12582912 | tf_op jit(solution)/shard_map/expert_grads/pallas_call | solution.py:864
  328.5 11.3 %collective-permute-done.64 = bf16[2,512,384]{2,1,0:T(8,128)(2,1)S(1)} collective-permute-done((bf16[2,512,384]{2,1,0:T(8,128)(2,1)S(1)}, bf16[2,512,384]{2,1,0:T(8,128)(2,1)S(1)}, u32[]{:S(2)}, u32[]{:S(2)}) %collective-permute-start.64) | collective-permute-done | bytes 786464 | tf_op jit(solution)/shard_map/ppermute | solution.py:915
  341.6 1.6 collective-permute-start.66
  343.2 1.6 fusion.15
  348.4 5.2 %expert_grads.7 = (f32[8,1536,128]{2,1,0:T(8,128)}, f32[8,1536,128]{2,1,0:T(8,128)}, f32[8,128,1536]{2,1,0:T(8,128)}) custom-call(bf16[8,2,80,1536]{3,2,1,0:T(8,128)(2,1)S(1)} %copy-done, bf16[8,2,80,1536]{3,2,1,0:T(8,128)(2,1)S(1)} %copy-done.1, ...), custom_call_target="tpu_custom_call", output_to_operand_aliasing={{0}: (16, {}), {1}: (17, {}), {2}: (18, {})} | custom-call | flops 1509949440 | bytes 12582912 | tf_op jit(solution)/shard_map/expert_grads/pallas_call | solution.py:864
  353.6 3.3 collective-permute-done.67
  356.9 5.7 %collective-permute-done.68 = bf16[512,384]{1,0:T(8,128)(2,1)S(1)} collective-permute-done((bf16[512,384]{1,0:T(8,128)(2,1)S(1)}, bf16[512,384]{1,0:T(8,128)(2,1)S(1)}, u32[]{:S(2)}, u32[]{:S(2)}) %collective-permute-start.68) | collective-permute-done | bytes 393248 | tf_op jit(solution)/shard_map/ppermute | solution.py:912
  363.1 2.3 collective-permute-done.69.fn_ref
  370.2 6.0 %hidden_back.1 = (f32[512,384]{1,0:T(8,128)S(1)}, bf16[512,384]{1,0:T(8,128)(2,1)S(1)}, bf16[192,512]{1,0:T(8,128)(2,1)S(1)}, bf16[192,512]{1,0:T(8,128)(2,1)S(1...) custom-call(s32[5]{0:T(128)S(1)} %copy-done.30, ...), custom_call_target="tpu_custom_call" | custom-call | flops 3000000000 | bytes 13926400 | tf_op jit(solution)/shard_map/hidden_back/pallas_call | solution.py:404
  376.2 3.7 collective-permute-done.70
  379.9 5.4 %collective-permute-done.72 = bf16[2,512,384]{2,1,0:T(8,128)(2,1)S(1)} collective-permute-done((bf16[2,512,384]{2,1,0:T(8,128)(2,1)S(1)}, bf16[2,512,384]{2,1,0:T(8,128)(2,1)S(1)}, u32[]{:S(2)}, u32[]{:S(2)}) %collective-permute-start.72) | collective-permute-done | bytes 786464 | tf_op jit(solution)/shard_map/ppermute | solution.py:915
  389.6 9.4 %attend_back.1 = (bf16[512,896]{1,0:T(8,128)(2,1)S(1)}, bf16[512,896]{1,0:T(8,128)(2,1)S(1)}, bf16[208,640]{1,0:T(8,128)(2,1)S(1)}, bf16[208,640]{1,0:T(8,128)(2...) custom-call(s32[5]{0:T(128)S(1)} %copy-done.30, ...), custom_call_target="tpu_custom_call" | custom-call | flops 5000000000 | bytes 13008896 | tf_op jit(solution)/shard_map/attend_back/pallas_call | solution.py:404
  405.5 2.9 collective-permute-done.78
  409.4 10.5 %collective-permute-done.79 = bf16[192,512]{1,0:T(8,128)(2,1)S(1)} collective-permute-done((bf16[192,512]{1,0:T(8,128)(2,1)S(1)}, bf16[192,512]{1,0:T(8,128)(2,1)S(1)}, u32[]{:S(2)}, u32[]{:S(2)}) %collective-permute-start.79) | collective-permute-done | bytes 196640 | tf_op jit(solution)/shard_map/ppermute | solution.py:909
  425.8 3.5 collective-permute-done.76
  430.3 5.6 %collective-permute-done.84 = bf16[192,512]{1,0:T(8,128)(2,1)S(1)} collective-permute-done((bf16[192,512]{1,0:T(8,128)(2,1)S(1)}, bf16[192,512]{1,0:T(8,128)(2,1)S(1)}, u32[]{:S(2)}, u32[]{:S(2)}) %collective-permute-start.84) | collective-permute-done | bytes 196640 | tf_op jit(solution)/shard_map/ppermute | solution.py:909
  438.7 7.4 %collective-permute-done.89.ring = bf16[192,512]{1,0:T(8,128)(2,1)S(1)} collective-permute-done((bf16[192,512]{1,0:T(8,128)(2,1)S(1)}, bf16[192,512]{1,0:T(8,128)(2,1)S(1)}, u32[]{:S(2)}, u32[]{:S(2)}) %collective-permute-start.89) | collective-permute-done | bytes 196640 | tf_op jit(solution)/shard_map/ppermute | solution.py:909
  446.1 2.9 collective-permute-done.87
  449.9 7.5 %collective-permute-done.91.ring = bf16[208,640]{1,0:T(8,128)(2,1)S(1)} collective-permute-done((bf16[208,640]{1,0:T(8,128)(2,1)S(1)}, bf16[208,640]{1,0:T(8,128)(2,1)S(1)}, u32[]{:S(2)}, u32[]{:S(2)}) %collective-permute-start.91) | collective-permute-done | bytes 266272 | tf_op jit(solution)/shard_map/ppermute | solution.py:909
  (396 shorter events, 97.2 us)
Async XLA Ops:
  4.2 17.0 %collective-permute-start.1 = (bf16[192,1152]{1,0:T(8,128)(2,1)S(1)}, bf16[192,1152]{1,0:T(8,128)(2,1)S(1)}, u32[]{:S(2)}, u32[]{:S(2)}) collective-permute-start(bf16[192,1152]{1,0:T(8,128)(2,1)S(1)} %concatenate.21.refs_0_), channel_id=1, source_target_pairs={{0,4},{4,0},{8,12},{12,8},{16,20},{20,16},{24,28},{28,24},{1,5},{5... | collective-permute-start | bytes 1327112 | tf_op jit(solution)/shard_map/ppermute | solution.py:912
  7.3 14.0 %collective-permute-start = (bf16[192,1152]{1,0:T(8,128)(2,1)S(1)}, bf16[192,1152]{1,0:T(8,128)(2,1)S(1)}, u32[]{:S(2)}, u32[]{:S(2)}) collective-permute-start(bf16[192,1152]{1,0:T(8,128)(2,1)S(1)} %concatenate.21.refs_0_), channel_id=1, source_target_pairs={{0,8},{4,12},{8,16},{12,20},{16,24},{20,28},{24,0},{28,4},{1,9},{5... | collective-permute-start | bytes 1327112 | tf_op jit(solution)/shard_map/ppermute | solution.py:909
  21.9 12.9 %collective-permute-start.2 = (bf16[192,1152]{1,0:T(8,128)(2,1)S(1)}, bf16[192,1152]{1,0:T(8,128)(2,1)S(1)}, u32[]{:S(2)}, u32[]{:S(2)}) collective-permute-start(bf16[192,1152]{1,0:T(8,128)(2,1)S(1)} %collective-permute-done.refs_1_), channel_id=1, source_target_pairs={{0,8},{4,12},{8,16},{12,20},{16,24},{20,28},{24,0},{28,4},{1,9},{5... | collective-permute-start | bytes 1327112 | tf_op jit(solution)/shard_map/ppermute | solution.py:909
  23.5 26.5 %collective-permute-start.7 = (bf16[2,192,384]{2,1,0:T(8,128)(2,1)S(1)}, bf16[2,192,384]{2,1,0:T(8,128)(2,1)S(1)}, u32[]{:S(2)}, u32[]{:S(2)}) collective-permute-start(bf16[2,192,384]{2,1,0:T(8,128)(2,1)S(1)} %pad_maximum_fusion.8), channel_id=1, source_target_pairs={{0,2},{1,3},{2,0},{3,1},{4,6},{5,7},{6,4},{7,5},{8,10},{9,11},{10,... | collective-permute-start | bytes 884744 | tf_op jit(solution)/shard_map/ppermute | solution.py:915
  36.3 29.8 %collective-permute-start.9 = (bf16[2,192,384]{2,1,0:T(8,128)(2,1)S(1)}, bf16[2,192,384]{2,1,0:T(8,128)(2,1)S(1)}, u32[]{:S(2)}, u32[]{:S(2)}) collective-permute-start(bf16[2,192,384]{2,1,0:T(8,128)(2,1)S(1)} %pad_maximum_fusion.9), channel_id=1, source_target_pairs={{0,2},{1,3},{2,0},{3,1},{4,6},{5,7},{6,4},{7,5},{8,10},{9,11},{10,... | collective-permute-start | bytes 884744 | tf_op jit(solution)/shard_map/ppermute | solution.py:915
  48.5 17.7 %collective-permute-start.10 = (bf16[2,192,384]{2,1,0:T(8,128)(2,1)S(1)}, bf16[2,192,384]{2,1,0:T(8,128)(2,1)S(1)}, u32[]{:S(2)}, u32[]{:S(2)}) collective-permute-start(bf16[2,192,384]{2,1,0:T(8,128)(2,1)S(1)} %pad_maximum_fusion.10), channel_id=1, source_target_pairs={{0,2},{1,3},{2,0},{3,1},{4,6},{5,7},{6,4},{7,5},{8,10},{9,11},{10,... | collective-permute-start | bytes 884744 | tf_op jit(solution)/shard_map/ppermute | solution.py:915
  50.0 16.1 %collective-permute-start.8 = (bf16[576,384]{1,0:T(8,128)(2,1)}, bf16[576,384]{1,0:T(8,128)(2,1)}, u32[]{:S(2)}, u32[]{:S(2)}) collective-permute-start(bf16[576,384]{1,0:T(8,128)(2,1)} %fusion.13), channel_id=1, source_target_pairs={{0,8},{4,12},{8,16},{12,20},{16,24},{20,28},{24,0},{28,4},{1,9},{5... | collective-permute-start | bytes 1327112 | tf_op jit(solution)/shard_map/ppermute | solution.py:909
  69.7 15.0 %collective-permute-start.13 = (bf16[2,1536,384]{2,1,0:T(8,128)(2,1)S(1)}, bf16[2,1536,384]{2,1,0:T(8,128)(2,1)}, u32[]{:S(2)}, u32[]{:S(2)}) collective-permute-start(bf16[2,1536,384]{2,1,0:T(8,128)(2,1)S(1)} %place.1.w01.w_ref), channel_id=1, source_target_pairs={{0,1},{1,0},{2,3},{3,2},{4,5},{5,4},{6,7},{7,6},{8,9},{9,8},{10,11... | collective-permute-start | bytes 7077896 | tf_op jit(solution)/shard_map/ppermute | solution.py:918
  69.8 12.8 %collective-permute-start.15 = (bf16[576,384]{1,0:T(8,128)(2,1)}, bf16[576,384]{1,0:T(8,128)(2,1)S(1)}, u32[]{:S(2)}, u32[]{:S(2)}) collective-permute-start(bf16[576,384]{1,0:T(8,128)(2,1)} %fusion.13), channel_id=1, source_target_pairs={{0,4},{4,0},{8,12},{12,8},{16,20},{20,16},{24,28},{28,24},{1,5},{5... | collective-permute-start | bytes 1327112 | tf_op jit(solution)/shard_map/ppermute | solution.py:912
  70.4 14.4 %collective-permute-start.14 = (bf16[576,384]{1,0:T(8,128)(2,1)}, bf16[576,384]{1,0:T(8,128)(2,1)}, u32[]{:S(2)}, u32[]{:S(2)}) collective-permute-start(bf16[576,384]{1,0:T(8,128)(2,1)} %collective-permute-done.8), channel_id=1, source_target_pairs={{0,8},{4,12},{8,16},{12,20},{16,24},{20,28},{24,0},{28,4},{1,9},{5... | collective-permute-start | bytes 1327112 | tf_op jit(solution)/shard_map/ppermute | solution.py:909
  87.3 16.5 %collective-permute-start.20 = (bf16[2,576,384]{2,1,0:T(8,128)(2,1)S(1)}, bf16[2,576,384]{2,1,0:T(8,128)(2,1)S(1)}, u32[]{:S(2)}, u32[]{:S(2)}) collective-permute-start(bf16[2,576,384]{2,1,0:T(8,128)(2,1)S(1)} %pad_maximum_fusion.1.refs_4_), channel_id=1, source_target_pairs={{0,1},{1,0},{2,3},{3,2},{4,5},{5,4},{6,7},{7,6},{8,9},{9,8},{10,11... | collective-permute-start | bytes 2654216 | tf_op jit(solution)/shard_map/ppermute | solution.py:918
  87.9 21.6 %collective-permute-start.19 = (bf16[2,576,384]{2,1,0:T(8,128)(2,1)S(1)}, bf16[2,576,384]{2,1,0:T(8,128)(2,1)S(1)}, u32[]{:S(2)}, u32[]{:S(2)}) collective-permute-start(bf16[2,576,384]{2,1,0:T(8,128)(2,1)S(1)} %pad_maximum_fusion.1.refs_4_), channel_id=1, source_target_pairs={{0,2},{1,3},{2,0},{3,1},{4,6},{5,7},{6,4},{7,5},{8,10},{9,11},{10,... | collective-permute-start | bytes 2654216 | tf_op jit(solution)/shard_map/ppermute | solution.py:915
  89.9 13.8 %collective-permute-start.17 = (bf16[576,384]{1,0:T(8,128)(2,1)}, bf16[576,384]{1,0:T(8,128)(2,1)S(1)}, u32[]{:S(2)}, u32[]{:S(2)}) collective-permute-start(bf16[576,384]{1,0:T(8,128)(2,1)} %collective-permute-done.14), channel_id=1, source_target_pairs={{0,8},{4,12},{8,16},{12,20},{16,24},{20,28},{24,0},{28,4},{1,9},{5... | collective-permute-start | bytes 1327112 | tf_op jit(solution)/shard_map/ppermute | solution.py:909
  111.0 24.0 %collective-permute-start.25 = (bf16[2,576,384]{2,1,0:T(8,128)(2,1)S(1)}, bf16[2,576,384]{2,1,0:T(8,128)(2,1)S(1)}, u32[]{:S(2)}, u32[]{:S(2)}) collective-permute-start(bf16[2,576,384]{2,1,0:T(8,128)(2,1)S(1)} %pad_maximum_fusion.2.refs_4_), channel_id=1, source_target_pairs={{0,1},{1,0},{2,3},{3,2},{4,5},{5,4},{6,7},{7,6},{8,9},{9,8},{10,11... | collective-permute-start | bytes 2654216 | tf_op jit(solution)/shard_map/ppermute | solution.py:918
  111.2 23.7 %collective-permute-start.24 = (bf16[2,576,384]{2,1,0:T(8,128)(2,1)S(1)}, bf16[2,576,384]{2,1,0:T(8,128)(2,1)}, u32[]{:S(2)}, u32[]{:S(2)}) collective-permute-start(bf16[2,576,384]{2,1,0:T(8,128)(2,1)S(1)} %pad_maximum_fusion.2.refs_4_), channel_id=1, source_target_pairs={{0,2},{1,3},{2,0},{3,1},{4,6},{5,7},{6,4},{7,5},{8,10},{9,11},{10,... | collective-permute-start | bytes 2654216 | tf_op jit(solution)/shard_map/ppermute | solution.py:915
  111.8 23.2 %collective-permute-start.26 = (bf16[2,576,384]{2,1,0:T(8,128)(2,1)S(1)}, bf16[2,576,384]{2,1,0:T(8,128)(2,1)S(1)}, u32[]{:S(2)}, u32[]{:S(2)}) collective-permute-start(bf16[2,576,384]{2,1,0:T(8,128)(2,1)S(1)} %collective-permute-done.19.refs_5_), channel_id=1, source_target_pairs={{0,1},{1,0},{2,3},{3,2},{4,5},{5,4},{6,7},{7,6},{8,9},{9,8},{10,11... | collective-permute-start | bytes 2654216 | tf_op jit(solution)/shard_map/ppermute | solution.py:918
  111.8 19.9 %collective-permute-start.22 = (bf16[512,768]{1,0:T(8,128)(2,1)S(1)}, bf16[512,768]{1,0:T(8,128)(2,1)S(1)}, u32[]{:S(2)}, u32[]{:S(2)}) collective-permute-start(bf16[512,768]{1,0:T(8,128)(2,1)S(1)} %get-tuple-element.319.refs_0_), channel_id=1, source_target_pairs={{0,4},{4,0},{8,12},{12,8},{16,20},{20,16},{24,28},{28,24},{1,5},{5... | collective-permute-start | bytes 2359304 | tf_op jit(solution)/shard_map/ppermute | solution.py:912
  113.3 21.6 %collective-permute-start.21 = (bf16[512,768]{1,0:T(8,128)(2,1)S(1)}, bf16[512,768]{1,0:T(8,128)(2,1)}, u32[]{:S(2)}, u32[]{:S(2)}) collective-permute-start(bf16[512,768]{1,0:T(8,128)(2,1)S(1)} %get-tuple-element.319.refs_0_), channel_id=1, source_target_pairs={{0,8},{4,12},{8,16},{12,20},{16,24},{20,28},{24,0},{28,4},{1,9},{5... | collective-permute-start | bytes 2359304 | tf_op jit(solution)/shard_map/ppermute | solution.py:909
  136.8 35.8 %collective-permute-start.31 = (bf16[576,384]{1,0:T(8,128)(2,1)}, bf16[576,384]{1,0:T(8,128)(2,1)}, u32[]{:S(2)}, u32[]{:S(2)}) collective-permute-start(bf16[576,384]{1,0:T(8,128)(2,1)} %collective-permute-done.14), channel_id=1, source_target_pairs={{0,4},{4,0},{8,12},{12,8},{16,20},{20,16},{24,28},{28,24},{1,5},{5... | collective-permute-start | bytes 1327112 | tf_op jit(solution)/shard_map/ppermute | solution.py:912
  138.1 34.4 %collective-permute-start.29 = (bf16[512,768]{1,0:T(8,128)(2,1)}, bf16[512,768]{1,0:T(8,128)(2,1)}, u32[]{:S(2)}, u32[]{:S(2)}) collective-permute-start(bf16[512,768]{1,0:T(8,128)(2,1)} %collective-permute-done.21.refs_0_), channel_id=1, source_target_pairs={{0,1},{1,0},{2,3},{3,2},{4,5},{5,4},{6,7},{7,6},{8,9},{9,8},{10,11... | collective-permute-start | bytes 2359304 | tf_op jit(solution)/shard_map/ppermute | solution.py:918
  138.1 34.5 %collective-permute-start.28 = (bf16[512,768]{1,0:T(8,128)(2,1)}, bf16[512,768]{1,0:T(8,128)(2,1)}, u32[]{:S(2)}, u32[]{:S(2)}) collective-permute-start(bf16[512,768]{1,0:T(8,128)(2,1)} %collective-permute-done.21.refs_0_), channel_id=1, source_target_pairs={{0,4},{4,0},{8,12},{12,8},{16,20},{20,16},{24,28},{28,24},{1,5},{5... | collective-permute-start | bytes 2359304 | tf_op jit(solution)/shard_map/ppermute | solution.py:912
  139.6 32.9 %collective-permute-start.27 = (bf16[512,768]{1,0:T(8,128)(2,1)}, bf16[512,768]{1,0:T(8,128)(2,1)}, u32[]{:S(2)}, u32[]{:S(2)}) collective-permute-start(bf16[512,768]{1,0:T(8,128)(2,1)} %collective-permute-done.21.refs_0_), channel_id=1, source_target_pairs={{0,8},{4,12},{8,16},{12,20},{16,24},{20,28},{24,0},{28,4},{1,9},{5... | collective-permute-start | bytes 2359304 | tf_op jit(solution)/shard_map/ppermute | solution.py:909
  139.7 33.0 %collective-permute-start.32 = (bf16[2,576,384]{2,1,0:T(8,128)(2,1)}, bf16[2,576,384]{2,1,0:T(8,128)(2,1)}, u32[]{:S(2)}, u32[]{:S(2)}) collective-permute-start(bf16[2,576,384]{2,1,0:T(8,128)(2,1)} %collective-permute-done.24.refs_5_), channel_id=1, source_target_pairs={{0,1},{1,0},{2,3},{3,2},{4,5},{5,4},{6,7},{7,6},{8,9},{9,8},{10,11... | collective-permute-start | bytes 2654216 | tf_op jit(solution)/shard_map/ppermute | solution.py:918
  172.6 14.3 %collective-permute-start.36 = (bf16[512,768]{1,0:T(8,128)(2,1)}, bf16[512,768]{1,0:T(8,128)(2,1)S(1)}, u32[]{:S(2)}, u32[]{:S(2)}) collective-permute-start(bf16[512,768]{1,0:T(8,128)(2,1)} %collective-permute-done.28.refs_1_), channel_id=1, source_target_pairs={{0,1},{1,0},{2,3},{3,2},{4,5},{5,4},{6,7},{7,6},{8,9},{9,8},{10,11... | collective-permute-start | bytes 2359304 | tf_op jit(solution)/shard_map/ppermute | solution.py:918
  172.9 13.2 %collective-permute-start.37 = (bf16[576,384]{1,0:T(8,128)(2,1)}, bf16[576,384]{1,0:T(8,128)(2,1)S(1)}, u32[]{:S(2)}, u32[]{:S(2)}) collective-permute-start(bf16[576,384]{1,0:T(8,128)(2,1)} %copy-done.71), channel_id=1, source_target_pairs={{0,4},{4,0},{8,12},{12,8},{16,20},{20,16},{24,28},{28,24},{1,5},{5... | collective-permute-start | bytes 1327112 | tf_op jit(solution)/shard_map/ppermute | solution.py:912
  173.4 39.0 %collective-permute-start.35 = (bf16[512,768]{1,0:T(8,128)(2,1)}, bf16[512,768]{1,0:T(8,128)(2,1)}, u32[]{:S(2)}, u32[]{:S(2)}) collective-permute-start(bf16[512,768]{1,0:T(8,128)(2,1)} %collective-permute-done.27.refs_0_), channel_id=1, source_target_pairs={{0,1},{1,0},{2,3},{3,2},{4,5},{5,4},{6,7},{7,6},{8,9},{9,8},{10,11... | collective-permute-start | bytes 2359304 | tf_op jit(solution)/shard_map/ppermute | solution.py:918
  173.4 39.0 %collective-permute-start.34 = (bf16[512,768]{1,0:T(8,128)(2,1)}, bf16[512,768]{1,0:T(8,128)(2,1)}, u32[]{:S(2)}, u32[]{:S(2)}) collective-permute-start(bf16[512,768]{1,0:T(8,128)(2,1)} %collective-permute-done.27.refs_0_), channel_id=1, source_target_pairs={{0,4},{4,0},{8,12},{12,8},{16,20},{20,16},{24,28},{28,24},{1,5},{5... | collective-permute-start | bytes 2359304 | tf_op jit(solution)/shard_map/ppermute | solution.py:912
  175.0 37.5 %collective-permute-start.33 = (bf16[512,768]{1,0:T(8,128)(2,1)}, bf16[512,768]{1,0:T(8,128)(2,1)}, u32[]{:S(2)}, u32[]{:S(2)}) collective-permute-start(bf16[512,768]{1,0:T(8,128)(2,1)} %collective-permute-done.27.refs_0_), channel_id=1, source_target_pairs={{0,8},{4,12},{8,16},{12,20},{16,24},{20,28},{24,0},{28,4},{1,9},{5... | collective-permute-start | bytes 2359304 | tf_op jit(solution)/shard_map/ppermute | solution.py:909
  186.1 26.3 %collective-permute-start.39 = (bf16[2,576,384]{2,1,0:T(8,128)(2,1)S(1)}, bf16[2,576,384]{2,1,0:T(8,128)(2,1)}, u32[]{:S(2)}, u32[]{:S(2)}) collective-permute-start(bf16[2,576,384]{2,1,0:T(8,128)(2,1)S(1)} %pad_maximum_fusion.3.refs_4_), channel_id=1, source_target_pairs={{0,1},{1,0},{2,3},{3,2},{4,5},{5,4},{6,7},{7,6},{8,9},{9,8},{10,11... | collective-permute-start | bytes 2654216 | tf_op jit(solution)/shard_map/ppermute | solution.py:918
  187.8 24.7 %collective-permute-start.38 = (bf16[2,576,384]{2,1,0:T(8,128)(2,1)S(1)}, bf16[2,576,384]{2,1,0:T(8,128)(2,1)}, u32[]{:S(2)}, u32[]{:S(2)}) collective-permute-start(bf16[2,576,384]{2,1,0:T(8,128)(2,1)S(1)} %pad_maximum_fusion.3.refs_4_), channel_id=1, source_target_pairs={{0,2},{1,3},{2,0},{3,1},{4,6},{5,7},{6,4},{7,5},{8,10},{9,11},{10,... | collective-permute-start | bytes 2654216 | tf_op jit(solution)/shard_map/ppermute | solution.py:915
  213.5 35.1 %collective-permute-start.40 = (bf16[512,768]{1,0:T(8,128)(2,1)}, bf16[512,768]{1,0:T(8,128)(2,1)}, u32[]{:S(2)}, u32[]{:S(2)}) collective-permute-start(bf16[512,768]{1,0:T(8,128)(2,1)} %collective-permute-done.33.refs_0_), channel_id=1, source_target_pairs={{0,4},{4,0},{8,12},{12,8},{16,20},{20,16},{24,28},{28,24},{1,5},{5... | collective-permute-start | bytes 2359304 | tf_op jit(solution)/shard_map/ppermute | solution.py:912
  220.7 30.6 %collective-permute-start.46 = (bf16[2,512,768]{2,1,0:T(8,128)(2,1)}, bf16[2,512,768]{2,1,0:T(8,128)(2,1)}, u32[]{:S(2)}, u32[]{:S(2)}) collective-permute-start(bf16[2,512,768]{2,1,0:T(8,128)(2,1)} %get-tuple-element.367), channel_id=1, source_target_pairs={{0,1},{1,0},{2,3},{3,2},{4,5},{5,4},{6,7},{7,6},{8,9},{9,8},{10,11... | collective-permute-start | bytes 4718600 | tf_op jit(solution)/shard_map/ppermute | solution.py:918
  223.1 25.5 %collective-permute-start.48 = (bf16[2,576,384]{2,1,0:T(8,128)(2,1)}, bf16[2,576,384]{2,1,0:T(8,128)(2,1)}, u32[]{:S(2)}, u32[]{:S(2)}) collective-permute-start(bf16[2,576,384]{2,1,0:T(8,128)(2,1)} %pad_maximum_fusion.4.refs_4_), channel_id=1, source_target_pairs={{0,1},{1,0},{2,3},{3,2},{4,5},{5,4},{6,7},{7,6},{8,9},{9,8},{10,11... | collective-permute-start | bytes 2654216 | tf_op jit(solution)/shard_map/ppermute | solution.py:918
  223.4 25.2 %collective-permute-start.47 = (bf16[2,576,384]{2,1,0:T(8,128)(2,1)}, bf16[2,576,384]{2,1,0:T(8,128)(2,1)}, u32[]{:S(2)}, u32[]{:S(2)}) collective-permute-start(bf16[2,576,384]{2,1,0:T(8,128)(2,1)} %pad_maximum_fusion.4.refs_4_), channel_id=1, source_target_pairs={{0,2},{1,3},{2,0},{3,1},{4,6},{5,7},{6,4},{7,5},{8,10},{9,11},{10,... | collective-permute-start | bytes 2654216 | tf_op jit(solution)/shard_map/ppermute | solution.py:915
  225.3 26.0 %collective-permute-start.45 = (bf16[544,768]{1,0:T(8,128)(2,1)}, bf16[544,768]{1,0:T(8,128)(2,1)}, u32[]{:S(2)}, u32[]{:S(2)}) collective-permute-start(bf16[544,768]{1,0:T(8,128)(2,1)} %get-tuple-element.632), channel_id=1, source_target_pairs={{0,4},{4,0},{8,12},{12,8},{16,20},{20,16},{24,28},{28,24},{1,5},{5... | collective-permute-start | bytes 2506760 | tf_op jit(solution)/shard_map/ppermute | solution.py:912
  254.0 32.1 %collective-permute-start.53 = (bf16[544,768]{1,0:T(8,128)(2,1)}, bf16[544,768]{1,0:T(8,128)(2,1)}, u32[]{:S(2)}, u32[]{:S(2)}) collective-permute-start(bf16[544,768]{1,0:T(8,128)(2,1)} %add_convert_fusion.7), channel_id=1, source_target_pairs={{0,8},{4,12},{8,16},{12,20},{16,24},{20,28},{24,0},{28,4},{1,9},{5... | collective-permute-start | bytes 2506760 | tf_op jit(solution)/shard_map/ppermute | solution.py:909
  257.5 28.7 %collective-permute-start.55 = (bf16[2,512,768]{2,1,0:T(8,128)(2,1)}, bf16[2,512,768]{2,1,0:T(8,128)(2,1)}, u32[]{:S(2)}, u32[]{:S(2)}) collective-permute-start(bf16[2,512,768]{2,1,0:T(8,128)(2,1)} %get-tuple-element.403), channel_id=1, source_target_pairs={{0,1},{1,0},{2,3},{3,2},{4,5},{5,4},{6,7},{7,6},{8,9},{9,8},{10,11... | collective-permute-start | bytes 4718600 | tf_op jit(solution)/shard_map/ppermute | solution.py:918
  260.3 25.9 %collective-permute-start.54 = (bf16[2,512,384]{2,1,0:T(8,128)(2,1)}, bf16[2,512,384]{2,1,0:T(8,128)(2,1)}, u32[]{:S(2)}, u32[]{:S(2)}) collective-permute-start(bf16[2,512,384]{2,1,0:T(8,128)(2,1)} %add_convert_fusion.16), channel_id=1, source_target_pairs={{0,2},{1,3},{2,0},{3,1},{4,6},{5,7},{6,4},{7,5},{8,10},{9,11},{10,... | collective-permute-start | bytes 2359304 | tf_op jit(solution)/shard_map/ppermute | solution.py:915
  262.5 23.7 %collective-permute-start.52 = (bf16[544,768]{1,0:T(8,128)(2,1)}, bf16[544,768]{1,0:T(8,128)(2,1)}, u32[]{:S(2)}, u32[]{:S(2)}) collective-permute-start(bf16[544,768]{1,0:T(8,128)(2,1)} %get-tuple-element.630), channel_id=1, source_target_pairs={{0,4},{4,0},{8,12},{12,8},{16,20},{20,16},{24,28},{28,24},{1,5},{5... | collective-permute-start | bytes 2506760 | tf_op jit(solution)/shard_map/ppermute | solution.py:912
  286.3 28.5 %collective-permute-start.59 = (bf16[2,544,768]{2,1,0:T(8,128)(2,1)}, bf16[2,544,768]{2,1,0:T(8,128)(2,1)S(1)}, u32[]{:S(2)}, u32[]{:S(2)}) collective-permute-start(bf16[2,544,768]{2,1,0:T(8,128)(2,1)} %get-tuple-element.430), channel_id=1, source_target_pairs={{0,1},{1,0},{2,3},{3,2},{4,5},{5,4},{6,7},{7,6},{8,9},{9,8},{10,11... | collective-permute-start | bytes 5013512 | tf_op jit(solution)/shard_map/ppermute | solution.py:918
  290.0 27.1 %collective-permute-start.61 = (bf16[2,512,768]{2,1,0:T(8,128)(2,1)}, bf16[2,512,768]{2,1,0:T(8,128)(2,1)S(1)}, u32[]{:S(2)}, u32[]{:S(2)}) collective-permute-start(bf16[2,512,768]{2,1,0:T(8,128)(2,1)} %get-tuple-element.433), channel_id=1, source_target_pairs={{0,1},{1,0},{2,3},{3,2},{4,5},{5,4},{6,7},{7,6},{8,9},{9,8},{10,11... | collective-permute-start | bytes 4718600 | tf_op jit(solution)/shard_map/ppermute | solution.py:918
  292.3 23.0 %collective-permute-start.58 = (bf16[544,768]{1,0:T(8,128)(2,1)S(1)}, bf16[544,768]{1,0:T(8,128)(2,1)S(1)}, u32[]{:S(2)}, u32[]{:S(2)}) collective-permute-start(bf16[544,768]{1,0:T(8,128)(2,1)S(1)} %add_convert_fusion.4), channel_id=1, source_target_pairs={{0,8},{4,12},{8,16},{12,20},{16,24},{20,28},{24,0},{28,4},{1,9},{5... | collective-permute-start | bytes 2506760 | tf_op jit(solution)/shard_map/ppermute | solution.py:909
  294.4 22.8 %collective-permute-start.57 = (bf16[544,768]{1,0:T(8,128)(2,1)S(1)}, bf16[544,768]{1,0:T(8,128)(2,1)S(1)}, u32[]{:S(2)}, u32[]{:S(2)}) collective-permute-start(bf16[544,768]{1,0:T(8,128)(2,1)S(1)} %get-tuple-element.628), channel_id=1, source_target_pairs={{0,4},{4,0},{8,12},{12,8},{16,20},{20,16},{24,28},{28,24},{1,5},{5... | collective-permute-start | bytes 2506760 | tf_op jit(solution)/shard_map/ppermute | solution.py:912
  297.5 19.6 %collective-permute-start.60 = (bf16[2,512,384]{2,1,0:T(8,128)(2,1)S(1)}, bf16[2,512,384]{2,1,0:T(8,128)(2,1)S(1)}, u32[]{:S(2)}, u32[]{:S(2)}) collective-permute-start(bf16[2,512,384]{2,1,0:T(8,128)(2,1)S(1)} %add_convert_fusion.15), channel_id=1, source_target_pairs={{0,2},{1,3},{2,0},{3,1},{4,6},{5,7},{6,4},{7,5},{8,10},{9,11},{10,... | collective-permute-start | bytes 2359304 | tf_op jit(solution)/shard_map/ppermute | solution.py:915
  314.7 13.8 %collective-permute-start.65 = (bf16[2,512,768]{2,1,0:T(8,128)(2,1)}, bf16[2,512,768]{2,1,0:T(8,128)(2,1)S(1)}, u32[]{:S(2)}, u32[]{:S(2)}) collective-permute-start(bf16[2,512,768]{2,1,0:T(8,128)(2,1)} %get-tuple-element.458), channel_id=1, source_target_pairs={{0,1},{1,0},{2,3},{3,2},{4,5},{5,4},{6,7},{7,6},{8,9},{9,8},{10,11... | collective-permute-start | bytes 4718600 | tf_op jit(solution)/shard_map/ppermute | solution.py:918
  319.2 22.0 %collective-permute-start.63 = (bf16[544,768]{1,0:T(8,128)(2,1)}, bf16[544,768]{1,0:T(8,128)(2,1)S(1)}, u32[]{:S(2)}, u32[]{:S(2)}) collective-permute-start(bf16[544,768]{1,0:T(8,128)(2,1)} %add_convert_fusion.1), channel_id=1, source_target_pairs={{0,8},{4,12},{8,16},{12,20},{16,24},{20,28},{24,0},{28,4},{1,9},{5... | collective-permute-start | bytes 2506760 | tf_op jit(solution)/shard_map/ppermute | solution.py:909
  320.8 20.4 %collective-permute-start.62 = (bf16[544,768]{1,0:T(8,128)(2,1)S(1)}, bf16[544,768]{1,0:T(8,128)(2,1)S(1)}, u32[]{:S(2)}, u32[]{:S(2)}) collective-permute-start(bf16[544,768]{1,0:T(8,128)(2,1)S(1)} %get-tuple-element.626), channel_id=1, source_target_pairs={{0,4},{4,0},{8,12},{12,8},{16,20},{20,16},{24,28},{28,24},{1,5},{5... | collective-permute-start | bytes 2506760 | tf_op jit(solution)/shard_map/ppermute | solution.py:912
  321.8 18.0 %collective-permute-start.64 = (bf16[2,512,384]{2,1,0:T(8,128)(2,1)S(1)}, bf16[2,512,384]{2,1,0:T(8,128)(2,1)S(1)}, u32[]{:S(2)}, u32[]{:S(2)}) collective-permute-start(bf16[2,512,384]{2,1,0:T(8,128)(2,1)S(1)} %add_convert_fusion.14), channel_id=1, source_target_pairs={{0,2},{1,3},{2,0},{3,1},{4,6},{5,7},{6,4},{7,5},{8,10},{9,11},{10,... | collective-permute-start | bytes 2359304 | tf_op jit(solution)/shard_map/ppermute | solution.py:915
  341.6 21.1 %collective-permute-start.66 = (bf16[544,768]{1,0:T(8,128)(2,1)S(1)}, bf16[544,768]{1,0:T(8,128)(2,1)S(1)}, u32[]{:S(2)}, u32[]{:S(2)}) collective-permute-start(bf16[544,768]{1,0:T(8,128)(2,1)S(1)} %add_convert_fusion), channel_id=1, source_target_pairs={{0,2},{1,3},{2,0},{3,1},{4,6},{5,7},{6,4},{7,5},{8,10},{9,11},{10,... | collective-permute-start | bytes 2506760 | tf_op jit(solution)/shard_map/ppermute | solution.py:915
  347.1 15.5 %collective-permute-start.68 = (bf16[512,384]{1,0:T(8,128)(2,1)S(1)}, bf16[512,384]{1,0:T(8,128)(2,1)S(1)}, u32[]{:S(2)}, u32[]{:S(2)}) collective-permute-start(bf16[512,384]{1,0:T(8,128)(2,1)S(1)} %get-tuple-element.622), channel_id=1, source_target_pairs={{0,4},{4,0},{8,12},{12,8},{16,20},{20,16},{24,28},{28,24},{1,5},{5... | collective-permute-start | bytes 1179656 | tf_op jit(solution)/shard_map/ppermute | solution.py:912
  365.7 19.6 %collective-permute-start.72 = (bf16[2,512,384]{2,1,0:T(8,128)(2,1)S(1)}, bf16[2,512,384]{2,1,0:T(8,128)(2,1)S(1)}, u32[]{:S(2)}, u32[]{:S(2)}) collective-permute-start(bf16[2,512,384]{2,1,0:T(8,128)(2,1)S(1)} %add_convert_fusion.12), channel_id=1, source_target_pairs={{0,2},{1,3},{2,0},{3,1},{4,6},{5,7},{6,4},{7,5},{8,10},{9,11},{10,... | collective-permute-start | bytes 2359304 | tf_op jit(solution)/shard_map/ppermute | solution.py:915
  367.2 12.7 %collective-permute-start.70 = (bf16[512,384]{1,0:T(8,128)(2,1)S(1)}, bf16[512,384]{1,0:T(8,128)(2,1)S(1)}, u32[]{:S(2)}, u32[]{:S(2)}) collective-permute-start(bf16[512,384]{1,0:T(8,128)(2,1)S(1)} %add_convert_fusion.24), channel_id=1, source_target_pairs={{0,8},{4,12},{8,16},{12,20},{16,24},{20,28},{24,0},{28,4},{1,9},{5... | collective-permute-start | bytes 1179656 | tf_op jit(solution)/shard_map/ppermute | solution.py:909
  385.7 13.3 %collective-permute-start.73 = (bf16[192,512]{1,0:T(8,128)(2,1)S(1)}, bf16[192,512]{1,0:T(8,128)(2,1)S(1)}, u32[]{:S(2)}, u32[]{:S(2)}) collective-permute-start(bf16[192,512]{1,0:T(8,128)(2,1)S(1)} %get-tuple-element.522), channel_id=1, source_target_pairs={{0,4},{4,0},{8,12},{12,8},{16,20},{20,16},{24,28},{28,24},{1,5},{5... | collective-permute-start | bytes 589832 | tf_op jit(solution)/shard_map/ppermute | solution.py:912
  386.8 13.5 %collective-permute-start.74 = (bf16[512,384]{1,0:T(8,128)(2,1)S(1)}, bf16[512,384]{1,0:T(8,128)(2,1)S(1)}, u32[]{:S(2)}, u32[]{:S(2)}) collective-permute-start(bf16[512,384]{1,0:T(8,128)(2,1)S(1)} %get-tuple-element.619), channel_id=1, source_target_pairs={{0,4},{4,0},{8,12},{12,8},{16,20},{20,16},{24,28},{28,24},{1,5},{5... | collective-permute-start | bytes 1179656 | tf_op jit(solution)/shard_map/ppermute | solution.py:912
  400.3 20.7 %collective-permute-start.81 = (bf16[512,896]{1,0:T(8,128)(2,1)S(1)}, bf16[512,896]{1,0:T(8,128)(2,1)S(1)}, u32[]{:S(2)}, u32[]{:S(2)}) collective-permute-start(bf16[512,896]{1,0:T(8,128)(2,1)S(1)} %get-tuple-element.536), channel_id=1, source_target_pairs={{0,1},{1,0},{2,3},{3,2},{4,5},{5,4},{6,7},{7,6},{8,9},{9,8},{10,11... | collective-permute-start | bytes 2752520 | tf_op jit(solution)/shard_map/ppermute | solution.py:918
  401.8 19.2 %collective-permute-start.77 = (bf16[208,640]{1,0:T(8,128)(2,1)S(1)}, bf16[208,640]{1,0:T(8,128)(2,1)S(1)}, u32[]{:S(2)}, u32[]{:S(2)}) collective-permute-start(bf16[208,640]{1,0:T(8,128)(2,1)S(1)} %get-tuple-element.529), channel_id=1, source_target_pairs={{0,4},{4,0},{8,12},{12,8},{16,20},{20,16},{24,28},{28,24},{1,5},{5... | collective-permute-start | bytes 798728 | tf_op jit(solution)/shard_map/ppermute | solution.py:912
  402.9 18.0 %collective-permute-start.80 = (bf16[512,384]{1,0:T(8,128)(2,1)S(1)}, bf16[512,384]{1,0:T(8,128)(2,1)S(1)}, u32[]{:S(2)}, u32[]{:S(2)}) collective-permute-start(bf16[512,384]{1,0:T(8,128)(2,1)S(1)} %add_convert_fusion.18), channel_id=1, source_target_pairs={{0,8},{4,12},{8,16},{12,20},{16,24},{20,28},{24,0},{28,4},{1,9},{5... | collective-permute-start | bytes 1179656 | tf_op jit(solution)/shard_map/ppermute | solution.py:909
  404.4 15.6 %collective-permute-start.79 = (bf16[192,512]{1,0:T(8,128)(2,1)S(1)}, bf16[192,512]{1,0:T(8,128)(2,1)S(1)}, u32[]{:S(2)}, u32[]{:S(2)}) collective-permute-start(bf16[192,512]{1,0:T(8,128)(2,1)S(1)} %add_convert_fusion.34), channel_id=1, source_target_pairs={{0,8},{4,12},{8,16},{12,20},{16,24},{20,28},{24,0},{28,4},{1,9},{5... | collective-permute-start | bytes 589832 | tf_op jit(solution)/shard_map/ppermute | solution.py:909
  408.4 16.3 %collective-permute-start.83 = (bf16[192,512]{1,0:T(8,128)(2,1)S(1)}, bf16[192,512]{1,0:T(8,128)(2,1)S(1)}, u32[]{:S(2)}, u32[]{:S(2)}) collective-permute-start(bf16[192,512]{1,0:T(8,128)(2,1)S(1)} %get-tuple-element.538), channel_id=1, source_target_pairs={{0,4},{4,0},{8,12},{12,8},{16,20},{20,16},{24,28},{28,24},{1,5},{5... | collective-permute-start | bytes 589832 | tf_op jit(solution)/shard_map/ppermute | solution.py:912
  421.6 15.4 %collective-permute-start.85 = (bf16[512,512]{1,0:T(8,128)(2,1)S(1)}, bf16[512,512]{1,0:T(8,128)(2,1)S(1)}, u32[]{:S(2)}, u32[]{:S(2)}) collective-permute-start(bf16[512,512]{1,0:T(8,128)(2,1)S(1)} %maximum_maximum_fusion), channel_id=1, source_target_pairs={{0,2},{1,3},{2,0},{3,1},{4,6},{5,7},{6,4},{7,5},{8,10},{9,11},{10,... | collective-permute-start | bytes 1572872 | tf_op jit(solution)/shard_map/ppermute | solution.py:915
  423.0 13.9 %collective-permute-start.82 = (bf16[208,640]{1,0:T(8,128)(2,1)S(1)}, bf16[208,640]{1,0:T(8,128)(2,1)S(1)}, u32[]{:S(2)}, u32[]{:S(2)}) collective-permute-start(bf16[208,640]{1,0:T(8,128)(2,1)S(1)} %add_convert_fusion.31), channel_id=1, source_target_pairs={{0,8},{4,12},{8,16},{12,20},{16,24},{20,28},{24,0},{28,4},{1,9},{5... | collective-permute-start | bytes 798728 | tf_op jit(solution)/shard_map/ppermute | solution.py:909
  423.2 12.7 %collective-permute-start.84 = (bf16[192,512]{1,0:T(8,128)(2,1)S(1)}, bf16[192,512]{1,0:T(8,128)(2,1)S(1)}, u32[]{:S(2)}, u32[]{:S(2)}) collective-permute-start(bf16[192,512]{1,0:T(8,128)(2,1)S(1)} %add_convert_fusion.33), channel_id=1, source_target_pairs={{0,8},{4,12},{8,16},{12,20},{16,24},{20,28},{24,0},{28,4},{1,9},{5... | collective-permute-start | bytes 589832 | tf_op jit(solution)/shard_map/ppermute | solution.py:909
  424.8 14.0 %collective-permute-start.88 = (bf16[192,512]{1,0:T(8,128)(2,1)S(1)}, bf16[192,512]{1,0:T(8,128)(2,1)S(1)}, u32[]{:S(2)}, u32[]{:S(2)}) collective-permute-start(bf16[192,512]{1,0:T(8,128)(2,1)S(1)} %get-tuple-element.552), channel_id=1, source_target_pairs={{0,4},{4,0},{8,12},{12,8},{16,20},{20,16},{24,28},{28,24},{1,5},{5... | collective-permute-start | bytes 589832 | tf_op jit(solution)/shard_map/ppermute | solution.py:912
  435.9 14.0 %collective-permute-start.90 = (bf16[208,640]{1,0:T(8,128)(2,1)S(1)}, bf16[208,640]{1,0:T(8,128)(2,1)S(1)}, u32[]{:S(2)}, u32[]{:S(2)}) collective-permute-start(bf16[208,640]{1,0:T(8,128)(2,1)S(1)} %get-tuple-element.560), channel_id=1, source_target_pairs={{0,4},{4,0},{8,12},{12,8},{16,20},{20,16},{24,28},{28,24},{1,5},{5... | collective-permute-start | bytes 798728 | tf_op jit(solution)/shard_map/ppermute | solution.py:912
  (117 other events, 1288.2 us)

commit v3 on v2

--- a/solution.py
+++ b/solution.py
@@ -521,10 +521,10 @@
     return [at(2 * x + c), at(2 * (1 - x) + c)], [at(2 * x + 1 - c), at(2 * (1 - x) + 1 - c)]
 
 
-def out_body(idx, x_ref, o0, o1, o23, w01, w23, aux_ref, h_ref, low_ref, ring_ref):
+def out_body(idx, x_ref, o0, o1, o2, o3, w01, w23, aux_ref, h_ref, low_ref, ring_ref):
     tok, width = x_ref.shape
     attn = mm_nt(o0[...], w01[0]) + mm_nt(o1[...], w01[1])
-    attn = attn + (mm_nt(o23[0], w23[0]) + mm_nt(o23[1], w23[1]))
+    attn = attn + (mm_nt(o2[...], w23[0]) + mm_nt(o3[...], w23[1]))
     h = x_ref[...].astype(F32) + attn
     h_ref[...] = h
     r2 = lax.rsqrt(jnp.mean(h * h, axis=1, keepdims=True) + epsilon)
@@ -694,11 +694,19 @@
     )(*kept, *moved)
 
 
-def in_ring_order(nz, idx, blocks_s, outs):
+def in_ring_order(nz, idx, blocks_s, groups, outs):
+    bases = [lax.rem(idx[1] - k + nz, nz) * 2 for k in range(nz)]
     for k in range(nz):
-        base = lax.rem(idx[1] - k + nz, nz) * 2
-        outs[k][...] = blocks_s[base + idx[2]]
-        outs[nz + k][...] = blocks_s[base + 1 - idx[2]]
+        outs[k][...] = blocks_s[bases[k] + idx[2]]
+    for out, group in zip(outs[nz:], groups):
+        for i, k in enumerate(group):
+            out[i] = blocks_s[bases[k] + 1 - idx[2]]
+
+
+def sent_groups(nz):
+    early = [list(range(1, nz)), [0]]
+    late = [[1], list(range(2, nz)), [0]]
+    return [g for g in early if g], [g for g in late if g]
 
 
 def hidden_back_body(nz, idx, fm_ref, fn_ref, h_ref, low_ref, aux_ref, pos_ref, dout_ref, o_ref, w_ref,
@@ -738,7 +746,7 @@
     for i in range(2 * nz):
         rs_s[i, :, :cols] = turned[i * rows : i * rows + rows]
         rs_s[i, :, cols:] = side[i * rows : i * rows + rows]
-    in_ring_order(nz, idx, rs_s, outs)
+    in_ring_order(nz, idx, rs_s, sent_groups(nz)[0], outs)
 
 
 def attend_back_body(nz, idx, do_ref, v_ref, k_ref, q_ref, cos_ref, sin_ref, x_ref, aux_ref, w_ref, *refs):
@@ -788,7 +796,7 @@
         tail = jnp.concatenate([gain_high[:, at].astype(F32), gain_low[:, at].astype(F32), pads.astype(F32)], axis=0)
         rs_ref[i, rows:, :] = jnp.zeros((16, used), BF16)
         rs_ref[i, rows:, :rows] = tail.astype(BF16)
-    in_ring_order(nz, idx, rs_ref, outs)
+    in_ring_order(nz, idx, rs_ref, sent_groups(nz)[1], outs)
     total = jnp.sum(dxn * xh * gain, axis=1, keepdims=True)
     high, low = split16(total)
     lane = lax.broadcasted_iota(jnp.int32, (tok, 128), 1)
@@ -942,14 +950,11 @@
         name="slots",
     )[0]
     part = tok // 4
-    pos_own = lax.dynamic_slice_in_dim(pos, t * part, part, 1)
-    d_own = jnp.concatenate(
-        [
-            lax.dynamic_slice_in_dim(cotangent, t * cols, cols, 1),
-            jnp.concatenate([pos_own, jnp.zeros((experts, cols - part), BF16)], axis=1),
-        ],
-        axis=0,
-    )
+    def quarter(t):
+        slots = jnp.pad(lax.dynamic_slice_in_dim(pos, t * part, part, 1), ((0, 0), (0, cols - part)))
+        return jnp.concatenate([lax.dynamic_slice_in_dim(cotangent, t * cols, cols, 1), slots], axis=0)
+
+    d_own, d_far = quarter(t), quarter(2 * (1 - x) + c)
 
     class Rows:
         def __init__(self, own):
@@ -971,18 +976,20 @@
             return [v[k] for v in (self.z, self.y, self.cz, self.cy)]
 
     class Split(Rows):
-        def __init__(self, own):
+        def __init__(self, own, far):
             super().__init__(own)
-            self.s, self.x, self.cs, self.cx = {}, {}, {}, {}
+            self.far, self.s, self.x, self.cs, self.cx = far, {}, {}, {}, {}
 
         def chip(self, k):
             self.s[k] = jnp.stack([self.z[k], self.y[k]])
-            self.x[k] = swap_x(self.s[k])
+            self.x[k] = swap_x(self.s[k] if k else self.y[0])
 
         def core_own(self, k):
             self.cs[k] = swap_c(self.s[k])
 
         def core(self, k):
+            if k == 0:
+                self.x[0] = jnp.stack([self.far, self.x[0]])
             self.cx[k] = swap_c(self.x[k])
 
         def all(self, k):
@@ -1001,14 +1008,14 @@
         if k:
             wx.append(out_pair(k - 1))
         if k == 0:
-            wz[1], wy[0], d_own = sync(wz[1], wy[0], d_own)
+            wz[1], wy[0], d_own, d_far = sync(wz[1], wy[0], d_own, d_far)
         else:
             wz[k + 1], wy[k] = sync(wz[k + 1], wy[k])
     wx.append(out_pair(last - 1))
     wy.append(swap_y(wz[last]))
-    d = Split(after(d_own, wz[last]))
+    d = Split(after(d_own, wz[last]), d_far)
     d.ring(1)
-    gu = jnp.concatenate([expert_gate, expert_up], axis=2)
+    gu = jnp.concatenate(sync(expert_gate, expert_up, wz[last])[:2], axis=2)
     wy[last], wx[0], gu = sync(wy[last], wx[0], gu)
     wx.append(out_pair(last))
 
@@ -1030,7 +1037,7 @@
         name="attend",
     )
     o, d.z[1], d.z[0], *wx[1:] = sync(o, d.z[1], d.z[0], *wx[1:])
-    o_x = swap_x(o)
+    o_x, o_c0 = swap_x(o), swap_c(o)
     d.ring(2)
     d.side(0)
     wo = kernel_call(
@@ -1041,20 +1048,21 @@
     sel = (r * local + slot_ids[:, None] // PAD == jnp.arange(experts)[None, :]).astype(BF16)
     slot_col = jnp.asarray((slot_ids % PAD).astype(np.float32)[:, None])
     slot_row = jnp.asarray((slot_ids % PAD).astype(np.float32)[None, :])
-    o_x, wo_c, sel, d.z[2], d.y[0] = sync(o_x, wo_c, sel, d.z[2], d.y[0])
+    o_x, o_c0, wo_c, sel, d.z[2], d.y[0] = sync(o_x, o_c0, wo_c, sel, d.z[2], d.y[0])
     d.ring(3)
     d.side(1)
+    d.side(2)
     d.chip(0)
     d.core_own(0)
-    o_c = swap_c(jnp.stack([o, o_x]))
+    o_c1 = swap_c(o_x)
     h, low, ring0 = kernel_call(
         out_body,
         [sds((tok, width), F32), sds((tok, width), BF16), sds((tok, 2 * cols), BF16)],
-        [idx, tokens, o, o_x, o_c, wo, wo_c, aux_t],
+        [idx, tokens, o, o_x, o_c0, o_c1, wo, wo_c, aux_t],
         flops=5e9,
         name="out",
     )
-    ring0, d.z[3], d.y[1], d.x[0], d.cs[0] = sync(ring0, d.z[3], d.y[1], d.x[0], d.cs[0])
+    ring0, d.y[1], d.y[2], d.z[3], d.x[0], d.cs[0] = sync(ring0, d.y[1], d.y[2], d.z[3], d.x[0], d.cs[0])
     a = Rows(ring0)
     done = {}
 
@@ -1102,53 +1110,57 @@
     ran = Ran()
     a.ring(1)
     a.side(0)
+    d.chip(1)
+    d.core(0)
+    meet((a, "z", 1), (a, "y", 0), (d, "x", 1), (d, "cx", 0))
+    a.core_side(0)
     a.core_ring(0)
-    d.chip(1)
     d.core_own(1)
-    d.core(0)
-    meet((a, "z", 1), (a, "y cz", 0), (d, "x cs", 1), (d, "cx", 0))
+    meet((a, "cy cz", 0), (d, "cs x", 1))
     a.ring(2)
     a.side(1)
-    a.core_side(0)
+    d.side(3)
+    d.chip(2)
+    run_experts(0)
+    meet((a, "z", 2), (a, "y", 1), (ran, "out", 0), (d, "y", 3), (d, "x", 2), (d, "x", 1))
+    a.core_side(1)
     a.core_ring(1)
-    d.side(2)
     d.core(1)
-    run_experts(0)
-    meet((a, "z", 2), (a, "y cz", 1), (ran, "out", 0), (d, "y", 2), (d, "cx", 1))
+    meet((a, "cy cz", 1), (d, "cx", 1), (d, "x", 2), (ran, "out", 0))
     a.ring(3)
     a.side(2)
-    a.core_side(1)
-    a.core_ring(2)
-    d.side(3)
-    d.chip(2)
+    d.chip(3)
     d.core_own(2)
+    d.core(2)
     run_experts(1)
-    meet((a, "z", 3), (a, "y cz", 2), (ran, "out", 1), (d, "y", 3), (d, "x cs", 2))
+    meet((a, "z", 3), (a, "y", 2), (ran, "out", 1), (d, "x", 3), (d, "cx cs", 2))
     a.side(3)
     a.core_side(2)
-    d.core(2)
+    a.core_ring(2)
     sx.core(1)
-    meet((a, "cy", 2), (sx, "c", 1), (d, "cx", 2), (ran, "out", 1))
-    a.core_ring(3)
-    d.chip(3)
+    sy.core(0)
+    meet((a, "cy cz", 2), (sx, "c", 1), (sy, "c", 0), (ran, "out", 1), (d, "x", 3))
+    sx.side(1)
+    sy.chip(0)
     d.core_own(3)
-    sx.side(1)
-    sy.core(1)
+    d.core(3)
     run_experts(2)
-    meet((a, "y cz", 3), (sx, "s y", 1), (sy, "c", 1), (ran, "out", 2), (d, "x cs", 3))
+    meet((a, "y", 3), (sx, "s y", 1), (sy, "x", 0), (ran, "out", 2), (d, "cs cx", 3))
     sx.ring(1)
     a.core_side(3)
-    d.core(3)
+    a.core_ring(3)
     sx.core(2)
-    meet((a, "cy", 3), (sx, "c", 2), (d, "cx", 3), (ran, "out", 1), (ran, "out", 2), (sy, "c", 1))
+    sy.core(1)
+    meet((a, "cy cz", 3), (sx, "c", 2), (ran, "out", 2), (sy, "c", 1))
     sx.side(2)
     sy.chip(1)
-    sy.core(2)
+    sy.side(0)
     run_experts(3)
-    meet((sx, "s y", 2), (sx, "total", 0), (sy, "x", 1), (sy, "c", 2), (ran, "out", 3))
+    meet((sx, "s y", 2), (sx, "total", 0), (sy, "x", 1), (sy, "s y", 0), (ran, "out", 3))
     grads = ExpertGrads(*[[done[k][i] for k in range(nz)] for i in range(4, 8)])
     sx.ring(2)
     sx.core(3)
+    sy.core(2)
     meet((sx, "c", 3), (ran, "out", 3), (sy, "c", 2))
     sx.side(3)
     sx.core(0)
@@ -1156,44 +1168,49 @@
     sy.core(3)
     grads.run(0)
     grads.run(1)
-    meet((sx, "s y", 3), (sx, "total", 0), (sx, "c", 0), (sy, "x", 2), (sy, "c", 3), (grads, "outs", 0))
+    meet((sx, "s y", 3), (sx, "total", 0), (sx, "c", 0), (sy, "x", 1), (sy, "x", 2), (sy, "c", 3), (grads, "outs", 0))
     sx.ring(3)
     sx.side(0)
     sy.chip(3)
-    sy.core(0)
     grads.run(2)
-    meet((sx, "s y", 0), (sx, "total", 0), (sy, "x", 3), (sy, "c", 0), (grads, "outs", 0))
+    meet((sx, "s y", 0), (sx, "total", 0), (sy, "x", 2), (sy, "x", 3), (grads, "outs", 0))
     sx.ring(0)
     far = swap_x(sx.total[0])
     sy.side(1)
     sy.side(2)
     grads.run(3)
-    sx.total[0], far, *rest = sync(sx.total[0], far, sy.s[1], sy.y[1], sy.s[2], sy.y[2], sy.x[3], sy.c[0], grads.outs[0])
-    sy.s[1], sy.y[1], sy.s[2], sy.y[2], sy.x[3], sy.c[0], grads.outs[0] = rest
+    sx.total[0], far, *rest = sync(sx.total[0], far, sy.s[1], sy.y[1], sy.s[2], sy.y[2], sy.x[3], grads.outs[0])
+    sy.s[1], sy.y[1], sy.s[2], sy.y[2], sy.x[3], grads.outs[0] = rest
     mine = sx.total[0].astype(F32) + jnp.concatenate([far[:, cols:], far[:, :cols]], axis=1).astype(F32)
     head, tail = mine[:tok], sx.total[0][tok:].astype(F32) + far[tok:].astype(F32)
     fm = jnp.concatenate([head.astype(BF16), tail.astype(BF16)], axis=0)
     fn = swap_c(fm)
-    fm, fn, sy.y[1], sy.x[3], sy.c[0] = sync(fm, fn, sy.y[1], sy.x[3], sy.c[0])
+    fm, fn, sy.y[1], sy.x[3] = sync(fm, fn, sy.y[1], sy.x[3])
     sy.side(3)
     sy.ring(1)
-    sy.chip(0)
+    groups = sent_groups(nz)
+
+    def blocks_of(n, width, groups):
+        return [sds((n, width), BF16)] * nz + [sds((len(g), n, width), BF16) for g in groups]
+
     d_h, d_o, *early = kernel_call(
         functools.partial(hidden_back_body, nz),
-        [sds((tok, cols), F32), sds((tok, qd), BF16)] + [sds((rows, qd + 128), BF16)] * n_dp,
+        [sds((tok, cols), F32), sds((tok, qd), BF16)] + blocks_of(rows, qd + 128, groups[0]),
         [idx, fm, fn, h, low, aux_t, pos, cotangent, o, wo],
         scratch=[pltpu.VMEM((tok, width), F32), pltpu.VMEM((experts, tok), F32), pltpu.VMEM((n_dp, rows, qd + 128), BF16)],
         flops=3e9,
         name="hidden_back",
     )
-    d_o, early, sy.total[0], sy.s[3], sy.y[3], sy.x[0] = sync(d_o, early, sy.total[0], sy.s[3], sy.y[3], sy.x[0])
+    d_o, early, sy.total[0], sy.s[3], sy.y[3] = sync(d_o, early, sy.total[0], sy.s[3], sy.y[3])
 
     class Weights:
-        def __init__(self, v):
-            self.kept, self.sent, self.y, self.total = v[:nz], v[nz:], {}, {}
-
-        def side(self, k):
-            self.y[k] = swap_y(self.sent[k])
+        def __init__(self, v, groups):
+            self.kept, self.sent, self.groups, self.y, self.total = v[:nz], v[nz:], groups, {}, {}
+
+        def side(self, i):
+            got = swap_y(self.sent[i])
+            for at, k in enumerate(self.groups[i]):
+                self.y[k] = got[at]
 
         def ring(self, k):
             total = self.kept[k].astype(F32) + self.y[k].astype(F32)
@@ -1204,14 +1221,12 @@
         def last(self):
             return self.kept[0], self.y[0], self.total[0]
 
-    early = Weights(early)
-    early.side(1)
-    sy.side(0)
+    early = Weights(early, groups[0])
+    early.side(0)
     sy.ring(2)
-    late, dxm, dxn = [], None, None
     dxm, dxn, *late = kernel_call(
         functools.partial(attend_back_body, nz),
-        [sds((tok, 2 * cols + 128), BF16), sds((tok, 2 * cols + 128), BF16)] + [sds((rows + 16, used), BF16)] * n_dp,
+        [sds((tok, 2 * cols + 128), BF16), sds((tok, 2 * cols + 128), BF16)] + blocks_of(rows + 16, used, groups[1]),
         [idx, d_o, v, k_rot, q, cos, sin, tokens, aux_t, w_all, *heads_p],
         scratch=[
             pltpu.VMEM((tok, used), F32), pltpu.VMEM((tok, used), BF16), pltpu.VMEM((4, tok, cols), BF16),
@@ -1220,22 +1235,15 @@
         flops=5e9,
         name="attend_back",
     )
-    late, dxm, dxn, early.y[1], sy.y[0], sy.s[0], sy.total[0] = sync(
-        late, dxm, dxn, early.y[1], sy.y[0], sy.s[0], sy.total[0]
-    )
-    late = Weights(late)
-    late.side(1)
-    early.side(2)
-    early.ring(1)
+    late, dxm, dxn, early.y, early.sent, sy.total[0] = sync(late, dxm, dxn, early.y, early.sent, sy.total[0])
+    late = Weights(late, groups[1])
+    late.side(0)
     sy.ring(3)
     got = swap_c(dxn)
-    late.y[1], early.y[2], early.total[0], sy.total[0], got = sync(
-        late.y[1], early.y[2], early.total[0], sy.total[0], got
-    )
-    late.side(2)
+    late.y, late.sent, early.sent, early.y, got = sync(late.y, late.sent, early.sent, early.y, got)
+    late.side(1)
     late.ring(1)
-    early.side(3)
-    early.ring(2)
+    early.ring(1)
     ours = dxm.astype(F32) + got.astype(F32)
     mean_part = ours[:, 2 * cols] + ours[:, 2 * cols + 1]
     high, lowp = split16(mean_part)
@@ -1243,15 +1251,15 @@
         [ours[:, cols : 2 * cols].astype(BF16), high[:, None], lowp[:, None], jnp.zeros((tok, 126), BF16)], axis=1
     )
     got = swap_x(send)
+    late.y, late.sent, late.total[0], early.total[0], got, sy.total[0] = sync(
+        late.y, late.sent, late.total[0], early.total[0], got, sy.total[0]
+    )
+    late.side(2)
+    late.ring(2)
+    early.side(1)
+    early.ring(2)
     y_sum = sy.s[0].astype(F32) + sy.y[0].astype(F32) + sy.total[0].astype(F32)
     mixed = (y_sum + lax.dynamic_slice_in_dim(h, t * cols, cols, 1)).astype(BF16)
-    late.y[2], late.total[0], early.y[3], early.total[0], got, mixed = sync(
-        late.y[2], late.total[0], early.y[3], early.total[0], got, mixed
-    )
-    late.side(3)
-    late.ring(2)
-    early.side(0)
-    early.ring(3)
     x_full = tokens.astype(F32)
     r1 = lax.rsqrt(jnp.mean(x_full * x_full, axis=-1, keepdims=True) + epsilon)
     d_norm = ours[:, :cols] + got[:, :cols].astype(F32)
@@ -1259,11 +1267,12 @@
     x_cols = lax.dynamic_slice_in_dim(tokens, t * cols, cols, 1).astype(F32) * r1
     gain_row = lax.dynamic_slice_in_dim(aux_t[64:65], t * cols, cols, 1).astype(F32)
     grad_tokens = d_h + r1 * (d_norm * gain_row - x_cols * mean)
-    late.y[3], late.total[0], early.y[0], early.total[0], grad_tokens = sync(
-        late.y[3], late.total[0], early.y[0], early.total[0], grad_tokens
-    )
-    late.side(0)
+    late.y, late.total[0], early.y, early.total[0], grad_tokens, mixed = sync(
+        late.y, late.total[0], early.y, early.total[0], grad_tokens, mixed
+    )
     late.ring(3)
+    early.ring(3)
+    late.total[0], early.total[0] = sync(late.total[0], early.total[0])
     grad_out, grad_router, gain_rows = kernel_call(
         early_end_body,
         [sds((qd, rows), F32), sds((rows, experts), F32), sds((8, rows), F32)],
@@ -1271,7 +1280,6 @@
         name="early_end",
     )
     grad_gain_moe = gain_rows[0]
-    late.y[0], late.total[0], grad_out = sync(late.y[0], late.total[0], grad_out)
     grad_query, grad_key, grad_value, gain_rows = kernel_call(
         late_end_body,
         [sds((rows, qd), F32), sds((rows, kd), F32), sds((rows, kd), F32), sds((8, rows), F32)],

time: 472 us -> 463 us (0.981)
  waiting for transfers between devices: 176 us -> 163 us
    ppermute x28 -> x25, waiting for transfers between devices: 71.5 us -> 48.4 us  [swap_y(): return lax.ppermute(v, 'dp', [(i, i ^ 1) for i in range(n_dp)])]
    ppermute x21, waiting for transfers between devices: 53.2 us -> 69.5 us  [shift_z(): lax.ppermute(v, 'dp', [(i, (i // 2 + 1) % nz * 2 + i % 2) for i in range(...]
    ppermute x16, waiting for transfers between devices: 35 us -> 25.1 us  [swap_x(): return lax.ppermute(v, 'tensor', [(i, i ^ 2) for i in range(4)])]
    ppermute x28 -> x25, starting transfers between devices: 29.6 us -> 25.3 us  [swap_y(): return lax.ppermute(v, 'dp', [(i, i ^ 1) for i in range(n_dp)])]
    ppermute x29 -> x30, waiting for transfers between devices: 15.9 us -> 19.8 us  [swap_c(): return lax.ppermute(v, 'tensor', [(i, i ^ 1) for i in range(4)])]
    unnamed x178 -> x188, local copies, waits for them, and re-layouts: 19.4 us -> 20.4 us
  transfers between devices with their start and end apart: 94 -> 92, of which waited for: 37 -> 32; matrix products, arithmetic and copies ran while one was open for 9% -> 9% of each run, Pallas kernels for 33% -> 34%
where the time goes in v3:
time: 463 us; the launch traced here: 456 us
  waiting for transfers between devices  163 us (35%)
  Pallas kernels  158 us (34%)
  starting transfers between devices  64.8 us (14%)
  other arithmetic  41 us (9%)
  local copies, waits for them, and re-layouts  26.6 us (6%)
    pallas_call x4, Pallas kernels, experts_call(): pl.pallas_call(functools.partial(experts_body, local), out_shape=outs, in...  102 us
    ppermute x21, waiting for transfers between devices, shift_z(): lax.ppermute(v, 'dp', [(i, (i // 2 + 1) % nz * 2 + i % 2) for i in range(...  69.5 us
    ppermute x25, waiting for transfers between devices, swap_y(): return lax.ppermute(v, 'dp', [(i, i ^ 1) for i in range(n_dp)])  48.4 us
    pallas_call x8, Pallas kernels, kernel_call(): pl.pallas_call(body, out_shape=[sds(o.shape, o.dtype) for o in outs], in_...  35.6 us
    ppermute x25, starting transfers between devices, swap_y(): return lax.ppermute(v, 'dp', [(i, i ^ 1) for i in range(n_dp)])  25.3 us
    ppermute x16, waiting for transfers between devices, swap_x(): return lax.ppermute(v, 'tensor', [(i, i ^ 2) for i in range(4)])  25.1 us
    pallas_call x4, Pallas kernels, run(): pl.pallas_call(with_earlier, grid=(each,), out_shape=[sds((local, width,...  21 us
    unnamed x188, local copies, waits for them, and re-layouts  20.4 us
  transfers between devices with their start and end apart: 92, of which 32 were waited for; matrix products, arithmetic and copies ran while one was open for 9% of the time, Pallas kernels for 34%

profile of v3, /device:TPU:0, one launch (start us, length us, event | category | flops | bytes accessed | tf_op | source)
XLA Modules:
  0.0 455.9 jit_solution(11901238093640907889)
XLA Ops:
  4.4 3.1 collective-permute-start
  7.4 1.5 collective-permute-start.1
  9.5 1.4 reduce.9
  11.4 1.8 slots.1.pos_ref
  14.4 5.2 %collective-permute-done.refs_1_ = bf16[192,1152]{1,0:T(8,128)(2,1)S(1)} collective-permute-done((bf16[192,1152]{1,0:T(8,128)(2,1)S(1)}, bf16[192,1152]{1,0:T(8,128)(2,1)S(1)}, u32[]{:S(2)}, u32[]{:S(2)}) %collective-permute-start) | collective-permute-done | bytes 442400 | tf_op jit(solution)/shard_map/ppermute | solution.py:917
  20.6 1.5 collective-permute-start.3
  22.2 1.6 collective-permute-start.7
  23.8 9.0 %collective-permute-done.2.refs_2_ = bf16[192,1152]{1,0:T(8,128)(2,1)S(1)} collective-permute-done((bf16[192,1152]{1,0:T(8,128)(2,1)S(1)}, bf16[192,1152]{1,0:T(8,128)(2,1)S(1)}, u32[]{:S(2)}, u32[]{:S(2)}) %collective-permute-start.2) | collective-permute-done | bytes 442400 | tf_op jit(solution)/shard_map/ppermute | solution.py:917
  34.2 1.6 collective-permute-start.9
  35.8 9.2 %collective-permute-done.4.refs_3_ = bf16[192,1152]{1,0:T(8,128)(2,1)S(1)} collective-permute-done((bf16[192,1152]{1,0:T(8,128)(2,1)S(1)}, bf16[192,1152]{1,0:T(8,128)(2,1)S(1)}, u32[]{:S(2)}, u32[]{:S(2)}) %collective-permute-start.4) | collective-permute-done | bytes 442400 | tf_op jit(solution)/shard_map/ppermute | solution.py:917
  46.2 1.6 collective-permute-start.10
  47.7 3.4 pad_maximum_fusion.refs_8_
  51.2 3.4 collective-permute-done.6.refs_7_
  55.4 8.3 %attend.1 = (bf16[512,384]{1,0:T(8,128)(2,1)}, bf16[512,384]{1,0:T(8,128)(2,1)S(1)}, bf16[512,128]{1,0:T(8,128)(2,1)S(1)}, bf16[512,128]{1,0:T(8,128)(2,1)S(1)},...) custom-call(s32[5]{0:T(128)S(1)} %stack.104.idx, ...), custom_call_target="tpu_custom_call" | custom-call | flops 4000000000 | bytes 12587008 | tf_op jit(solution)/shard_map/attend/pallas_call | solution.py:404
  66.4 1.6 collective-permute-start.16
  68.6 10.8 %collective-permute-done.12.o1 = bf16[512,384]{1,0:T(8,128)(2,1)S(1)} collective-permute-done((bf16[512,384]{1,0:T(8,128)(2,1)}, bf16[512,384]{1,0:T(8,128)(2,1)S(1)}, u32[]{:S(2)}, u32[]{:S(2)}) %collective-permute-start.12) | collective-permute-done | bytes 393248 | tf_op jit(solution)/shard_map/ppermute | solution.py:923
  82.9 1.5 collective-permute-start.18
  88.7 6.7 %out.1 = (f32[512,1536]{1,0:T(8,128)S(1)}, bf16[512,1536]{1,0:T(8,128)(2,1)S(1)}, bf16[512,768]{1,0:T(8,128)(2,1)}) custom-call(s32[5]{0:T(128)S(1)} %stack.104.idx, bf16[512,1536]{1,0:T(8,128)(2,1)S(1)} %copy-done.19, bf16[512,384]{1,0:T(8,128)(2,1)} %get-tuple-element.322.o0.o_ref, bf16[512,384]{1,0:T(8,128)(2,1)S(1)} %collective-permute-done.12.o1, ...), custom_call_target="tpu_custom_call" | custom-call | flops 5000000000 | bytes 13762560 | tf_op jit(solution)/shard_map/out/pallas_call | solution.py:404
  96.5 8.2 %collective-permute-done.19 = bf16[576,384]{1,0:T(8,128)(2,1)S(1)} collective-permute-done((bf16[576,384]{1,0:T(8,128)(2,1)}, bf16[576,384]{1,0:T(8,128)(2,1)S(1)}, u32[]{:S(2)}, u32[]{:S(2)}) %collective-permute-start.19) | collective-permute-done | bytes 442400 | tf_op jit(solution)/shard_map/ppermute | solution.py:920
  104.8 1.4 pad_maximum_fusion.2.refs_4_
  108.8 21.1 %collective-permute-done.23.refs_0_ = bf16[512,768]{1,0:T(8,128)(2,1)} collective-permute-done((bf16[512,768]{1,0:T(8,128)(2,1)}, bf16[512,768]{1,0:T(8,128)(2,1)}, u32[]{:S(2)}, u32[]{:S(2)}) %collective-permute-start.23) | collective-permute-done | bytes 786464 | tf_op jit(solution)/shard_map/ppermute | solution.py:917
  132.9 2.2 pad_maximum_fusion.4.refs_4_
  135.1 1.5 collective-permute-start.33
  137.2 32.6 %experts.4 = (bf16[2,544,768]{2,1,0:T(8,128)(2,1)}, bf16[2,544,768]{2,1,0:T(8,128)(2,1)}, bf16[2,512,768]{2,1,0:T(8,128)(2,1)}, bf16[2,512,768]{2,1,0:T(8,128)(2...) custom-call(s32[5]{0:T(128)} %copy-done.28, ...), custom_call_target="tpu_custom_call" | custom-call | flops 12582912000 | bytes 31457280 | tf_op jit(solution)/shard_map/experts/pallas_call | solution.py:681
  174.5 1.5 collective-permute-start.38
  178.3 23.1 %experts.5 = (bf16[2,544,768]{2,1,0:T(8,128)(2,1)}, bf16[2,544,768]{2,1,0:T(8,128)(2,1)}, bf16[2,512,768]{2,1,0:T(8,128)(2,1)}, bf16[2,512,768]{2,1,0:T(8,128)(2...) custom-call(s32[5]{0:T(128)} %copy-done.28, ...), custom_call_target="tpu_custom_call" | custom-call | flops 12582912000 | bytes 31457280 | tf_op jit(solution)/shard_map/experts/pallas_call | solution.py:681
  203.1 8.1 %collective-permute-done.44.refs_2_ = bf16[512,768]{1,0:T(8,128)(2,1)S(1)} collective-permute-done((bf16[512,768]{1,0:T(8,128)(2,1)}, bf16[512,768]{1,0:T(8,128)(2,1)S(1)}, u32[]{:S(2)}, u32[]{:S(2)}) %collective-permute-start.44) | collective-permute-done | bytes 786464 | tf_op jit(solution)/shard_map/ppermute | solution.py:926
  213.3 2.8 fusion.3
  219.4 22.9 %experts.6 = (bf16[2,544,768]{2,1,0:T(8,128)(2,1)}, bf16[2,544,768]{2,1,0:T(8,128)(2,1)}, bf16[2,512,768]{2,1,0:T(8,128)(2,1)}, bf16[2,512,768]{2,1,0:T(8,128)(2...) custom-call(s32[5]{0:T(128)} %copy-done.28, ...), custom_call_target="tpu_custom_call" | custom-call | flops 12582912000 | bytes 31457280 | tf_op jit(solution)/shard_map/experts/pallas_call | solution.py:681
  242.4 6.9 %collective-permute-done.47 = bf16[544,768]{1,0:T(8,128)(2,1)} collective-permute-done((bf16[544,768]{1,0:T(8,128)(2,1)}, bf16[544,768]{1,0:T(8,128)(2,1)}, u32[]{:S(2)}, u32[]{:S(2)}) %collective-permute-start.47) | collective-permute-done | bytes 835616 | tf_op jit(solution)/shard_map/ppermute | solution.py:920
  250.3 2.3 add_convert_fusion.7
  253.0 2.6 fusion.17
  258.7 1.6 fusion.5
  262.1 1.6 collective-permute-start.57
  263.7 23.1 %experts.7 = (bf16[2,544,768]{2,1,0:T(8,128)(2,1)}, bf16[2,544,768]{2,1,0:T(8,128)(2,1)}, bf16[2,512,768]{2,1,0:T(8,128)(2,1)}, bf16[2,512,768]{2,1,0:T(8,128)(2...) custom-call(s32[5]{0:T(128)} %copy-done.28, ...), custom_call_target="tpu_custom_call" | custom-call | flops 12582912000 | bytes 31457280 | tf_op jit(solution)/shard_map/experts/pallas_call | solution.py:681
  287.6 5.4 %collective-permute-done.60 = bf16[2,512,768]{2,1,0:T(8,128)(2,1)S(1)} collective-permute-done((bf16[2,512,768]{2,1,0:T(8,128)(2,1)}, bf16[2,512,768]{2,1,0:T(8,128)(2,1)S(1)}, u32[]{:S(2)}, u32[]{:S(2)}) %collective-permute-start.60) | collective-permute-done | bytes 1572896 | tf_op jit(solution)/shard_map/ppermute | solution.py:926
  293.1 2.1 add_convert_fusion.4
  295.8 1.9 fusion.7
  299.0 2.2 add_convert_fusion.14
  301.9 2.1 copy-done.2
  304.0 2.1 copy-done.3
  307.1 5.2 %expert_grads.4 = (f32[8,1536,128]{2,1,0:T(8,128)}, f32[8,1536,128]{2,1,0:T(8,128)}, f32[8,128,1536]{2,1,0:T(8,128)}) custom-call(bf16[8,2,80,1536]{3,2,1,0:T(8,128)(2,1)S(1)} %copy-done, bf16[8,2,80,1536]{3,2,1,0:T(8,128)(2,1)S(1)} %copy-done.1, bf16[8,2,80,1536]{3,2,1,0:T(8,128)(2,1)S(1)} %copy-done.2, bf16[8,2,80,1536]{3,2,1,0:T(8,128)(2,1)S(1)} %copy-done.3, ...), custom_call_target="tpu_custom_call" | custom-call | flops 1509949440 | bytes 12582912 | tf_op jit(solution)/shard_map/expert_grads/pallas_call | solution.py:872
  312.3 5.3 %expert_grads.5 = (f32[8,1536,128]{2,1,0:T(8,128)}, f32[8,1536,128]{2,1,0:T(8,128)}, f32[8,128,1536]{2,1,0:T(8,128)}) custom-call(bf16[8,2,80,1536]{3,2,1,0:T(8,128)(2,1)S(1)} %copy-done, bf16[8,2,80,1536]{3,2,1,0:T(8,128)(2,1)S(1)} %copy-done.1, ...), custom_call_target="tpu_custom_call", output_to_operand_aliasing={{0}: (16, {}), {1}: (17, {}), {2}: (18, {})} | custom-call | flops 1509949440 | bytes 12582912 | tf_op jit(solution)/shard_map/expert_grads/pallas_call | solution.py:872
  318.2 2.6 collective-permute-done.64
  323.3 2.6 collective-permute-start.67
  327.2 5.2 %expert_grads.6 = (f32[8,1536,128]{2,1,0:T(8,128)}, f32[8,1536,128]{2,1,0:T(8,128)}, f32[8,128,1536]{2,1,0:T(8,128)}) custom-call(bf16[8,2,80,1536]{3,2,1,0:T(8,128)(2,1)S(1)} %copy-done, bf16[8,2,80,1536]{3,2,1,0:T(8,128)(2,1)S(1)} %copy-done.1, ...), custom_call_target="tpu_custom_call", output_to_operand_aliasing={{0}: (16, {}), {1}: (17, {}), {2}: (18, {})} | custom-call | flops 1509949440 | bytes 12582912 | tf_op jit(solution)/shard_map/expert_grads/pallas_call | solution.py:872
  332.4 11.8 %collective-permute-done.68 = bf16[2,512,384]{2,1,0:T(8,128)(2,1)S(1)} collective-permute-done((bf16[2,512,384]{2,1,0:T(8,128)(2,1)S(1)}, bf16[2,512,384]{2,1,0:T(8,128)(2,1)S(1)}, u32[]{:S(2)}, u32[]{:S(2)}) %collective-permute-start.68) | collective-permute-done | bytes 786464 | tf_op jit(solution)/shard_map/ppermute | solution.py:923
  346.9 1.4 fusion.19
  349.5 1.4 fusion.21
  351.9 5.3 %expert_grads.7 = (f32[8,1536,128]{2,1,0:T(8,128)}, f32[8,1536,128]{2,1,0:T(8,128)}, f32[8,128,1536]{2,1,0:T(8,128)}) custom-call(bf16[8,2,80,1536]{3,2,1,0:T(8,128)(2,1)S(1)} %copy-done, bf16[8,2,80,1536]{3,2,1,0:T(8,128)(2,1)S(1)} %copy-done.1, ...), custom_call_target="tpu_custom_call", output_to_operand_aliasing={{0}: (16, {}), {1}: (17, {}), {2}: (18, {})} | custom-call | flops 1509949440 | bytes 12582912 | tf_op jit(solution)/shard_map/expert_grads/pallas_call | solution.py:872
  357.2 3.2 collective-permute-done.70
  360.5 5.2 %collective-permute-done.71 = bf16[512,384]{1,0:T(8,128)(2,1)S(1)} collective-permute-done((bf16[512,384]{1,0:T(8,128)(2,1)S(1)}, bf16[512,384]{1,0:T(8,128)(2,1)S(1)}, u32[]{:S(2)}, u32[]{:S(2)}) %collective-permute-start.71) | collective-permute-done | bytes 393248 | tf_op jit(solution)/shard_map/ppermute | solution.py:920
  368.1 2.3 collective-permute-done.72.fn_ref
  370.6 1.4 collective-permute-start.73
  373.7 6.6 %hidden_back.1 = (f32[512,384]{1,0:T(8,128)S(1)}, bf16[512,384]{1,0:T(8,128)(2,1)S(1)}, bf16[192,512]{1,0:T(8,128)(2,1)S(1)}, bf16[192,512]{1,0:T(8,128)(2,1)S(1...) custom-call(s32[5]{0:T(128)S(1)} %copy-done.29, ...), custom_call_target="tpu_custom_call" | custom-call | flops 3000000000 | bytes 13926400 | tf_op jit(solution)/shard_map/hidden_back/pallas_call | solution.py:404
  380.4 3.2 collective-permute-done.73
  385.8 9.3 %attend_back.1 = (bf16[512,896]{1,0:T(8,128)(2,1)S(1)}, bf16[512,896]{1,0:T(8,128)(2,1)S(1)}, bf16[208,640]{1,0:T(8,128)(2,1)S(1)}, bf16[208,640]{1,0:T(8,128)(2...) custom-call(s32[5]{0:T(128)S(1)} %copy-done.29, ...), custom_call_target="tpu_custom_call" | custom-call | flops 5000000000 | bytes 13008896 | tf_op jit(solution)/shard_map/attend_back/pallas_call | solution.py:404
  395.2 3.0 collective-permute-done.75
  400.5 7.0 %collective-permute-done.77 = bf16[1,208,640]{2,1,0:T(8,128)(2,1)S(1)} collective-permute-done((bf16[1,208,640]{2,1,0:T(8,128)(2,1)S(1)}, bf16[1,208,640]{2,1,0:T(8,128)(2,1)S(1)}, u32[]{:S(2)}, u32[]{:S(2)}) %collective-permute-start.77) | collective-permute-done | bytes 266272 | tf_op jit(solution)/shard_map/ppermute | solution.py:920
  411.2 10.4 %collective-permute-done.79 = bf16[2,208,640]{2,1,0:T(8,128)(2,1)S(1)} collective-permute-done((bf16[2,208,640]{2,1,0:T(8,128)(2,1)S(1)}, bf16[2,208,640]{2,1,0:T(8,128)(2,1)S(1)}, u32[]{:S(2)}, u32[]{:S(2)}) %collective-permute-start.79) | collective-permute-done | bytes 532512 | tf_op jit(solution)/shard_map/ppermute | solution.py:920
  426.6 1.9 add_convert_fusion.17
  429.5 7.3 %collective-permute-done.87 = bf16[192,512]{1,0:T(8,128)(2,1)S(1)} collective-permute-done((bf16[192,512]{1,0:T(8,128)(2,1)S(1)}, bf16[192,512]{1,0:T(8,128)(2,1)S(1)}, u32[]{:S(2)}, u32[]{:S(2)}) %collective-permute-start.87) | collective-permute-done | bytes 196640 | tf_op jit(solution)/shard_map/ppermute | solution.py:917
  437.1 11.2 %collective-permute-done.89.ring = bf16[192,512]{1,0:T(8,128)(2,1)S(1)} collective-permute-done((bf16[192,512]{1,0:T(8,128)(2,1)S(1)}, bf16[192,512]{1,0:T(8,128)(2,1)S(1)}, u32[]{:S(2)}, u32[]{:S(2)}) %collective-permute-start.89) | collective-permute-done | bytes 196640 | tf_op jit(solution)/shard_map/ppermute | solution.py:917
  450.8 1.5 collective-permute-start.91
  (404 shorter events, 86.5 us)
Async XLA Ops:
  4.4 15.3 %collective-permute-start = (bf16[192,1152]{1,0:T(8,128)(2,1)S(1)}, bf16[192,1152]{1,0:T(8,128)(2,1)S(1)}, u32[]{:S(2)}, u32[]{:S(2)}) collective-permute-start(bf16[192,1152]{1,0:T(8,128)(2,1)S(1)} %concatenate.21.refs_0_), channel_id=1, source_target_pairs={{0,8},{4,12},{8,16},{12,20},{16,24},{20,28},{24,0},{28,4},{1,9},{5... | collective-permute-start | bytes 1327112 | tf_op jit(solution)/shard_map/ppermute | solution.py:917
  7.4 12.2 %collective-permute-start.1 = (bf16[192,1152]{1,0:T(8,128)(2,1)S(1)}, bf16[192,1152]{1,0:T(8,128)(2,1)S(1)}, u32[]{:S(2)}, u32[]{:S(2)}) collective-permute-start(bf16[192,1152]{1,0:T(8,128)(2,1)S(1)} %concatenate.21.refs_0_), channel_id=1, source_target_pairs={{0,4},{4,0},{8,12},{12,8},{16,20},{20,16},{24,28},{28,24},{1,5},{5... | collective-permute-start | bytes 1327112 | tf_op jit(solution)/shard_map/ppermute | solution.py:920
  19.6 13.2 %collective-permute-start.2 = (bf16[192,1152]{1,0:T(8,128)(2,1)S(1)}, bf16[192,1152]{1,0:T(8,128)(2,1)S(1)}, u32[]{:S(2)}, u32[]{:S(2)}) collective-permute-start(bf16[192,1152]{1,0:T(8,128)(2,1)S(1)} %collective-permute-done.refs_1_), channel_id=1, source_target_pairs={{0,8},{4,12},{8,16},{12,20},{16,24},{20,28},{24,0},{28,4},{1,9},{5... | collective-permute-start | bytes 1327112 | tf_op jit(solution)/shard_map/ppermute | solution.py:917
  20.6 12.1 %collective-permute-start.3 = (bf16[192,1152]{1,0:T(8,128)(2,1)S(1)}, bf16[192,1152]{1,0:T(8,128)(2,1)S(1)}, u32[]{:S(2)}, u32[]{:S(2)}) collective-permute-start(bf16[192,1152]{1,0:T(8,128)(2,1)S(1)} %collective-permute-done.refs_1_), channel_id=1, source_target_pairs={{0,4},{4,0},{8,12},{12,8},{16,20},{20,16},{24,28},{28,24},{1,5},{5... | collective-permute-start | bytes 1327112 | tf_op jit(solution)/shard_map/ppermute | solution.py:920
  22.2 28.9 %collective-permute-start.7 = (bf16[2,192,384]{2,1,0:T(8,128)(2,1)S(1)}, bf16[2,192,384]{2,1,0:T(8,128)(2,1)S(1)}, u32[]{:S(2)}, u32[]{:S(2)}) collective-permute-start(bf16[2,192,384]{2,1,0:T(8,128)(2,1)S(1)} %pad_maximum_fusion.8), channel_id=1, source_target_pairs={{0,2},{1,3},{2,0},{3,1},{4,6},{5,7},{6,4},{7,5},{8,10},{9,11},{10,... | collective-permute-start | bytes 884744 | tf_op jit(solution)/shard_map/ppermute | solution.py:923
  32.8 12.2 %collective-permute-start.4 = (bf16[192,1152]{1,0:T(8,128)(2,1)S(1)}, bf16[192,1152]{1,0:T(8,128)(2,1)S(1)}, u32[]{:S(2)}, u32[]{:S(2)}) collective-permute-start(bf16[192,1152]{1,0:T(8,128)(2,1)S(1)} %collective-permute-done.2.refs_2_), channel_id=1, source_target_pairs={{0,8},{4,12},{8,16},{12,20},{16,24},{20,28},{24,0},{28,4},{1,9},{5... | collective-permute-start | bytes 1327112 | tf_op jit(solution)/shard_map/ppermute | solution.py:917
  32.8 12.2 %collective-permute-start.5 = (bf16[192,1152]{1,0:T(8,128)(2,1)S(1)}, bf16[192,1152]{1,0:T(8,128)(2,1)S(1)}, u32[]{:S(2)}, u32[]{:S(2)}) collective-permute-start(bf16[192,1152]{1,0:T(8,128)(2,1)S(1)} %collective-permute-done.2.refs_2_), channel_id=1, source_target_pairs={{0,4},{4,0},{8,12},{12,8},{16,20},{20,16},{24,28},{28,24},{1,5},{5... | collective-permute-start | bytes 1327112 | tf_op jit(solution)/shard_map/ppermute | solution.py:920
  34.2 29.5 %collective-permute-start.9 = (bf16[2,192,384]{2,1,0:T(8,128)(2,1)S(1)}, bf16[2,192,384]{2,1,0:T(8,128)(2,1)S(1)}, u32[]{:S(2)}, u32[]{:S(2)}) collective-permute-start(bf16[2,192,384]{2,1,0:T(8,128)(2,1)S(1)} %pad_maximum_fusion.9), channel_id=1, source_target_pairs={{0,2},{1,3},{2,0},{3,1},{4,6},{5,7},{6,4},{7,5},{8,10},{9,11},{10,... | collective-permute-start | bytes 884744 | tf_op jit(solution)/shard_map/ppermute | solution.py:923
  46.1 17.8 %collective-permute-start.8 = (bf16[576,384]{1,0:T(8,128)(2,1)}, bf16[576,384]{1,0:T(8,128)(2,1)}, u32[]{:S(2)}, u32[]{:S(2)}) collective-permute-start(bf16[576,384]{1,0:T(8,128)(2,1)} %get-tuple-element.328), channel_id=1, source_target_pairs={{0,8},{4,12},{8,16},{12,20},{16,24},{20,28},{24,0},{28,4},{1,9},{5... | collective-permute-start | bytes 1327112 | tf_op jit(solution)/shard_map/ppermute | solution.py:917
  46.2 17.6 %collective-permute-start.10 = (bf16[2,192,384]{2,1,0:T(8,128)(2,1)S(1)}, bf16[2,192,384]{2,1,0:T(8,128)(2,1)S(1)}, u32[]{:S(2)}, u32[]{:S(2)}) collective-permute-start(bf16[2,192,384]{2,1,0:T(8,128)(2,1)S(1)} %pad_maximum_fusion.10), channel_id=1, source_target_pairs={{0,2},{1,3},{2,0},{3,1},{4,6},{5,7},{6,4},{7,5},{8,10},{9,11},{10,... | collective-permute-start | bytes 884744 | tf_op jit(solution)/shard_map/ppermute | solution.py:923
  66.4 14.7 %collective-permute-start.14 = (bf16[2,1536,384]{2,1,0:T(8,128)(2,1)S(1)}, bf16[2,1536,384]{2,1,0:T(8,128)(2,1)}, u32[]{:S(2)}, u32[]{:S(2)}) collective-permute-start(bf16[2,1536,384]{2,1,0:T(8,128)(2,1)S(1)} %place.1.w01.w_ref), channel_id=1, source_target_pairs={{0,1},{1,0},{2,3},{3,2},{4,5},{5,4},{6,7},{7,6},{8,9},{9,8},{10,11... | collective-permute-start | bytes 7077896 | tf_op jit(solution)/shard_map/ppermute | solution.py:926
  66.4 14.7 %collective-permute-start.15 = (bf16[576,384]{1,0:T(8,128)(2,1)}, bf16[576,384]{1,0:T(8,128)(2,1)}, u32[]{:S(2)}, u32[]{:S(2)}) collective-permute-start(bf16[576,384]{1,0:T(8,128)(2,1)} %collective-permute-done.8), channel_id=1, source_target_pairs={{0,8},{4,12},{8,16},{12,20},{16,24},{20,28},{24,0},{28,4},{1,9},{5... | collective-permute-start | bytes 1327112 | tf_op jit(solution)/shard_map/ppermute | solution.py:917
  66.4 14.7 %collective-permute-start.16 = (bf16[576,384]{1,0:T(8,128)(2,1)}, bf16[576,384]{1,0:T(8,128)(2,1)}, u32[]{:S(2)}, u32[]{:S(2)}) collective-permute-start(bf16[576,384]{1,0:T(8,128)(2,1)} %get-tuple-element.328), channel_id=1, source_target_pairs={{0,4},{4,0},{8,12},{12,8},{16,20},{20,16},{24,28},{28,24},{1,5},{5... | collective-permute-start | bytes 1327112 | tf_op jit(solution)/shard_map/ppermute | solution.py:920
  82.4 22.4 %collective-permute-start.22 = (bf16[2,576,384]{2,1,0:T(8,128)(2,1)S(1)}, bf16[2,576,384]{2,1,0:T(8,128)(2,1)S(1)}, u32[]{:S(2)}, u32[]{:S(2)}) collective-permute-start(bf16[2,576,384]{2,1,0:T(8,128)(2,1)S(1)} %pad_maximum_fusion.1.refs_4_), channel_id=1, source_target_pairs={{0,1},{1,0},{2,3},{3,2},{4,5},{5,4},{6,7},{7,6},{8,9},{9,8},{10,11... | collective-permute-start | bytes 2654216 | tf_op jit(solution)/shard_map/ppermute | solution.py:926
  82.9 13.6 %collective-permute-start.18 = (bf16[576,384]{1,0:T(8,128)(2,1)}, bf16[576,384]{1,0:T(8,128)(2,1)S(1)}, u32[]{:S(2)}, u32[]{:S(2)}) collective-permute-start(bf16[576,384]{1,0:T(8,128)(2,1)} %collective-permute-done.8), channel_id=1, source_target_pairs={{0,4},{4,0},{8,12},{12,8},{16,20},{20,16},{24,28},{28,24},{1,5},{5... | collective-permute-start | bytes 1327112 | tf_op jit(solution)/shard_map/ppermute | solution.py:920
  84.5 20.3 %collective-permute-start.19 = (bf16[576,384]{1,0:T(8,128)(2,1)}, bf16[576,384]{1,0:T(8,128)(2,1)S(1)}, u32[]{:S(2)}, u32[]{:S(2)}) collective-permute-start(bf16[576,384]{1,0:T(8,128)(2,1)} %collective-permute-done.15), channel_id=1, source_target_pairs={{0,4},{4,0},{8,12},{12,8},{16,20},{20,16},{24,28},{28,24},{1,5},{5... | collective-permute-start | bytes 1327112 | tf_op jit(solution)/shard_map/ppermute | solution.py:920
  85.0 19.8 %collective-permute-start.20 = (bf16[576,384]{1,0:T(8,128)(2,1)}, bf16[576,384]{1,0:T(8,128)(2,1)}, u32[]{:S(2)}, u32[]{:S(2)}) collective-permute-start(bf16[576,384]{1,0:T(8,128)(2,1)} %collective-permute-done.15), channel_id=1, source_target_pairs={{0,8},{4,12},{8,16},{12,20},{16,24},{20,28},{24,0},{28,4},{1,9},{5... | collective-permute-start | bytes 1327112 | tf_op jit(solution)/shard_map/ppermute | solution.py:917
  85.4 19.4 %collective-permute-start.21 = (bf16[576,384]{1,0:T(8,128)(2,1)}, bf16[576,384]{1,0:T(8,128)(2,1)S(1)}, u32[]{:S(2)}, u32[]{:S(2)}) collective-permute-start(bf16[576,384]{1,0:T(8,128)(2,1)} %collective-permute-done.16), channel_id=1, source_target_pairs={{0,2},{1,3},{2,0},{3,1},{4,6},{5,7},{6,4},{7,5},{8,10},{9,11},{10,... | collective-permute-start | bytes 1327112 | tf_op jit(solution)/shard_map/ppermute | solution.py:923
  106.2 23.6 %collective-permute-start.25 = (bf16[2,576,384]{2,1,0:T(8,128)(2,1)S(1)}, bf16[2,576,384]{2,1,0:T(8,128)(2,1)}, u32[]{:S(2)}, u32[]{:S(2)}) collective-permute-start(bf16[2,576,384]{2,1,0:T(8,128)(2,1)S(1)} %pad_maximum_fusion.2.refs_4_), channel_id=1, source_target_pairs={{0,2},{1,3},{2,0},{3,1},{4,6},{5,7},{6,4},{7,5},{8,10},{9,11},{10,... | collective-permute-start | bytes 2654216 | tf_op jit(solution)/shard_map/ppermute | solution.py:923
  107.7 22.2 %collective-permute-start.26 = (bf16[2,576,384]{2,1,0:T(8,128)(2,1)S(1)}, bf16[2,576,384]{2,1,0:T(8,128)(2,1)S(1)}, u32[]{:S(2)}, u32[]{:S(2)}) collective-permute-start(bf16[2,576,384]{2,1,0:T(8,128)(2,1)S(1)} %pad_maximum_fusion.3.refs_5_), channel_id=1, source_target_pairs={{0,1},{1,0},{2,3},{3,2},{4,5},{5,4},{6,7},{7,6},{8,9},{9,8},{10,11... | collective-permute-start | bytes 2654216 | tf_op jit(solution)/shard_map/ppermute | solution.py:926
  107.8 22.1 %collective-permute-start.23 = (bf16[512,768]{1,0:T(8,128)(2,1)}, bf16[512,768]{1,0:T(8,128)(2,1)}, u32[]{:S(2)}, u32[]{:S(2)}) collective-permute-start(bf16[512,768]{1,0:T(8,128)(2,1)} %get-tuple-element.336.refs_0_), channel_id=1, source_target_pairs={{0,8},{4,12},{8,16},{12,20},{16,24},{20,28},{24,0},{28,4},{1,9},{5... | collective-permute-start | bytes 2359304 | tf_op jit(solution)/shard_map/ppermute | solution.py:917
  107.9 22.0 %collective-permute-start.24 = (bf16[512,768]{1,0:T(8,128)(2,1)}, bf16[512,768]{1,0:T(8,128)(2,1)}, u32[]{:S(2)}, u32[]{:S(2)}) collective-permute-start(bf16[512,768]{1,0:T(8,128)(2,1)} %get-tuple-element.336.refs_0_), channel_id=1, source_target_pairs={{0,4},{4,0},{8,12},{12,8},{16,20},{20,16},{24,28},{28,24},{1,5},{5... | collective-permute-start | bytes 2359304 | tf_op jit(solution)/shard_map/ppermute | solution.py:920
  108.7 27.9 %collective-permute-start.31 = (bf16[2,576,384]{2,1,0:T(8,128)(2,1)S(1)}, bf16[2,576,384]{2,1,0:T(8,128)(2,1)S(1)}, u32[]{:S(2)}, u32[]{:S(2)}) collective-permute-start(bf16[2,576,384]{2,1,0:T(8,128)(2,1)S(1)} %pad_maximum_fusion.2.refs_4_), channel_id=1, source_target_pairs={{0,1},{1,0},{2,3},{3,2},{4,5},{5,4},{6,7},{7,6},{8,9},{9,8},{10,11... | collective-permute-start | bytes 2654216 | tf_op jit(solution)/shard_map/ppermute | solution.py:926
  132.1 37.7 %collective-permute-start.32 = (bf16[576,384]{1,0:T(8,128)(2,1)}, bf16[576,384]{1,0:T(8,128)(2,1)S(1)}, u32[]{:S(2)}, u32[]{:S(2)}) collective-permute-start(bf16[576,384]{1,0:T(8,128)(2,1)} %collective-permute-done.20), channel_id=1, source_target_pairs={{0,4},{4,0},{8,12},{12,8},{16,20},{20,16},{24,28},{28,24},{1,5},{5... | collective-permute-start | bytes 1327112 | tf_op jit(solution)/shard_map/ppermute | solution.py:920
  135.1 34.8 %collective-permute-start.33 = (bf16[2,576,384]{2,1,0:T(8,128)(2,1)}, bf16[2,576,384]{2,1,0:T(8,128)(2,1)}, u32[]{:S(2)}, u32[]{:S(2)}) collective-permute-start(bf16[2,576,384]{2,1,0:T(8,128)(2,1)} %pad_maximum_fusion.4.refs_4_), channel_id=1, source_target_pairs={{0,2},{1,3},{2,0},{3,1},{4,6},{5,7},{6,4},{7,5},{8,10},{9,11},{10,... | collective-permute-start | bytes 2654216 | tf_op jit(solution)/shard_map/ppermute | solution.py:923
  136.6 33.3 %collective-permute-start.27 = (bf16[512,768]{1,0:T(8,128)(2,1)}, bf16[512,768]{1,0:T(8,128)(2,1)}, u32[]{:S(2)}, u32[]{:S(2)}) collective-permute-start(bf16[512,768]{1,0:T(8,128)(2,1)} %collective-permute-done.23.refs_0_), channel_id=1, source_target_pairs={{0,8},{4,12},{8,16},{12,20},{16,24},{20,28},{24,0},{28,4},{1,9},{5... | collective-permute-start | bytes 2359304 | tf_op jit(solution)/shard_map/ppermute | solution.py:917
  136.7 33.2 %collective-permute-start.28 = (bf16[512,768]{1,0:T(8,128)(2,1)}, bf16[512,768]{1,0:T(8,128)(2,1)}, u32[]{:S(2)}, u32[]{:S(2)}) collective-permute-start(bf16[512,768]{1,0:T(8,128)(2,1)} %collective-permute-done.23.refs_0_), channel_id=1, source_target_pairs={{0,4},{4,0},{8,12},{12,8},{16,20},{20,16},{24,28},{28,24},{1,5},{5... | collective-permute-start | bytes 2359304 | tf_op jit(solution)/shard_map/ppermute | solution.py:920
  170.6 30.9 %collective-permute-start.41 = (bf16[2,576,384]{2,1,0:T(8,128)(2,1)}, bf16[2,576,384]{2,1,0:T(8,128)(2,1)}, u32[]{:S(2)}, u32[]{:S(2)}) collective-permute-start(bf16[2,576,384]{2,1,0:T(8,128)(2,1)} %pad_maximum_fusion.4.refs_4_), channel_id=1, source_target_pairs={{0,1},{1,0},{2,3},{3,2},{4,5},{5,4},{6,7},{7,6},{8,9},{9,8},{10,11... | collective-permute-start | bytes 2654216 | tf_op jit(solution)/shard_map/ppermute | solution.py:926
  171.0 30.4 %collective-permute-start.37 = (bf16[512,768]{1,0:T(8,128)(2,1)}, bf16[512,768]{1,0:T(8,128)(2,1)}, u32[]{:S(2)}, u32[]{:S(2)}) collective-permute-start(bf16[512,768]{1,0:T(8,128)(2,1)} %collective-permute-done.27.refs_0_), channel_id=1, source_target_pairs={{0,8},{4,12},{8,16},{12,20},{16,24},{20,28},{24,0},{28,4},{1,9},{5... | collective-permute-start | bytes 2359304 | tf_op jit(solution)/shard_map/ppermute | solution.py:917
  174.5 27.0 %collective-permute-start.38 = (bf16[512,768]{1,0:T(8,128)(2,1)}, bf16[512,768]{1,0:T(8,128)(2,1)S(1)}, u32[]{:S(2)}, u32[]{:S(2)}) collective-permute-start(bf16[512,768]{1,0:T(8,128)(2,1)} %collective-permute-done.27.refs_0_), channel_id=1, source_target_pairs={{0,4},{4,0},{8,12},{12,8},{16,20},{20,16},{24,28},{28,24},{1,5},{5... | collective-permute-start | bytes 2359304 | tf_op jit(solution)/shard_map/ppermute | solution.py:920
  177.0 24.5 %collective-permute-start.39 = (bf16[2,576,384]{2,1,0:T(8,128)(2,1)S(1)}, bf16[2,576,384]{2,1,0:T(8,128)(2,1)}, u32[]{:S(2)}, u32[]{:S(2)}) collective-permute-start(bf16[2,576,384]{2,1,0:T(8,128)(2,1)S(1)} %pad_maximum_fusion.5.refs_4_), channel_id=1, source_target_pairs={{0,2},{1,3},{2,0},{3,1},{4,6},{5,7},{6,4},{7,5},{8,10},{9,11},{10,... | collective-permute-start | bytes 2654216 | tf_op jit(solution)/shard_map/ppermute | solution.py:923
  178.3 23.2 %collective-permute-start.40 = (bf16[2,576,384]{2,1,0:T(8,128)(2,1)}, bf16[2,576,384]{2,1,0:T(8,128)(2,1)}, u32[]{:S(2)}, u32[]{:S(2)}) collective-permute-start(bf16[2,576,384]{2,1,0:T(8,128)(2,1)} %collective-permute-done.33.refs_5_), channel_id=1, source_target_pairs={{0,1},{1,0},{2,3},{3,2},{4,5},{5,4},{6,7},{7,6},{8,9},{9,8},{10,11... | collective-permute-start | bytes 2654216 | tf_op jit(solution)/shard_map/ppermute | solution.py:926
  201.5 11.8 %collective-permute-start.45 = (bf16[2,544,768]{2,1,0:T(8,128)(2,1)}, bf16[2,544,768]{2,1,0:T(8,128)(2,1)S(1)}, u32[]{:S(2)}, u32[]{:S(2)}) collective-permute-start(bf16[2,544,768]{2,1,0:T(8,128)(2,1)} %get-tuple-element.389), channel_id=1, source_target_pairs={{0,1},{1,0},{2,3},{3,2},{4,5},{5,4},{6,7},{7,6},{8,9},{9,8},{10,11... | collective-permute-start | bytes 5013512 | tf_op jit(solution)/shard_map/ppermute | solution.py:926
  202.7 39.7 %collective-permute-start.49 = (bf16[2,576,384]{2,1,0:T(8,128)(2,1)S(1)}, bf16[2,576,384]{2,1,0:T(8,128)(2,1)}, u32[]{:S(2)}, u32[]{:S(2)}) collective-permute-start(bf16[2,576,384]{2,1,0:T(8,128)(2,1)S(1)} %pad_maximum_fusion.5.refs_4_), channel_id=1, source_target_pairs={{0,1},{1,0},{2,3},{3,2},{4,5},{5,4},{6,7},{7,6},{8,9},{9,8},{10,11... | collective-permute-start | bytes 2654216 | tf_op jit(solution)/shard_map/ppermute | solution.py:926
  211.2 31.1 %collective-permute-start.42 = (bf16[512,768]{1,0:T(8,128)(2,1)}, bf16[512,768]{1,0:T(8,128)(2,1)}, u32[]{:S(2)}, u32[]{:S(2)}) collective-permute-start(bf16[512,768]{1,0:T(8,128)(2,1)} %collective-permute-done.37.refs_0_), channel_id=1, source_target_pairs={{0,4},{4,0},{8,12},{12,8},{16,20},{20,16},{24,28},{28,24},{1,5},{5... | collective-permute-start | bytes 2359304 | tf_op jit(solution)/shard_map/ppermute | solution.py:920
  216.1 33.2 %collective-permute-start.47 = (bf16[544,768]{1,0:T(8,128)(2,1)}, bf16[544,768]{1,0:T(8,128)(2,1)}, u32[]{:S(2)}, u32[]{:S(2)}) collective-permute-start(bf16[544,768]{1,0:T(8,128)(2,1)} %get-tuple-element.660), channel_id=1, source_target_pairs={{0,4},{4,0},{8,12},{12,8},{16,20},{20,16},{24,28},{28,24},{1,5},{5... | collective-permute-start | bytes 2506760 | tf_op jit(solution)/shard_map/ppermute | solution.py:920
  218.2 24.2 %collective-permute-start.48 = (bf16[2,512,384]{2,1,0:T(8,128)(2,1)}, bf16[2,512,384]{2,1,0:T(8,128)(2,1)}, u32[]{:S(2)}, u32[]{:S(2)}) collective-permute-start(bf16[2,512,384]{2,1,0:T(8,128)(2,1)} %add_convert_fusion.16), channel_id=1, source_target_pairs={{0,2},{1,3},{2,0},{3,1},{4,6},{5,7},{6,4},{7,5},{8,10},{9,11},{10,... | collective-permute-start | bytes 2359304 | tf_op jit(solution)/shard_map/ppermute | solution.py:923
  219.4 29.9 %collective-permute-start.50 = (bf16[2,576,384]{2,1,0:T(8,128)(2,1)}, bf16[2,576,384]{2,1,0:T(8,128)(2,1)}, u32[]{:S(2)}, u32[]{:S(2)}) collective-permute-start(bf16[2,576,384]{2,1,0:T(8,128)(2,1)} %collective-permute-done.39.refs_5_), channel_id=1, source_target_pairs={{0,1},{1,0},{2,3},{3,2},{4,5},{5,4},{6,7},{7,6},{8,9},{9,8},{10,11... | collective-permute-start | bytes 2654216 | tf_op jit(solution)/shard_map/ppermute | solution.py:926
  252.6 34.3 %collective-permute-start.56 = (bf16[544,768]{1,0:T(8,128)(2,1)}, bf16[544,768]{1,0:T(8,128)(2,1)}, u32[]{:S(2)}, u32[]{:S(2)}) collective-permute-start(bf16[544,768]{1,0:T(8,128)(2,1)} %add_convert_fusion.7), channel_id=1, source_target_pairs={{0,8},{4,12},{8,16},{12,20},{16,24},{20,28},{24,0},{28,4},{1,9},{5... | collective-permute-start | bytes 2506760 | tf_op jit(solution)/shard_map/ppermute | solution.py:917
  256.4 30.5 %collective-permute-start.58 = (bf16[512,384]{1,0:T(8,128)(2,1)}, bf16[512,384]{1,0:T(8,128)(2,1)}, u32[]{:S(2)}, u32[]{:S(2)}) collective-permute-start(bf16[512,384]{1,0:T(8,128)(2,1)} %get-tuple-element.652), channel_id=1, source_target_pairs={{0,4},{4,0},{8,12},{12,8},{16,20},{20,16},{24,28},{28,24},{1,5},{5... | collective-permute-start | bytes 1179656 | tf_op jit(solution)/shard_map/ppermute | solution.py:920
  260.4 26.6 %collective-permute-start.55 = (bf16[544,768]{1,0:T(8,128)(2,1)}, bf16[544,768]{1,0:T(8,128)(2,1)}, u32[]{:S(2)}, u32[]{:S(2)}) collective-permute-start(bf16[544,768]{1,0:T(8,128)(2,1)} %get-tuple-element.658), channel_id=1, source_target_pairs={{0,4},{4,0},{8,12},{12,8},{16,20},{20,16},{24,28},{28,24},{1,5},{5... | collective-permute-start | bytes 2506760 | tf_op jit(solution)/shard_map/ppermute | solution.py:920
  262.1 24.8 %collective-permute-start.57 = (bf16[2,512,384]{2,1,0:T(8,128)(2,1)}, bf16[2,512,384]{2,1,0:T(8,128)(2,1)}, u32[]{:S(2)}, u32[]{:S(2)}) collective-permute-start(bf16[2,512,384]{2,1,0:T(8,128)(2,1)} %add_convert_fusion.15), channel_id=1, source_target_pairs={{0,2},{1,3},{2,0},{3,1},{4,6},{5,7},{6,4},{7,5},{8,10},{9,11},{10,... | collective-permute-start | bytes 2359304 | tf_op jit(solution)/shard_map/ppermute | solution.py:923
  287.5 30.1 %collective-permute-start.63 = (bf16[2,544,768]{2,1,0:T(8,128)(2,1)}, bf16[2,544,768]{2,1,0:T(8,128)(2,1)S(1)}, u32[]{:S(2)}, u32[]{:S(2)}) collective-permute-start(bf16[2,544,768]{2,1,0:T(8,128)(2,1)} %get-tuple-element.459), channel_id=1, source_target_pairs={{0,1},{1,0},{2,3},{3,2},{4,5},{5,4},{6,7},{7,6},{8,9},{9,8},{10,11... | collective-permute-start | bytes 5013512 | tf_op jit(solution)/shard_map/ppermute | solution.py:926
  293.0 27.8 %collective-permute-start.65 = (bf16[2,512,768]{2,1,0:T(8,128)(2,1)}, bf16[2,512,768]{2,1,0:T(8,128)(2,1)S(1)}, u32[]{:S(2)}, u32[]{:S(2)}) collective-permute-start(bf16[2,512,768]{2,1,0:T(8,128)(2,1)} %get-tuple-element.463), channel_id=1, source_target_pairs={{0,1},{1,0},{2,3},{3,2},{4,5},{5,4},{6,7},{7,6},{8,9},{9,8},{10,11... | collective-permute-start | bytes 4718600 | tf_op jit(solution)/shard_map/ppermute | solution.py:926
  295.2 23.0 %collective-permute-start.62 = (bf16[544,768]{1,0:T(8,128)(2,1)S(1)}, bf16[544,768]{1,0:T(8,128)(2,1)S(1)}, u32[]{:S(2)}, u32[]{:S(2)}) collective-permute-start(bf16[544,768]{1,0:T(8,128)(2,1)S(1)} %add_convert_fusion.4), channel_id=1, source_target_pairs={{0,8},{4,12},{8,16},{12,20},{16,24},{20,28},{24,0},{28,4},{1,9},{5... | collective-permute-start | bytes 2506760 | tf_op jit(solution)/shard_map/ppermute | solution.py:917
  297.8 23.0 %collective-permute-start.61 = (bf16[544,768]{1,0:T(8,128)(2,1)S(1)}, bf16[544,768]{1,0:T(8,128)(2,1)S(1)}, u32[]{:S(2)}, u32[]{:S(2)}) collective-permute-start(bf16[544,768]{1,0:T(8,128)(2,1)S(1)} %get-tuple-element.656), channel_id=1, source_target_pairs={{0,4},{4,0},{8,12},{12,8},{16,20},{20,16},{24,28},{28,24},{1,5},{5... | collective-permute-start | bytes 2506760 | tf_op jit(solution)/shard_map/ppermute | solution.py:920
  301.2 19.6 %collective-permute-start.64 = (bf16[2,512,384]{2,1,0:T(8,128)(2,1)}, bf16[2,512,384]{2,1,0:T(8,128)(2,1)}, u32[]{:S(2)}, u32[]{:S(2)}) collective-permute-start(bf16[2,512,384]{2,1,0:T(8,128)(2,1)} %add_convert_fusion.14), channel_id=1, source_target_pairs={{0,2},{1,3},{2,0},{3,1},{4,6},{5,7},{6,4},{7,5},{8,10},{9,11},{10,... | collective-permute-start | bytes 2359304 | tf_op jit(solution)/shard_map/ppermute | solution.py:923
  322.1 22.1 %collective-permute-start.66 = (bf16[544,768]{1,0:T(8,128)(2,1)S(1)}, bf16[544,768]{1,0:T(8,128)(2,1)S(1)}, u32[]{:S(2)}, u32[]{:S(2)}) collective-permute-start(bf16[544,768]{1,0:T(8,128)(2,1)S(1)} %get-tuple-element.654), channel_id=1, source_target_pairs={{0,4},{4,0},{8,12},{12,8},{16,20},{20,16},{24,28},{28,24},{1,5},{5... | collective-permute-start | bytes 2506760 | tf_op jit(solution)/shard_map/ppermute | solution.py:920
  323.3 21.4 %collective-permute-start.67 = (bf16[544,768]{1,0:T(8,128)(2,1)S(1)}, bf16[544,768]{1,0:T(8,128)(2,1)S(1)}, u32[]{:S(2)}, u32[]{:S(2)}) collective-permute-start(bf16[544,768]{1,0:T(8,128)(2,1)S(1)} %add_convert_fusion.1), channel_id=1, source_target_pairs={{0,8},{4,12},{8,16},{12,20},{16,24},{20,28},{24,0},{28,4},{1,9},{5... | collective-permute-start | bytes 2506760 | tf_op jit(solution)/shard_map/ppermute | solution.py:917
  326.2 18.0 %collective-permute-start.68 = (bf16[2,512,384]{2,1,0:T(8,128)(2,1)S(1)}, bf16[2,512,384]{2,1,0:T(8,128)(2,1)S(1)}, u32[]{:S(2)}, u32[]{:S(2)}) collective-permute-start(bf16[2,512,384]{2,1,0:T(8,128)(2,1)S(1)} %add_convert_fusion.13), channel_id=1, source_target_pairs={{0,2},{1,3},{2,0},{3,1},{4,6},{5,7},{6,4},{7,5},{8,10},{9,11},{10,... | collective-permute-start | bytes 2359304 | tf_op jit(solution)/shard_map/ppermute | solution.py:923
  345.4 20.3 %collective-permute-start.69 = (bf16[544,768]{1,0:T(8,128)(2,1)S(1)}, bf16[544,768]{1,0:T(8,128)(2,1)}, u32[]{:S(2)}, u32[]{:S(2)}) collective-permute-start(bf16[544,768]{1,0:T(8,128)(2,1)S(1)} %add_convert_fusion), channel_id=1, source_target_pairs={{0,2},{1,3},{2,0},{3,1},{4,6},{5,7},{6,4},{7,5},{8,10},{9,11},{10,... | collective-permute-start | bytes 2506760 | tf_op jit(solution)/shard_map/ppermute | solution.py:923
  348.3 12.1 %collective-permute-start.70 = (bf16[512,384]{1,0:T(8,128)(2,1)S(1)}, bf16[512,384]{1,0:T(8,128)(2,1)S(1)}, u32[]{:S(2)}, u32[]{:S(2)}) collective-permute-start(bf16[512,384]{1,0:T(8,128)(2,1)S(1)} %get-tuple-element.650), channel_id=1, source_target_pairs={{0,4},{4,0},{8,12},{12,8},{16,20},{20,16},{24,28},{28,24},{1,5},{5... | collective-permute-start | bytes 1179656 | tf_op jit(solution)/shard_map/ppermute | solution.py:920
  350.9 14.8 %collective-permute-start.71 = (bf16[512,384]{1,0:T(8,128)(2,1)S(1)}, bf16[512,384]{1,0:T(8,128)(2,1)S(1)}, u32[]{:S(2)}, u32[]{:S(2)}) collective-permute-start(bf16[512,384]{1,0:T(8,128)(2,1)S(1)} %get-tuple-element.648), channel_id=1, source_target_pairs={{0,4},{4,0},{8,12},{12,8},{16,20},{20,16},{24,28},{28,24},{1,5},{5... | collective-permute-start | bytes 1179656 | tf_op jit(solution)/shard_map/ppermute | solution.py:920
  370.6 13.0 %collective-permute-start.73 = (bf16[512,384]{1,0:T(8,128)(2,1)S(1)}, bf16[512,384]{1,0:T(8,128)(2,1)S(1)}, u32[]{:S(2)}, u32[]{:S(2)}) collective-permute-start(bf16[512,384]{1,0:T(8,128)(2,1)S(1)} %add_convert_fusion.22), channel_id=1, source_target_pairs={{0,8},{4,12},{8,16},{12,20},{16,24},{20,28},{24,0},{28,4},{1,9},{5... | collective-permute-start | bytes 1179656 | tf_op jit(solution)/shard_map/ppermute | solution.py:917
  383.6 14.5 %collective-permute-start.75 = (bf16[3,192,512]{2,1,0:T(8,128)(2,1)S(1)}, bf16[3,192,512]{2,1,0:T(8,128)(2,1)S(1)}, u32[]{:S(2)}, u32[]{:S(2)}) collective-permute-start(bf16[3,192,512]{2,1,0:T(8,128)(2,1)S(1)} %get-tuple-element.545), channel_id=1, source_target_pairs={{0,4},{4,0},{8,12},{12,8},{16,20},{20,16},{24,28},{28,24},{1,5},{5... | collective-permute-start | bytes 1769480 | tf_op jit(solution)/shard_map/ppermute | solution.py:920
  384.6 13.6 %collective-permute-start.76 = (bf16[512,384]{1,0:T(8,128)(2,1)S(1)}, bf16[512,384]{1,0:T(8,128)(2,1)S(1)}, u32[]{:S(2)}, u32[]{:S(2)}) collective-permute-start(bf16[512,384]{1,0:T(8,128)(2,1)S(1)} %add_convert_fusion.19), channel_id=1, source_target_pairs={{0,8},{4,12},{8,16},{12,20},{16,24},{20,28},{24,0},{28,4},{1,9},{5... | collective-permute-start | bytes 1179656 | tf_op jit(solution)/shard_map/ppermute | solution.py:917
  399.7 22.7 %collective-permute-start.83 = (bf16[512,384]{1,0:T(8,128)(2,1)S(1)}, bf16[512,384]{1,0:T(8,128)(2,1)S(1)}, u32[]{:S(2)}, u32[]{:S(2)}) collective-permute-start(bf16[512,384]{1,0:T(8,128)(2,1)S(1)} %add_convert_fusion.18), channel_id=1, source_target_pairs={{0,8},{4,12},{8,16},{12,20},{16,24},{20,28},{24,0},{28,4},{1,9},{5... | collective-permute-start | bytes 1179656 | tf_op jit(solution)/shard_map/ppermute | solution.py:917
  407.9 13.8 %collective-permute-start.79 = (bf16[2,208,640]{2,1,0:T(8,128)(2,1)S(1)}, bf16[2,208,640]{2,1,0:T(8,128)(2,1)S(1)}, u32[]{:S(2)}, u32[]{:S(2)}) collective-permute-start(bf16[2,208,640]{2,1,0:T(8,128)(2,1)S(1)} %get-tuple-element.559), channel_id=1, source_target_pairs={{0,4},{4,0},{8,12},{12,8},{16,20},{20,16},{24,28},{28,24},{1,5},{5... | collective-permute-start | bytes 1597448 | tf_op jit(solution)/shard_map/ppermute | solution.py:920
  408.8 14.8 %collective-permute-start.82 = (bf16[512,512]{1,0:T(8,128)(2,1)S(1)}, bf16[512,512]{1,0:T(8,128)(2,1)S(1)}, u32[]{:S(2)}, u32[]{:S(2)}) collective-permute-start(bf16[512,512]{1,0:T(8,128)(2,1)S(1)} %maximum_maximum_fusion), channel_id=1, source_target_pairs={{0,2},{1,3},{2,0},{3,1},{4,6},{5,7},{6,4},{7,5},{8,10},{9,11},{10,... | collective-permute-start | bytes 1572872 | tf_op jit(solution)/shard_map/ppermute | solution.py:923
  410.1 13.5 %collective-permute-start.80 = (bf16[208,640]{1,0:T(8,128)(2,1)S(1)}, bf16[208,640]{1,0:T(8,128)(2,1)S(1)}, u32[]{:S(2)}, u32[]{:S(2)}) collective-permute-start(bf16[208,640]{1,0:T(8,128)(2,1)S(1)} %add_convert_fusion.31), channel_id=1, source_target_pairs={{0,8},{4,12},{8,16},{12,20},{16,24},{20,28},{24,0},{28,4},{1,9},{5... | collective-permute-start | bytes 798728 | tf_op jit(solution)/shard_map/ppermute | solution.py:917
  410.5 13.2 %collective-permute-start.81 = (bf16[192,512]{1,0:T(8,128)(2,1)S(1)}, bf16[192,512]{1,0:T(8,128)(2,1)S(1)}, u32[]{:S(2)}, u32[]{:S(2)}) collective-permute-start(bf16[192,512]{1,0:T(8,128)(2,1)S(1)} %add_convert_fusion.34), channel_id=1, source_target_pairs={{0,8},{4,12},{8,16},{12,20},{16,24},{20,28},{24,0},{28,4},{1,9},{5... | collective-permute-start | bytes 589832 | tf_op jit(solution)/shard_map/ppermute | solution.py:917
  423.6 13.1 %collective-permute-start.84 = (bf16[1,208,640]{2,1,0:T(8,128)(2,1)S(1)}, bf16[1,208,640]{2,1,0:T(8,128)(2,1)S(1)}, u32[]{:S(2)}, u32[]{:S(2)}) collective-permute-start(bf16[1,208,640]{2,1,0:T(8,128)(2,1)S(1)} %get-tuple-element.569), channel_id=1, source_target_pairs={{0,4},{4,0},{8,12},{12,8},{16,20},{20,16},{24,28},{28,24},{1,5},{5... | collective-permute-start | bytes 798728 | tf_op jit(solution)/shard_map/ppermute | solution.py:920
  424.4 12.3 %collective-permute-start.85 = (bf16[208,640]{1,0:T(8,128)(2,1)S(1)}, bf16[208,640]{1,0:T(8,128)(2,1)S(1)}, u32[]{:S(2)}, u32[]{:S(2)}) collective-permute-start(bf16[208,640]{1,0:T(8,128)(2,1)S(1)} %add_convert_fusion.30), channel_id=1, source_target_pairs={{0,8},{4,12},{8,16},{12,20},{16,24},{20,28},{24,0},{28,4},{1,9},{5... | collective-permute-start | bytes 798728 | tf_op jit(solution)/shard_map/ppermute | solution.py:917
  424.6 12.2 %collective-permute-start.87 = (bf16[192,512]{1,0:T(8,128)(2,1)S(1)}, bf16[192,512]{1,0:T(8,128)(2,1)S(1)}, u32[]{:S(2)}, u32[]{:S(2)}) collective-permute-start(bf16[192,512]{1,0:T(8,128)(2,1)S(1)} %add_convert_fusion.33), channel_id=1, source_target_pairs={{0,8},{4,12},{8,16},{12,20},{16,24},{20,28},{24,0},{28,4},{1,9},{5... | collective-permute-start | bytes 589832 | tf_op jit(solution)/shard_map/ppermute | solution.py:917
  (120 other events, 1243.4 us)

commit v4 on v3

--- a/solution.py
+++ b/solution.py
@@ -400,7 +400,7 @@
     smem = pl.BlockSpec(memory_space=pltpu.SMEM)
     vmem = pl.BlockSpec(memory_space=pltpu.VMEM)
     nbytes = bytes_of(list(ins[1:]) + list(outs))
-    need = nbytes + bytes_of(scratch) + (16 << 20)
+    need = nbytes + bytes_of(scratch) + (24 << 20)
     return pl.pallas_call(
         body,
         out_shape=[sds(o.shape, o.dtype) for o in outs],

time: 463 us -> 462 us (level)
    unnamed x188 -> x192, local copies, waits for them, and re-layouts: 20.4 us -> 19.7 us
  transfers between devices with their start and end apart: 92 -> 92, of which waited for: 32 -> 32; matrix products, arithmetic and copies ran while one was open for 9% -> 9% of each run, Pallas kernels for 34% -> 35%
where the time goes in v4:
time: 462 us; the launch traced here: 455 us
  waiting for transfers between devices  164 us (35%)
  Pallas kernels  160 us (35%)
  starting transfers between devices  63.7 us (14%)
  other arithmetic  40.6 us (9%)
  local copies, waits for them, and re-layouts  24.7 us (5%)
    pallas_call x4, Pallas kernels, experts_call(): pl.pallas_call(functools.partial(experts_body, local), out_shape=outs, in...  102 us
    ppermute x21, waiting for transfers between devices, shift_z(): lax.ppermute(v, 'dp', [(i, (i // 2 + 1) % nz * 2 + i % 2) for i in range(...  70.3 us
    ppermute x25, waiting for transfers between devices, swap_y(): return lax.ppermute(v, 'dp', [(i, i ^ 1) for i in range(n_dp)])  47.9 us
    pallas_call x8, Pallas kernels, kernel_call(): pl.pallas_call(body, out_shape=[sds(o.shape, o.dtype) for o in outs], in_...  37.5 us
    ppermute x25, starting transfers between devices, swap_y(): return lax.ppermute(v, 'dp', [(i, i ^ 1) for i in range(n_dp)])  26.3 us
    ppermute x16, waiting for transfers between devices, swap_x(): return lax.ppermute(v, 'tensor', [(i, i ^ 2) for i in range(4)])  25 us
    pallas_call x4, Pallas kernels, run(): pl.pallas_call(with_earlier, grid=(each,), out_shape=[sds((local, width,...  20.9 us
    ppermute x30, waiting for transfers between devices, swap_c(): return lax.ppermute(v, 'tensor', [(i, i ^ 1) for i in range(4)])  20.6 us
  transfers between devices with their start and end apart: 92, of which 32 were waited for; matrix products, arithmetic and copies ran while one was open for 9% of the time, Pallas kernels for 35%

profile of v4, /device:TPU:0, one launch (start us, length us, event | category | flops | bytes accessed | tf_op | source)
XLA Modules:
  0.0 455.3 jit_solution(10918846351635014979)
XLA Ops:
  4.4 3.1 collective-permute-start
  7.4 1.5 collective-permute-start.1
  11.4 1.8 slots.1.pos_ref
  14.4 5.2 %collective-permute-done.refs_1_ = bf16[192,1152]{1,0:T(8,128)(2,1)S(1)} collective-permute-done((bf16[192,1152]{1,0:T(8,128)(2,1)S(1)}, bf16[192,1152]{1,0:T(8,128)(2,1)S(1)}, u32[]{:S(2)}, u32[]{:S(2)}) %collective-permute-start) | collective-permute-done | bytes 442400 | tf_op jit(solution)/shard_map/ppermute | solution.py:917
  20.6 1.5 collective-permute-start.3
  22.2 1.6 collective-permute-start.7
  23.8 9.0 %collective-permute-done.2.refs_2_ = bf16[192,1152]{1,0:T(8,128)(2,1)S(1)} collective-permute-done((bf16[192,1152]{1,0:T(8,128)(2,1)S(1)}, bf16[192,1152]{1,0:T(8,128)(2,1)S(1)}, u32[]{:S(2)}, u32[]{:S(2)}) %collective-permute-start.2) | collective-permute-done | bytes 442400 | tf_op jit(solution)/shard_map/ppermute | solution.py:917
  34.2 1.6 collective-permute-start.9
  35.8 9.2 %collective-permute-done.4.refs_3_ = bf16[192,1152]{1,0:T(8,128)(2,1)S(1)} collective-permute-done((bf16[192,1152]{1,0:T(8,128)(2,1)S(1)}, bf16[192,1152]{1,0:T(8,128)(2,1)S(1)}, u32[]{:S(2)}, u32[]{:S(2)}) %collective-permute-start.4) | collective-permute-done | bytes 442400 | tf_op jit(solution)/shard_map/ppermute | solution.py:917
  46.2 1.6 collective-permute-start.10
  47.7 3.4 pad_maximum_fusion.refs_8_
  51.1 3.4 collective-permute-done.6.refs_7_
  55.4 8.3 %attend.1 = (bf16[512,384]{1,0:T(8,128)(2,1)}, bf16[512,384]{1,0:T(8,128)(2,1)S(1)}, bf16[512,128]{1,0:T(8,128)(2,1)S(1)}, bf16[512,128]{1,0:T(8,128)(2,1)S(1)},...) custom-call(s32[5]{0:T(128)S(1)} %stack.104.idx, ...), custom_call_target="tpu_custom_call" | custom-call | flops 4000000000 | bytes 12587008 | tf_op jit(solution)/shard_map/attend/pallas_call | solution.py:404
  66.4 1.6 collective-permute-start.16
  68.6 10.8 %collective-permute-done.12.o1 = bf16[512,384]{1,0:T(8,128)(2,1)S(1)} collective-permute-done((bf16[512,384]{1,0:T(8,128)(2,1)}, bf16[512,384]{1,0:T(8,128)(2,1)S(1)}, u32[]{:S(2)}, u32[]{:S(2)}) %collective-permute-start.12) | collective-permute-done | bytes 393248 | tf_op jit(solution)/shard_map/ppermute | solution.py:923
  82.9 1.5 collective-permute-start.18
  88.7 6.7 %out.1 = (f32[512,1536]{1,0:T(8,128)S(1)}, bf16[512,1536]{1,0:T(8,128)(2,1)S(1)}, bf16[512,768]{1,0:T(8,128)(2,1)}) custom-call(s32[5]{0:T(128)S(1)} %stack.104.idx, bf16[512,1536]{1,0:T(8,128)(2,1)S(1)} %copy-done.18, bf16[512,384]{1,0:T(8,128)(2,1)} %get-tuple-element.322.o0.o_ref, bf16[512,384]{1,0:T(8,128)(2,1)S(1)} %collective-permute-done.12.o1, ...), custom_call_target="tpu_custom_call" | custom-call | flops 5000000000 | bytes 13762560 | tf_op jit(solution)/shard_map/out/pallas_call | solution.py:404
  96.5 8.2 %collective-permute-done.19 = bf16[576,384]{1,0:T(8,128)(2,1)S(1)} collective-permute-done((bf16[576,384]{1,0:T(8,128)(2,1)}, bf16[576,384]{1,0:T(8,128)(2,1)S(1)}, u32[]{:S(2)}, u32[]{:S(2)}) %collective-permute-start.19) | collective-permute-done | bytes 442400 | tf_op jit(solution)/shard_map/ppermute | solution.py:920
  104.8 1.4 pad_maximum_fusion.2.refs_4_
  108.8 21.1 %collective-permute-done.23.refs_0_ = bf16[512,768]{1,0:T(8,128)(2,1)} collective-permute-done((bf16[512,768]{1,0:T(8,128)(2,1)}, bf16[512,768]{1,0:T(8,128)(2,1)}, u32[]{:S(2)}, u32[]{:S(2)}) %collective-permute-start.23) | collective-permute-done | bytes 786464 | tf_op jit(solution)/shard_map/ppermute | solution.py:917
  132.9 2.2 pad_maximum_fusion.4.refs_4_
  135.1 1.5 collective-permute-start.33
  137.2 32.7 %experts.4 = (bf16[2,544,768]{2,1,0:T(8,128)(2,1)}, bf16[2,544,768]{2,1,0:T(8,128)(2,1)}, bf16[2,512,768]{2,1,0:T(8,128)(2,1)}, bf16[2,512,768]{2,1,0:T(8,128)(2...) custom-call(s32[5]{0:T(128)} %copy-done.27, ...), custom_call_target="tpu_custom_call" | custom-call | flops 12582912000 | bytes 31457280 | tf_op jit(solution)/shard_map/experts/pallas_call | solution.py:681
  174.5 1.5 collective-permute-start.38
  178.3 23.1 %experts.5 = (bf16[2,544,768]{2,1,0:T(8,128)(2,1)}, bf16[2,544,768]{2,1,0:T(8,128)(2,1)}, bf16[2,512,768]{2,1,0:T(8,128)(2,1)}, bf16[2,512,768]{2,1,0:T(8,128)(2...) custom-call(s32[5]{0:T(128)} %copy-done.27, ...), custom_call_target="tpu_custom_call" | custom-call | flops 12582912000 | bytes 31457280 | tf_op jit(solution)/shard_map/experts/pallas_call | solution.py:681
  203.1 8.1 %collective-permute-done.44.refs_2_ = bf16[512,768]{1,0:T(8,128)(2,1)S(1)} collective-permute-done((bf16[512,768]{1,0:T(8,128)(2,1)}, bf16[512,768]{1,0:T(8,128)(2,1)S(1)}, u32[]{:S(2)}, u32[]{:S(2)}) %collective-permute-start.44) | collective-permute-done | bytes 786464 | tf_op jit(solution)/shard_map/ppermute | solution.py:926
  213.1 2.8 fusion.3
  219.4 22.9 %experts.6 = (bf16[2,544,768]{2,1,0:T(8,128)(2,1)}, bf16[2,544,768]{2,1,0:T(8,128)(2,1)}, bf16[2,512,768]{2,1,0:T(8,128)(2,1)}, bf16[2,512,768]{2,1,0:T(8,128)(2...) custom-call(s32[5]{0:T(128)} %copy-done.27, ...), custom_call_target="tpu_custom_call" | custom-call | flops 12582912000 | bytes 31457280 | tf_op jit(solution)/shard_map/experts/pallas_call | solution.py:681
  242.4 6.9 %collective-permute-done.47 = bf16[544,768]{1,0:T(8,128)(2,1)} collective-permute-done((bf16[544,768]{1,0:T(8,128)(2,1)}, bf16[544,768]{1,0:T(8,128)(2,1)}, u32[]{:S(2)}, u32[]{:S(2)}) %collective-permute-start.47) | collective-permute-done | bytes 835616 | tf_op jit(solution)/shard_map/ppermute | solution.py:920
  250.3 2.3 add_convert_fusion.7
  252.9 2.7 fusion.17
  255.6 1.9 collective-permute-done.52.refs_2_
  259.2 1.7 fusion.5
  264.0 23.1 %experts.7 = (bf16[2,544,768]{2,1,0:T(8,128)(2,1)}, bf16[2,544,768]{2,1,0:T(8,128)(2,1)}, bf16[2,512,768]{2,1,0:T(8,128)(2,1)}, bf16[2,512,768]{2,1,0:T(8,128)(2...) custom-call(s32[5]{0:T(128)} %copy-done.27, ...), custom_call_target="tpu_custom_call" | custom-call | flops 12582912000 | bytes 31457280 | tf_op jit(solution)/shard_map/experts/pallas_call | solution.py:681
  288.3 5.5 %collective-permute-done.60 = bf16[2,512,768]{2,1,0:T(8,128)(2,1)S(1)} collective-permute-done((bf16[2,512,768]{2,1,0:T(8,128)(2,1)}, bf16[2,512,768]{2,1,0:T(8,128)(2,1)S(1)}, u32[]{:S(2)}, u32[]{:S(2)}) %collective-permute-start.60) | collective-permute-done | bytes 1572896 | tf_op jit(solution)/shard_map/ppermute | solution.py:926
  293.9 2.1 add_convert_fusion.4
  296.7 1.9 fusion.7
  299.8 2.2 add_convert_fusion.14
  303.0 2.1 copy-done.2
  305.1 2.1 copy-done.3
  308.2 5.2 %expert_grads.4 = (f32[8,1536,128]{2,1,0:T(8,128)}, f32[8,1536,128]{2,1,0:T(8,128)}, f32[8,128,1536]{2,1,0:T(8,128)}) custom-call(bf16[8,2,80,1536]{3,2,1,0:T(8,128)(2,1)S(1)} %copy-done, bf16[8,2,80,1536]{3,2,1,0:T(8,128)(2,1)S(1)} %copy-done.1, bf16[8,2,80,1536]{3,2,1,0:T(8,128)(2,1)S(1)} %copy-done.2, bf16[8,2,80,1536]{3,2,1,0:T(8,128)(2,1)S(1)} %copy-done.3, ...), custom_call_target="tpu_custom_call" | custom-call | flops 1509949440 | bytes 12582912 | tf_op jit(solution)/shard_map/expert_grads/pallas_call | solution.py:872
  313.3 5.3 %expert_grads.5 = (f32[8,1536,128]{2,1,0:T(8,128)}, f32[8,1536,128]{2,1,0:T(8,128)}, f32[8,128,1536]{2,1,0:T(8,128)}) custom-call(bf16[8,2,80,1536]{3,2,1,0:T(8,128)(2,1)S(1)} %copy-done, bf16[8,2,80,1536]{3,2,1,0:T(8,128)(2,1)S(1)} %copy-done.1, ...), custom_call_target="tpu_custom_call", output_to_operand_aliasing={{0}: (16, {}), {1}: (17, {}), {2}: (18, {})} | custom-call | flops 1509949440 | bytes 12582912 | tf_op jit(solution)/shard_map/expert_grads/pallas_call | solution.py:872
  319.1 2.5 collective-permute-done.64
  324.2 1.9 collective-permute-start.67
  327.4 5.2 %expert_grads.6 = (f32[8,1536,128]{2,1,0:T(8,128)}, f32[8,1536,128]{2,1,0:T(8,128)}, f32[8,128,1536]{2,1,0:T(8,128)}) custom-call(bf16[8,2,80,1536]{3,2,1,0:T(8,128)(2,1)S(1)} %copy-done, bf16[8,2,80,1536]{3,2,1,0:T(8,128)(2,1)S(1)} %copy-done.1, ...), custom_call_target="tpu_custom_call", output_to_operand_aliasing={{0}: (16, {}), {1}: (17, {}), {2}: (18, {})} | custom-call | flops 1509949440 | bytes 12582912 | tf_op jit(solution)/shard_map/expert_grads/pallas_call | solution.py:872
  332.6 11.7 %collective-permute-done.68 = bf16[2,512,384]{2,1,0:T(8,128)(2,1)S(1)} collective-permute-done((bf16[2,512,384]{2,1,0:T(8,128)(2,1)S(1)}, bf16[2,512,384]{2,1,0:T(8,128)(2,1)S(1)}, u32[]{:S(2)}, u32[]{:S(2)}) %collective-permute-start.68) | collective-permute-done | bytes 786464 | tf_op jit(solution)/shard_map/ppermute | solution.py:923
  347.5 1.4 fusion.19
  349.9 1.4 fusion.21
  352.5 5.2 %expert_grads.7 = (f32[8,1536,128]{2,1,0:T(8,128)}, f32[8,1536,128]{2,1,0:T(8,128)}, f32[8,128,1536]{2,1,0:T(8,128)}) custom-call(bf16[8,2,80,1536]{3,2,1,0:T(8,128)(2,1)S(1)} %copy-done, bf16[8,2,80,1536]{3,2,1,0:T(8,128)(2,1)S(1)} %copy-done.1, ...), custom_call_target="tpu_custom_call", output_to_operand_aliasing={{0}: (16, {}), {1}: (17, {}), {2}: (18, {})} | custom-call | flops 1509949440 | bytes 12582912 | tf_op jit(solution)/shard_map/expert_grads/pallas_call | solution.py:872
  357.7 3.3 collective-permute-done.70
  361.0 5.5 %collective-permute-done.71 = bf16[512,384]{1,0:T(8,128)(2,1)S(1)} collective-permute-done((bf16[512,384]{1,0:T(8,128)(2,1)S(1)}, bf16[512,384]{1,0:T(8,128)(2,1)S(1)}, u32[]{:S(2)}, u32[]{:S(2)}) %collective-permute-start.71) | collective-permute-done | bytes 393248 | tf_op jit(solution)/shard_map/ppermute | solution.py:920
  367.4 2.3 collective-permute-done.72.fn_ref
  369.9 1.5 collective-permute-start.73
  372.8 7.5 %hidden_back.1 = (f32[512,384]{1,0:T(8,128)S(1)}, bf16[512,384]{1,0:T(8,128)(2,1)S(1)}, bf16[192,512]{1,0:T(8,128)(2,1)S(1)}, bf16[192,512]{1,0:T(8,128)(2,1)S(1...) custom-call(s32[5]{0:T(128)S(1)} %copy-done.28, ...), custom_call_target="tpu_custom_call" | custom-call | flops 3000000000 | bytes 13926400 | tf_op jit(solution)/shard_map/hidden_back/pallas_call | solution.py:404
  380.3 2.5 collective-permute-done.73
  385.0 10.4 %attend_back.1 = (bf16[512,896]{1,0:T(8,128)(2,1)S(1)}, bf16[512,896]{1,0:T(8,128)(2,1)S(1)}, bf16[208,640]{1,0:T(8,128)(2,1)S(1)}, bf16[208,640]{1,0:T(8,128)(2...) custom-call(s32[5]{0:T(128)S(1)} %copy-done.28, ...), custom_call_target="tpu_custom_call" | custom-call | flops 5000000000 | bytes 13008896 | tf_op jit(solution)/shard_map/attend_back/pallas_call | solution.py:404
  395.4 2.0 collective-permute-done.75
  399.6 7.2 %collective-permute-done.77 = bf16[1,208,640]{2,1,0:T(8,128)(2,1)S(1)} collective-permute-done((bf16[1,208,640]{2,1,0:T(8,128)(2,1)S(1)}, bf16[1,208,640]{2,1,0:T(8,128)(2,1)S(1)}, u32[]{:S(2)}, u32[]{:S(2)}) %collective-permute-start.77) | collective-permute-done | bytes 266272 | tf_op jit(solution)/shard_map/ppermute | solution.py:920
  408.3 1.7 collective-permute-start.82
  411.1 10.0 %collective-permute-done.79 = bf16[2,208,640]{2,1,0:T(8,128)(2,1)S(1)} collective-permute-done((bf16[2,208,640]{2,1,0:T(8,128)(2,1)S(1)}, bf16[2,208,640]{2,1,0:T(8,128)(2,1)S(1)}, u32[]{:S(2)}, u32[]{:S(2)}) %collective-permute-start.79) | collective-permute-done | bytes 532512 | tf_op jit(solution)/shard_map/ppermute | solution.py:920
  421.9 1.6 collective-permute-done.81
  426.0 2.1 add_convert_fusion.17
  428.8 7.8 %collective-permute-done.87 = bf16[192,512]{1,0:T(8,128)(2,1)S(1)} collective-permute-done((bf16[192,512]{1,0:T(8,128)(2,1)S(1)}, bf16[192,512]{1,0:T(8,128)(2,1)S(1)}, u32[]{:S(2)}, u32[]{:S(2)}) %collective-permute-start.87) | collective-permute-done | bytes 196640 | tf_op jit(solution)/shard_map/ppermute | solution.py:917
  437.0 11.2 %collective-permute-done.89.ring = bf16[192,512]{1,0:T(8,128)(2,1)S(1)} collective-permute-done((bf16[192,512]{1,0:T(8,128)(2,1)S(1)}, bf16[192,512]{1,0:T(8,128)(2,1)S(1)}, u32[]{:S(2)}, u32[]{:S(2)}) %collective-permute-start.89) | collective-permute-done | bytes 196640 | tf_op jit(solution)/shard_map/ppermute | solution.py:917
  (408 shorter events, 85.0 us)
Async XLA Ops:
  4.4 15.3 %collective-permute-start = (bf16[192,1152]{1,0:T(8,128)(2,1)S(1)}, bf16[192,1152]{1,0:T(8,128)(2,1)S(1)}, u32[]{:S(2)}, u32[]{:S(2)}) collective-permute-start(bf16[192,1152]{1,0:T(8,128)(2,1)S(1)} %concatenate.21.refs_0_), channel_id=1, source_target_pairs={{0,8},{4,12},{8,16},{12,20},{16,24},{20,28},{24,0},{28,4},{1,9},{5... | collective-permute-start | bytes 1327112 | tf_op jit(solution)/shard_map/ppermute | solution.py:917
  7.4 12.2 %collective-permute-start.1 = (bf16[192,1152]{1,0:T(8,128)(2,1)S(1)}, bf16[192,1152]{1,0:T(8,128)(2,1)S(1)}, u32[]{:S(2)}, u32[]{:S(2)}) collective-permute-start(bf16[192,1152]{1,0:T(8,128)(2,1)S(1)} %concatenate.21.refs_0_), channel_id=1, source_target_pairs={{0,4},{4,0},{8,12},{12,8},{16,20},{20,16},{24,28},{28,24},{1,5},{5... | collective-permute-start | bytes 1327112 | tf_op jit(solution)/shard_map/ppermute | solution.py:920
  19.6 13.2 %collective-permute-start.2 = (bf16[192,1152]{1,0:T(8,128)(2,1)S(1)}, bf16[192,1152]{1,0:T(8,128)(2,1)S(1)}, u32[]{:S(2)}, u32[]{:S(2)}) collective-permute-start(bf16[192,1152]{1,0:T(8,128)(2,1)S(1)} %collective-permute-done.refs_1_), channel_id=1, source_target_pairs={{0,8},{4,12},{8,16},{12,20},{16,24},{20,28},{24,0},{28,4},{1,9},{5... | collective-permute-start | bytes 1327112 | tf_op jit(solution)/shard_map/ppermute | solution.py:917
  20.6 12.1 %collective-permute-start.3 = (bf16[192,1152]{1,0:T(8,128)(2,1)S(1)}, bf16[192,1152]{1,0:T(8,128)(2,1)S(1)}, u32[]{:S(2)}, u32[]{:S(2)}) collective-permute-start(bf16[192,1152]{1,0:T(8,128)(2,1)S(1)} %collective-permute-done.refs_1_), channel_id=1, source_target_pairs={{0,4},{4,0},{8,12},{12,8},{16,20},{20,16},{24,28},{28,24},{1,5},{5... | collective-permute-start | bytes 1327112 | tf_op jit(solution)/shard_map/ppermute | solution.py:920
  22.2 28.9 %collective-permute-start.7 = (bf16[2,192,384]{2,1,0:T(8,128)(2,1)S(1)}, bf16[2,192,384]{2,1,0:T(8,128)(2,1)S(1)}, u32[]{:S(2)}, u32[]{:S(2)}) collective-permute-start(bf16[2,192,384]{2,1,0:T(8,128)(2,1)S(1)} %pad_maximum_fusion.8), channel_id=1, source_target_pairs={{0,2},{1,3},{2,0},{3,1},{4,6},{5,7},{6,4},{7,5},{8,10},{9,11},{10,... | collective-permute-start | bytes 884744 | tf_op jit(solution)/shard_map/ppermute | solution.py:923
  32.8 12.2 %collective-permute-start.4 = (bf16[192,1152]{1,0:T(8,128)(2,1)S(1)}, bf16[192,1152]{1,0:T(8,128)(2,1)S(1)}, u32[]{:S(2)}, u32[]{:S(2)}) collective-permute-start(bf16[192,1152]{1,0:T(8,128)(2,1)S(1)} %collective-permute-done.2.refs_2_), channel_id=1, source_target_pairs={{0,8},{4,12},{8,16},{12,20},{16,24},{20,28},{24,0},{28,4},{1,9},{5... | collective-permute-start | bytes 1327112 | tf_op jit(solution)/shard_map/ppermute | solution.py:917
  32.8 12.2 %collective-permute-start.5 = (bf16[192,1152]{1,0:T(8,128)(2,1)S(1)}, bf16[192,1152]{1,0:T(8,128)(2,1)S(1)}, u32[]{:S(2)}, u32[]{:S(2)}) collective-permute-start(bf16[192,1152]{1,0:T(8,128)(2,1)S(1)} %collective-permute-done.2.refs_2_), channel_id=1, source_target_pairs={{0,4},{4,0},{8,12},{12,8},{16,20},{20,16},{24,28},{28,24},{1,5},{5... | collective-permute-start | bytes 1327112 | tf_op jit(solution)/shard_map/ppermute | solution.py:920
  34.2 29.5 %collective-permute-start.9 = (bf16[2,192,384]{2,1,0:T(8,128)(2,1)S(1)}, bf16[2,192,384]{2,1,0:T(8,128)(2,1)S(1)}, u32[]{:S(2)}, u32[]{:S(2)}) collective-permute-start(bf16[2,192,384]{2,1,0:T(8,128)(2,1)S(1)} %pad_maximum_fusion.9), channel_id=1, source_target_pairs={{0,2},{1,3},{2,0},{3,1},{4,6},{5,7},{6,4},{7,5},{8,10},{9,11},{10,... | collective-permute-start | bytes 884744 | tf_op jit(solution)/shard_map/ppermute | solution.py:923
  46.1 17.7 %collective-permute-start.8 = (bf16[576,384]{1,0:T(8,128)(2,1)}, bf16[576,384]{1,0:T(8,128)(2,1)}, u32[]{:S(2)}, u32[]{:S(2)}) collective-permute-start(bf16[576,384]{1,0:T(8,128)(2,1)} %get-tuple-element.328), channel_id=1, source_target_pairs={{0,8},{4,12},{8,16},{12,20},{16,24},{20,28},{24,0},{28,4},{1,9},{5... | collective-permute-start | bytes 1327112 | tf_op jit(solution)/shard_map/ppermute | solution.py:917
  46.2 17.6 %collective-permute-start.10 = (bf16[2,192,384]{2,1,0:T(8,128)(2,1)S(1)}, bf16[2,192,384]{2,1,0:T(8,128)(2,1)S(1)}, u32[]{:S(2)}, u32[]{:S(2)}) collective-permute-start(bf16[2,192,384]{2,1,0:T(8,128)(2,1)S(1)} %pad_maximum_fusion.10), channel_id=1, source_target_pairs={{0,2},{1,3},{2,0},{3,1},{4,6},{5,7},{6,4},{7,5},{8,10},{9,11},{10,... | collective-permute-start | bytes 884744 | tf_op jit(solution)/shard_map/ppermute | solution.py:923
  66.4 14.7 %collective-permute-start.14 = (bf16[2,1536,384]{2,1,0:T(8,128)(2,1)S(1)}, bf16[2,1536,384]{2,1,0:T(8,128)(2,1)}, u32[]{:S(2)}, u32[]{:S(2)}) collective-permute-start(bf16[2,1536,384]{2,1,0:T(8,128)(2,1)S(1)} %place.1.w01.w_ref), channel_id=1, source_target_pairs={{0,1},{1,0},{2,3},{3,2},{4,5},{5,4},{6,7},{7,6},{8,9},{9,8},{10,11... | collective-permute-start | bytes 7077896 | tf_op jit(solution)/shard_map/ppermute | solution.py:926
  66.4 14.7 %collective-permute-start.15 = (bf16[576,384]{1,0:T(8,128)(2,1)}, bf16[576,384]{1,0:T(8,128)(2,1)}, u32[]{:S(2)}, u32[]{:S(2)}) collective-permute-start(bf16[576,384]{1,0:T(8,128)(2,1)} %collective-permute-done.8), channel_id=1, source_target_pairs={{0,8},{4,12},{8,16},{12,20},{16,24},{20,28},{24,0},{28,4},{1,9},{5... | collective-permute-start | bytes 1327112 | tf_op jit(solution)/shard_map/ppermute | solution.py:917
  66.4 14.7 %collective-permute-start.16 = (bf16[576,384]{1,0:T(8,128)(2,1)}, bf16[576,384]{1,0:T(8,128)(2,1)}, u32[]{:S(2)}, u32[]{:S(2)}) collective-permute-start(bf16[576,384]{1,0:T(8,128)(2,1)} %get-tuple-element.328), channel_id=1, source_target_pairs={{0,4},{4,0},{8,12},{12,8},{16,20},{20,16},{24,28},{28,24},{1,5},{5... | collective-permute-start | bytes 1327112 | tf_op jit(solution)/shard_map/ppermute | solution.py:920
  82.3 22.4 %collective-permute-start.22 = (bf16[2,576,384]{2,1,0:T(8,128)(2,1)S(1)}, bf16[2,576,384]{2,1,0:T(8,128)(2,1)S(1)}, u32[]{:S(2)}, u32[]{:S(2)}) collective-permute-start(bf16[2,576,384]{2,1,0:T(8,128)(2,1)S(1)} %pad_maximum_fusion.1.refs_4_), channel_id=1, source_target_pairs={{0,1},{1,0},{2,3},{3,2},{4,5},{5,4},{6,7},{7,6},{8,9},{9,8},{10,11... | collective-permute-start | bytes 2654216 | tf_op jit(solution)/shard_map/ppermute | solution.py:926
  82.9 13.6 %collective-permute-start.18 = (bf16[576,384]{1,0:T(8,128)(2,1)}, bf16[576,384]{1,0:T(8,128)(2,1)S(1)}, u32[]{:S(2)}, u32[]{:S(2)}) collective-permute-start(bf16[576,384]{1,0:T(8,128)(2,1)} %collective-permute-done.8), channel_id=1, source_target_pairs={{0,4},{4,0},{8,12},{12,8},{16,20},{20,16},{24,28},{28,24},{1,5},{5... | collective-permute-start | bytes 1327112 | tf_op jit(solution)/shard_map/ppermute | solution.py:920
  84.4 20.3 %collective-permute-start.19 = (bf16[576,384]{1,0:T(8,128)(2,1)}, bf16[576,384]{1,0:T(8,128)(2,1)S(1)}, u32[]{:S(2)}, u32[]{:S(2)}) collective-permute-start(bf16[576,384]{1,0:T(8,128)(2,1)} %collective-permute-done.15), channel_id=1, source_target_pairs={{0,4},{4,0},{8,12},{12,8},{16,20},{20,16},{24,28},{28,24},{1,5},{5... | collective-permute-start | bytes 1327112 | tf_op jit(solution)/shard_map/ppermute | solution.py:920
  85.0 19.8 %collective-permute-start.20 = (bf16[576,384]{1,0:T(8,128)(2,1)}, bf16[576,384]{1,0:T(8,128)(2,1)}, u32[]{:S(2)}, u32[]{:S(2)}) collective-permute-start(bf16[576,384]{1,0:T(8,128)(2,1)} %collective-permute-done.15), channel_id=1, source_target_pairs={{0,8},{4,12},{8,16},{12,20},{16,24},{20,28},{24,0},{28,4},{1,9},{5... | collective-permute-start | bytes 1327112 | tf_op jit(solution)/shard_map/ppermute | solution.py:917
  85.4 19.4 %collective-permute-start.21 = (bf16[576,384]{1,0:T(8,128)(2,1)}, bf16[576,384]{1,0:T(8,128)(2,1)S(1)}, u32[]{:S(2)}, u32[]{:S(2)}) collective-permute-start(bf16[576,384]{1,0:T(8,128)(2,1)} %collective-permute-done.16), channel_id=1, source_target_pairs={{0,2},{1,3},{2,0},{3,1},{4,6},{5,7},{6,4},{7,5},{8,10},{9,11},{10,... | collective-permute-start | bytes 1327112 | tf_op jit(solution)/shard_map/ppermute | solution.py:923
  106.2 23.6 %collective-permute-start.25 = (bf16[2,576,384]{2,1,0:T(8,128)(2,1)S(1)}, bf16[2,576,384]{2,1,0:T(8,128)(2,1)}, u32[]{:S(2)}, u32[]{:S(2)}) collective-permute-start(bf16[2,576,384]{2,1,0:T(8,128)(2,1)S(1)} %pad_maximum_fusion.2.refs_4_), channel_id=1, source_target_pairs={{0,2},{1,3},{2,0},{3,1},{4,6},{5,7},{6,4},{7,5},{8,10},{9,11},{10,... | collective-permute-start | bytes 2654216 | tf_op jit(solution)/shard_map/ppermute | solution.py:923
  107.7 22.2 %collective-permute-start.26 = (bf16[2,576,384]{2,1,0:T(8,128)(2,1)S(1)}, bf16[2,576,384]{2,1,0:T(8,128)(2,1)S(1)}, u32[]{:S(2)}, u32[]{:S(2)}) collective-permute-start(bf16[2,576,384]{2,1,0:T(8,128)(2,1)S(1)} %pad_maximum_fusion.3.refs_5_), channel_id=1, source_target_pairs={{0,1},{1,0},{2,3},{3,2},{4,5},{5,4},{6,7},{7,6},{8,9},{9,8},{10,11... | collective-permute-start | bytes 2654216 | tf_op jit(solution)/shard_map/ppermute | solution.py:926
  107.8 22.1 %collective-permute-start.23 = (bf16[512,768]{1,0:T(8,128)(2,1)}, bf16[512,768]{1,0:T(8,128)(2,1)}, u32[]{:S(2)}, u32[]{:S(2)}) collective-permute-start(bf16[512,768]{1,0:T(8,128)(2,1)} %get-tuple-element.336.refs_0_), channel_id=1, source_target_pairs={{0,8},{4,12},{8,16},{12,20},{16,24},{20,28},{24,0},{28,4},{1,9},{5... | collective-permute-start | bytes 2359304 | tf_op jit(solution)/shard_map/ppermute | solution.py:917
  107.9 22.0 %collective-permute-start.24 = (bf16[512,768]{1,0:T(8,128)(2,1)}, bf16[512,768]{1,0:T(8,128)(2,1)}, u32[]{:S(2)}, u32[]{:S(2)}) collective-permute-start(bf16[512,768]{1,0:T(8,128)(2,1)} %get-tuple-element.336.refs_0_), channel_id=1, source_target_pairs={{0,4},{4,0},{8,12},{12,8},{16,20},{20,16},{24,28},{28,24},{1,5},{5... | collective-permute-start | bytes 2359304 | tf_op jit(solution)/shard_map/ppermute | solution.py:920
  108.7 27.9 %collective-permute-start.31 = (bf16[2,576,384]{2,1,0:T(8,128)(2,1)S(1)}, bf16[2,576,384]{2,1,0:T(8,128)(2,1)S(1)}, u32[]{:S(2)}, u32[]{:S(2)}) collective-permute-start(bf16[2,576,384]{2,1,0:T(8,128)(2,1)S(1)} %pad_maximum_fusion.2.refs_4_), channel_id=1, source_target_pairs={{0,1},{1,0},{2,3},{3,2},{4,5},{5,4},{6,7},{7,6},{8,9},{9,8},{10,11... | collective-permute-start | bytes 2654216 | tf_op jit(solution)/shard_map/ppermute | solution.py:926
  132.1 37.7 %collective-permute-start.32 = (bf16[576,384]{1,0:T(8,128)(2,1)}, bf16[576,384]{1,0:T(8,128)(2,1)S(1)}, u32[]{:S(2)}, u32[]{:S(2)}) collective-permute-start(bf16[576,384]{1,0:T(8,128)(2,1)} %collective-permute-done.20), channel_id=1, source_target_pairs={{0,4},{4,0},{8,12},{12,8},{16,20},{20,16},{24,28},{28,24},{1,5},{5... | collective-permute-start | bytes 1327112 | tf_op jit(solution)/shard_map/ppermute | solution.py:920
  135.1 34.8 %collective-permute-start.33 = (bf16[2,576,384]{2,1,0:T(8,128)(2,1)}, bf16[2,576,384]{2,1,0:T(8,128)(2,1)}, u32[]{:S(2)}, u32[]{:S(2)}) collective-permute-start(bf16[2,576,384]{2,1,0:T(8,128)(2,1)} %pad_maximum_fusion.4.refs_4_), channel_id=1, source_target_pairs={{0,2},{1,3},{2,0},{3,1},{4,6},{5,7},{6,4},{7,5},{8,10},{9,11},{10,... | collective-permute-start | bytes 2654216 | tf_op jit(solution)/shard_map/ppermute | solution.py:923
  136.6 33.3 %collective-permute-start.27 = (bf16[512,768]{1,0:T(8,128)(2,1)}, bf16[512,768]{1,0:T(8,128)(2,1)}, u32[]{:S(2)}, u32[]{:S(2)}) collective-permute-start(bf16[512,768]{1,0:T(8,128)(2,1)} %collective-permute-done.23.refs_0_), channel_id=1, source_target_pairs={{0,8},{4,12},{8,16},{12,20},{16,24},{20,28},{24,0},{28,4},{1,9},{5... | collective-permute-start | bytes 2359304 | tf_op jit(solution)/shard_map/ppermute | solution.py:917
  136.6 33.3 %collective-permute-start.28 = (bf16[512,768]{1,0:T(8,128)(2,1)}, bf16[512,768]{1,0:T(8,128)(2,1)}, u32[]{:S(2)}, u32[]{:S(2)}) collective-permute-start(bf16[512,768]{1,0:T(8,128)(2,1)} %collective-permute-done.23.refs_0_), channel_id=1, source_target_pairs={{0,4},{4,0},{8,12},{12,8},{16,20},{20,16},{24,28},{28,24},{1,5},{5... | collective-permute-start | bytes 2359304 | tf_op jit(solution)/shard_map/ppermute | solution.py:920
  170.6 30.8 %collective-permute-start.41 = (bf16[2,576,384]{2,1,0:T(8,128)(2,1)}, bf16[2,576,384]{2,1,0:T(8,128)(2,1)}, u32[]{:S(2)}, u32[]{:S(2)}) collective-permute-start(bf16[2,576,384]{2,1,0:T(8,128)(2,1)} %pad_maximum_fusion.4.refs_4_), channel_id=1, source_target_pairs={{0,1},{1,0},{2,3},{3,2},{4,5},{5,4},{6,7},{7,6},{8,9},{9,8},{10,11... | collective-permute-start | bytes 2654216 | tf_op jit(solution)/shard_map/ppermute | solution.py:926
  171.0 30.4 %collective-permute-start.37 = (bf16[512,768]{1,0:T(8,128)(2,1)}, bf16[512,768]{1,0:T(8,128)(2,1)}, u32[]{:S(2)}, u32[]{:S(2)}) collective-permute-start(bf16[512,768]{1,0:T(8,128)(2,1)} %collective-permute-done.27.refs_0_), channel_id=1, source_target_pairs={{0,8},{4,12},{8,16},{12,20},{16,24},{20,28},{24,0},{28,4},{1,9},{5... | collective-permute-start | bytes 2359304 | tf_op jit(solution)/shard_map/ppermute | solution.py:917
  174.5 26.9 %collective-permute-start.38 = (bf16[512,768]{1,0:T(8,128)(2,1)}, bf16[512,768]{1,0:T(8,128)(2,1)S(1)}, u32[]{:S(2)}, u32[]{:S(2)}) collective-permute-start(bf16[512,768]{1,0:T(8,128)(2,1)} %collective-permute-done.27.refs_0_), channel_id=1, source_target_pairs={{0,4},{4,0},{8,12},{12,8},{16,20},{20,16},{24,28},{28,24},{1,5},{5... | collective-permute-start | bytes 2359304 | tf_op jit(solution)/shard_map/ppermute | solution.py:920
  177.0 24.4 %collective-permute-start.39 = (bf16[2,576,384]{2,1,0:T(8,128)(2,1)S(1)}, bf16[2,576,384]{2,1,0:T(8,128)(2,1)}, u32[]{:S(2)}, u32[]{:S(2)}) collective-permute-start(bf16[2,576,384]{2,1,0:T(8,128)(2,1)S(1)} %pad_maximum_fusion.5.refs_4_), channel_id=1, source_target_pairs={{0,2},{1,3},{2,0},{3,1},{4,6},{5,7},{6,4},{7,5},{8,10},{9,11},{10,... | collective-permute-start | bytes 2654216 | tf_op jit(solution)/shard_map/ppermute | solution.py:923
  178.3 23.1 %collective-permute-start.40 = (bf16[2,576,384]{2,1,0:T(8,128)(2,1)}, bf16[2,576,384]{2,1,0:T(8,128)(2,1)}, u32[]{:S(2)}, u32[]{:S(2)}) collective-permute-start(bf16[2,576,384]{2,1,0:T(8,128)(2,1)} %collective-permute-done.33.refs_5_), channel_id=1, source_target_pairs={{0,1},{1,0},{2,3},{3,2},{4,5},{5,4},{6,7},{7,6},{8,9},{9,8},{10,11... | collective-permute-start | bytes 2654216 | tf_op jit(solution)/shard_map/ppermute | solution.py:926
  201.5 11.6 %collective-permute-start.45 = (bf16[2,544,768]{2,1,0:T(8,128)(2,1)}, bf16[2,544,768]{2,1,0:T(8,128)(2,1)S(1)}, u32[]{:S(2)}, u32[]{:S(2)}) collective-permute-start(bf16[2,544,768]{2,1,0:T(8,128)(2,1)} %get-tuple-element.389), channel_id=1, source_target_pairs={{0,1},{1,0},{2,3},{3,2},{4,5},{5,4},{6,7},{7,6},{8,9},{9,8},{10,11... | collective-permute-start | bytes 5013512 | tf_op jit(solution)/shard_map/ppermute | solution.py:926
  202.7 39.7 %collective-permute-start.49 = (bf16[2,576,384]{2,1,0:T(8,128)(2,1)S(1)}, bf16[2,576,384]{2,1,0:T(8,128)(2,1)}, u32[]{:S(2)}, u32[]{:S(2)}) collective-permute-start(bf16[2,576,384]{2,1,0:T(8,128)(2,1)S(1)} %pad_maximum_fusion.5.refs_4_), channel_id=1, source_target_pairs={{0,1},{1,0},{2,3},{3,2},{4,5},{5,4},{6,7},{7,6},{8,9},{9,8},{10,11... | collective-permute-start | bytes 2654216 | tf_op jit(solution)/shard_map/ppermute | solution.py:926
  211.2 31.1 %collective-permute-start.42 = (bf16[512,768]{1,0:T(8,128)(2,1)}, bf16[512,768]{1,0:T(8,128)(2,1)}, u32[]{:S(2)}, u32[]{:S(2)}) collective-permute-start(bf16[512,768]{1,0:T(8,128)(2,1)} %collective-permute-done.37.refs_0_), channel_id=1, source_target_pairs={{0,4},{4,0},{8,12},{12,8},{16,20},{20,16},{24,28},{28,24},{1,5},{5... | collective-permute-start | bytes 2359304 | tf_op jit(solution)/shard_map/ppermute | solution.py:920
  215.9 33.3 %collective-permute-start.47 = (bf16[544,768]{1,0:T(8,128)(2,1)}, bf16[544,768]{1,0:T(8,128)(2,1)}, u32[]{:S(2)}, u32[]{:S(2)}) collective-permute-start(bf16[544,768]{1,0:T(8,128)(2,1)} %get-tuple-element.660), channel_id=1, source_target_pairs={{0,4},{4,0},{8,12},{12,8},{16,20},{20,16},{24,28},{28,24},{1,5},{5... | collective-permute-start | bytes 2506760 | tf_op jit(solution)/shard_map/ppermute | solution.py:920
  218.2 24.1 %collective-permute-start.48 = (bf16[2,512,384]{2,1,0:T(8,128)(2,1)}, bf16[2,512,384]{2,1,0:T(8,128)(2,1)}, u32[]{:S(2)}, u32[]{:S(2)}) collective-permute-start(bf16[2,512,384]{2,1,0:T(8,128)(2,1)} %add_convert_fusion.16), channel_id=1, source_target_pairs={{0,2},{1,3},{2,0},{3,1},{4,6},{5,7},{6,4},{7,5},{8,10},{9,11},{10,... | collective-permute-start | bytes 2359304 | tf_op jit(solution)/shard_map/ppermute | solution.py:923
  219.4 29.8 %collective-permute-start.50 = (bf16[2,576,384]{2,1,0:T(8,128)(2,1)}, bf16[2,576,384]{2,1,0:T(8,128)(2,1)}, u32[]{:S(2)}, u32[]{:S(2)}) collective-permute-start(bf16[2,576,384]{2,1,0:T(8,128)(2,1)} %collective-permute-done.39.refs_5_), channel_id=1, source_target_pairs={{0,1},{1,0},{2,3},{3,2},{4,5},{5,4},{6,7},{7,6},{8,9},{9,8},{10,11... | collective-permute-start | bytes 2654216 | tf_op jit(solution)/shard_map/ppermute | solution.py:926
  252.6 34.6 %collective-permute-start.56 = (bf16[544,768]{1,0:T(8,128)(2,1)}, bf16[544,768]{1,0:T(8,128)(2,1)}, u32[]{:S(2)}, u32[]{:S(2)}) collective-permute-start(bf16[544,768]{1,0:T(8,128)(2,1)} %add_convert_fusion.7), channel_id=1, source_target_pairs={{0,8},{4,12},{8,16},{12,20},{16,24},{20,28},{24,0},{28,4},{1,9},{5... | collective-permute-start | bytes 2506760 | tf_op jit(solution)/shard_map/ppermute | solution.py:917
  258.4 28.7 %collective-permute-start.58 = (bf16[512,384]{1,0:T(8,128)(2,1)}, bf16[512,384]{1,0:T(8,128)(2,1)S(1)}, u32[]{:S(2)}, u32[]{:S(2)}) collective-permute-start(bf16[512,384]{1,0:T(8,128)(2,1)} %get-tuple-element.652), channel_id=1, source_target_pairs={{0,4},{4,0},{8,12},{12,8},{16,20},{20,16},{24,28},{28,24},{1,5},{5... | collective-permute-start | bytes 1179656 | tf_op jit(solution)/shard_map/ppermute | solution.py:920
  260.9 26.9 %collective-permute-start.55 = (bf16[544,768]{1,0:T(8,128)(2,1)}, bf16[544,768]{1,0:T(8,128)(2,1)}, u32[]{:S(2)}, u32[]{:S(2)}) collective-permute-start(bf16[544,768]{1,0:T(8,128)(2,1)} %get-tuple-element.658), channel_id=1, source_target_pairs={{0,4},{4,0},{8,12},{12,8},{16,20},{20,16},{24,28},{28,24},{1,5},{5... | collective-permute-start | bytes 2506760 | tf_op jit(solution)/shard_map/ppermute | solution.py:920
  263.2 23.9 %collective-permute-start.57 = (bf16[2,512,384]{2,1,0:T(8,128)(2,1)}, bf16[2,512,384]{2,1,0:T(8,128)(2,1)}, u32[]{:S(2)}, u32[]{:S(2)}) collective-permute-start(bf16[2,512,384]{2,1,0:T(8,128)(2,1)} %add_convert_fusion.15), channel_id=1, source_target_pairs={{0,2},{1,3},{2,0},{3,1},{4,6},{5,7},{6,4},{7,5},{8,10},{9,11},{10,... | collective-permute-start | bytes 2359304 | tf_op jit(solution)/shard_map/ppermute | solution.py:923
  288.3 30.4 %collective-permute-start.63 = (bf16[2,544,768]{2,1,0:T(8,128)(2,1)}, bf16[2,544,768]{2,1,0:T(8,128)(2,1)S(1)}, u32[]{:S(2)}, u32[]{:S(2)}) collective-permute-start(bf16[2,544,768]{2,1,0:T(8,128)(2,1)} %get-tuple-element.459), channel_id=1, source_target_pairs={{0,1},{1,0},{2,3},{3,2},{4,5},{5,4},{6,7},{7,6},{8,9},{9,8},{10,11... | collective-permute-start | bytes 5013512 | tf_op jit(solution)/shard_map/ppermute | solution.py:926
  293.8 27.7 %collective-permute-start.65 = (bf16[2,512,768]{2,1,0:T(8,128)(2,1)}, bf16[2,512,768]{2,1,0:T(8,128)(2,1)S(1)}, u32[]{:S(2)}, u32[]{:S(2)}) collective-permute-start(bf16[2,512,768]{2,1,0:T(8,128)(2,1)} %get-tuple-element.463), channel_id=1, source_target_pairs={{0,1},{1,0},{2,3},{3,2},{4,5},{5,4},{6,7},{7,6},{8,9},{9,8},{10,11... | collective-permute-start | bytes 4718600 | tf_op jit(solution)/shard_map/ppermute | solution.py:926
  296.1 23.0 %collective-permute-start.62 = (bf16[544,768]{1,0:T(8,128)(2,1)S(1)}, bf16[544,768]{1,0:T(8,128)(2,1)S(1)}, u32[]{:S(2)}, u32[]{:S(2)}) collective-permute-start(bf16[544,768]{1,0:T(8,128)(2,1)S(1)} %add_convert_fusion.4), channel_id=1, source_target_pairs={{0,8},{4,12},{8,16},{12,20},{16,24},{20,28},{24,0},{28,4},{1,9},{5... | collective-permute-start | bytes 2506760 | tf_op jit(solution)/shard_map/ppermute | solution.py:917
  298.7 22.9 %collective-permute-start.61 = (bf16[544,768]{1,0:T(8,128)(2,1)S(1)}, bf16[544,768]{1,0:T(8,128)(2,1)S(1)}, u32[]{:S(2)}, u32[]{:S(2)}) collective-permute-start(bf16[544,768]{1,0:T(8,128)(2,1)S(1)} %get-tuple-element.656), channel_id=1, source_target_pairs={{0,4},{4,0},{8,12},{12,8},{16,20},{20,16},{24,28},{28,24},{1,5},{5... | collective-permute-start | bytes 2506760 | tf_op jit(solution)/shard_map/ppermute | solution.py:920
  302.0 19.6 %collective-permute-start.64 = (bf16[2,512,384]{2,1,0:T(8,128)(2,1)}, bf16[2,512,384]{2,1,0:T(8,128)(2,1)}, u32[]{:S(2)}, u32[]{:S(2)}) collective-permute-start(bf16[2,512,384]{2,1,0:T(8,128)(2,1)} %add_convert_fusion.14), channel_id=1, source_target_pairs={{0,2},{1,3},{2,0},{3,1},{4,6},{5,7},{6,4},{7,5},{8,10},{9,11},{10,... | collective-permute-start | bytes 2359304 | tf_op jit(solution)/shard_map/ppermute | solution.py:923
  322.9 21.4 %collective-permute-start.66 = (bf16[544,768]{1,0:T(8,128)(2,1)S(1)}, bf16[544,768]{1,0:T(8,128)(2,1)S(1)}, u32[]{:S(2)}, u32[]{:S(2)}) collective-permute-start(bf16[544,768]{1,0:T(8,128)(2,1)S(1)} %get-tuple-element.654), channel_id=1, source_target_pairs={{0,4},{4,0},{8,12},{12,8},{16,20},{20,16},{24,28},{28,24},{1,5},{5... | collective-permute-start | bytes 2506760 | tf_op jit(solution)/shard_map/ppermute | solution.py:920
  324.2 21.4 %collective-permute-start.67 = (bf16[544,768]{1,0:T(8,128)(2,1)S(1)}, bf16[544,768]{1,0:T(8,128)(2,1)S(1)}, u32[]{:S(2)}, u32[]{:S(2)}) collective-permute-start(bf16[544,768]{1,0:T(8,128)(2,1)S(1)} %add_convert_fusion.1), channel_id=1, source_target_pairs={{0,8},{4,12},{8,16},{12,20},{16,24},{20,28},{24,0},{28,4},{1,9},{5... | collective-permute-start | bytes 2506760 | tf_op jit(solution)/shard_map/ppermute | solution.py:917
  326.3 18.0 %collective-permute-start.68 = (bf16[2,512,384]{2,1,0:T(8,128)(2,1)S(1)}, bf16[2,512,384]{2,1,0:T(8,128)(2,1)S(1)}, u32[]{:S(2)}, u32[]{:S(2)}) collective-permute-start(bf16[2,512,384]{2,1,0:T(8,128)(2,1)S(1)} %add_convert_fusion.13), channel_id=1, source_target_pairs={{0,2},{1,3},{2,0},{3,1},{4,6},{5,7},{6,4},{7,5},{8,10},{9,11},{10,... | collective-permute-start | bytes 2359304 | tf_op jit(solution)/shard_map/ppermute | solution.py:923
  345.9 20.6 %collective-permute-start.69 = (bf16[544,768]{1,0:T(8,128)(2,1)S(1)}, bf16[544,768]{1,0:T(8,128)(2,1)S(1)}, u32[]{:S(2)}, u32[]{:S(2)}) collective-permute-start(bf16[544,768]{1,0:T(8,128)(2,1)S(1)} %add_convert_fusion), channel_id=1, source_target_pairs={{0,2},{1,3},{2,0},{3,1},{4,6},{5,7},{6,4},{7,5},{8,10},{9,11},{10,... | collective-permute-start | bytes 2506760 | tf_op jit(solution)/shard_map/ppermute | solution.py:923
  348.9 12.1 %collective-permute-start.70 = (bf16[512,384]{1,0:T(8,128)(2,1)S(1)}, bf16[512,384]{1,0:T(8,128)(2,1)S(1)}, u32[]{:S(2)}, u32[]{:S(2)}) collective-permute-start(bf16[512,384]{1,0:T(8,128)(2,1)S(1)} %get-tuple-element.650), channel_id=1, source_target_pairs={{0,4},{4,0},{8,12},{12,8},{16,20},{20,16},{24,28},{28,24},{1,5},{5... | collective-permute-start | bytes 1179656 | tf_op jit(solution)/shard_map/ppermute | solution.py:920
  351.3 15.2 %collective-permute-start.71 = (bf16[512,384]{1,0:T(8,128)(2,1)S(1)}, bf16[512,384]{1,0:T(8,128)(2,1)S(1)}, u32[]{:S(2)}, u32[]{:S(2)}) collective-permute-start(bf16[512,384]{1,0:T(8,128)(2,1)S(1)} %get-tuple-element.648), channel_id=1, source_target_pairs={{0,4},{4,0},{8,12},{12,8},{16,20},{20,16},{24,28},{28,24},{1,5},{5... | collective-permute-start | bytes 1179656 | tf_op jit(solution)/shard_map/ppermute | solution.py:920
  369.9 13.0 %collective-permute-start.73 = (bf16[512,384]{1,0:T(8,128)(2,1)S(1)}, bf16[512,384]{1,0:T(8,128)(2,1)S(1)}, u32[]{:S(2)}, u32[]{:S(2)}) collective-permute-start(bf16[512,384]{1,0:T(8,128)(2,1)S(1)} %add_convert_fusion.22), channel_id=1, source_target_pairs={{0,8},{4,12},{8,16},{12,20},{16,24},{20,28},{24,0},{28,4},{1,9},{5... | collective-permute-start | bytes 1179656 | tf_op jit(solution)/shard_map/ppermute | solution.py:917
  382.9 14.5 %collective-permute-start.75 = (bf16[3,192,512]{2,1,0:T(8,128)(2,1)S(1)}, bf16[3,192,512]{2,1,0:T(8,128)(2,1)S(1)}, u32[]{:S(2)}, u32[]{:S(2)}) collective-permute-start(bf16[3,192,512]{2,1,0:T(8,128)(2,1)S(1)} %get-tuple-element.545), channel_id=1, source_target_pairs={{0,4},{4,0},{8,12},{12,8},{16,20},{20,16},{24,28},{28,24},{1,5},{5... | collective-permute-start | bytes 1769480 | tf_op jit(solution)/shard_map/ppermute | solution.py:920
  383.9 13.6 %collective-permute-start.76 = (bf16[512,384]{1,0:T(8,128)(2,1)S(1)}, bf16[512,384]{1,0:T(8,128)(2,1)S(1)}, u32[]{:S(2)}, u32[]{:S(2)}) collective-permute-start(bf16[512,384]{1,0:T(8,128)(2,1)S(1)} %add_convert_fusion.19), channel_id=1, source_target_pairs={{0,8},{4,12},{8,16},{12,20},{16,24},{20,28},{24,0},{28,4},{1,9},{5... | collective-permute-start | bytes 1179656 | tf_op jit(solution)/shard_map/ppermute | solution.py:917
  399.1 22.8 %collective-permute-start.83 = (bf16[512,384]{1,0:T(8,128)(2,1)S(1)}, bf16[512,384]{1,0:T(8,128)(2,1)S(1)}, u32[]{:S(2)}, u32[]{:S(2)}) collective-permute-start(bf16[512,384]{1,0:T(8,128)(2,1)S(1)} %add_convert_fusion.18), channel_id=1, source_target_pairs={{0,8},{4,12},{8,16},{12,20},{16,24},{20,28},{24,0},{28,4},{1,9},{5... | collective-permute-start | bytes 1179656 | tf_op jit(solution)/shard_map/ppermute | solution.py:917
  407.2 13.8 %collective-permute-start.79 = (bf16[2,208,640]{2,1,0:T(8,128)(2,1)S(1)}, bf16[2,208,640]{2,1,0:T(8,128)(2,1)S(1)}, u32[]{:S(2)}, u32[]{:S(2)}) collective-permute-start(bf16[2,208,640]{2,1,0:T(8,128)(2,1)S(1)} %get-tuple-element.559), channel_id=1, source_target_pairs={{0,4},{4,0},{8,12},{12,8},{16,20},{20,16},{24,28},{28,24},{1,5},{5... | collective-permute-start | bytes 1597448 | tf_op jit(solution)/shard_map/ppermute | solution.py:920
  408.3 15.3 %collective-permute-start.82 = (bf16[512,512]{1,0:T(8,128)(2,1)S(1)}, bf16[512,512]{1,0:T(8,128)(2,1)S(1)}, u32[]{:S(2)}, u32[]{:S(2)}) collective-permute-start(bf16[512,512]{1,0:T(8,128)(2,1)S(1)} %maximum_maximum_fusion), channel_id=1, source_target_pairs={{0,2},{1,3},{2,0},{3,1},{4,6},{5,7},{6,4},{7,5},{8,10},{9,11},{10,... | collective-permute-start | bytes 1572872 | tf_op jit(solution)/shard_map/ppermute | solution.py:923
  410.0 13.5 %collective-permute-start.80 = (bf16[208,640]{1,0:T(8,128)(2,1)S(1)}, bf16[208,640]{1,0:T(8,128)(2,1)S(1)}, u32[]{:S(2)}, u32[]{:S(2)}) collective-permute-start(bf16[208,640]{1,0:T(8,128)(2,1)S(1)} %add_convert_fusion.31), channel_id=1, source_target_pairs={{0,8},{4,12},{8,16},{12,20},{16,24},{20,28},{24,0},{28,4},{1,9},{5... | collective-permute-start | bytes 798728 | tf_op jit(solution)/shard_map/ppermute | solution.py:917
  410.3 13.3 %collective-permute-start.81 = (bf16[192,512]{1,0:T(8,128)(2,1)S(1)}, bf16[192,512]{1,0:T(8,128)(2,1)S(1)}, u32[]{:S(2)}, u32[]{:S(2)}) collective-permute-start(bf16[192,512]{1,0:T(8,128)(2,1)S(1)} %add_convert_fusion.34), channel_id=1, source_target_pairs={{0,8},{4,12},{8,16},{12,20},{16,24},{20,28},{24,0},{28,4},{1,9},{5... | collective-permute-start | bytes 589832 | tf_op jit(solution)/shard_map/ppermute | solution.py:917
  423.6 13.1 %collective-permute-start.84 = (bf16[1,208,640]{2,1,0:T(8,128)(2,1)S(1)}, bf16[1,208,640]{2,1,0:T(8,128)(2,1)S(1)}, u32[]{:S(2)}, u32[]{:S(2)}) collective-permute-start(bf16[1,208,640]{2,1,0:T(8,128)(2,1)S(1)} %get-tuple-element.569), channel_id=1, source_target_pairs={{0,4},{4,0},{8,12},{12,8},{16,20},{20,16},{24,28},{28,24},{1,5},{5... | collective-permute-start | bytes 798728 | tf_op jit(solution)/shard_map/ppermute | solution.py:920
  424.3 12.3 %collective-permute-start.85 = (bf16[208,640]{1,0:T(8,128)(2,1)S(1)}, bf16[208,640]{1,0:T(8,128)(2,1)S(1)}, u32[]{:S(2)}, u32[]{:S(2)}) collective-permute-start(bf16[208,640]{1,0:T(8,128)(2,1)S(1)} %add_convert_fusion.30), channel_id=1, source_target_pairs={{0,8},{4,12},{8,16},{12,20},{16,24},{20,28},{24,0},{28,4},{1,9},{5... | collective-permute-start | bytes 798728 | tf_op jit(solution)/shard_map/ppermute | solution.py:917
  424.5 12.2 %collective-permute-start.87 = (bf16[192,512]{1,0:T(8,128)(2,1)S(1)}, bf16[192,512]{1,0:T(8,128)(2,1)S(1)}, u32[]{:S(2)}, u32[]{:S(2)}) collective-permute-start(bf16[192,512]{1,0:T(8,128)(2,1)S(1)} %add_convert_fusion.33), channel_id=1, source_target_pairs={{0,8},{4,12},{8,16},{12,20},{16,24},{20,28},{24,0},{28,4},{1,9},{5... | collective-permute-start | bytes 589832 | tf_op jit(solution)/shard_map/ppermute | solution.py:917
  (122 other events, 1238.5 us)
